TPU v7x, 256 devices: a whole 4x4x8 slice. The times are simulated.
256 devices in a mesh: row: 8 (over x, core), col: 32 (over y, z).
Axes of the slice: x: 4, y: 4, z: 8, core: 2. Of those that a mesh axis runs over, the one named last changes fastest.
Arguments:
- tokens: bfloat16 [1024, 8192], P('col', 'row'), may hold values from -6 to 6
- gate_weight: bfloat16 [8192, 16384], P('row', 'col'), may hold values from -0.0625 to 0.0625
- up_weight: bfloat16 [8192, 16384], P('row', 'col'), may hold values from -0.0625 to 0.0625
- down_weight: bfloat16 [16384, 8192], P('col', 'row'), may hold values from -0.046875 to 0.046875
- out_grad: bfloat16 [1024, 8192], P('col', 'row'), may hold values from -1.5 to 1.5
Outputs:
- layer_output: bfloat16 [1024, 8192], P('col', 'row')
- input_grad: bfloat16 [1024, 8192], P('col', 'row')
- gate_weight_grad: float32 [8192, 16384], P('row', 'col')
- up_weight_grad: float32 [8192, 16384], P('row', 'col')
- down_weight_grad: float32 [16384, 8192], P('col', 'row')
All inputs are finite; a program needn't handle non-finite values.
Results may differ from a plain program's by a relative error of at most 0.022.
Values may be sent and summed in bfloat16 or wider, within the bound.
No kernel may reach another device: no remote copies, remote signals or barrier semaphores. Data moves between devices by JAX's collectives and lax.ppermute only.
A program may use at most 64 MiB of HBM per device.

v0:
```python
import jax
import jax.numpy as jnp
from jax import lax
from jax.sharding import PartitionSpec as P


def product(left_side, right_side):
    return jnp.dot(left_side, right_side, preferred_element_type=jnp.float32)


def product_right_t(left_side, right_side):
    return lax.dot_general(
        left_side, right_side, (((1,), (1,)), ((), ())), preferred_element_type=jnp.float32
    )


def product_left_t(left_side, right_side):
    return lax.dot_general(
        left_side, right_side, (((0,), (0,)), ((), ())), preferred_element_type=jnp.float32
    )


def gather_tokens(shard_block):
    return lax.all_gather(shard_block, "col", axis=0, tiled=True)


def gather_shares(stacked):
    return lax.all_gather(stacked, "row", axis=1, tiled=True)


def sum_over_rows(make_term, keep_rows):
    return lax.psum_scatter(
        make_term(jnp.int32(0), keep_rows * lax.axis_size("row")),
        "row",
        scatter_dimension=0,
        tiled=True,
    )


def sum_over_cols(make_term, keep_rows):
    return lax.psum_scatter(
        make_term(jnp.int32(0), lax.axis_size("col") * keep_rows).astype(jnp.bfloat16),
        "col",
        scatter_dimension=0,
        tiled=True,
    ).astype(jnp.float32)


def body(tokens, gate_weight, up_weight, down_weight, out_grad):
    hidden_width = gate_weight.shape[1]
    gathered = gather_tokens(tokens)
    all_tokens = gathered.shape[0]
    share_rows = all_tokens // lax.axis_size("row")
    output_rows = all_tokens // lax.axis_size("col")

    def gate_terms(first_row, row_count):
        return jnp.concatenate(
            [product(gathered, gate_weight), product(gathered, up_weight)], axis=1
        )

    gate_up = sum_over_rows(gate_terms, share_rows)
    gate_value = gate_up[:, :hidden_width]
    up_value = gate_up[:, hidden_width:]
    sigmoid_gate = jax.nn.sigmoid(gate_value)
    silu_gate = gate_value * sigmoid_gate
    hidden = (silu_gate * up_value).astype(jnp.bfloat16)
    hidden_all = gather_shares(hidden[None])[0]

    def output_terms(first_row, row_count):
        return product(hidden_all, down_weight)

    layer_output = sum_over_cols(output_terms, output_rows).astype(jnp.bfloat16)
    grads_all = gather_tokens(out_grad)

    def hidden_terms(first_row, row_count):
        return product_right_t(grads_all, down_weight)

    hidden_grad = sum_over_rows(hidden_terms, share_rows)
    gate_grad = (
        hidden_grad * up_value * sigmoid_gate * (1.0 + gate_value * (1.0 - sigmoid_gate))
    ).astype(jnp.bfloat16)
    up_grad = (hidden_grad * silu_gate).astype(jnp.bfloat16)
    grads_both = gather_shares(jnp.stack([gate_grad, up_grad]))

    def input_terms(first_row, row_count):
        gate_rows = grads_both[0]
        up_rows = grads_both[1]
        return product_right_t(gate_rows, gate_weight) + product_right_t(up_rows, up_weight)

    input_grad = sum_over_cols(input_terms, output_rows).astype(jnp.bfloat16)
    tokens_later, hidden_later, input_grad = lax.optimization_barrier((tokens, hidden, input_grad))
    gathered = gather_tokens(tokens_later)
    hidden_all = gather_shares(hidden_later[None])[0]
    gate_weight_grad = product_left_t(gathered, grads_both[0])
    up_weight_grad = product_left_t(gathered, grads_both[1])
    down_weight_grad = product_left_t(hidden_all, grads_all)
    return (layer_output, input_grad, gate_weight_grad, up_weight_grad, down_weight_grad)


def solution(mesh):
    in_specs = (P("col", "row"), P("row", "col"), P("row", "col"), P("col", "row"), P("col", "row"))
    out_specs = (
        P("col", "row"),
        P("col", "row"),
        P("row", "col"),
        P("row", "col"),
        P("col", "row"),
    )
    return jax.shard_map(body, mesh=mesh, in_specs=in_specs, out_specs=out_specs, check_vma=False)
```

profile of v0, /device:TPU:2, one launch (start us, length us, event | category | flops | bytes accessed | tf_op | source)
XLA Modules:
  0.0 865.4 jit_solution(9351332811908970550)
XLA Ops:
  7.2 0.7 all-gather.11.cloned.1.call-update
  8.0 0.7 all-gather.9.cloned.1.call-update
  8.7 0.0 reduce-scatter.9.cloned.1.call-start
  8.7 82.8 %all-gather.11.cloned.1.call-done = bf16[1024,1024]{1,0:T(8,128)(2,1)} async-done(((bf16[32,1024]{1,0:T(8,128)(2,1)}), bf16[1024,1024]{1,0:T(8,128)(2,1)}) %all-gather.11.cloned.1.call-update) | async-done | bytes 2097168 | tf_op jit(solution)/shard_map/all_gather | solution.py:24
  91.5 4.5 fusion.8
  96.0 0.0 reduce-scatter.5.cloned.1.call-start
  96.0 73.2 %all-gather.9.cloned.1.call-done = bf16[1024,1024]{1,0:T(8,128)(2,1)} async-done(((bf16[32,1024]{1,0:T(8,128)(2,1)}), bf16[1024,1024]{1,0:T(8,128)(2,1)}) %all-gather.9.cloned.1.call-update) | async-done | bytes 2097168 | tf_op jit(solution)/shard_map/all_gather | solution.py:24
  169.3 3.0 fusion.7
  172.3 1.3 fusion.6
  173.7 2.5 pad_maximum_fusion
  176.2 0.0 all-gather.13.cloned.1.call-start
  176.2 26.3 %reduce-scatter.9.cloned.1.call-done = f32[128,512]{0,1:T(8,128)} async-done(((f32[1024,512]{0,1:T(8,128)}), f32[128,512]{0,1:T(8,128)}) %reduce-scatter.9.cloned.1.call-update) | async-done | bytes 262160 | tf_op jit(solution)/shard_map/reduce_scatter | solution.py:32
  202.5 41.4 %reduce-scatter.5.cloned.1.call-done = f32[128,1024]{0,1:T(8,128)} async-done(((f32[1024,1024]{0,1:T(8,128)}), f32[128,1024]{0,1:T(8,128)}) %reduce-scatter.5.cloned.1.call-update) | async-done | bytes 524304 | tf_op jit(solution)/shard_map/reduce_scatter | solution.py:32
  243.9 1.9 fusion.5
  245.8 0.7 pad_maximum_fusion.1
  246.6 0.0 reduce-scatter.11.cloned.1.call-start
  246.6 32.0 %all-gather.13.cloned.1.call-done = bf16[2,1024,512]{1,2,0:T(8,128)(2,1)} async-done(((bf16[2,128,512]{1,2,0:T(8,128)(2,1)}), bf16[2,1024,512]{1,2,0:T(8,128)(2,1)}) %all-gather.13.cloned.1.call-update) | async-done | bytes 2097168 | tf_op jit(solution)/shard_map/all_gather | solution.py:28
  278.6 2.7 fusion.1
  281.3 2.7 add_convert_fusion
  284.0 0.0 all-gather.17.cloned.1.call-start
  284.0 0.7 all-gather.17.cloned.1.call-update
  284.8 217.3 %reduce-scatter.11.cloned.1.call-done = bf16[32,1024]{1,0:T(8,128)(2,1)} async-done(((bf16[1024,1024]{1,0:T(8,128)(2,1)}), bf16[32,1024]{1,0:T(8,128)(2,1)}) %reduce-scatter.11.cloned.1.call-update) | async-done | bytes 65552 | tf_op jit(solution)/shard_map/reduce_scatter | solution.py:41
  502.2 0.7 all-gather.15.cloned.1.call-update
  502.8 0.2 reduce-scatter.7.cloned.1.call-start
  503.1 25.1 %all-gather.17.cloned.1.call-done = bf16[1024,512]{0,1:T(8,128)(2,1)} async-done(((bf16[128,512]{0,1:T(8,128)(2,1)}), bf16[1024,512]{0,1:T(8,128)(2,1)}) %all-gather.17.cloned.1.call-update) | async-done | bytes 1048592 | tf_op jit(solution)/shard_map/all_gather | solution.py:28
  528.2 3.9 convolution_convert_fusion
  532.1 25.5 %all-gather.19.cloned.1.call-done = bf16[1024,512]{0,1:T(8,128)(2,1)} async-done(((bf16[128,512]{0,1:T(8,128)(2,1)}), bf16[1024,512]{0,1:T(8,128)(2,1)}) %all-gather.19.cloned.1.call-update) | async-done | bytes 1048592 | tf_op jit(solution)/shard_map/all_gather | solution.py:28
  557.6 4.5 fusion.9
  562.1 78.0 %all-gather.15.cloned.1.call-done = bf16[1024,1024]{1,0:T(8,128)(2,1)} async-done(((bf16[32,1024]{1,0:T(8,128)(2,1)}), bf16[1024,1024]{1,0:T(8,128)(2,1)}) %all-gather.15.cloned.1.call-update) | async-done | bytes 2097168 | tf_op jit(solution)/shard_map/all_gather | solution.py:24
  640.2 4.4 fusion.2
  644.5 2.6 fusion
  647.2 211.4 %reduce-scatter.7.cloned.1.call-done = bf16[32,1024]{1,0:T(8,128)(2,1)} async-done(((bf16[1024,1024]{1,0:T(8,128)(2,1)}), bf16[32,1024]{1,0:T(8,128)(2,1)}) %reduce-scatter.7.cloned.1.call-update) | async-done | bytes 65552 | tf_op jit(solution)/shard_map/reduce_scatter | solution.py:41
  (24 shorter events, 0.3 us)
Async XLA Ops:
  7.2 165.2 %copy-start = (bf16[1024,512]{1,0:T(8,128)(2,1)S(1)}, bf16[1024,512]{1,0:T(8,128)(2,1)}, u32[]{:S(2)}) copy-start(bf16[1024,512]{1,0:T(8,128)(2,1)} %param.6) | copy-start | bytes 3145732
  7.2 84.3 %all-gather.11.cloned.1.call-start = ((), (), s32[]{:S(2)}) async-start(), calls=%async_computation.7 | async-start | bytes 2162688 | tf_op jit(solution)/shard_map/all_gather | solution.py:24
  7.9 161.4 %all-gather.9.cloned.1.call-start = ((), (), s32[]{:S(2)}) async-start(), calls=%async_computation.4 | async-start | bytes 2162688 | tf_op jit(solution)/shard_map/all_gather | solution.py:24
  8.7 193.8 %reduce-scatter.9.cloned.1.call-start = ((), (), s32[]{:S(2)}) async-start(), calls=%async_computation.8 | async-start | bytes 2359296 | tf_op jit(solution)/shard_map/reduce_scatter | solution.py:32
  96.0 73.3 %copy-start.1 = (bf16[1024,512]{1,0:T(8,128)(2,1)S(1)}, bf16[1024,512]{1,0:T(8,128)(2,1)}, u32[]{:S(2)}) copy-start(bf16[1024,512]{1,0:T(8,128)(2,1)} %param.7) | copy-start | bytes 3145732
  96.0 147.9 %reduce-scatter.5.cloned.1.call-start = ((), (), s32[]{:S(2)}) async-start(), calls=%async_computation.5 | async-start | bytes 4718592 | tf_op jit(solution)/shard_map/reduce_scatter | solution.py:32
  169.3 3.1 copy-start.5
  176.2 102.5 %all-gather.13.cloned.1.call-start = ((), (), s32[]{:S(2)}) async-start(), calls=%async_computation.9 | async-start | bytes 2359296 | tf_op jit(solution)/shard_map/all_gather | solution.py:28
  246.6 255.5 %reduce-scatter.11.cloned.1.call-start = ((), (), s32[]{:S(2)}) async-start(), calls=%async_computation.10 | async-start | bytes 2162688 | tf_op jit(solution)/shard_map/reduce_scatter | solution.py:41
  278.6 2.7 copy-start.2
  284.0 244.2 %copy-start.6 = (bf16[512,1024]{1,0:T(8,128)(2,1)S(1)}, bf16[512,1024]{1,0:T(8,128)(2,1)}, u32[]{:S(2)}) copy-start(bf16[512,1024]{1,0:T(8,128)(2,1)} %param.8) | copy-start | bytes 3145732
  284.0 244.2 %all-gather.17.cloned.1.call-start = ((), (), s32[]{:S(2)}) async-start(), calls=%async_computation.12 | async-start | bytes 1179648 | tf_op jit(solution)/shard_map/all_gather | solution.py:28
  284.7 272.9 %all-gather.19.cloned.1.call-start = ((), (), s32[]{:S(2)}) async-start(), calls=%async_computation.13 | async-start | bytes 1179648 | tf_op jit(solution)/shard_map/all_gather | solution.py:28
  502.1 138.0 %all-gather.15.cloned.1.call-start = ((), (), s32[]{:S(2)}) async-start(), calls=%async_computation.11 | async-start | bytes 2162688 | tf_op jit(solution)/shard_map/all_gather | solution.py:24
  502.8 355.7 %reduce-scatter.7.cloned.1.call-start = ((), (), s32[]{:S(2)}) async-start(), calls=%async_computation.6 | async-start | bytes 2162688 | tf_op jit(solution)/shard_map/reduce_scatter | solution.py:41
  532.1 108.1 %copy-start.3 = (bf16[2,1024,512]{1,2,0:T(8,128)(2,1)S(1)}, bf16[2,1024,512]{1,2,0:T(8,128)(2,1)}, u32[]{:S(2)}) copy-start(bf16[2,1024,512]{1,2,0:T(8,128)(2,1)} %all-gather.13.cloned.1.call-done) | copy-start | bytes 6291460
  640.2 4.4 copy-start.4
Sparse Core Ops, SparseCore 0:
  10.6 80.8 all-gather.10
  94.1 75.1 all-gather.8
  172.4 30.0 reduce-scatter.8
  204.9 38.9 reduce-scatter.4
  246.7 31.8 all-gather.12
  284.1 217.9 reduce-scatter.10
  504.6 23.4 all-gather.16
  530.7 26.8 all-gather.18
  560.6 79.5 all-gather.14
  644.9 213.5 reduce-scatter.6
where the time goes:
time: 866 us; the launch traced here: 865 us
  waiting for transfers between devices  816 us (94%)
  matrix products  29.5 us (3%)
  between operations  14.2 us (2%)
    reduce_scatter x2, waiting for transfers between devices, sum_over_cols(): lax.psum_scatter(make_term(jnp.int32(0), lax.axis_size('col') * keep_rows...  429 us
    all_gather x3, waiting for transfers between devices, gather_tokens(): return lax.all_gather(shard_block, 'col', axis=0, tiled=True)  234 us
    all_gather x3, waiting for transfers between devices, gather_shares(): return lax.all_gather(stacked, 'row', axis=1, tiled=True)  82.6 us
    reduce_scatter x2, waiting for transfers between devices, sum_over_rows(): lax.psum_scatter(make_term(jnp.int32(0), keep_rows * lax.axis_size('row')...  67.7 us
  transfers between devices with their start and end apart: 10, of which 10 were waited for; matrix products, arithmetic and copies ran while one was open for 3% of the time, Pallas kernels for 0%

commit v1 on v0

v1 whole, which is shorter than its diff:
```python
import jax
import jax.numpy as jnp
from jax import lax
from jax.sharding import Mesh, PartitionSpec as P

BF = jnp.bfloat16
F32 = jnp.float32
X, CORE, Y, Z = 4, 2, 4, 8


def product(left_side, right_side):
    return jnp.dot(left_side, right_side, preferred_element_type=F32)


def product_right_t(left_side, right_side):
    return lax.dot_general(left_side, right_side, (((1,), (1,)), ((), ())), preferred_element_type=F32)


def product_left_t(left_side, right_side):
    return lax.dot_general(left_side, right_side, (((0,), (0,)), ((), ())), preferred_element_type=F32)


def shift(block, axis, size, step):
    return lax.ppermute(block, axis, [(i, (i + step) % size) for i in range(size)])


def exchange(blocks, axis):
    return lax.all_to_all(blocks, axis, split_axis=0, concat_axis=0, tiled=True)


def gather_z(block):
    rows, width = block.shape
    copies = jnp.broadcast_to(block[None], (Z, rows, width)).reshape(Z * rows, width)
    return exchange(copies, "z")


def gather_y(block):
    return [block, shift(block, "y", Y, 1), shift(block, "y", Y, 3), shift(block, "y", Y, 2)]


def gather_col(block):
    own, one, three, two = gather_y(gather_z(block))
    return jnp.concatenate([own, one, two, three], axis=0)


def sum_parts(parts, count):
    rows = parts.shape[0] // count
    return jnp.sum(parts.reshape((count, rows) + parts.shape[1:]).astype(F32), axis=0)


def reduce_row(partial):
    pair = sum_parts(exchange(partial, "core"), CORE).astype(BF)
    return sum_parts(exchange(pair, "x"), X)


def gather_row(share):
    return lax.all_gather(lax.all_gather(share, "x", axis=0, tiled=True), "core", axis=0, tiled=True)


def reduce_col(partial):
    rows = partial.shape[0] // Y
    pieces = [partial[j * rows : (j + 1) * rows] for j in range(Y)]
    total = (
        pieces[0].astype(F32)
        + shift(pieces[1], "y", Y, 3).astype(F32)
        + shift(pieces[3], "y", Y, 1).astype(F32)
        + shift(pieces[2], "y", Y, 2).astype(F32)
    ).astype(BF)
    return sum_parts(exchange(total, "z"), Z).astype(BF)


def body(tokens, gate_weight, up_weight, down_weight, out_grad):
    width = gate_weight.shape[1]
    all_tokens = gather_col(tokens)
    all_grads = gather_col(out_grad)
    partial = jnp.concatenate(
        [product(all_tokens, gate_weight).astype(BF), product(all_tokens, up_weight).astype(BF)], axis=1
    )
    gate_up = reduce_row(partial)
    gate_value = gate_up[:, :width]
    up_value = gate_up[:, width:]
    sigmoid_gate = jax.nn.sigmoid(gate_value)
    silu_gate = gate_value * sigmoid_gate
    hidden = gather_row((silu_gate * up_value).astype(BF))
    layer_output = reduce_col(product(hidden, down_weight).astype(BF))

    hidden_grad = reduce_row(product_right_t(all_grads, down_weight).astype(BF))
    gate_grad = (hidden_grad * up_value * sigmoid_gate * (1.0 + gate_value * (1.0 - sigmoid_gate))).astype(BF)
    up_grad = (hidden_grad * silu_gate).astype(BF)
    both = gather_row(jnp.concatenate([gate_grad, up_grad], axis=1))
    gate_grads = both[:, :width]
    up_grads = both[:, width:]
    input_partial = product_right_t(gate_grads, gate_weight) + product_right_t(up_grads, up_weight)
    input_grad = reduce_col(input_partial.astype(BF))
    gate_weight_grad = product_left_t(all_tokens, gate_grads)
    up_weight_grad = product_left_t(all_tokens, up_grads)
    down_weight_grad = product_left_t(hidden, all_grads)
    return (layer_output, input_grad, gate_weight_grad, up_weight_grad, down_weight_grad)


def solution(mesh):
    grid = Mesh(mesh.devices.reshape(X, CORE, Y, Z), ("x", "core", "y", "z"))
    row, col = ("x", "core"), ("y", "z")
    in_specs = (P(col, row), P(row, col), P(row, col), P(col, row), P(col, row))
    out_specs = (P(col, row), P(col, row), P(row, col), P(row, col), P(col, row))
    return jax.shard_map(body, mesh=grid, in_specs=in_specs, out_specs=out_specs, check_vma=False)
```

time: 866 us -> 282 us (0.33)
  waiting for transfers between devices: 816 us -> 125 us
  starting transfers between devices: 0.58 us -> 51.4 us
  blocking collectives: 0 us -> 46.1 us
    reduce_scatter x4 -> x0, waiting for transfers between devices: 496 us -> none  [the longest x2 429 us: sum_over_cols(): lax.psum_scatter(make_term(jnp.int32(0), lax.axis_size('col') * keep_rows...]
    all_gather x6 -> x3, waiting for transfers between devices: 317 us -> 30.2 us  [the longest x2 17.9 us: gather_row(): lax.all_gather(lax.all_gather(share, 'x', axis=0, tiled=True), 'core', ax...]
    ppermute x0 -> x12, waiting for transfers between devices: none -> 65 us  [shift(): lax.ppermute(block, axis, [(i, (i + step) % size) for i in range(size)])]
    all_to_all x0 -> x2, blocking collectives: none -> 31.1 us  [exchange(): return lax.all_to_all(blocks, axis, split_axis=0, concat_axis=0, tiled=True)]
    all_to_all x0 -> x6, starting transfers between devices: none -> 30.9 us  [exchange(): return lax.all_to_all(blocks, axis, split_axis=0, concat_axis=0, tiled=True)]
    all_to_all x0 -> x6, waiting for transfers between devices: none -> 30 us  [exchange(): return lax.all_to_all(blocks, axis, split_axis=0, concat_axis=0, tiled=True)]
    ppermute x0 -> x12, starting transfers between devices: none -> 20.2 us  [shift(): lax.ppermute(block, axis, [(i, (i + step) % size) for i in range(size)])]
    all_gather x0 -> x1, blocking collectives: none -> 14.9 us  [gather_row(): lax.all_gather(share, 'x', axis=0, tiled=True)]
  transfers between devices with their start and end apart: 10 -> 21, of which waited for: 10 -> 14; matrix products, arithmetic and copies ran while one was open for 3% -> 13% of each run, Pallas kernels for 0% -> 0%
where the time goes in v1:
time: 282 us; the launch traced here: 280 us
  waiting for transfers between devices  125 us (44%)
  starting transfers between devices  51.4 us (18%)
  blocking collectives  46.1 us (16%)
  matrix products  26.2 us (9%)
  between operations  14 us (5%)
  other arithmetic  10.2 us (4%)
  local copies, waits for them, and re-layouts  7.02 us (2%)
    ppermute x12, waiting for transfers between devices, shift(): lax.ppermute(block, axis, [(i, (i + step) % size) for i in range(size)])  65 us
    all_to_all x2, blocking collectives, exchange(): return lax.all_to_all(blocks, axis, split_axis=0, concat_axis=0, tiled=True)  31.1 us
    all_to_all x6, starting transfers between devices, exchange(): return lax.all_to_all(blocks, axis, split_axis=0, concat_axis=0, tiled=True)  30.9 us
    all_to_all x6, waiting for transfers between devices, exchange(): return lax.all_to_all(blocks, axis, split_axis=0, concat_axis=0, tiled=True)  30 us
    ppermute x12, starting transfers between devices, shift(): lax.ppermute(block, axis, [(i, (i + step) % size) for i in range(size)])  20.2 us
    all_gather x2, waiting for transfers between devices, gather_row(): lax.all_gather(lax.all_gather(share, 'x', axis=0, tiled=True), 'core', ax...  17.9 us
    all_gather x1, blocking collectives, gather_row(): lax.all_gather(share, 'x', axis=0, tiled=True)  14.9 us
    dot_general x3, matrix products, product_left_t(): lax.dot_general(left_side, right_side, (((0,), (0,)), ((), ())), preferre...  12.8 us
  transfers between devices with their start and end apart: 21, of which 14 were waited for; matrix products, arithmetic and copies ran while one was open for 13% of the time, Pallas kernels for 0%

profile of v1, /device:TPU:2, one launch (start us, length us, event | category | flops | bytes accessed | tf_op | source)
XLA Modules:
  0.0 280.1 jit_solution(13352202071107221000)
XLA Ops:
  8.2 25.8 %all_to_all.72 = bf16[8,32,1024]{2,1,0:T(8,128)(2,1)S(1)} all-to-all(bf16[8,32,1024]{2,1,0:T(8,128)(2,1)S(1)} %broadcast_in_dim.4), channel_id=1, replica_groups=mesh['x'=4,'core'=2,'y'=4,'z'=8] {'z'}, dimensions={0} | all-to-all | bytes 1048576 | tf_op jit(solution)/shard_map/all_to_all | solution.py:28
  35.7 3.5 %all-to-all-start.4 = ((bf16[8,32,1024]{2,1,0:T(8,128)(2,1)}), bf16[8,32,1024]{2,1,0:T(8,128)(2,1)S(1)}, u32[]{:S(2)}, u32[]{:S(2)}) async-start(bf16[8,32,1024]{2,1,0:T(8,128)(2,1)} %broadcast_in_dim.5), calls=%async_computation.4 | async-start | bytes 1048576 | tf_op jit(solution)/shard_map/all_to_all | solution.py:28
  40.9 2.9 %collective-permute-start.1 = (bf16[256,1024]{1,0:T(8,128)(2,1)S(1)}, bf16[256,1024]{1,0:T(8,128)(2,1)}, u32[]{:S(2)}, u32[]{:S(2)}) collective-permute-start(bf16[256,1024]{1,0:T(8,128)(2,1)S(1)} %bitcast.27), channel_id=1, source_target_pairs={{0,16},{8,24},{16,0},{24,8},{1,17},{9,25},{17,1},{25,9},{2,18},{10... | collective-permute-start | bytes 1572872 | tf_op jit(solution)/shard_map/ppermute | solution.py:24
  45.1 10.0 %all-to-all-done.4 = bf16[8,32,1024]{2,1,0:T(8,128)(2,1)S(1)} async-done(((bf16[8,32,1024]{2,1,0:T(8,128)(2,1)}), bf16[8,32,1024]{2,1,0:T(8,128)(2,1)S(1)}, u32[]{:S(2)}, u32[]{:S(2)}) %all-to-all-start.4) | async-done | bytes 524320 | tf_op jit(solution)/shard_map/all_to_all | solution.py:28
  56.7 2.9 %collective-permute-start.7 = (bf16[256,1024]{1,0:T(8,128)(2,1)S(1)}, bf16[256,1024]{1,0:T(8,128)(2,1)S(1)}, u32[]{:S(2)}, u32[]{:S(2)}) collective-permute-start(bf16[256,1024]{1,0:T(8,128)(2,1)S(1)} %bitcast.34), channel_id=1, source_target_pairs={{0,16},{8,24},{16,0},{24,8},{1,17},{9,25},{17,1},{25,9},{2,18},{10... | collective-permute-start | bytes 1572872 | tf_op jit(solution)/shard_map/ppermute | solution.py:24
  61.0 7.0 %collective-permute-done.1 = bf16[256,1024]{1,0:T(8,128)(2,1)} collective-permute-done((bf16[256,1024]{1,0:T(8,128)(2,1)S(1)}, bf16[256,1024]{1,0:T(8,128)(2,1)}, u32[]{:S(2)}, u32[]{:S(2)}) %collective-permute-start.1) | collective-permute-done | bytes 524320 | tf_op jit(solution)/shard_map/ppermute | solution.py:24
  68.0 2.6 convolution_convert_fusion.2
  70.7 2.7 convolution_convert_fusion.3
  75.1 3.4 %collective-permute-done.6 = bf16[256,1024]{1,0:T(8,128)(2,1)S(1)} collective-permute-done((bf16[256,1024]{1,0:T(8,128)(2,1)S(1)}, bf16[256,1024]{1,0:T(8,128)(2,1)S(1)}, u32[]{:S(2)}, u32[]{:S(2)}) %collective-permute-start.6) | collective-permute-done | bytes 524320 | tf_op jit(solution)/shard_map/ppermute | solution.py:24
  78.5 8.9 %collective-permute-done.7 = bf16[256,1024]{1,0:T(8,128)(2,1)S(1)} collective-permute-done((bf16[256,1024]{1,0:T(8,128)(2,1)S(1)}, bf16[256,1024]{1,0:T(8,128)(2,1)S(1)}, u32[]{:S(2)}, u32[]{:S(2)}) %collective-permute-start.7) | collective-permute-done | bytes 524320 | tf_op jit(solution)/shard_map/ppermute | solution.py:24
  88.8 5.4 %all_to_all.73 = bf16[2,512,512]{2,1,0:T(8,128)(2,1)} all-to-all(bf16[2,512,512]{2,1,0:T(8,128)(2,1)S(1)} %bitcast.25), channel_id=1, replica_groups=mesh['x'=4,'core'=2,'y'=4,'z'=8] {'core'}, dimensions={0} | all-to-all | bytes 2097152 | tf_op jit(solution)/shard_map/all_to_all | solution.py:28
  94.1 3.8 %all-to-all-start.1 = ((bf16[2,512,1024]{1,2,0:T(8,128)(2,1)}), bf16[2,512,1024]{1,2,0:T(8,128)(2,1)S(1)}, u32[]{:S(2)}, u32[]{:S(2)}) async-start(bf16[2,512,1024]{1,2,0:T(8,128)(2,1)} %bitcast.22), calls=%async_computation.1 | async-start | bytes 4194304 | tf_op jit(solution)/shard_map/all_to_all | solution.py:28
  100.8 4.8 %all-to-all-start.6 = ((bf16[4,128,512]{2,1,0:T(8,128)(2,1)}), bf16[4,128,512]{2,1,0:T(8,128)(2,1)}, u32[]{:S(2)}, u32[]{:S(2)}) async-start(bf16[4,128,512]{2,1,0:T(8,128)(2,1)} %bitcast.24), calls=%async_computation.6 | async-start | bytes 1048576 | tf_op jit(solution)/shard_map/all_to_all | solution.py:28
  107.2 2.4 copy_bitcast_fusion.1
  109.6 4.5 %all-to-all-done.6 = bf16[4,128,512]{2,1,0:T(8,128)(2,1)} async-done(((bf16[4,128,512]{2,1,0:T(8,128)(2,1)}), bf16[4,128,512]{2,1,0:T(8,128)(2,1)}, u32[]{:S(2)}, u32[]{:S(2)}) %all-to-all-start.6) | async-done | bytes 524320 | tf_op jit(solution)/shard_map/all_to_all | solution.py:28
  114.1 4.9 %all-to-all-start.2 = ((bf16[4,128,1024]{1,2,0:T(8,128)(2,1)}), bf16[4,128,1024]{1,2,0:T(8,128)(2,1)S(1)}, u32[]{:S(2)}, u32[]{:S(2)}) async-start(bf16[4,128,1024]{1,2,0:T(8,128)(2,1)} %copy_bitcast_fusion.1), calls=%async_computation.2 | async-start | bytes 2097152 | tf_op jit(solution)/shard_map/all_to_all | solution.py:28
  120.3 11.9 %all-to-all-done.2 = bf16[4,128,1024]{1,2,0:T(8,128)(2,1)S(1)} async-done(((bf16[4,128,1024]{1,2,0:T(8,128)(2,1)}), bf16[4,128,1024]{1,2,0:T(8,128)(2,1)S(1)}, u32[]{:S(2)}, u32[]{:S(2)}) %all-to-all-start.2) | async-done | bytes 1048608 | tf_op jit(solution)/shard_map/all_to_all | solution.py:28
  133.4 14.9 %all_gather.12 = bf16[512,512]{0,1:T(8,128)(2,1)} all-gather(bf16[128,512]{0,1:T(8,128)(2,1)S(1)} %get-tuple-element.13), channel_id=1, replica_groups=mesh['x'=4,'core'=2,'y'=4,'z'=8] {'x'}, dimensions={0}, use_global_device_ids=true | all-gather | bytes 655360 | tf_op jit(solution)/shard_map/all_gather | solution.py:57
  148.6 12.3 %all-gather.6.cloned.1.call-done = bf16[512,1024]{0,1:T(8,128)(2,1)} async-done(((bf16[128,1024]{0,1:T(8,128)(2,1)}), bf16[512,1024]{0,1:T(8,128)(2,1)}) %all-gather.6.cloned.1.call-update) | async-done | bytes 1048592 | tf_op jit(solution)/shard_map/all_gather | solution.py:57
  160.9 17.9 %all-gather.4.cloned.1.call-done = bf16[1024,512]{0,1:T(8,128)(2,1)} async-done(((bf16[512,512]{0,1:T(8,128)(2,1)}), bf16[1024,512]{0,1:T(8,128)(2,1)}) %all-gather.4.cloned.1.call-update) | async-done | bytes 1048592 | tf_op jit(solution)/shard_map/all_gather | solution.py:57
  178.7 2.5 convolution_convert_fusion
  181.4 2.8 %collective-permute-start.3 = (bf16[256,1024]{1,0:T(8,128)(2,1)S(1)}, bf16[256,1024]{1,0:T(8,128)(2,1)S(1)}, u32[]{:S(2)}, u32[]{:S(2)}) collective-permute-start(bf16[256,1024]{1,0:T(8,128)(2,1)S(1)} %get-tuple-element.8), channel_id=1, source_target_pairs={{0,24},{8,0},{16,8},{24,16},{1,25},{9,1},{17,9},{25,17},{2,26},{10... | collective-permute-start | bytes 1572872 | tf_op jit(solution)/shard_map/ppermute | solution.py:24
  186.5 20.6 %collective-permute-done.3 = bf16[256,1024]{1,0:T(8,128)(2,1)S(1)} collective-permute-done((bf16[256,1024]{1,0:T(8,128)(2,1)S(1)}, bf16[256,1024]{1,0:T(8,128)(2,1)S(1)}, u32[]{:S(2)}, u32[]{:S(2)}) %collective-permute-start.3) | collective-permute-done | bytes 524320 | tf_op jit(solution)/shard_map/ppermute | solution.py:24
  207.1 3.4 %collective-permute-done.4 = bf16[256,1024]{1,0:T(8,128)(2,1)S(1)} collective-permute-done((bf16[256,1024]{1,0:T(8,128)(2,1)S(1)}, bf16[256,1024]{1,0:T(8,128)(2,1)S(1)}, u32[]{:S(2)}, u32[]{:S(2)}) %collective-permute-start.4) | collective-permute-done | bytes 524320 | tf_op jit(solution)/shard_map/ppermute | solution.py:24
  211.7 7.0 %all-to-all-start.3 = ((bf16[8,32,1024]{2,1,0:T(8,128)(2,1)}), bf16[8,32,1024]{2,1,0:T(8,128)(2,1)S(1)}, u32[]{:S(2)}, u32[]{:S(2)}) async-start(bf16[8,32,1024]{2,1,0:T(8,128)(2,1)} %bitcast.1), calls=%async_computation.3 | async-start | bytes 1048576 | tf_op jit(solution)/shard_map/all_to_all | solution.py:28
  218.7 3.0 %fusion.5 = f32[1024,1024]{1,0:T(8,128)S(1)} fusion(bf16[1024,512]{1,0:T(8,128)(2,1)} %param.6, bf16[1024,1024]{0,1:T(8,128)(2,1)} %all-gather.8.cloned.1.call-done), kind=kOutput, calls=%fused_computation.19 | convolution fusion | flops 1073741824 | bytes 6291456 | tf_op jit(solution)/shard_map/dot_general | solution.py:16
  226.5 21.0 %collective-permute-done.10 = bf16[256,1024]{1,0:T(8,128)(2,1)S(1)} collective-permute-done((bf16[256,1024]{1,0:T(8,128)(2,1)S(1)}, bf16[256,1024]{1,0:T(8,128)(2,1)S(1)}, u32[]{:S(2)}, u32[]{:S(2)}) %collective-permute-start.10) | collective-permute-done | bytes 524320 | tf_op jit(solution)/shard_map/ppermute | solution.py:24
  249.4 6.9 %all-to-all-start.7 = ((bf16[8,32,1024]{2,1,0:T(8,128)(2,1)}), bf16[8,32,1024]{2,1,0:T(8,128)(2,1)S(1)}, u32[]{:S(2)}, u32[]{:S(2)}) async-start(bf16[8,32,1024]{2,1,0:T(8,128)(2,1)} %bitcast.5), calls=%async_computation.7 | async-start | bytes 1048576 | tf_op jit(solution)/shard_map/all_to_all | solution.py:28
  256.3 4.3 %fusion.7 = f32[512,1024]{1,0:T(8,128)} fusion(bf16[1024,512]{0,1:T(8,128)(2,1)} %all-gather.4.cloned.1.call-done, bf16[256,1024]{1,0:T(8,128)(2,1)} %copy-done.12, bf16[256,1024]{1,0:T(8,128)(2,1)} %copy-done.11, bf16[256,1024]{1,0:T(8,128)(2,1)} %copy-done.10, bf16[256,1024]{1,0:T(8,128)(2,1)S(1)} %bitcast.37), kind=kOutput, calls=%fused_computation.21 | convolution fusion | flops 1082130432 | bytes 5242880 | tf_op jit(solution)/shard_map/dot_general | solution.py:20
  261.3 4.5 %fusion = f32[1024,512]{1,0:T(8,128)} fusion(bf16[1024,1024]{0,1:T(8,128)(2,1)} %all-gather.8.cloned.1.call-done, bf16[256,1024]{1,0:T(8,128)(2,1)} %collective-permute-done.2, bf16[256,1024]{1,0:T(8,128)(2,1)} %collective-permute-done.1, bf16[256,1024]{1,0:T(8,128)(2,1)} %collective-permute-done, bf16[256,1024]{1,0:T(8,128)(2,1)S(1)} %bitcast.31), kind=kOutput, calls=%fused_computation.14 | convolution fusion | flops 1082130432 | bytes 5242880 | tf_op jit(solution)/shard_map/dot_general | solution.py:20
  265.8 4.0 %fusion.3 = f32[1024,512]{1,0:T(8,128)} fusion(bf16[1024,1024]{0,1:T(8,128)(2,1)S(1)} %copy-done.8, bf16[256,1024]{1,0:T(8,128)(2,1)} %collective-permute-done.2, bf16[256,1024]{1,0:T(8,128)(2,1)} %collective-permute-done.1, bf16[256,1024]{1,0:T(8,128)(2,1)} %collective-permute-done, bf16[256,1024]{1,0:T(8,128)(2,1)S(1)} %bitcast.32), kind=kOutput, calls=%fused_computation.17 | convolution fusion | flops 1082130432 | bytes 5242880 | tf_op jit(solution)/shard_map/dot_general | solution.py:20
  269.7 3.1 %all-to-all-done.7 = bf16[8,32,1024]{2,1,0:T(8,128)(2,1)S(1)} async-done(((bf16[8,32,1024]{2,1,0:T(8,128)(2,1)}), bf16[8,32,1024]{2,1,0:T(8,128)(2,1)S(1)}, u32[]{:S(2)}, u32[]{:S(2)}) %all-to-all-start.7) | async-done | bytes 524320 | tf_op jit(solution)/shard_map/all_to_all | solution.py:28
  (69 shorter events, 30.5 us)
Async XLA Ops:
  7.2 80.2 %copy-start = (bf16[512,1024]{1,0:T(8,128)(2,1)S(1)}, bf16[512,1024]{1,0:T(8,128)(2,1)}, u32[]{:S(2)}) copy-start(bf16[512,1024]{1,0:T(8,128)(2,1)} %param.8) | copy-start | bytes 3145732
  7.2 60.8 %copy-start.1 = (bf16[1024,512]{1,0:T(8,128)(2,1)S(1)}, bf16[1024,512]{1,0:T(8,128)(2,1)}, u32[]{:S(2)}) copy-start(bf16[1024,512]{1,0:T(8,128)(2,1)} %param.7) | copy-start | bytes 3145732
  34.0 36.7 %copy-start.3 = (bf16[8,32,1024]{2,1,0:T(8,128)(2,1)}, bf16[8,32,1024]{2,1,0:T(8,128)(2,1)S(1)}, u32[]{:S(2)}) copy-start(bf16[8,32,1024]{2,1,0:T(8,128)(2,1)S(1)} %all_to_all.72) | copy-start | bytes 1572868
  35.7 19.4 %all-to-all-start.4 = ((bf16[8,32,1024]{2,1,0:T(8,128)(2,1)}), bf16[8,32,1024]{2,1,0:T(8,128)(2,1)S(1)}, u32[]{:S(2)}, u32[]{:S(2)}) async-start(bf16[8,32,1024]{2,1,0:T(8,128)(2,1)} %broadcast_in_dim.5), calls=%async_computation.4 | async-start | bytes 1048576 | tf_op jit(solution)/shard_map/all_to_all | solution.py:28
  39.2 20.4 %collective-permute-start = (bf16[256,1024]{1,0:T(8,128)(2,1)S(1)}, bf16[256,1024]{1,0:T(8,128)(2,1)}, u32[]{:S(2)}, u32[]{:S(2)}) collective-permute-start(bf16[256,1024]{1,0:T(8,128)(2,1)S(1)} %bitcast.26), channel_id=1, source_target_pairs={{0,8},{8,16},{16,24},{24,0},{1,9},{9,17},{17,25},{25,1},{2,10},{10... | collective-permute-start | bytes 1572872 | tf_op jit(solution)/shard_map/ppermute | solution.py:24
  40.9 27.1 %collective-permute-start.1 = (bf16[256,1024]{1,0:T(8,128)(2,1)S(1)}, bf16[256,1024]{1,0:T(8,128)(2,1)}, u32[]{:S(2)}, u32[]{:S(2)}) collective-permute-start(bf16[256,1024]{1,0:T(8,128)(2,1)S(1)} %bitcast.27), channel_id=1, source_target_pairs={{0,16},{8,24},{16,0},{24,8},{1,17},{9,25},{17,1},{25,9},{2,18},{10... | collective-permute-start | bytes 1572872 | tf_op jit(solution)/shard_map/ppermute | solution.py:24
  43.8 24.2 %collective-permute-start.2 = (bf16[256,1024]{1,0:T(8,128)(2,1)S(1)}, bf16[256,1024]{1,0:T(8,128)(2,1)}, u32[]{:S(2)}, u32[]{:S(2)}) collective-permute-start(bf16[256,1024]{1,0:T(8,128)(2,1)S(1)} %bitcast.28), channel_id=1, source_target_pairs={{0,24},{8,0},{16,8},{24,16},{1,25},{9,1},{17,9},{25,17},{2,26},{10... | collective-permute-start | bytes 1572872 | tf_op jit(solution)/shard_map/ppermute | solution.py:24
  55.1 32.3 %copy-start.5 = (bf16[8,32,1024]{2,1,0:T(8,128)(2,1)}, bf16[8,32,1024]{2,1,0:T(8,128)(2,1)S(1)}, u32[]{:S(2)}) copy-start(bf16[8,32,1024]{2,1,0:T(8,128)(2,1)S(1)} %all-to-all-done.4) | copy-start | bytes 1572868
  55.1 15.5 %copy-start.9 = (bf16[1024,512]{1,0:T(8,128)(2,1)S(1)}, bf16[1024,512]{1,0:T(8,128)(2,1)}, u32[]{:S(2)}) copy-start(bf16[1024,512]{1,0:T(8,128)(2,1)} %param.6) | copy-start | bytes 3145732
  55.1 23.4 %collective-permute-start.6 = (bf16[256,1024]{1,0:T(8,128)(2,1)S(1)}, bf16[256,1024]{1,0:T(8,128)(2,1)S(1)}, u32[]{:S(2)}, u32[]{:S(2)}) collective-permute-start(bf16[256,1024]{1,0:T(8,128)(2,1)S(1)} %bitcast.33), channel_id=1, source_target_pairs={{0,8},{8,16},{16,24},{24,0},{1,9},{9,17},{17,25},{25,1},{2,10},{10... | collective-permute-start | bytes 1572872 | tf_op jit(solution)/shard_map/ppermute | solution.py:24
  56.7 30.7 %collective-permute-start.7 = (bf16[256,1024]{1,0:T(8,128)(2,1)S(1)}, bf16[256,1024]{1,0:T(8,128)(2,1)S(1)}, u32[]{:S(2)}, u32[]{:S(2)}) collective-permute-start(bf16[256,1024]{1,0:T(8,128)(2,1)S(1)} %bitcast.34), channel_id=1, source_target_pairs={{0,16},{8,24},{16,0},{24,8},{1,17},{9,25},{17,1},{25,9},{2,18},{10... | collective-permute-start | bytes 1572872 | tf_op jit(solution)/shard_map/ppermute | solution.py:24
  59.6 27.8 %collective-permute-start.8 = (bf16[256,1024]{1,0:T(8,128)(2,1)S(1)}, bf16[256,1024]{1,0:T(8,128)(2,1)S(1)}, u32[]{:S(2)}, u32[]{:S(2)}) collective-permute-start(bf16[256,1024]{1,0:T(8,128)(2,1)S(1)} %bitcast.35), channel_id=1, source_target_pairs={{0,24},{8,0},{16,8},{24,16},{1,25},{9,1},{17,9},{25,17},{2,26},{10... | collective-permute-start | bytes 1572872 | tf_op jit(solution)/shard_map/ppermute | solution.py:24
  78.5 10.2 %copy-start.10 = (bf16[256,1024]{1,0:T(8,128)(2,1)}, bf16[256,1024]{1,0:T(8,128)(2,1)S(1)}, u32[]{:S(2)}) copy-start(bf16[256,1024]{1,0:T(8,128)(2,1)S(1)} %collective-permute-done.6) | copy-start | bytes 1572868
  94.1 6.6 %all-to-all-start.1 = ((bf16[2,512,1024]{1,2,0:T(8,128)(2,1)}), bf16[2,512,1024]{1,2,0:T(8,128)(2,1)S(1)}, u32[]{:S(2)}, u32[]{:S(2)}) async-start(bf16[2,512,1024]{1,2,0:T(8,128)(2,1)} %bitcast.22), calls=%async_computation.1 | async-start | bytes 4194304 | tf_op jit(solution)/shard_map/all_to_all | solution.py:28
  100.8 13.3 %all-to-all-start.6 = ((bf16[4,128,512]{2,1,0:T(8,128)(2,1)}), bf16[4,128,512]{2,1,0:T(8,128)(2,1)}, u32[]{:S(2)}, u32[]{:S(2)}) async-start(bf16[4,128,512]{2,1,0:T(8,128)(2,1)} %bitcast.24), calls=%async_computation.6 | async-start | bytes 1048576 | tf_op jit(solution)/shard_map/all_to_all | solution.py:28
  114.1 18.1 %all-to-all-start.2 = ((bf16[4,128,1024]{1,2,0:T(8,128)(2,1)}), bf16[4,128,1024]{1,2,0:T(8,128)(2,1)S(1)}, u32[]{:S(2)}, u32[]{:S(2)}) async-start(bf16[4,128,1024]{1,2,0:T(8,128)(2,1)} %copy_bitcast_fusion.1), calls=%async_computation.2 | async-start | bytes 2097152 | tf_op jit(solution)/shard_map/all_to_all | solution.py:28
  119.1 41.8 %all-gather.6.cloned.1.call-start = ((), (), s32[]{:S(2)}) async-start(), calls=%async_computation.9 | async-start | bytes 1310720 | tf_op jit(solution)/shard_map/all_gather | solution.py:57
  133.3 45.4 %all-gather.4.cloned.1.call-start = ((), (), s32[]{:S(2)}) async-start(), calls=%async_computation.8 | async-start | bytes 1572864 | tf_op jit(solution)/shard_map/all_gather | solution.py:57
  148.3 70.4 %all-gather.8.cloned.1.call-start = ((), (), s32[]{:S(2)}) async-start(), calls=%async_computation.10 | async-start | bytes 3145728 | tf_op jit(solution)/shard_map/all_gather | solution.py:57
  181.4 25.7 %collective-permute-start.3 = (bf16[256,1024]{1,0:T(8,128)(2,1)S(1)}, bf16[256,1024]{1,0:T(8,128)(2,1)S(1)}, u32[]{:S(2)}, u32[]{:S(2)}) collective-permute-start(bf16[256,1024]{1,0:T(8,128)(2,1)S(1)} %get-tuple-element.8), channel_id=1, source_target_pairs={{0,24},{8,0},{16,8},{24,16},{1,25},{9,1},{17,9},{25,17},{2,26},{10... | collective-permute-start | bytes 1572872 | tf_op jit(solution)/shard_map/ppermute | solution.py:24
  184.2 26.3 %collective-permute-start.4 = (bf16[256,1024]{1,0:T(8,128)(2,1)S(1)}, bf16[256,1024]{1,0:T(8,128)(2,1)S(1)}, u32[]{:S(2)}, u32[]{:S(2)}) collective-permute-start(bf16[256,1024]{1,0:T(8,128)(2,1)S(1)} %get-tuple-element.10), channel_id=1, source_target_pairs={{0,8},{8,16},{16,24},{24,0},{1,9},{9,17},{17,25},{25,1},{2,10},{10... | collective-permute-start | bytes 1572872 | tf_op jit(solution)/shard_map/ppermute | solution.py:24
  184.2 26.3 %collective-permute-start.5 = (bf16[256,1024]{1,0:T(8,128)(2,1)S(1)}, bf16[256,1024]{1,0:T(8,128)(2,1)S(1)}, u32[]{:S(2)}, u32[]{:S(2)}) collective-permute-start(bf16[256,1024]{1,0:T(8,128)(2,1)S(1)} %get-tuple-element.9), channel_id=1, source_target_pairs={{0,16},{8,24},{16,0},{24,8},{1,17},{9,25},{17,1},{25,9},{2,18},{10... | collective-permute-start | bytes 1572872 | tf_op jit(solution)/shard_map/ppermute | solution.py:24
  211.7 37.7 %all-to-all-start.3 = ((bf16[8,32,1024]{2,1,0:T(8,128)(2,1)}), bf16[8,32,1024]{2,1,0:T(8,128)(2,1)S(1)}, u32[]{:S(2)}, u32[]{:S(2)}) async-start(bf16[8,32,1024]{2,1,0:T(8,128)(2,1)} %bitcast.1), calls=%async_computation.3 | async-start | bytes 1048576 | tf_op jit(solution)/shard_map/all_to_all | solution.py:28
  218.7 3.0 %copy-start.2 = (bf16[1024,512]{1,0:T(8,128)(2,1)S(1)}, bf16[1024,512]{1,0:T(8,128)(2,1)}, u32[]{:S(2)}) copy-start(bf16[1024,512]{1,0:T(8,128)(2,1)} %param.7) | copy-start | bytes 3145732
  218.7 3.0 %copy-start.7 = (bf16[1024,1024]{0,1:T(8,128)(2,1)S(1)}, bf16[1024,1024]{0,1:T(8,128)(2,1)}, u32[]{:S(2)}) copy-start(bf16[1024,1024]{0,1:T(8,128)(2,1)} %all-gather.8.cloned.1.call-done) | copy-start | bytes 6291460
  223.2 33.0 %copy-start.6 = (bf16[8,32,1024]{2,1,0:T(8,128)(2,1)S(1)}, bf16[8,32,1024]{2,1,0:T(8,128)(2,1)}, u32[]{:S(2)}) copy-start(bf16[8,32,1024]{2,1,0:T(8,128)(2,1)} %copy-done.5) | copy-start | bytes 1572868
  223.2 24.3 %collective-permute-start.10 = (bf16[256,1024]{1,0:T(8,128)(2,1)S(1)}, bf16[256,1024]{1,0:T(8,128)(2,1)S(1)}, u32[]{:S(2)}, u32[]{:S(2)}) collective-permute-start(bf16[256,1024]{1,0:T(8,128)(2,1)S(1)} %get-tuple-element.7), channel_id=1, source_target_pairs={{0,8},{8,16},{16,24},{24,0},{1,9},{9,17},{17,25},{25,1},{2,10},{10... | collective-permute-start | bytes 1572872 | tf_op jit(solution)/shard_map/ppermute | solution.py:24
  223.3 24.3 %collective-permute-start.11 = (bf16[256,1024]{1,0:T(8,128)(2,1)S(1)}, bf16[256,1024]{1,0:T(8,128)(2,1)S(1)}, u32[]{:S(2)}, u32[]{:S(2)}) collective-permute-start(bf16[256,1024]{1,0:T(8,128)(2,1)S(1)} %get-tuple-element.6), channel_id=1, source_target_pairs={{0,16},{8,24},{16,0},{24,8},{1,17},{9,25},{17,1},{25,9},{2,18},{10... | collective-permute-start | bytes 1572872 | tf_op jit(solution)/shard_map/ppermute | solution.py:24
  225.0 23.1 %collective-permute-start.9 = (bf16[256,1024]{1,0:T(8,128)(2,1)S(1)}, bf16[256,1024]{1,0:T(8,128)(2,1)S(1)}, u32[]{:S(2)}, u32[]{:S(2)}) collective-permute-start(bf16[256,1024]{1,0:T(8,128)(2,1)S(1)} %get-tuple-element.5), channel_id=1, source_target_pairs={{0,24},{8,0},{16,8},{24,16},{1,25},{9,1},{17,9},{25,17},{2,26},{10... | collective-permute-start | bytes 1572872 | tf_op jit(solution)/shard_map/ppermute | solution.py:24
  249.4 23.5 %all-to-all-start.7 = ((bf16[8,32,1024]{2,1,0:T(8,128)(2,1)}), bf16[8,32,1024]{2,1,0:T(8,128)(2,1)S(1)}, u32[]{:S(2)}, u32[]{:S(2)}) async-start(bf16[8,32,1024]{2,1,0:T(8,128)(2,1)} %bitcast.5), calls=%async_computation.7 | async-start | bytes 1048576 | tf_op jit(solution)/shard_map/all_to_all | solution.py:28
  256.3 5.0 %copy-start.4 = (bf16[8,32,1024]{2,1,0:T(8,128)(2,1)S(1)}, bf16[8,32,1024]{2,1,0:T(8,128)(2,1)}, u32[]{:S(2)}) copy-start(bf16[8,32,1024]{2,1,0:T(8,128)(2,1)} %copy-done.3) | copy-start | bytes 1572868
  261.3 4.5 %copy-start.8 = (bf16[1024,1024]{0,1:T(8,128)(2,1)S(1)}, bf16[1024,1024]{0,1:T(8,128)(2,1)}, u32[]{:S(2)}) copy-start(bf16[1024,1024]{0,1:T(8,128)(2,1)} %all-gather.8.cloned.1.call-done) | copy-start | bytes 6291460
  (2 other events, 2.7 us)
Sparse Core Ops, SparseCore 0:
  133.4 27.3 all-gather.5
  162.7 16.0 all-gather.3
  180.5 17.1 all-gather.7

commit v2 on v1

v2 whole, which is shorter than its diff:
```python
import jax
import jax.numpy as jnp
from jax import lax
from jax.sharding import Mesh, PartitionSpec as P

BF = jnp.bfloat16
F32 = jnp.float32
X, CORE, Y, Z = 4, 2, 4, 8


def product(left_side, right_side):
    return jnp.dot(left_side, right_side, preferred_element_type=F32)


def product_right_t(left_side, right_side):
    return lax.dot_general(left_side, right_side, (((1,), (1,)), ((), ())), preferred_element_type=F32)


def product_left_t(left_side, right_side):
    return lax.dot_general(left_side, right_side, (((0,), (0,)), ((), ())), preferred_element_type=F32)


def shift(block, axis, step):
    size = lax.axis_size(axis)
    return lax.ppermute(block, axis, [(i, (i + step) % size) for i in range(size)])


def exchange(blocks, axis):
    return lax.all_to_all(blocks, axis, split_axis=0, concat_axis=0, tiled=True)


def gather(block, axis):
    count = lax.axis_size(axis)
    rows, width = block.shape
    copies = jnp.broadcast_to(block[None], (count, rows, width)).reshape(count * rows, width)
    return exchange(copies, axis)


def after(block, *earlier):
    return lax.optimization_barrier((block,) + earlier)[0]


def gather_y(own):
    near = [shift(own, "y", 1), shift(own, "y", 3)]
    return jnp.concatenate([own, near[0], shift(own, "y", 2), near[1]], axis=0)


def gather_y_later(own):
    pieces = lax.all_gather(own, "y", axis=0, tiled=False)
    place = lax.axis_index("y") + Y
    return jnp.concatenate(
        [lax.dynamic_index_in_dim(pieces, lax.bitwise_and(place - j, Y - 1), axis=0, keepdims=False) for j in range(Y)], axis=0
    )


def swap_core(low, high):
    first = lax.axis_index("core") == 0
    return jnp.where(first, low, high), shift(jnp.where(first, high, low), "core", 1)


def sum_parts(parts, count):
    rows = parts.shape[0] // count
    return jnp.sum(parts.reshape((count, rows) + parts.shape[1:]).astype(F32), axis=0)


def reduce_core(partial):
    rows = partial.shape[0] // CORE
    kept, received = swap_core(partial[:rows], partial[rows:])
    return (kept.astype(F32) + received.astype(F32)).astype(BF)


def reduce_x(partial):
    return sum_parts(exchange(partial, "x"), X)


def gather_core(half):
    other = shift(half, "core", 1)
    first = lax.axis_index("core") == 0
    return jnp.concatenate([jnp.where(first, half, other), jnp.where(first, other, half)], axis=0)


def reduce_col(partial):
    rows = partial.shape[0] // Y
    pieces = [partial[j * rows : (j + 1) * rows] for j in range(Y)]
    moved = [shift(pieces[1], "y", 3), shift(pieces[3], "y", 1), shift(pieces[2], "y", 2)]
    total = pieces[0].astype(F32) + moved[0].astype(F32) + moved[1].astype(F32) + moved[2].astype(F32)
    return sum_parts(exchange(total.astype(BF), "z"), Z).astype(BF)


def body(tokens, gate_weight, up_weight, down_weight, out_grad):
    width = gate_weight.shape[1]
    both_weights = jnp.concatenate([gate_weight, up_weight], axis=1)
    tokens_z = gather(tokens, "z")
    all_tokens = gather_y(tokens_z)
    grads_z = gather(after(out_grad, tokens_z), "z")
    all_grads = gather_y_later(grads_z)
    gate_up = reduce_x(reduce_core(product(all_tokens, both_weights).astype(BF)))
    gate_value = gate_up[:, :width]
    up_value = gate_up[:, width:]
    sigmoid_gate = jax.nn.sigmoid(gate_value)
    silu_gate = gate_value * sigmoid_gate
    hidden_half = gather((silu_gate * up_value).astype(BF), "x")
    hidden = gather_core(hidden_half)
    output_partial = product(hidden, down_weight).astype(BF)
    layer_output = reduce_col(output_partial)

    hidden_partial = reduce_core(product_right_t(all_grads, down_weight).astype(BF))
    hidden_grad = reduce_x(after(hidden_partial, hidden_half))
    gate_grad = (hidden_grad * up_value * sigmoid_gate * (1.0 + gate_value * (1.0 - sigmoid_gate))).astype(BF)
    up_grad = (hidden_grad * silu_gate).astype(BF)
    both_share = after(jnp.concatenate([gate_grad, up_grad], axis=1), output_partial)
    both_grads = gather_core(gather(both_share, "x"))
    input_grad = reduce_col(product_right_t(both_grads, both_weights).astype(BF))
    gate_weight_grad = product_left_t(all_tokens, both_grads[:, :width])
    up_weight_grad = product_left_t(all_tokens, both_grads[:, width:])
    down_weight_grad = product_left_t(hidden, all_grads)
    return (layer_output, input_grad, gate_weight_grad, up_weight_grad, down_weight_grad)


def solution(mesh):
    grid = Mesh(mesh.devices.reshape(X, CORE, Y, Z), ("x", "core", "y", "z"))
    row, col = ("x", "core"), ("y", "z")
    in_specs = (P(col, row), P(row, col), P(row, col), P(col, row), P(col, row))
    out_specs = (P(col, row), P(col, row), P(row, col), P(row, col), P(col, row))
    return jax.shard_map(body, mesh=grid, in_specs=in_specs, out_specs=out_specs, check_vma=False)
```

time: 282 us -> 247 us (0.88)
  waiting for transfers between devices: 125 us -> 97.6 us
  starting transfers between devices: 51.4 us -> 41.2 us
  local copies, waits for them, and re-layouts: 7.02 us -> 10.1 us
    all_gather x3 -> x1, waiting for transfers between devices: 30.2 us -> 0.01 us  [gather_y_later(): pieces = lax.all_gather(own, 'y', axis=0, tiled=False)]
    all_gather x1 -> x0, blocking collectives: 14.9 us -> none  [gather_row(): lax.all_gather(share, 'x', axis=0, tiled=True)]
    all_to_all x2, blocking collectives: 31.1 us -> 43.6 us  [exchange(): return lax.all_to_all(blocks, axis, split_axis=0, concat_axis=0, tiled=True)]
    ppermute x12 -> x13, starting transfers between devices: 20.2 us -> 9.43 us  [shift(): lax.ppermute(block, axis, [(i, (i + step) % size) for i in range(size)])]
    reduce_sum x6 -> x4, other arithmetic: 6.69 us -> 1.67 us  [sum_parts(): jnp.sum(parts.reshape((count, rows) + parts.shape[1:]).astype(F32), axis=0)]
    all_to_all x6, waiting for transfers between devices: 30 us -> 34.3 us  [exchange(): return lax.all_to_all(blocks, axis, split_axis=0, concat_axis=0, tiled=True)]
    all_to_all x2 -> x0, local copies, waits for them, and re-layouts: 3.83 us -> none  [exchange(): return lax.all_to_all(blocks, axis, split_axis=0, concat_axis=0, tiled=True)]
    convert_element_type x2 -> x5, other arithmetic: 2.32 us -> 6 us  [the longest x2 3.64 us: reduce_core(): return (kept.astype(F32) + received.astype(F32)).astype(BF)]
  transfers between devices with their start and end apart: 21 -> 20, of which waited for: 14 -> 14; matrix products, arithmetic and copies ran while one was open for 13% -> 17% of each run, Pallas kernels for 0% -> 0%
where the time goes in v2:
time: 247 us; the launch traced here: 244 us
  waiting for transfers between devices  97.6 us (40%)
  blocking collectives  43.6 us (18%)
  starting transfers between devices  41.2 us (17%)
  matrix products  25.9 us (10%)
  between operations  14.3 us (6%)
  other arithmetic  11.3 us (5%)
  local copies, waits for them, and re-layouts  10.1 us (4%)
    ppermute x13, waiting for transfers between devices, shift(): lax.ppermute(block, axis, [(i, (i + step) % size) for i in range(size)])  63.2 us
    all_to_all x2, blocking collectives, exchange(): return lax.all_to_all(blocks, axis, split_axis=0, concat_axis=0, tiled=True)  43.6 us
    all_to_all x6, waiting for transfers between devices, exchange(): return lax.all_to_all(blocks, axis, split_axis=0, concat_axis=0, tiled=True)  34.3 us
    all_to_all x6, starting transfers between devices, exchange(): return lax.all_to_all(blocks, axis, split_axis=0, concat_axis=0, tiled=True)  31.8 us
    dot_general x3, matrix products, product_left_t(): lax.dot_general(left_side, right_side, (((0,), (0,)), ((), ())), preferre...  12.9 us
    ppermute x13, starting transfers between devices, shift(): lax.ppermute(block, axis, [(i, (i + step) % size) for i in range(size)])  9.43 us
    dot_general x2, matrix products, product(): return jnp.dot(left_side, right_side, preferred_element_type=F32)  6.98 us
    dot_general x2, matrix products, product_right_t(): lax.dot_general(left_side, right_side, (((1,), (1,)), ((), ())), preferre...  6.02 us
  transfers between devices with their start and end apart: 20, of which 14 were waited for; matrix products, arithmetic and copies ran while one was open for 17% of the time, Pallas kernels for 0%

profile of v2, /device:TPU:2, one launch (start us, length us, event | category | flops | bytes accessed | tf_op | source)
XLA Modules:
  0.0 244.0 jit_solution(8338838943110518518)
XLA Ops:
  8.2 25.8 %all_to_all.69 = bf16[8,32,1024]{2,1,0:T(8,128)(2,1)S(1)} all-to-all(bf16[8,32,1024]{2,1,0:T(8,128)(2,1)S(1)} %broadcast_in_dim.8), channel_id=1, replica_groups=mesh['x'=4,'core'=2,'y'=4,'z'=8] {'z'}, dimensions={0} | all-to-all | bytes 1048576 | tf_op jit(solution)/shard_map/all_to_all | solution.py:29
  34.0 1.7 broadcast_in_dim.10
  35.7 3.5 %all-to-all-start.4 = ((bf16[8,32,1024]{2,1,0:T(8,128)(2,1)}), bf16[8,32,1024]{2,1,0:T(8,128)(2,1)S(1)}, u32[]{:S(2)}, u32[]{:S(2)}) async-start(bf16[8,32,1024]{2,1,0:T(8,128)(2,1)} %broadcast_in_dim.10), calls=%async_computation.4 | async-start | bytes 1048576 | tf_op jit(solution)/shard_map/all_to_all | solution.py:29
  39.3 3.1 %collective-permute-start.2 = (bf16[256,1024]{1,0:T(8,128)(2,1)S(1)}, bf16[256,1024]{1,0:T(8,128)(2,1)}, u32[]{:S(2)}, u32[]{:S(2)}) collective-permute-start(bf16[256,1024]{1,0:T(8,128)(2,1)S(1)} %bitcast.28), channel_id=1, source_target_pairs={{0,24},{8,0},{16,8},{24,16},{1,25},{9,1},{17,9},{25,17},{2,26},{10... | collective-permute-start | bytes 1572872 | tf_op jit(solution)/shard_map/ppermute | solution.py:25
  46.6 8.5 %all-to-all-done.4 = bf16[8,32,1024]{2,1,0:T(8,128)(2,1)S(1)} async-done(((bf16[8,32,1024]{2,1,0:T(8,128)(2,1)}), bf16[8,32,1024]{2,1,0:T(8,128)(2,1)S(1)}, u32[]{:S(2)}, u32[]{:S(2)}) %all-to-all-start.4) | async-done | bytes 524320 | tf_op jit(solution)/shard_map/all_to_all | solution.py:29
  56.0 7.1 %collective-permute-done.2 = bf16[256,1024]{1,0:T(8,128)(2,1)} collective-permute-done((bf16[256,1024]{1,0:T(8,128)(2,1)S(1)}, bf16[256,1024]{1,0:T(8,128)(2,1)}, u32[]{:S(2)}, u32[]{:S(2)}) %collective-permute-start.2) | collective-permute-done | bytes 524320 | tf_op jit(solution)/shard_map/ppermute | solution.py:25
  63.0 3.8 %collective-permute-done = bf16[256,1024]{1,0:T(8,128)(2,1)} collective-permute-done((bf16[256,1024]{1,0:T(8,128)(2,1)S(1)}, bf16[256,1024]{1,0:T(8,128)(2,1)}, u32[]{:S(2)}, u32[]{:S(2)}) %collective-permute-start) | collective-permute-done | bytes 524320 | tf_op jit(solution)/shard_map/ppermute | solution.py:25
  66.8 4.4 %convolution_convert_fusion.1 = bf16[1024,1024]{1,0:T(8,128)(2,1)S(1)} fusion(bf16[1024,1024]{1,0:T(8,128)(2,1)} %constant_dynamic-update-slice_fusion, bf16[256,1024]{1,0:T(8,128)(2,1)} %collective-permute-done.2, bf16[256,1024]{1,0:T(8,128)(2,1)} %collective-permute-done.1, bf16[256,1024]{1,0:T(8,128)(2,1)} %collective-permute-done, ...), kind=kOutput, calls=%fused_computation.12 | convolution fusion | flops 2156920832 | bytes 6291456 | tf_op jit(solution)/shard_map/dot_general | solution.py:12
  71.5 2.6 %collective-permute-done.3 = bf16[512,1024]{1,0:T(8,128)(2,1)S(1)} collective-permute-done((bf16[512,1024]{1,0:T(8,128)(2,1)S(1)}, bf16[512,1024]{1,0:T(8,128)(2,1)S(1)}, u32[]{:S(2)}, u32[]{:S(2)}) %collective-permute-start.3) | collective-permute-done | bytes 1048608 | tf_op jit(solution)/shard_map/ppermute | solution.py:25
  75.7 4.8 %all-to-all-start.1 = ((bf16[4,128,1024]{2,1,0:T(8,128)(2,1)}), bf16[4,128,1024]{2,1,0:T(8,128)(2,1)S(1)}, u32[]{:S(2)}, u32[]{:S(2)}) async-start(bf16[4,128,1024]{2,1,0:T(8,128)(2,1)} %bitcast.1), calls=%async_computation.1 | async-start | bytes 2097152 | tf_op jit(solution)/shard_map/all_to_all | solution.py:29
  80.5 13.9 %all-to-all-done.1 = bf16[4,128,1024]{2,1,0:T(8,128)(2,1)S(1)} async-done(((bf16[4,128,1024]{2,1,0:T(8,128)(2,1)}), bf16[4,128,1024]{2,1,0:T(8,128)(2,1)S(1)}, u32[]{:S(2)}, u32[]{:S(2)}) %all-to-all-start.1) | async-done | bytes 1048608 | tf_op jit(solution)/shard_map/all_to_all | solution.py:29
  95.6 4.9 %all-to-all-start.2 = ((bf16[4,128,512]{2,1,0:T(8,128)(2,1)}), bf16[4,128,512]{2,1,0:T(8,128)(2,1)S(1)}, u32[]{:S(2)}, u32[]{:S(2)}) async-start(bf16[4,128,512]{2,1,0:T(8,128)(2,1)} %broadcast_in_dim.9), calls=%async_computation.2 | async-start | bytes 1048576 | tf_op jit(solution)/shard_map/all_to_all | solution.py:29
  100.5 1.7 dynamic-slice_bitcast_fusion.3
  104.4 3.5 %all-to-all-done.2 = bf16[4,128,512]{2,1,0:T(8,128)(2,1)S(1)} async-done(((bf16[4,128,512]{2,1,0:T(8,128)(2,1)}), bf16[4,128,512]{2,1,0:T(8,128)(2,1)S(1)}, u32[]{:S(2)}, u32[]{:S(2)}) %all-to-all-start.2) | async-done | bytes 524320 | tf_op jit(solution)/shard_map/all_to_all | solution.py:29
  107.9 2.0 add_convert_fusion.2
  110.0 4.9 %all-to-all-start.5 = ((bf16[4,128,512]{2,1,0:T(8,128)(2,1)}), bf16[4,128,512]{2,1,0:T(8,128)(2,1)S(1)}, u32[]{:S(2)}, u32[]{:S(2)}) async-start(bf16[4,128,512]{2,1,0:T(8,128)(2,1)} %bitcast.26), calls=%async_computation.5 | async-start | bytes 1048576 | tf_op jit(solution)/shard_map/all_to_all | solution.py:29
  117.0 2.6 %convolution_convert_fusion = bf16[1024,1024]{1,0:T(8,128)(2,1)} fusion(bf16[512,1024]{1,0:T(8,128)(2,1)S(1)} %copy-done, bf16[512,512]{1,0:T(8,128)(2,1)S(1)} %get-tuple-element.24, bf16[512,512]{1,0:T(8,128)(2,1)S(1)} %get-tuple-element.23), kind=kOutput, calls=%fused_computation.11 | convolution fusion | flops 1076887552 | bytes 4194304 | tf_op jit(solution)/shard_map/dot_general | solution.py:12
  119.6 4.3 %all-to-all-done.5 = bf16[4,128,512]{2,1,0:T(8,128)(2,1)S(1)} async-done(((bf16[4,128,512]{2,1,0:T(8,128)(2,1)}), bf16[4,128,512]{2,1,0:T(8,128)(2,1)S(1)}, u32[]{:S(2)}, u32[]{:S(2)}) %all-to-all-start.5) | async-done | bytes 524320 | tf_op jit(solution)/shard_map/all_to_all | solution.py:29
  124.3 17.8 %all_to_all.70 = bf16[4,128,1024]{2,1,0:T(8,128)(2,1)S(1)} all-to-all(bf16[4,128,1024]{2,1,0:T(8,128)(2,1)S(1)} %broadcast_in_dim.11), channel_id=1, replica_groups=mesh['x'=4,'core'=2,'y'=4,'z'=8] {'x'}, dimensions={0} | all-to-all | bytes 2097152 | tf_op jit(solution)/shard_map/all_to_all | solution.py:29
  144.7 12.5 %collective-permute-done.5 = bf16[256,1024]{1,0:T(8,128)(2,1)S(1)} collective-permute-done((bf16[256,1024]{1,0:T(8,128)(2,1)S(1)}, bf16[256,1024]{1,0:T(8,128)(2,1)S(1)}, u32[]{:S(2)}, u32[]{:S(2)}) %collective-permute-start.5) | collective-permute-done | bytes 524320 | tf_op jit(solution)/shard_map/ppermute | solution.py:25
  157.2 2.4 collective-permute-done.7
  159.6 10.5 %collective-permute-done.6 = bf16[256,1024]{1,0:T(8,128)(2,1)S(1)} collective-permute-done((bf16[256,1024]{1,0:T(8,128)(2,1)S(1)}, bf16[256,1024]{1,0:T(8,128)(2,1)S(1)}, u32[]{:S(2)}, u32[]{:S(2)}) %collective-permute-start.6) | collective-permute-done | bytes 524320 | tf_op jit(solution)/shard_map/ppermute | solution.py:25
  171.2 6.7 %all-to-all-start.3 = ((bf16[8,32,1024]{2,1,0:T(8,128)(2,1)}), bf16[8,32,1024]{2,1,0:T(8,128)(2,1)S(1)}, u32[]{:S(2)}, u32[]{:S(2)}) async-start(bf16[8,32,1024]{2,1,0:T(8,128)(2,1)} %bitcast.3), calls=%async_computation.3 | async-start | bytes 1048576 | tf_op jit(solution)/shard_map/all_to_all | solution.py:29
  179.3 4.7 %fusion.1 = bf16[1024,1024]{1,0:T(8,128)(2,1)S(1)} fusion(bf16[1024,1024]{1,0:T(8,128)(2,1)} %constant_dynamic-update-slice_fusion, bf16[512,1024]{1,0:T(8,128)(2,1)S(1)} %get-tuple-element.15, bf16[512,1024]{1,0:T(8,128)(2,1)S(1)} %get-tuple-element.14), kind=kOutput, calls=%fused_computation.10 | convolution fusion | flops 2152726528 | bytes 6291456 | tf_op jit(solution)/shard_map/dot_general | solution.py:16
  186.3 12.8 %collective-permute-done.10 = bf16[256,1024]{1,0:T(8,128)(2,1)S(1)} collective-permute-done((bf16[256,1024]{1,0:T(8,128)(2,1)S(1)}, bf16[256,1024]{1,0:T(8,128)(2,1)S(1)}, u32[]{:S(2)}, u32[]{:S(2)}) %collective-permute-start.10) | collective-permute-done | bytes 524320 | tf_op jit(solution)/shard_map/ppermute | solution.py:25
  199.1 2.2 collective-permute-done.12
  201.4 9.4 %collective-permute-done.11 = bf16[256,1024]{1,0:T(8,128)(2,1)S(1)} collective-permute-done((bf16[256,1024]{1,0:T(8,128)(2,1)S(1)}, bf16[256,1024]{1,0:T(8,128)(2,1)S(1)}, u32[]{:S(2)}, u32[]{:S(2)}) %collective-permute-start.11) | collective-permute-done | bytes 524320 | tf_op jit(solution)/shard_map/ppermute | solution.py:25
  211.9 6.9 %all-to-all-start.7 = ((bf16[8,32,1024]{2,1,0:T(8,128)(2,1)}), bf16[8,32,1024]{2,1,0:T(8,128)(2,1)S(1)}, u32[]{:S(2)}, u32[]{:S(2)}) async-start(bf16[8,32,1024]{2,1,0:T(8,128)(2,1)} %bitcast.11), calls=%async_computation.7 | async-start | bytes 1048576 | tf_op jit(solution)/shard_map/all_to_all | solution.py:29
  218.8 4.5 %fusion.8 = f32[512,1024]{1,0:T(8,128)} fusion(bf16[512,512]{1,0:T(8,128)(2,1)} %copy-done.10, bf16[512,512]{1,0:T(8,128)(2,1)} %copy-done.9, bf16[256,1024]{1,0:T(8,128)(2,1)} %copy-done.14, bf16[256,1024]{1,0:T(8,128)(2,1)} %copy-done.15, bf16[256,1024]{1,0:T(8,128)(2,1)} %copy-done.16, bf16[256,1024]{1,0:T(8,128)(2,1)} %copy-done.13), kind=kOutput, calls=%fused_computation.26 | convolution fusion | flops 1084227584 | bytes 5242880 | tf_op jit(solution)/shard_map/dot_general | solution.py:20
  224.0 4.4 %fusion.3 = f32[1024,512]{1,0:T(8,128)} fusion(bf16[512,1024]{1,0:T(8,128)(2,1)S(1)} %copy-done.4, bf16[512,1024]{1,0:T(8,128)(2,1)} %copy-done.5, bf16[256,1024]{1,0:T(8,128)(2,1)} %collective-permute-done.2, bf16[256,1024]{1,0:T(8,128)(2,1)} %collective-permute-done.1, bf16[256,1024]{1,0:T(8,128)(2,1)} %collective-permute-done, bf16[256,1024]{1,0:T(8,128)(2,1)} %bitcast.32), kind=kOutput, calls=%fused_computation.15 | convolution fusion | flops 1084227584 | bytes 6291456 | tf_op jit(solution)/shard_map/dot_general | solution.py:20
  228.4 4.0 %fusion.6 = f32[1024,512]{1,0:T(8,128)} fusion(bf16[512,1024]{1,0:T(8,128)(2,1)S(1)} %copy-done.4, bf16[512,1024]{1,0:T(8,128)(2,1)S(1)} %copy-done.6, bf16[256,1024]{1,0:T(8,128)(2,1)} %collective-permute-done.2, bf16[256,1024]{1,0:T(8,128)(2,1)} %collective-permute-done.1, bf16[256,1024]{1,0:T(8,128)(2,1)} %collective-permute-done, ...), kind=kOutput, calls=%fused_computation.17 | convolution fusion | flops 1084227584 | bytes 6291456 | tf_op jit(solution)/shard_map/dot_general | solution.py:20
  232.4 4.1 %all-to-all-done.7 = bf16[8,32,1024]{2,1,0:T(8,128)(2,1)S(1)} async-done(((bf16[8,32,1024]{2,1,0:T(8,128)(2,1)}), bf16[8,32,1024]{2,1,0:T(8,128)(2,1)S(1)}, u32[]{:S(2)}, u32[]{:S(2)}) %all-to-all-start.7) | async-done | bytes 524320 | tf_op jit(solution)/shard_map/all_to_all | solution.py:29
  (76 shorter events, 23.7 us)
Async XLA Ops:
  7.2 95.1 %copy-start = (bf16[512,1024]{1,0:T(8,128)(2,1)S(1)}, bf16[512,1024]{1,0:T(8,128)(2,1)}, u32[]{:S(2)}) copy-start(bf16[512,1024]{1,0:T(8,128)(2,1)} %param.8) | copy-start | bytes 3145732
  7.2 36.8 %copy-start.7 = (bf16[1024,512]{1,0:T(8,128)(2,1)S(1)}, bf16[1024,512]{1,0:T(8,128)(2,1)}, u32[]{:S(2)}) copy-start(bf16[1024,512]{1,0:T(8,128)(2,1)} %param.6) | copy-start | bytes 3145732
  34.0 32.8 %copy-start.11 = (bf16[8,32,1024]{2,1,0:T(8,128)(2,1)}, bf16[8,32,1024]{2,1,0:T(8,128)(2,1)S(1)}, u32[]{:S(2)}) copy-start(bf16[8,32,1024]{2,1,0:T(8,128)(2,1)S(1)} %all_to_all.69) | copy-start | bytes 1572868
  35.7 19.4 %all-to-all-start.4 = ((bf16[8,32,1024]{2,1,0:T(8,128)(2,1)}), bf16[8,32,1024]{2,1,0:T(8,128)(2,1)S(1)}, u32[]{:S(2)}, u32[]{:S(2)}) async-start(bf16[8,32,1024]{2,1,0:T(8,128)(2,1)} %broadcast_in_dim.10), calls=%async_computation.4 | async-start | bytes 1048576 | tf_op jit(solution)/shard_map/all_to_all | solution.py:29
  39.2 61.3 %all-gather.2.cloned.1.call-start = ((), (), s32[]{:S(2)}) async-start(), calls=%async_computation.8 | async-start | bytes 2621440 | tf_op jit(solution)/shard_map/all_gather | solution.py:49
  39.3 23.7 %collective-permute-start.2 = (bf16[256,1024]{1,0:T(8,128)(2,1)S(1)}, bf16[256,1024]{1,0:T(8,128)(2,1)}, u32[]{:S(2)}, u32[]{:S(2)}) collective-permute-start(bf16[256,1024]{1,0:T(8,128)(2,1)S(1)} %bitcast.28), channel_id=1, source_target_pairs={{0,24},{8,0},{16,8},{24,16},{1,25},{9,1},{17,9},{25,17},{2,26},{10... | collective-permute-start | bytes 1572872 | tf_op jit(solution)/shard_map/ppermute | solution.py:25
  42.4 20.6 %collective-permute-start.1 = (bf16[256,1024]{1,0:T(8,128)(2,1)S(1)}, bf16[256,1024]{1,0:T(8,128)(2,1)}, u32[]{:S(2)}, u32[]{:S(2)}) collective-permute-start(bf16[256,1024]{1,0:T(8,128)(2,1)S(1)} %bitcast.29), channel_id=1, source_target_pairs={{0,16},{8,24},{16,0},{24,8},{1,17},{9,25},{17,1},{25,9},{2,18},{10... | collective-permute-start | bytes 1572872 | tf_op jit(solution)/shard_map/ppermute | solution.py:25
  43.0 23.8 %collective-permute-start = (bf16[256,1024]{1,0:T(8,128)(2,1)S(1)}, bf16[256,1024]{1,0:T(8,128)(2,1)}, u32[]{:S(2)}, u32[]{:S(2)}) collective-permute-start(bf16[256,1024]{1,0:T(8,128)(2,1)S(1)} %bitcast.30), channel_id=1, source_target_pairs={{0,8},{8,16},{16,24},{24,0},{1,9},{9,17},{17,25},{25,1},{2,10},{10... | collective-permute-start | bytes 1572872 | tf_op jit(solution)/shard_map/ppermute | solution.py:25
  44.0 1.6 copy-start.8
  71.4 2.7 %collective-permute-start.3 = (bf16[512,1024]{1,0:T(8,128)(2,1)S(1)}, bf16[512,1024]{1,0:T(8,128)(2,1)S(1)}, u32[]{:S(2)}, u32[]{:S(2)}) collective-permute-start(bf16[512,1024]{1,0:T(8,128)(2,1)S(1)} %broadcast_select_fusion.2), channel_id=1, source_target_pairs={{0,32},{32,0},{1,33},{33,1},{2,34},{34,2},{3,35},{35,3},{4,36},{36... | collective-permute-start | bytes 3145736 | tf_op jit(solution)/shard_map/ppermute | solution.py:25
  75.7 18.8 %all-to-all-start.1 = ((bf16[4,128,1024]{2,1,0:T(8,128)(2,1)}), bf16[4,128,1024]{2,1,0:T(8,128)(2,1)S(1)}, u32[]{:S(2)}, u32[]{:S(2)}) async-start(bf16[4,128,1024]{2,1,0:T(8,128)(2,1)} %bitcast.1), calls=%async_computation.1 | async-start | bytes 2097152 | tf_op jit(solution)/shard_map/all_to_all | solution.py:29
  95.6 12.4 %all-to-all-start.2 = ((bf16[4,128,512]{2,1,0:T(8,128)(2,1)}), bf16[4,128,512]{2,1,0:T(8,128)(2,1)S(1)}, u32[]{:S(2)}, u32[]{:S(2)}) async-start(bf16[4,128,512]{2,1,0:T(8,128)(2,1)} %broadcast_in_dim.9), calls=%async_computation.2 | async-start | bytes 1048576 | tf_op jit(solution)/shard_map/all_to_all | solution.py:29
  102.2 1.4 copy-start.13
  102.2 1.4 copy-start.14
  104.4 3.5 %collective-permute-start.8 = (bf16[512,512]{1,0:T(8,128)(2,1)}, bf16[512,512]{1,0:T(8,128)(2,1)}, u32[]{:S(2)}, u32[]{:S(2)}) collective-permute-start(bf16[512,512]{1,0:T(8,128)(2,1)} %broadcast_select_fusion.3), channel_id=1, source_target_pairs={{0,32},{32,0},{1,33},{33,1},{2,34},{34,2},{3,35},{35,3},{4,36},{36... | collective-permute-start | bytes 1572872 | tf_op jit(solution)/shard_map/ppermute | solution.py:25
  107.9 6.9 %collective-permute-start.4 = (bf16[512,512]{1,0:T(8,128)(2,1)S(1)}, bf16[512,512]{1,0:T(8,128)(2,1)}, u32[]{:S(2)}, u32[]{:S(2)}) collective-permute-start(bf16[512,512]{1,0:T(8,128)(2,1)S(1)} %bitcast.25), channel_id=1, source_target_pairs={{0,32},{32,0},{1,33},{33,1},{2,34},{34,2},{3,35},{35,3},{4,36},{36... | collective-permute-start | bytes 1572872 | tf_op jit(solution)/shard_map/ppermute | solution.py:25
  110.0 13.9 %all-to-all-start.5 = ((bf16[4,128,512]{2,1,0:T(8,128)(2,1)}), bf16[4,128,512]{2,1,0:T(8,128)(2,1)S(1)}, u32[]{:S(2)}, u32[]{:S(2)}) async-start(bf16[4,128,512]{2,1,0:T(8,128)(2,1)} %bitcast.26), calls=%async_computation.5 | async-start | bytes 1048576 | tf_op jit(solution)/shard_map/all_to_all | solution.py:29
  124.1 18.0 %copy-start.1 = (bf16[1024,1024]{1,0:T(8,128)(2,1)S(1)}, bf16[1024,1024]{1,0:T(8,128)(2,1)}, u32[]{:S(2)}) copy-start(bf16[1024,1024]{1,0:T(8,128)(2,1)} %convolution_convert_fusion) | copy-start | bytes 6291460
  142.1 35.9 %collective-permute-start.9 = (bf16[512,1024]{1,0:T(8,128)(2,1)S(1)}, bf16[512,1024]{1,0:T(8,128)(2,1)}, u32[]{:S(2)}, u32[]{:S(2)}) collective-permute-start(bf16[512,1024]{1,0:T(8,128)(2,1)S(1)} %bitcast.24), channel_id=1, source_target_pairs={{0,32},{32,0},{1,33},{33,1},{2,34},{34,2},{3,35},{35,3},{4,36},{36... | collective-permute-start | bytes 3145736 | tf_op jit(solution)/shard_map/ppermute | solution.py:25
  142.2 15.0 %collective-permute-start.5 = (bf16[256,1024]{1,0:T(8,128)(2,1)S(1)}, bf16[256,1024]{1,0:T(8,128)(2,1)S(1)}, u32[]{:S(2)}, u32[]{:S(2)}) collective-permute-start(bf16[256,1024]{1,0:T(8,128)(2,1)S(1)} %get-tuple-element.20), channel_id=1, source_target_pairs={{0,24},{8,0},{16,8},{24,16},{1,25},{9,1},{17,9},{25,17},{2,26},{10... | collective-permute-start | bytes 1572872 | tf_op jit(solution)/shard_map/ppermute | solution.py:25
  143.3 16.3 %collective-permute-start.7 = (bf16[256,1024]{1,0:T(8,128)(2,1)S(1)}, bf16[256,1024]{1,0:T(8,128)(2,1)S(1)}, u32[]{:S(2)}, u32[]{:S(2)}) collective-permute-start(bf16[256,1024]{1,0:T(8,128)(2,1)S(1)} %get-tuple-element.21), channel_id=1, source_target_pairs={{0,16},{8,24},{16,0},{24,8},{1,17},{9,25},{17,1},{25,9},{2,18},{10... | collective-permute-start | bytes 1572872 | tf_op jit(solution)/shard_map/ppermute | solution.py:25
  143.9 26.2 %collective-permute-start.6 = (bf16[256,1024]{1,0:T(8,128)(2,1)S(1)}, bf16[256,1024]{1,0:T(8,128)(2,1)S(1)}, u32[]{:S(2)}, u32[]{:S(2)}) collective-permute-start(bf16[256,1024]{1,0:T(8,128)(2,1)S(1)} %get-tuple-element.22), channel_id=1, source_target_pairs={{0,8},{8,16},{16,24},{24,0},{1,9},{9,17},{17,25},{25,1},{2,10},{10... | collective-permute-start | bytes 1572872 | tf_op jit(solution)/shard_map/ppermute | solution.py:25
  171.2 40.7 %all-to-all-start.3 = ((bf16[8,32,1024]{2,1,0:T(8,128)(2,1)}), bf16[8,32,1024]{2,1,0:T(8,128)(2,1)S(1)}, u32[]{:S(2)}, u32[]{:S(2)}) async-start(bf16[8,32,1024]{2,1,0:T(8,128)(2,1)} %bitcast.3), calls=%async_computation.3 | async-start | bytes 1048576 | tf_op jit(solution)/shard_map/all_to_all | solution.py:29
  179.3 4.7 %copy-start.3 = (bf16[512,1024]{1,0:T(8,128)(2,1)}, bf16[512,1024]{1,0:T(8,128)(2,1)S(1)}, u32[]{:S(2)}) copy-start(bf16[512,1024]{1,0:T(8,128)(2,1)S(1)} %get-tuple-element.14) | copy-start | bytes 3145732
  179.3 4.7 %copy-start.5 = (bf16[512,1024]{1,0:T(8,128)(2,1)}, bf16[512,1024]{1,0:T(8,128)(2,1)S(1)}, u32[]{:S(2)}) copy-start(bf16[512,1024]{1,0:T(8,128)(2,1)S(1)} %get-tuple-element.15) | copy-start | bytes 3145732
  184.2 14.9 %collective-permute-start.10 = (bf16[256,1024]{1,0:T(8,128)(2,1)S(1)}, bf16[256,1024]{1,0:T(8,128)(2,1)S(1)}, u32[]{:S(2)}, u32[]{:S(2)}) collective-permute-start(bf16[256,1024]{1,0:T(8,128)(2,1)S(1)} %get-tuple-element.11), channel_id=1, source_target_pairs={{0,24},{8,0},{16,8},{24,16},{1,25},{9,1},{17,9},{25,17},{2,26},{10... | collective-permute-start | bytes 1572872 | tf_op jit(solution)/shard_map/ppermute | solution.py:25
  184.9 16.4 %collective-permute-start.12 = (bf16[256,1024]{1,0:T(8,128)(2,1)S(1)}, bf16[256,1024]{1,0:T(8,128)(2,1)S(1)}, u32[]{:S(2)}, u32[]{:S(2)}) collective-permute-start(bf16[256,1024]{1,0:T(8,128)(2,1)S(1)} %get-tuple-element.12), channel_id=1, source_target_pairs={{0,16},{8,24},{16,0},{24,8},{1,17},{9,25},{17,1},{25,9},{2,18},{10... | collective-permute-start | bytes 1572872 | tf_op jit(solution)/shard_map/ppermute | solution.py:25
  185.5 25.2 %collective-permute-start.11 = (bf16[256,1024]{1,0:T(8,128)(2,1)S(1)}, bf16[256,1024]{1,0:T(8,128)(2,1)S(1)}, u32[]{:S(2)}, u32[]{:S(2)}) collective-permute-start(bf16[256,1024]{1,0:T(8,128)(2,1)S(1)} %get-tuple-element.13), channel_id=1, source_target_pairs={{0,8},{8,16},{16,24},{24,0},{1,9},{9,17},{17,25},{25,1},{2,10},{10... | collective-permute-start | bytes 1572872 | tf_op jit(solution)/shard_map/ppermute | solution.py:25
  211.9 24.6 %all-to-all-start.7 = ((bf16[8,32,1024]{2,1,0:T(8,128)(2,1)}), bf16[8,32,1024]{2,1,0:T(8,128)(2,1)S(1)}, u32[]{:S(2)}, u32[]{:S(2)}) async-start(bf16[8,32,1024]{2,1,0:T(8,128)(2,1)} %bitcast.11), calls=%async_computation.7 | async-start | bytes 1048576 | tf_op jit(solution)/shard_map/all_to_all | solution.py:29
  218.8 5.2 %copy-start.4 = (bf16[512,1024]{1,0:T(8,128)(2,1)S(1)}, bf16[512,1024]{1,0:T(8,128)(2,1)}, u32[]{:S(2)}) copy-start(bf16[512,1024]{1,0:T(8,128)(2,1)} %copy-done.3) | copy-start | bytes 3145732
  224.0 4.4 %copy-start.6 = (bf16[512,1024]{1,0:T(8,128)(2,1)S(1)}, bf16[512,1024]{1,0:T(8,128)(2,1)}, u32[]{:S(2)}) copy-start(bf16[512,1024]{1,0:T(8,128)(2,1)} %copy-done.5) | copy-start | bytes 3145732
  224.0 4.4 %copy-start.12 = (bf16[8,32,1024]{2,1,0:T(8,128)(2,1)S(1)}, bf16[8,32,1024]{2,1,0:T(8,128)(2,1)}, u32[]{:S(2)}) copy-start(bf16[8,32,1024]{2,1,0:T(8,128)(2,1)} %copy-done.11) | copy-start | bytes 1572868
  (5 other events, 5.3 us)
Sparse Core Ops, SparseCore 0:
  56.1 29.7 all-gather.1

commit v3 on v2

--- a/solution.py
+++ b/solution.py
@@ -41,8 +41,10 @@
 
 
 def gather_y(own):
-    near = [shift(own, "y", 1), shift(own, "y", 3)]
-    return jnp.concatenate([own, near[0], shift(own, "y", 2), near[1]], axis=0)
+    rows = own.shape[0] // 2
+    from_left, from_right = shift(own, "y", 1), shift(own, "y", 3)
+    far = [shift(from_left[:rows], "y", 1), shift(from_right[rows:], "y", 3)]
+    return jnp.concatenate([own, from_left] + far + [from_right], axis=0)
 
 
 def gather_y_later(own):
@@ -79,12 +81,33 @@
     return jnp.concatenate([jnp.where(first, half, other), jnp.where(first, other, half)], axis=0)
 
 
-def reduce_col(partial):
+def add(left_side, right_side):
+    return (left_side.astype(F32) + right_side.astype(F32)).astype(BF)
+
+
+def split_y(partial):
     rows = partial.shape[0] // Y
-    pieces = [partial[j * rows : (j + 1) * rows] for j in range(Y)]
-    moved = [shift(pieces[1], "y", 3), shift(pieces[3], "y", 1), shift(pieces[2], "y", 2)]
-    total = pieces[0].astype(F32) + moved[0].astype(F32) + moved[1].astype(F32) + moved[2].astype(F32)
-    return sum_parts(exchange(total.astype(BF), "z"), Z).astype(BF)
+    return [partial[j * rows : (j + 1) * rows] for j in range(Y)]
+
+
+def reduce_y_far(pieces):
+    rows = pieces[2].shape[0] // 2
+    return shift(pieces[2][:rows], "y", 1), shift(pieces[2][rows:], "y", 3)
+
+
+def reduce_y_near(pieces, from_left, from_right):
+    rows = pieces[2].shape[0] // 2
+    to_right = jnp.concatenate([add(pieces[3][:rows], from_left), pieces[3][rows:]], axis=0)
+    to_left = jnp.concatenate([pieces[1][:rows], add(pieces[1][rows:], from_right)], axis=0)
+    return shift(to_right, "y", 1), shift(to_left, "y", 3)
+
+
+def sum_y(own, from_left, from_right):
+    return (own.astype(F32) + from_left.astype(F32) + from_right.astype(F32)).astype(BF)
+
+
+def reduce_z(total):
+    return sum_parts(exchange(total, "z"), Z).astype(BF)
 
 
 def body(tokens, gate_weight, up_weight, down_weight, out_grad):
@@ -94,27 +117,41 @@
     all_tokens = gather_y(tokens_z)
     grads_z = gather(after(out_grad, tokens_z), "z")
     all_grads = gather_y_later(grads_z)
+
     gate_up = reduce_x(reduce_core(product(all_tokens, both_weights).astype(BF)))
     gate_value = gate_up[:, :width]
     up_value = gate_up[:, width:]
     sigmoid_gate = jax.nn.sigmoid(gate_value)
     silu_gate = gate_value * sigmoid_gate
-    hidden_half = gather((silu_gate * up_value).astype(BF), "x")
-    hidden = gather_core(hidden_half)
-    output_partial = product(hidden, down_weight).astype(BF)
-    layer_output = reduce_col(output_partial)
+    hidden_share = (silu_gate * up_value).astype(BF)
 
     hidden_partial = reduce_core(product_right_t(all_grads, down_weight).astype(BF))
-    hidden_grad = reduce_x(after(hidden_partial, hidden_half))
+    rows = hidden_share.shape[0]
+    mixed = jnp.concatenate(
+        [jnp.broadcast_to(hidden_share[None], (X, rows, width)), hidden_partial.reshape(X, rows, width)], axis=1
+    )
+    mixed = exchange(mixed.reshape(2 * X * rows, width), "x").reshape(X, 2 * rows, width)
+    hidden = gather_core(mixed[:, :rows].reshape(X * rows, width))
+    hidden_grad = jnp.sum(mixed[:, rows:].astype(F32), axis=0)
+
+    output_pieces = split_y(product(hidden, down_weight).astype(BF))
+    output_far = reduce_y_far(output_pieces)
+    output_near = reduce_y_near(output_pieces, *output_far)
+
     gate_grad = (hidden_grad * up_value * sigmoid_gate * (1.0 + gate_value * (1.0 - sigmoid_gate))).astype(BF)
     up_grad = (hidden_grad * silu_gate).astype(BF)
-    both_share = after(jnp.concatenate([gate_grad, up_grad], axis=1), output_partial)
-    both_grads = gather_core(gather(both_share, "x"))
-    input_grad = reduce_col(product_right_t(both_grads, both_weights).astype(BF))
+    both_half = after(gather(jnp.concatenate([gate_grad, up_grad], axis=1), "x"), *output_far)
+    both_grads = after(gather_core(both_half), *output_near)
+
+    input_pieces = split_y(product_right_t(both_grads, both_weights).astype(BF))
+    input_near = reduce_y_near(input_pieces, *reduce_y_far(input_pieces))
+    layer_output = reduce_z(sum_y(output_pieces[0], *output_near))
     gate_weight_grad = product_left_t(all_tokens, both_grads[:, :width])
     up_weight_grad = product_left_t(all_tokens, both_grads[:, width:])
     down_weight_grad = product_left_t(hidden, all_grads)
-    return (layer_output, input_grad, gate_weight_grad, up_weight_grad, down_weight_grad)
+    weight_grads = (gate_weight_grad, up_weight_grad, down_weight_grad)
+    input_total, weight_grads = lax.optimization_barrier((sum_y(input_pieces[0], *input_near), weight_grads))
+    return (layer_output, reduce_z(input_total)) + weight_grads
 
 
 def solution(mesh):

time: 247 us -> 218 us (0.88)
  waiting for transfers between devices: 97.6 us -> 70.2 us
  matrix products: 25.9 us -> 15.1 us
  other arithmetic: 11.3 us -> 18.8 us
  starting transfers between devices: 41.2 us -> 43.8 us
    ppermute x13 -> x16, waiting for transfers between devices: 63.2 us -> 27.4 us  [shift(): lax.ppermute(block, axis, [(i, (i + step) % size) for i in range(size)])]
    ppermute x13 -> x16, starting transfers between devices: 9.43 us -> 20.8 us  [shift(): lax.ppermute(block, axis, [(i, (i + step) % size) for i in range(size)])]
    all_to_all x6 -> x5, starting transfers between devices: 31.8 us -> 23 us  [exchange(): return lax.all_to_all(blocks, axis, split_axis=0, concat_axis=0, tiled=True)]
    dot_general x3, matrix products: 12.9 us -> 7.84 us  [product_left_t(): lax.dot_general(left_side, right_side, (((0,), (0,)), ((), ())), preferre...]
    convert_element_type x3 -> x5, other arithmetic: 2.37 us -> 7.31 us  [the longest x2 4.25 us: sum_y(): (own.astype(F32) + from_left.astype(F32) + from_right.astype(F32)).astype...]
    all_gather x1, waiting for transfers between devices: 0.01 us -> 4.36 us  [gather_y_later(): pieces = lax.all_gather(own, 'y', axis=0, tiled=False)]
    all_to_all x6 -> x5, waiting for transfers between devices: 34.3 us -> 38.5 us  [exchange(): return lax.all_to_all(blocks, axis, split_axis=0, concat_axis=0, tiled=True)]
    dot_general x2, matrix products: 6.98 us -> 3.6 us  [product(): return jnp.dot(left_side, right_side, preferred_element_type=F32)]
  transfers between devices with their start and end apart: 20 -> 22, of which waited for: 14 -> 12; matrix products, arithmetic and copies ran while one was open for 17% -> 16% of each run, Pallas kernels for 0% -> 0%
where the time goes in v3:
time: 218 us; the launch traced here: 217 us
  waiting for transfers between devices  70.2 us (32%)
  starting transfers between devices  43.8 us (20%)
  blocking collectives  42.7 us (20%)
  other arithmetic  18.8 us (9%)
  matrix products  15.1 us (7%)
  between operations  14.6 us (7%)
  local copies, waits for them, and re-layouts  11.5 us (5%)
    all_to_all x2, blocking collectives, exchange(): return lax.all_to_all(blocks, axis, split_axis=0, concat_axis=0, tiled=True)  42.7 us
    all_to_all x5, waiting for transfers between devices, exchange(): return lax.all_to_all(blocks, axis, split_axis=0, concat_axis=0, tiled=True)  38.5 us
    ppermute x16, waiting for transfers between devices, shift(): lax.ppermute(block, axis, [(i, (i + step) % size) for i in range(size)])  27.4 us
    all_to_all x5, starting transfers between devices, exchange(): return lax.all_to_all(blocks, axis, split_axis=0, concat_axis=0, tiled=True)  23 us
    ppermute x16, starting transfers between devices, shift(): lax.ppermute(block, axis, [(i, (i + step) % size) for i in range(size)])  20.8 us
    dot_general x3, matrix products, product_left_t(): lax.dot_general(left_side, right_side, (((0,), (0,)), ((), ())), preferre...  7.84 us
    all_gather x1, waiting for transfers between devices, gather_y_later(): pieces = lax.all_gather(own, 'y', axis=0, tiled=False)  4.36 us
  transfers between devices with their start and end apart: 22, of which 12 were waited for; matrix products, arithmetic and copies ran while one was open for 16% of the time, Pallas kernels for 0%

profile of v3, /device:TPU:2, one launch (start us, length us, event | category | flops | bytes accessed | tf_op | source)
XLA Modules:
  0.0 216.8 jit_solution(3421922338420741083)
XLA Ops:
  8.2 25.8 %all_to_all.57 = bf16[8,32,1024]{2,1,0:T(8,128)(2,1)S(1)} all-to-all(bf16[8,32,1024]{2,1,0:T(8,128)(2,1)S(1)} %broadcast_in_dim.8), channel_id=1, replica_groups=mesh['x'=4,'core'=2,'y'=4,'z'=8] {'z'}, dimensions={0} | all-to-all | bytes 1048576 | tf_op jit(solution)/shard_map/all_to_all | solution.py:29
  35.6 3.5 %all-to-all-start.2 = ((bf16[8,32,1024]{2,1,0:T(8,128)(2,1)}), bf16[8,32,1024]{2,1,0:T(8,128)(2,1)S(1)}, u32[]{:S(2)}, u32[]{:S(2)}) async-start(bf16[8,32,1024]{2,1,0:T(8,128)(2,1)} %broadcast_in_dim.10), calls=%async_computation.2 | async-start | bytes 1048576 | tf_op jit(solution)/shard_map/all_to_all | solution.py:29
  42.5 12.5 %all-to-all-done.2 = bf16[8,32,1024]{2,1,0:T(8,128)(2,1)S(1)} async-done(((bf16[8,32,1024]{2,1,0:T(8,128)(2,1)}), bf16[8,32,1024]{2,1,0:T(8,128)(2,1)S(1)}, u32[]{:S(2)}, u32[]{:S(2)}) %all-to-all-start.2) | async-done | bytes 524320 | tf_op jit(solution)/shard_map/all_to_all | solution.py:29
  62.4 2.7 %collective-permute-done.1 = bf16[128,1024]{1,0:T(8,128)(2,1)S(1)} collective-permute-done((bf16[128,1024]{1,0:T(8,128)(2,1)S(1)}, bf16[128,1024]{1,0:T(8,128)(2,1)S(1)}, u32[]{:S(2)}, u32[]{:S(2)}) %collective-permute-start.1) | collective-permute-done | bytes 262176 | tf_op jit(solution)/shard_map/ppermute | solution.py:25
  65.0 2.1 collective-permute-done.3
  67.2 2.3 %convolution_convert_fusion.2 = bf16[1024,1024]{1,0:T(8,128)(2,1)S(1)} fusion(bf16[1024,1024]{1,0:T(8,128)(2,1)S(1)} %constant_dynamic-update-slice_fusion, bf16[1024,1024]{1,0:T(8,128)(2,1)S(1)} %copy-done.8), kind=kOutput, calls=%fused_computation.6 | convolution fusion | flops 2148532224 | bytes 6291456 | tf_op jit(solution)/shard_map/dot_general | solution.py:12
  70.7 3.0 %collective-permute-done.4 = bf16[512,1024]{1,0:T(8,128)(2,1)} collective-permute-done((bf16[512,1024]{1,0:T(8,128)(2,1)}, bf16[512,1024]{1,0:T(8,128)(2,1)}, u32[]{:S(2)}, u32[]{:S(2)}) %collective-permute-start.4) | collective-permute-done | bytes 1048608 | tf_op jit(solution)/shard_map/ppermute | solution.py:25
  73.7 2.8 %add_convert_fusion = bf16[512,1024]{1,0:T(8,128)(2,1)} fusion(bf16[512,1024]{1,0:T(8,128)(2,1)} %collective-permute-done.4, pred[]{:T(512)S(6)} %eq.2, bf16[1024,1024]{1,0:T(8,128)(2,1)S(1)} %convolution_convert_fusion.2), kind=kLoop, calls=%fused_computation.3 | loop fusion | flops 2621440 | bytes 4194305 | tf_op jit(solution)/shard_map/convert_element_type | solution.py:71
  76.5 4.9 %all-to-all-start.1 = ((bf16[4,128,1024]{2,1,0:T(8,128)(2,1)}), bf16[4,128,1024]{2,1,0:T(8,128)(2,1)S(1)}, u32[]{:S(2)}, u32[]{:S(2)}) async-start(bf16[4,128,1024]{2,1,0:T(8,128)(2,1)} %bitcast.28), calls=%async_computation.1 | async-start | bytes 2097152 | tf_op jit(solution)/shard_map/all_to_all | solution.py:29
  81.4 4.4 %all-gather.2.cloned.1.call-done = bf16[4,256,1024]{2,1,0:T(8,128)(2,1)} async-done(((bf16[1,256,1024]{2,1,0:T(8,128)(2,1)}), bf16[4,256,1024]{2,1,0:T(8,128)(2,1)}) %all-gather.2.cloned.1.call-update) | async-done | bytes 2097168 | tf_op jit(solution)/shard_map/all_gather | solution.py:51
  89.7 5.6 %all-to-all-done.1 = bf16[4,128,1024]{2,1,0:T(8,128)(2,1)S(1)} async-done(((bf16[4,128,1024]{2,1,0:T(8,128)(2,1)}), bf16[4,128,1024]{2,1,0:T(8,128)(2,1)S(1)}, u32[]{:S(2)}, u32[]{:S(2)}) %all-to-all-start.1) | async-done | bytes 1048608 | tf_op jit(solution)/shard_map/all_to_all | solution.py:29
  97.0 16.9 %all_to_all.58 = bf16[4,256,512]{2,1,0:T(8,128)(2,1)S(1)} all-to-all(bf16[4,256,512]{2,1,0:T(8,128)(2,1)S(1)} %pad_maximum_fusion.2), channel_id=1, replica_groups=mesh['x'=4,'core'=2,'y'=4,'z'=8] {'x'}, dimensions={0} | all-to-all | bytes 2097152 | tf_op jit(solution)/shard_map/all_to_all | solution.py:29
  115.4 4.9 %all-to-all-start.5 = ((bf16[4,128,1024]{2,1,0:T(8,128)(2,1)}), bf16[4,128,1024]{2,1,0:T(8,128)(2,1)S(1)}, u32[]{:S(2)}, u32[]{:S(2)}) async-start(bf16[4,128,1024]{2,1,0:T(8,128)(2,1)} %broadcast_in_dim.11), calls=%async_computation.5 | async-start | bytes 2097152 | tf_op jit(solution)/shard_map/all_to_all | solution.py:29
  125.2 2.7 %collective-permute-start.9 = (bf16[128,1024]{1,0:T(8,128)(2,1)}, bf16[128,1024]{1,0:T(8,128)(2,1)}, u32[]{:S(2)}, u32[]{:S(2)}) collective-permute-start(bf16[128,1024]{1,0:T(8,128)(2,1)} %get-tuple-element.30), channel_id=1, source_target_pairs={{0,24},{8,0},{16,8},{24,16},{1,25},{9,1},{17,9},{25,17},{2,26},{10... | collective-permute-start | bytes 786440 | tf_op jit(solution)/shard_map/ppermute | solution.py:25
  128.0 7.0 %all-to-all-done.5 = bf16[4,128,1024]{2,1,0:T(8,128)(2,1)S(1)} async-done(((bf16[4,128,1024]{2,1,0:T(8,128)(2,1)}), bf16[4,128,1024]{2,1,0:T(8,128)(2,1)S(1)}, u32[]{:S(2)}, u32[]{:S(2)}) %all-to-all-start.5) | async-done | bytes 1048608 | tf_op jit(solution)/shard_map/all_to_all | solution.py:29
  136.6 3.8 %collective-permute-start.10 = (bf16[256,1024]{1,0:T(8,128)(2,1)S(1)}, bf16[256,1024]{1,0:T(8,128)(2,1)S(1)}, u32[]{:S(2)}, u32[]{:S(2)}) collective-permute-start(bf16[256,1024]{1,0:T(8,128)(2,1)S(1)} %pad_maximum_fusion.7), channel_id=1, source_target_pairs={{0,24},{8,0},{16,8},{24,16},{1,25},{9,1},{17,9},{25,17},{2,26},{10... | collective-permute-start | bytes 1572872 | tf_op jit(solution)/shard_map/ppermute | solution.py:25
  140.5 2.6 %fusion.4 = f32[512,1024]{1,0:T(8,128)} fusion(bf16[512,512]{1,0:T(8,128)(2,1)S(1)} %copy-done.6, bf16[512,512]{1,0:T(8,128)(2,1)S(1)} %get-tuple-element.37, bf16[256,1024]{1,0:T(8,128)(2,1)S(1)} %copy-done.13, bf16[256,1024]{1,0:T(8,128)(2,1)S(1)} %copy-done.15, bf16[256,1024]{1,0:T(8,128)(2,1)S(1)} %copy-done.17, bf16[256,1024]{1,0:T(8,128)(2,1)S(1)} %copy-done.11), kind=kOutput, calls=%fused_computation.21 | convolution fusion | flops 1084227584 | bytes 5242880 | tf_op jit(solution)/shard_map/dot_general | solution.py:20
  143.5 8.6 %collective-permute-done.10 = bf16[256,1024]{1,0:T(8,128)(2,1)S(1)} collective-permute-done((bf16[256,1024]{1,0:T(8,128)(2,1)S(1)}, bf16[256,1024]{1,0:T(8,128)(2,1)S(1)}, u32[]{:S(2)}, u32[]{:S(2)}) %collective-permute-start.10) | collective-permute-done | bytes 524320 | tf_op jit(solution)/shard_map/ppermute | solution.py:25
  152.1 3.5 %collective-permute-done.8 = bf16[256,1024]{1,0:T(8,128)(2,1)S(1)} collective-permute-done((bf16[256,1024]{1,0:T(8,128)(2,1)S(1)}, bf16[256,1024]{1,0:T(8,128)(2,1)S(1)}, u32[]{:S(2)}, u32[]{:S(2)}) %collective-permute-start.8) | collective-permute-done | bytes 524320 | tf_op jit(solution)/shard_map/ppermute | solution.py:25
  155.6 2.4 %convolution_convert_fusion = bf16[1024,1024]{1,0:T(8,128)(2,1)S(1)} fusion(bf16[1024,1024]{1,0:T(8,128)(2,1)S(1)} %pad_maximum_fusion.1, bf16[1024,1024]{1,0:T(8,128)(2,1)S(1)} %copy-done.9), kind=kOutput, calls=%fused_computation.4 | convolution fusion | flops 2148532224 | bytes 6291456 | tf_op jit(solution)/shard_map/dot_general | solution.py:16
  159.0 3.2 %collective-permute-start.14 = (bf16[128,1024]{1,0:T(8,128)(2,1)}, bf16[128,1024]{1,0:T(8,128)(2,1)}, u32[]{:S(2)}, u32[]{:S(2)}) collective-permute-start(bf16[128,1024]{1,0:T(8,128)(2,1)} %get-tuple-element.22), channel_id=1, source_target_pairs={{0,24},{8,0},{16,8},{24,16},{1,25},{9,1},{17,9},{25,17},{2,26},{10... | collective-permute-start | bytes 786440 | tf_op jit(solution)/shard_map/ppermute | solution.py:25
  162.2 2.1 add_convert_fusion.2
  164.4 4.1 %all-to-all-start.4 = ((bf16[8,32,1024]{2,1,0:T(8,128)(2,1)}), bf16[8,32,1024]{2,1,0:T(8,128)(2,1)}, u32[]{:S(2)}, u32[]{:S(2)}) async-start(bf16[8,32,1024]{2,1,0:T(8,128)(2,1)} %bitcast.35), calls=%async_computation.4 | async-start | bytes 1048576 | tf_op jit(solution)/shard_map/all_to_all | solution.py:29
  171.1 2.3 %collective-permute-start.15 = (bf16[256,1024]{1,0:T(8,128)(2,1)S(1)}, bf16[256,1024]{1,0:T(8,128)(2,1)S(1)}, u32[]{:S(2)}, u32[]{:S(2)}) collective-permute-start(bf16[256,1024]{1,0:T(8,128)(2,1)S(1)} %pad_maximum_fusion.9), channel_id=1, source_target_pairs={{0,24},{8,0},{16,8},{24,16},{1,25},{9,1},{17,9},{25,17},{2,26},{10... | collective-permute-start | bytes 1572872 | tf_op jit(solution)/shard_map/ppermute | solution.py:25
  173.7 2.6 %fusion = f32[1024,512]{1,0:T(8,128)} fusion(bf16[1024,1024]{1,0:T(8,128)(2,1)S(1)} %copy-done.19, bf16[1024,1024]{1,0:T(8,128)(2,1)S(1)} %pad_maximum_fusion.1), kind=kOutput, calls=%fused_computation.10 | convolution fusion | flops 1073741824 | bytes 5242880 | tf_op jit(solution)/shard_map/dot_general | solution.py:20
  176.3 2.6 %fusion.2 = f32[1024,512]{1,0:T(8,128)} fusion(bf16[1024,1024]{1,0:T(8,128)(2,1)S(1)} %copy-done.19, bf16[1024,1024]{1,0:T(8,128)(2,1)S(1)} %pad_maximum_fusion.1), kind=kOutput, calls=%fused_computation.12 | convolution fusion | flops 1073741824 | bytes 5242880 | tf_op jit(solution)/shard_map/dot_general | solution.py:20
  179.0 4.7 %collective-permute-done.15 = bf16[256,1024]{1,0:T(8,128)(2,1)S(1)} collective-permute-done((bf16[256,1024]{1,0:T(8,128)(2,1)S(1)}, bf16[256,1024]{1,0:T(8,128)(2,1)S(1)}, u32[]{:S(2)}, u32[]{:S(2)}) %collective-permute-start.15) | collective-permute-done | bytes 524320 | tf_op jit(solution)/shard_map/ppermute | solution.py:25
  183.7 2.8 %collective-permute-done.13 = bf16[256,1024]{1,0:T(8,128)(2,1)S(1)} collective-permute-done((bf16[256,1024]{1,0:T(8,128)(2,1)S(1)}, bf16[256,1024]{1,0:T(8,128)(2,1)S(1)}, u32[]{:S(2)}, u32[]{:S(2)}) %collective-permute-start.13) | collective-permute-done | bytes 524320 | tf_op jit(solution)/shard_map/ppermute | solution.py:25
  186.5 2.1 add_convert_fusion.1
  188.6 5.6 %all-to-all-start.6 = ((bf16[8,32,1024]{2,1,0:T(8,128)(2,1)}), bf16[8,32,1024]{2,1,0:T(8,128)(2,1)S(1)}, u32[]{:S(2)}, u32[]{:S(2)}) async-start(bf16[8,32,1024]{2,1,0:T(8,128)(2,1)} %bitcast.11), calls=%async_computation.6 | async-start | bytes 1048576 | tf_op jit(solution)/shard_map/all_to_all | solution.py:29
  194.1 1.8 reduce_sum.43
  195.9 13.4 %all-to-all-done.6 = bf16[8,32,1024]{2,1,0:T(8,128)(2,1)S(1)} async-done(((bf16[8,32,1024]{2,1,0:T(8,128)(2,1)}), bf16[8,32,1024]{2,1,0:T(8,128)(2,1)S(1)}, u32[]{:S(2)}, u32[]{:S(2)}) %all-to-all-start.6) | async-done | bytes 524320 | tf_op jit(solution)/shard_map/all_to_all | solution.py:29
  (102 shorter events, 32.9 us)
Async XLA Ops:
  7.2 80.3 %copy-start = (bf16[512,1024]{1,0:T(8,128)(2,1)S(1)}, bf16[512,1024]{1,0:T(8,128)(2,1)}, u32[]{:S(2)}) copy-start(bf16[512,1024]{1,0:T(8,128)(2,1)} %param.8) | copy-start | bytes 3145732
  35.6 19.4 %all-to-all-start.2 = ((bf16[8,32,1024]{2,1,0:T(8,128)(2,1)}), bf16[8,32,1024]{2,1,0:T(8,128)(2,1)S(1)}, u32[]{:S(2)}, u32[]{:S(2)}) async-start(bf16[8,32,1024]{2,1,0:T(8,128)(2,1)} %broadcast_in_dim.10), calls=%async_computation.2 | async-start | bytes 1048576 | tf_op jit(solution)/shard_map/all_to_all | solution.py:29
  39.1 46.6 %all-gather.2.cloned.1.call-start = ((), (), s32[]{:S(2)}) async-start(), calls=%async_computation.7 | async-start | bytes 2621440 | tf_op jit(solution)/shard_map/all_gather | solution.py:51
  39.2 18.2 %collective-permute-start = (bf16[256,1024]{1,0:T(8,128)(2,1)S(1)}, bf16[256,1024]{1,0:T(8,128)(2,1)S(1)}, u32[]{:S(2)}, u32[]{:S(2)}) collective-permute-start(bf16[256,1024]{1,0:T(8,128)(2,1)S(1)} %bitcast.31), channel_id=1, source_target_pairs={{0,8},{8,16},{16,24},{24,0},{1,9},{9,17},{17,25},{25,1},{2,10},{10... | collective-permute-start | bytes 1572872 | tf_op jit(solution)/shard_map/ppermute | solution.py:25
  40.8 19.7 %collective-permute-start.2 = (bf16[256,1024]{1,0:T(8,128)(2,1)S(1)}, bf16[256,1024]{1,0:T(8,128)(2,1)S(1)}, u32[]{:S(2)}, u32[]{:S(2)}) collective-permute-start(bf16[256,1024]{1,0:T(8,128)(2,1)S(1)} %bitcast.32), channel_id=1, source_target_pairs={{0,24},{8,0},{16,8},{24,16},{1,25},{9,1},{17,9},{25,17},{2,26},{10... | collective-permute-start | bytes 1572872 | tf_op jit(solution)/shard_map/ppermute | solution.py:25
  57.4 7.7 %collective-permute-start.1 = (bf16[128,1024]{1,0:T(8,128)(2,1)S(1)}, bf16[128,1024]{1,0:T(8,128)(2,1)S(1)}, u32[]{:S(2)}, u32[]{:S(2)}) collective-permute-start(bf16[128,1024]{1,0:T(8,128)(2,1)S(1)} %slice.122), channel_id=1, source_target_pairs={{0,8},{8,16},{16,24},{24,0},{1,9},{9,17},{17,25},{25,1},{2,10},{10... | collective-permute-start | bytes 786440 | tf_op jit(solution)/shard_map/ppermute | solution.py:25
  60.5 6.7 %copy-start.8 = (bf16[1024,1024]{1,0:T(8,128)(2,1)S(1)}, bf16[1024,1024]{1,0:T(8,128)(2,1)}, u32[]{:S(2)}) copy-start(bf16[1024,1024]{1,0:T(8,128)(2,1)} %copy-done.7) | copy-start | bytes 6291460
  60.5 6.6 %collective-permute-start.3 = (bf16[128,1024]{1,0:T(8,128)(2,1)S(1)}, bf16[128,1024]{1,0:T(8,128)(2,1)S(1)}, u32[]{:S(2)}, u32[]{:S(2)}) collective-permute-start(bf16[128,1024]{1,0:T(8,128)(2,1)S(1)} %slice.123), channel_id=1, source_target_pairs={{0,24},{8,0},{16,8},{24,16},{1,25},{9,1},{17,9},{25,17},{2,26},{10... | collective-permute-start | bytes 786440 | tf_op jit(solution)/shard_map/ppermute | solution.py:25
  70.7 3.0 %collective-permute-start.4 = (bf16[512,1024]{1,0:T(8,128)(2,1)}, bf16[512,1024]{1,0:T(8,128)(2,1)}, u32[]{:S(2)}, u32[]{:S(2)}) collective-permute-start(bf16[512,1024]{1,0:T(8,128)(2,1)} %broadcast_select_fusion.2), channel_id=1, source_target_pairs={{0,32},{32,0},{1,33},{33,1},{2,34},{34,2},{3,35},{35,3},{4,36},{36... | collective-permute-start | bytes 3145736 | tf_op jit(solution)/shard_map/ppermute | solution.py:25
  76.5 18.8 %all-to-all-start.1 = ((bf16[4,128,1024]{2,1,0:T(8,128)(2,1)}), bf16[4,128,1024]{2,1,0:T(8,128)(2,1)S(1)}, u32[]{:S(2)}, u32[]{:S(2)}) async-start(bf16[4,128,1024]{2,1,0:T(8,128)(2,1)} %bitcast.28), calls=%async_computation.1 | async-start | bytes 2097152 | tf_op jit(solution)/shard_map/all_to_all | solution.py:29
  89.7 5.9 %collective-permute-start.5 = (bf16[512,512]{1,0:T(8,128)(2,1)}, bf16[512,512]{1,0:T(8,128)(2,1)}, u32[]{:S(2)}, u32[]{:S(2)}) collective-permute-start(bf16[512,512]{1,0:T(8,128)(2,1)} %broadcast_select_fusion.5), channel_id=1, source_target_pairs={{0,32},{32,0},{1,33},{33,1},{2,34},{34,2},{3,35},{35,3},{4,36},{36... | collective-permute-start | bytes 1572872 | tf_op jit(solution)/shard_map/ppermute | solution.py:25
  113.9 6.4 %collective-permute-start.6 = (bf16[512,512]{1,0:T(8,128)(2,1)S(1)}, bf16[512,512]{1,0:T(8,128)(2,1)}, u32[]{:S(2)}, u32[]{:S(2)}) collective-permute-start(bf16[512,512]{1,0:T(8,128)(2,1)S(1)} %bitcast.29), channel_id=1, source_target_pairs={{0,32},{32,0},{1,33},{33,1},{2,34},{34,2},{3,35},{35,3},{4,36},{36... | collective-permute-start | bytes 1572872 | tf_op jit(solution)/shard_map/ppermute | solution.py:25
  115.4 19.5 %all-to-all-start.5 = ((bf16[4,128,1024]{2,1,0:T(8,128)(2,1)}), bf16[4,128,1024]{2,1,0:T(8,128)(2,1)S(1)}, u32[]{:S(2)}, u32[]{:S(2)}) async-start(bf16[4,128,1024]{2,1,0:T(8,128)(2,1)} %broadcast_in_dim.11), calls=%async_computation.5 | async-start | bytes 2097152 | tf_op jit(solution)/shard_map/all_to_all | solution.py:29
  123.8 11.2 %collective-permute-start.7 = (bf16[128,1024]{1,0:T(8,128)(2,1)}, bf16[128,1024]{1,0:T(8,128)(2,1)S(1)}, u32[]{:S(2)}, u32[]{:S(2)}) collective-permute-start(bf16[128,1024]{1,0:T(8,128)(2,1)} %get-tuple-element.29), channel_id=1, source_target_pairs={{0,8},{8,16},{16,24},{24,0},{1,9},{9,17},{17,25},{25,1},{2,10},{10... | collective-permute-start | bytes 786440 | tf_op jit(solution)/shard_map/ppermute | solution.py:25
  125.2 9.7 %collective-permute-start.9 = (bf16[128,1024]{1,0:T(8,128)(2,1)}, bf16[128,1024]{1,0:T(8,128)(2,1)}, u32[]{:S(2)}, u32[]{:S(2)}) collective-permute-start(bf16[128,1024]{1,0:T(8,128)(2,1)} %get-tuple-element.30), channel_id=1, source_target_pairs={{0,24},{8,0},{16,8},{24,16},{1,25},{9,1},{17,9},{25,17},{2,26},{10... | collective-permute-start | bytes 786440 | tf_op jit(solution)/shard_map/ppermute | solution.py:25
  134.9 5.6 %copy-start.6 = (bf16[512,512]{1,0:T(8,128)(2,1)S(1)}, bf16[512,512]{1,0:T(8,128)(2,1)}, u32[]{:S(2)}) copy-start(bf16[512,512]{1,0:T(8,128)(2,1)} %copy-done.5) | copy-start | bytes 1572868
  134.9 5.6 %copy-start.11 = (bf16[256,1024]{1,0:T(8,128)(2,1)S(1)}, bf16[256,1024]{1,0:T(8,128)(2,1)}, u32[]{:S(2)}) copy-start(bf16[256,1024]{1,0:T(8,128)(2,1)} %copy-done.10) | copy-start | bytes 1572868
  134.9 5.6 %copy-start.13 = (bf16[256,1024]{1,0:T(8,128)(2,1)S(1)}, bf16[256,1024]{1,0:T(8,128)(2,1)}, u32[]{:S(2)}) copy-start(bf16[256,1024]{1,0:T(8,128)(2,1)} %copy-done.12) | copy-start | bytes 1572868
  134.9 5.6 %copy-start.15 = (bf16[256,1024]{1,0:T(8,128)(2,1)S(1)}, bf16[256,1024]{1,0:T(8,128)(2,1)}, u32[]{:S(2)}) copy-start(bf16[256,1024]{1,0:T(8,128)(2,1)} %copy-done.14) | copy-start | bytes 1572868
  134.9 5.6 %copy-start.17 = (bf16[256,1024]{1,0:T(8,128)(2,1)S(1)}, bf16[256,1024]{1,0:T(8,128)(2,1)}, u32[]{:S(2)}) copy-start(bf16[256,1024]{1,0:T(8,128)(2,1)} %copy-done.16) | copy-start | bytes 1572868
  135.0 8.2 %collective-permute-start.11 = (bf16[512,1024]{1,0:T(8,128)(2,1)S(1)}, bf16[512,1024]{1,0:T(8,128)(2,1)S(1)}, u32[]{:S(2)}, u32[]{:S(2)}) collective-permute-start(bf16[512,1024]{1,0:T(8,128)(2,1)S(1)} %bitcast.26), channel_id=1, source_target_pairs={{0,32},{32,0},{1,33},{33,1},{2,34},{34,2},{3,35},{35,3},{4,36},{36... | collective-permute-start | bytes 3145736 | tf_op jit(solution)/shard_map/ppermute | solution.py:25
  136.6 15.5 %collective-permute-start.10 = (bf16[256,1024]{1,0:T(8,128)(2,1)S(1)}, bf16[256,1024]{1,0:T(8,128)(2,1)S(1)}, u32[]{:S(2)}, u32[]{:S(2)}) collective-permute-start(bf16[256,1024]{1,0:T(8,128)(2,1)S(1)} %pad_maximum_fusion.7), channel_id=1, source_target_pairs={{0,24},{8,0},{16,8},{24,16},{1,25},{9,1},{17,9},{25,17},{2,26},{10... | collective-permute-start | bytes 1572872 | tf_op jit(solution)/shard_map/ppermute | solution.py:25
  140.4 15.2 %collective-permute-start.8 = (bf16[256,1024]{1,0:T(8,128)(2,1)S(1)}, bf16[256,1024]{1,0:T(8,128)(2,1)S(1)}, u32[]{:S(2)}, u32[]{:S(2)}) collective-permute-start(bf16[256,1024]{1,0:T(8,128)(2,1)S(1)} %pad_maximum_fusion.6), channel_id=1, source_target_pairs={{0,8},{8,16},{16,24},{24,0},{1,9},{9,17},{17,25},{25,1},{2,10},{10... | collective-permute-start | bytes 1572872 | tf_op jit(solution)/shard_map/ppermute | solution.py:25
  143.3 12.3 %copy-start.9 = (bf16[1024,1024]{1,0:T(8,128)(2,1)S(1)}, bf16[1024,1024]{1,0:T(8,128)(2,1)}, u32[]{:S(2)}) copy-start(bf16[1024,1024]{1,0:T(8,128)(2,1)} %copy-done.7) | copy-start | bytes 6291460
  158.0 6.4 %copy-start.2 = (bf16[1024,1024]{1,0:T(8,128)(2,1)}, bf16[1024,1024]{1,0:T(8,128)(2,1)S(1)}, u32[]{:S(2)}) copy-start(bf16[1024,1024]{1,0:T(8,128)(2,1)S(1)} %convolution_convert_fusion) | copy-start | bytes 6291460
  159.0 9.6 %collective-permute-start.12 = (bf16[128,1024]{1,0:T(8,128)(2,1)}, bf16[128,1024]{1,0:T(8,128)(2,1)}, u32[]{:S(2)}, u32[]{:S(2)}) collective-permute-start(bf16[128,1024]{1,0:T(8,128)(2,1)} %get-tuple-element.21), channel_id=1, source_target_pairs={{0,8},{8,16},{16,24},{24,0},{1,9},{9,17},{17,25},{25,1},{2,10},{10... | collective-permute-start | bytes 786440 | tf_op jit(solution)/shard_map/ppermute | solution.py:25
  159.0 9.6 %collective-permute-start.14 = (bf16[128,1024]{1,0:T(8,128)(2,1)}, bf16[128,1024]{1,0:T(8,128)(2,1)}, u32[]{:S(2)}, u32[]{:S(2)}) collective-permute-start(bf16[128,1024]{1,0:T(8,128)(2,1)} %get-tuple-element.22), channel_id=1, source_target_pairs={{0,24},{8,0},{16,8},{24,16},{1,25},{9,1},{17,9},{25,17},{2,26},{10... | collective-permute-start | bytes 786440 | tf_op jit(solution)/shard_map/ppermute | solution.py:25
  164.4 24.2 %all-to-all-start.4 = ((bf16[8,32,1024]{2,1,0:T(8,128)(2,1)}), bf16[8,32,1024]{2,1,0:T(8,128)(2,1)}, u32[]{:S(2)}, u32[]{:S(2)}) async-start(bf16[8,32,1024]{2,1,0:T(8,128)(2,1)} %bitcast.35), calls=%async_computation.4 | async-start | bytes 1048576 | tf_op jit(solution)/shard_map/all_to_all | solution.py:29
  168.5 5.2 %copy-start.19 = (bf16[1024,1024]{1,0:T(8,128)(2,1)S(1)}, bf16[1024,1024]{1,0:T(8,128)(2,1)}, u32[]{:S(2)}) copy-start(bf16[1024,1024]{1,0:T(8,128)(2,1)} %copy-done.18) | copy-start | bytes 6291460
  171.1 12.6 %collective-permute-start.15 = (bf16[256,1024]{1,0:T(8,128)(2,1)S(1)}, bf16[256,1024]{1,0:T(8,128)(2,1)S(1)}, u32[]{:S(2)}, u32[]{:S(2)}) collective-permute-start(bf16[256,1024]{1,0:T(8,128)(2,1)S(1)} %pad_maximum_fusion.9), channel_id=1, source_target_pairs={{0,24},{8,0},{16,8},{24,16},{1,25},{9,1},{17,9},{25,17},{2,26},{10... | collective-permute-start | bytes 1572872 | tf_op jit(solution)/shard_map/ppermute | solution.py:25
  173.4 13.1 %collective-permute-start.13 = (bf16[256,1024]{1,0:T(8,128)(2,1)S(1)}, bf16[256,1024]{1,0:T(8,128)(2,1)S(1)}, u32[]{:S(2)}, u32[]{:S(2)}) collective-permute-start(bf16[256,1024]{1,0:T(8,128)(2,1)S(1)} %pad_maximum_fusion.8), channel_id=1, source_target_pairs={{0,8},{8,16},{16,24},{24,0},{1,9},{9,17},{17,25},{25,1},{2,10},{10... | collective-permute-start | bytes 1572872 | tf_op jit(solution)/shard_map/ppermute | solution.py:25
  188.6 20.7 %all-to-all-start.6 = ((bf16[8,32,1024]{2,1,0:T(8,128)(2,1)}), bf16[8,32,1024]{2,1,0:T(8,128)(2,1)S(1)}, u32[]{:S(2)}, u32[]{:S(2)}) async-start(bf16[8,32,1024]{2,1,0:T(8,128)(2,1)} %bitcast.11), calls=%async_computation.6 | async-start | bytes 1048576 | tf_op jit(solution)/shard_map/all_to_all | solution.py:29
  (10 other events, 16.8 us)
Sparse Core Ops, SparseCore 0:
  56.0 29.7 all-gather.1

commit v4 on v2

v4 whole, which is shorter than its diff:
```python
import jax
import jax.numpy as jnp
from jax import lax
from jax.sharding import Mesh, PartitionSpec as P

BF = jnp.bfloat16
F32 = jnp.float32
X, CORE, Y, Z = 4, 2, 4, 8


def product(left_side, right_side):
    return jnp.dot(left_side, right_side, preferred_element_type=F32)


def product_right_t(left_side, right_side):
    return lax.dot_general(left_side, right_side, (((1,), (1,)), ((), ())), preferred_element_type=F32)


def product_left_t(left_side, right_side):
    return lax.dot_general(left_side, right_side, (((0,), (0,)), ((), ())), preferred_element_type=F32)


def shift(block, axis, step):
    size = lax.axis_size(axis)
    return lax.ppermute(block, axis, [(i, (i + step) % size) for i in range(size)])


def exchange(blocks, axis):
    return lax.all_to_all(blocks, axis, split_axis=0, concat_axis=0, tiled=True)


def gather(block, axis):
    count = lax.axis_size(axis)
    rows, width = block.shape
    copies = jnp.broadcast_to(block[None], (count, rows, width)).reshape(count * rows, width)
    return exchange(copies, axis)


def after(block, *earlier):
    return lax.optimization_barrier((block,) + earlier)[0]


def gather_y(own):
    near = [shift(own, "y", 1), shift(own, "y", 3)]
    return [own, near[0], shift(own, "y", 2), near[1]]


def other_core(block):
    return shift(block, "core", 1)


def sum_parts(parts, count):
    rows = parts.shape[0] // count
    return jnp.sum(parts.reshape((count, rows) + parts.shape[1:]).astype(F32), axis=0)


def reduce_x(partial):
    return sum_parts(exchange(partial, "x"), X)


def split_y(partial):
    rows = partial.shape[0] // Y
    return [partial[j * rows : (j + 1) * rows] for j in range(Y)]


def move_y(pieces):
    return [shift(pieces[1], "y", 3), shift(pieces[3], "y", 1), shift(pieces[2], "y", 2)]


def sum_y(own, moved):
    total = own.astype(F32)
    for piece in moved:
        total = total + piece.astype(F32)
    return total.astype(BF)


def reduce_z(total):
    return sum_parts(exchange(total, "z"), Z).astype(BF)


def own_rows(blocks, first):
    rows = blocks[0].shape[0] // CORE
    kept = [jnp.where(first, block[:rows], block[rows:]) for block in blocks]
    sent = [jnp.where(first, block[rows:], block[:rows]) for block in blocks]
    received = other_core(jnp.concatenate(sent, axis=0)).reshape((len(blocks), rows, -1))
    return [jnp.concatenate([kept[i], received[i]], axis=1) for i in range(len(blocks))]


def own_columns(blocks, first):
    columns = blocks[0].shape[1] // CORE
    received = other_core(jnp.stack([block[:, columns:] for block in blocks]))
    return [
        jnp.where(
            first,
            jnp.concatenate([block[:, :columns], received[i]], axis=0),
            jnp.concatenate([received[i], block[:, :columns]], axis=0),
        )
        for i, block in enumerate(blocks)
    ]


def both_halves(half):
    return jnp.concatenate([half, other_core(half)], axis=0)


def body(tokens, gate_weight, up_weight, down_weight, out_grad):
    width = gate_weight.shape[1]
    features = gate_weight.shape[0]
    first = lax.axis_index("core") == 0

    own_tokens, own_grads = own_rows((tokens, out_grad), first)
    tokens_z, grads_y = lax.optimization_barrier((gather(own_tokens, "z"), jnp.stack(gather_y(own_grads))))
    tokens_half = jnp.concatenate(gather_y(tokens_z), axis=0)
    grads_half = lax.all_gather(grads_y, "z", axis=0, tiled=False)
    grads_half = jnp.swapaxes(grads_half, 0, 1).reshape(tokens_half.shape)
    both_weights = jnp.concatenate([gate_weight, up_weight], axis=1)
    both_weights = jnp.concatenate([both_weights, other_core(both_weights)], axis=0)
    down_weights = jnp.concatenate([down_weight, other_core(down_weight)], axis=1)

    def all_rows(half):
        return jnp.concatenate([half[:, :features], other_core(half[:, features:])], axis=0)

    gate_up_partial = product(tokens_half, both_weights).astype(BF)
    gate_up = sum_parts(exchange(gate_up_partial, "x"), X)
    gate_up, all_tokens = lax.optimization_barrier((gate_up, all_rows(after(tokens_half, gate_up_partial))))
    gate_value = gate_up[:, :width]
    up_value = gate_up[:, width:]
    sigmoid_gate = jax.nn.sigmoid(gate_value)
    silu_gate = gate_value * sigmoid_gate
    hidden_share = (silu_gate * up_value).astype(BF)

    hidden_partial = product_right_t(grads_half, down_weights).astype(BF)
    rows = hidden_share.shape[0]
    mixed = jnp.concatenate(
        [jnp.broadcast_to(hidden_share[None], (X, rows, width)), hidden_partial.reshape(X, rows, width)], axis=1
    )
    mixed = exchange(mixed.reshape(2 * X * rows, width), "x").reshape(X, 2 * rows, width)
    hidden_half = mixed[:, :rows].reshape(X * rows, width)
    hidden_grad = jnp.sum(mixed[:, rows:].astype(F32), axis=0)
    hidden_grad, all_out_grads = lax.optimization_barrier((hidden_grad, all_rows(grads_half)))

    output_pieces = split_y(product(hidden_half, down_weights).astype(BF))
    output_moved = move_y(output_pieces)

    gate_grad = (hidden_grad * up_value * sigmoid_gate * (1.0 + gate_value * (1.0 - sigmoid_gate))).astype(BF)
    up_grad = (hidden_grad * silu_gate).astype(BF)
    grads_both = gather(jnp.concatenate([gate_grad, up_grad], axis=1), "x")
    down_weight_grad = product_left_t(both_halves(hidden_half), all_out_grads)
    grads_both, down_weight_grad, *output_moved = lax.optimization_barrier(
        (grads_both, down_weight_grad, *output_moved)
    )
    input_pieces = split_y(product_right_t(grads_both, both_weights).astype(BF))
    input_moved = move_y(input_pieces)
    all_grads = both_halves(after(grads_both, *input_pieces))
    output_total = reduce_z(after(sum_y(output_pieces[0], output_moved), all_grads))
    gate_weight_grad = product_left_t(all_tokens, all_grads[:, :width])
    up_weight_grad = product_left_t(all_tokens, all_grads[:, width:])
    earlier = lax.optimization_barrier((output_total, gate_weight_grad, up_weight_grad))
    input_total, *earlier = lax.optimization_barrier((sum_y(input_pieces[0], input_moved), *earlier))
    layer_output, input_grad = own_columns((earlier[0], reduce_z(input_total)), first)
    return (layer_output, input_grad, earlier[1], earlier[2], down_weight_grad)


def solution(mesh):
    grid = Mesh(mesh.devices.reshape(X, CORE, Y, Z), ("x", "core", "y", "z"))
    row, col = ("x", "core"), ("y", "z")
    in_specs = (P(col, row), P(row, col), P(row, col), P(col, row), P(col, row))
    out_specs = (P(col, row), P(col, row), P(row, col), P(row, col), P(col, row))
    return jax.shard_map(body, mesh=grid, in_specs=in_specs, out_specs=out_specs, check_vma=False)
```

time: 247 us -> 240 us (0.972)
  blocking collectives: 43.6 us -> 0 us
  starting transfers between devices: 41.2 us -> 52.8 us
  local copies, waits for them, and re-layouts: 10.1 us -> 21.1 us
  waiting for transfers between devices: 97.6 us -> 107 us
  other arithmetic: 11.3 us -> 14.9 us
    all_to_all x2 -> x0, blocking collectives: 43.6 us -> none  [exchange(): return lax.all_to_all(blocks, axis, split_axis=0, concat_axis=0, tiled=True)]
    ppermute x13 -> x20, starting transfers between devices: 9.43 us -> 21.6 us  [shift(): lax.ppermute(block, axis, [(i, (i + step) % size) for i in range(size)])]
    all_to_all x6, waiting for transfers between devices: 34.3 us -> 45.9 us  [exchange(): return lax.all_to_all(blocks, axis, split_axis=0, concat_axis=0, tiled=True)]
    slice x2 -> x8, local copies, waits for them, and re-layouts: 0.24 us -> 7.35 us  [the longest x2 2.71 us: all_rows(): half[:, :features]]
    concatenate x1 -> x6, other arithmetic: 0.02 us -> 5.2 us  [the longest x2 4.13 us: all_rows(): jnp.concatenate([half[:, :features], other_core(half[:, features:])], axi...]
    unnamed x35 -> x28, local copies, waits for them, and re-layouts: 3.45 us -> 6.59 us
    dot_general x2, matrix products: 6.98 us -> 9.96 us  [product(): return jnp.dot(left_side, right_side, preferred_element_type=F32)]
    dot_general x3, matrix products: 12.9 us -> 10.4 us  [product_left_t(): lax.dot_general(left_side, right_side, (((0,), (0,)), ((), ())), preferre...]
  transfers between devices with their start and end apart: 20 -> 27, of which waited for: 14 -> 14; matrix products, arithmetic and copies ran while one was open for 17% -> 19% of each run, Pallas kernels for 0% -> 0%
where the time goes in v4:
time: 240 us; the launch traced here: 238 us
  waiting for transfers between devices  107 us (45%)
  starting transfers between devices  52.8 us (22%)
  matrix products  27.8 us (12%)
  local copies, waits for them, and re-layouts  21.1 us (9%)
  other arithmetic  14.9 us (6%)
  between operations  14.4 us (6%)
    ppermute x20, waiting for transfers between devices, shift(): lax.ppermute(block, axis, [(i, (i + step) % size) for i in range(size)])  61.3 us
    all_to_all x6, waiting for transfers between devices, exchange(): return lax.all_to_all(blocks, axis, split_axis=0, concat_axis=0, tiled=True)  45.9 us
    all_to_all x6, starting transfers between devices, exchange(): return lax.all_to_all(blocks, axis, split_axis=0, concat_axis=0, tiled=True)  31.1 us
    ppermute x20, starting transfers between devices, shift(): lax.ppermute(block, axis, [(i, (i + step) % size) for i in range(size)])  21.6 us
    dot_general x3, matrix products, product_left_t(): lax.dot_general(left_side, right_side, (((0,), (0,)), ((), ())), preferre...  10.4 us
    dot_general x2, matrix products, product(): return jnp.dot(left_side, right_side, preferred_element_type=F32)  9.96 us
    dot_general x2, matrix products, product_right_t(): lax.dot_general(left_side, right_side, (((1,), (1,)), ((), ())), preferre...  7.46 us
    unnamed x28, local copies, waits for them, and re-layouts  6.59 us
  transfers between devices with their start and end apart: 27, of which 14 were waited for; matrix products, arithmetic and copies ran while one was open for 19% of the time, Pallas kernels for 0%

profile of v4, /device:TPU:2, one launch (start us, length us, event | category | flops | bytes accessed | tf_op | source)
XLA Modules:
  0.0 238.1 jit_solution(9094001344544429580)
XLA Ops:
  11.1 8.5 %all-to-all-start = ((bf16[8,16,2048]{2,1,0:T(8,128)(2,1)}), bf16[8,16,2048]{2,1,0:T(8,128)(2,1)S(1)}, u32[]{:S(2)}, u32[]{:S(2)}) async-start(bf16[8,16,2048]{2,1,0:T(8,128)(2,1)} %broadcast_in_dim.6), calls=%async_computation | async-start | bytes 1048576 | tf_op jit(solution)/shard_map/all_to_all | solution.py:29
  21.7 3.3 %collective-permute-start.2 = (bf16[16,2048]{1,0:T(8,128)(2,1)S(1)}, bf16[16,2048]{1,0:T(8,128)(2,1)S(1)}, u32[]{:S(2)}, u32[]{:S(2)}) collective-permute-start(bf16[16,2048]{1,0:T(8,128)(2,1)S(1)} %get-tuple-element.66), channel_id=1, source_target_pairs={{0,16},{8,24},{16,0},{24,8},{1,17},{9,25},{17,1},{25,9},{2,18},{10... | collective-permute-start | bytes 196616 | tf_op jit(solution)/shard_map/ppermute | solution.py:25
  25.6 2.6 %collective-permute-start.3 = (bf16[16,2048]{1,0:T(8,128)(2,1)S(1)}, bf16[16,2048]{1,0:T(8,128)(2,1)S(1)}, u32[]{:S(2)}, u32[]{:S(2)}) collective-permute-start(bf16[16,2048]{1,0:T(8,128)(2,1)S(1)} %get-tuple-element.66), channel_id=1, source_target_pairs={{0,24},{8,0},{16,8},{24,16},{1,25},{9,1},{17,9},{25,17},{2,26},{10... | collective-permute-start | bytes 196616 | tf_op jit(solution)/shard_map/ppermute | solution.py:25
  31.2 6.2 %all-to-all-done = bf16[8,16,2048]{2,1,0:T(8,128)(2,1)S(1)} async-done(((bf16[8,16,2048]{2,1,0:T(8,128)(2,1)}), bf16[8,16,2048]{2,1,0:T(8,128)(2,1)S(1)}, u32[]{:S(2)}, u32[]{:S(2)}) %all-to-all-start) | async-done | bytes 524320 | tf_op jit(solution)/shard_map/all_to_all | solution.py:29
  39.0 2.9 %collective-permute-start.5 = (bf16[128,2048]{1,0:T(8,128)(2,1)S(1)}, bf16[128,2048]{1,0:T(8,128)(2,1)S(1)}, u32[]{:S(2)}, u32[]{:S(2)}) collective-permute-start(bf16[128,2048]{1,0:T(8,128)(2,1)S(1)} %bitcast.40), channel_id=1, source_target_pairs={{0,16},{8,24},{16,0},{24,8},{1,17},{9,25},{17,1},{25,9},{2,18},{10... | collective-permute-start | bytes 1572872 | tf_op jit(solution)/shard_map/ppermute | solution.py:25
  43.3 9.2 %collective-permute-done.4 = bf16[128,2048]{1,0:T(8,128)(2,1)S(1)} collective-permute-done((bf16[128,2048]{1,0:T(8,128)(2,1)S(1)}, bf16[128,2048]{1,0:T(8,128)(2,1)S(1)}, u32[]{:S(2)}, u32[]{:S(2)}) %collective-permute-start.4) | collective-permute-done | bytes 524320 | tf_op jit(solution)/shard_map/ppermute | solution.py:25
  52.6 12.4 %collective-permute-done.5 = bf16[128,2048]{1,0:T(8,128)(2,1)S(1)} collective-permute-done((bf16[128,2048]{1,0:T(8,128)(2,1)S(1)}, bf16[128,2048]{1,0:T(8,128)(2,1)S(1)}, u32[]{:S(2)}, u32[]{:S(2)}) %collective-permute-start.5) | collective-permute-done | bytes 524320 | tf_op jit(solution)/shard_map/ppermute | solution.py:25
  65.1 5.5 %fusion.1 = bf16[512,1024]{1,0:T(8,128)(2,1)} fusion(bf16[512,2048]{1,0:T(8,128)(2,1)S(1)} %constant_dynamic-update-slice_fusion, bf16[1024,1024]{1,0:T(8,128)(2,1)} %collective-permute-done.7, bf16[1024,1024]{1,0:T(8,128)(2,1)} %constant_dynamic-update-slice_fusion.4), kind=kOutput, calls=%fused_computation.7 | convolution fusion | flops 2156396544 | bytes 7340032 | tf_op jit(solution)/shard_map/dot_general | solution.py:12
  71.8 4.8 %all-to-all-start.1 = ((bf16[4,128,1024]{2,1,0:T(8,128)(2,1)}), bf16[4,128,1024]{2,1,0:T(8,128)(2,1)S(1)}, u32[]{:S(2)}, u32[]{:S(2)}) async-start(bf16[4,128,1024]{2,1,0:T(8,128)(2,1)} %bitcast.43), calls=%async_computation.1 | async-start | bytes 2097152 | tf_op jit(solution)/shard_map/all_to_all | solution.py:29
  81.2 9.8 %all-to-all-done.1 = bf16[4,128,1024]{2,1,0:T(8,128)(2,1)S(1)} async-done(((bf16[4,128,1024]{2,1,0:T(8,128)(2,1)}), bf16[4,128,1024]{2,1,0:T(8,128)(2,1)S(1)}, u32[]{:S(2)}, u32[]{:S(2)}) %all-to-all-start.1) | async-done | bytes 1048608 | tf_op jit(solution)/shard_map/all_to_all | solution.py:29
  91.2 2.7 %pad_maximum_fusion.3 = bf16[1024,1024]{1,0:T(8,128)(2,1)} fusion(bf16[512,1024]{1,0:T(8,128)(2,1)} %collective-permute-done.8, bf16[512,1024]{1,0:T(8,128)(2,1)S(1)} %get-tuple-element.55), kind=kLoop, calls=%fused_computation.4 | loop fusion | flops 4194304 | bytes 4194304 | tf_op jit(solution)/shard_map/concatenate | solution.py:121
  95.7 2.9 %convolution_convert_fusion.2 = bf16[512,512]{1,0:T(8,128)(2,1)S(1)} fusion(bf16[512,2048]{1,0:T(8,128)(2,1)S(1)} %bitcast.33, bf16[512,2048]{1,0:T(8,128)(2,1)} %constant_dynamic-update-slice_fusion.6), kind=kOutput, calls=%fused_computation.8 | convolution fusion | flops 1074003968 | bytes 4718592 | tf_op jit(solution)/shard_map/dot_general | solution.py:16
  99.7 5.7 %all-to-all-start.2 = ((bf16[4,256,512]{2,1,0:T(8,128)(2,1)}), bf16[4,256,512]{2,1,0:T(8,128)(2,1)}, u32[]{:S(2)}, u32[]{:S(2)}) async-start(bf16[4,256,512]{2,1,0:T(8,128)(2,1)} %pad_maximum_fusion.7), calls=%async_computation.2 | async-start | bytes 2097152 | tf_op jit(solution)/shard_map/all_to_all | solution.py:29
  106.9 12.1 %all-to-all-done.2 = bf16[4,256,512]{2,1,0:T(8,128)(2,1)} async-done(((bf16[4,256,512]{2,1,0:T(8,128)(2,1)}), bf16[4,256,512]{2,1,0:T(8,128)(2,1)}, u32[]{:S(2)}, u32[]{:S(2)}) %all-to-all-start.2) | async-done | bytes 1048608 | tf_op jit(solution)/shard_map/all_to_all | solution.py:29
  122.1 4.4 %convolution_convert_fusion.1 = bf16[512,2048]{1,0:T(8,128)(2,1)} fusion(bf16[512,512]{1,0:T(8,128)(2,1)} %bitcast.11, bf16[512,2048]{1,0:T(8,128)(2,1)} %constant_dynamic-update-slice_fusion.6), kind=kOutput, calls=%fused_computation.2 | convolution fusion | flops 1074790400 | bytes 4718592 | tf_op jit(solution)/shard_map/dot_general | solution.py:12
  130.2 4.9 %all-to-all-start.3 = ((bf16[4,128,1024]{2,1,0:T(8,128)(2,1)}), bf16[4,128,1024]{2,1,0:T(8,128)(2,1)S(1)}, u32[]{:S(2)}, u32[]{:S(2)}) async-start(bf16[4,128,1024]{2,1,0:T(8,128)(2,1)} %broadcast_in_dim.8), calls=%async_computation.3 | async-start | bytes 2097152 | tf_op jit(solution)/shard_map/all_to_all | solution.py:29
  136.7 2.6 %collective-permute-start.14 = (bf16[128,2048]{1,0:T(8,128)(2,1)S(1)}, bf16[128,2048]{1,0:T(8,128)(2,1)S(1)}, u32[]{:S(2)}, u32[]{:S(2)}) collective-permute-start(bf16[128,2048]{1,0:T(8,128)(2,1)S(1)} %get-tuple-element.50), channel_id=1, source_target_pairs={{0,16},{8,24},{16,0},{24,8},{1,17},{9,25},{17,1},{25,9},{2,18},{10... | collective-permute-start | bytes 1572872 | tf_op jit(solution)/shard_map/ppermute | solution.py:25
  139.6 2.9 %collective-permute-start.12 = (bf16[128,2048]{1,0:T(8,128)(2,1)S(1)}, bf16[128,2048]{1,0:T(8,128)(2,1)}, u32[]{:S(2)}, u32[]{:S(2)}) collective-permute-start(bf16[128,2048]{1,0:T(8,128)(2,1)S(1)} %get-tuple-element.52), channel_id=1, source_target_pairs={{0,24},{8,0},{16,8},{24,16},{1,25},{9,1},{17,9},{25,17},{2,26},{10... | collective-permute-start | bytes 1572872 | tf_op jit(solution)/shard_map/ppermute | solution.py:25
  142.5 3.8 %fusion.6 = f32[512,1024]{1,0:T(8,128)} fusion(bf16[1024,1024]{1,0:T(8,128)(2,1)S(1)} %pad_maximum_fusion.4, bf16[512,512]{1,0:T(8,128)(2,1)} %collective-permute-done.11, bf16[512,512]{1,0:T(8,128)(2,1)} %bitcast.11), kind=kOutput, calls=%fused_computation.14 | convolution fusion | flops 1075838976 | bytes 5242880 | tf_op jit(solution)/shard_map/dot_general | solution.py:20
  146.3 6.8 %collective-permute-done.14 = bf16[128,2048]{1,0:T(8,128)(2,1)S(1)} collective-permute-done((bf16[128,2048]{1,0:T(8,128)(2,1)S(1)}, bf16[128,2048]{1,0:T(8,128)(2,1)S(1)}, u32[]{:S(2)}, u32[]{:S(2)}) %collective-permute-start.14) | collective-permute-done | bytes 524320 | tf_op jit(solution)/shard_map/ppermute | solution.py:25
  153.1 10.5 %collective-permute-done.13 = bf16[128,2048]{1,0:T(8,128)(2,1)S(1)} collective-permute-done((bf16[128,2048]{1,0:T(8,128)(2,1)S(1)}, bf16[128,2048]{1,0:T(8,128)(2,1)S(1)}, u32[]{:S(2)}, u32[]{:S(2)}) %collective-permute-start.13) | collective-permute-done | bytes 524320 | tf_op jit(solution)/shard_map/ppermute | solution.py:25
  164.3 4.6 %convolution_convert_fusion = bf16[512,2048]{1,0:T(8,128)(2,1)S(1)} fusion(bf16[512,1024]{1,0:T(8,128)(2,1)S(1)} %bitcast.35, bf16[1024,1024]{1,0:T(8,128)(2,1)} %collective-permute-done.7, bf16[1024,1024]{1,0:T(8,128)(2,1)} %constant_dynamic-update-slice_fusion.4), kind=kOutput, calls=%fused_computation.1 | convolution fusion | flops 2156920832 | bytes 7340032 | tf_op jit(solution)/shard_map/dot_general | solution.py:16
  173.4 2.4 add_convert_fusion
  177.2 3.7 %all-to-all-start.4 = ((bf16[8,16,2048]{2,1,0:T(8,128)(2,1)}), bf16[8,16,2048]{2,1,0:T(8,128)(2,1)S(1)}, u32[]{:S(2)}, u32[]{:S(2)}) async-start(bf16[8,16,2048]{2,1,0:T(8,128)(2,1)} %bitcast.12), calls=%async_computation.4 | async-start | bytes 1048576 | tf_op jit(solution)/shard_map/all_to_all | solution.py:29
  180.9 4.3 %collective-permute-done.15 = bf16[128,2048]{1,0:T(8,128)(2,1)} collective-permute-done((bf16[128,2048]{1,0:T(8,128)(2,1)}, bf16[128,2048]{1,0:T(8,128)(2,1)}, u32[]{:S(2)}, u32[]{:S(2)}) %collective-permute-start.15) | collective-permute-done | bytes 524320 | tf_op jit(solution)/shard_map/ppermute | solution.py:25
  185.2 2.9 %collective-permute-done.17 = bf16[128,2048]{1,0:T(8,128)(2,1)} collective-permute-done((bf16[128,2048]{1,0:T(8,128)(2,1)}, bf16[128,2048]{1,0:T(8,128)(2,1)}, u32[]{:S(2)}, u32[]{:S(2)}) %collective-permute-start.17) | collective-permute-done | bytes 524320 | tf_op jit(solution)/shard_map/ppermute | solution.py:25
  188.1 10.5 %collective-permute-done.16 = bf16[128,2048]{1,0:T(8,128)(2,1)} collective-permute-done((bf16[128,2048]{1,0:T(8,128)(2,1)}, bf16[128,2048]{1,0:T(8,128)(2,1)}, u32[]{:S(2)}, u32[]{:S(2)}) %collective-permute-start.16) | collective-permute-done | bytes 524320 | tf_op jit(solution)/shard_map/ppermute | solution.py:25
  198.6 2.5 %add_convert_fusion.1 = bf16[128,2048]{1,0:T(8,128)(2,1)} fusion(bf16[128,2048]{1,0:T(8,128)(2,1)} %collective-permute-done.17, bf16[128,2048]{1,0:T(8,128)(2,1)} %collective-permute-done.16, bf16[128,2048]{1,0:T(8,128)(2,1)} %collective-permute-done.15, bf16[512,2048]{1,0:T(8,128)(2,1)S(1)} %convolution_convert_fusion), kind=kLoop, calls=%fused_computation.19 | loop fusion | flops 2097152 | bytes 2621440 | tf_op jit(solution)/shard_map/convert_element_type | solution.py:74
  201.1 4.0 %fusion.2 = f32[1024,512]{1,0:T(8,128)} fusion(bf16[1024,1024]{1,0:T(8,128)(2,1)S(1)} %copy-done.1, bf16[1024,1024]{1,0:T(8,128)(2,1)} %copy-done.9), kind=kOutput, calls=%fused_computation.9 | convolution fusion | flops 1073741824 | bytes 5242880 | tf_op jit(solution)/shard_map/dot_general | solution.py:20
  205.1 2.6 %fusion.4 = f32[1024,512]{1,0:T(8,128)} fusion(bf16[1024,1024]{1,0:T(8,128)(2,1)S(1)} %copy-done.1, bf16[1024,1024]{1,0:T(8,128)(2,1)S(1)} %copy-done.10), kind=kOutput, calls=%fused_computation.11 | convolution fusion | flops 1073741824 | bytes 5242880 | tf_op jit(solution)/shard_map/dot_general | solution.py:20
  207.8 3.5 %all-to-all-start.5 = ((bf16[8,16,2048]{2,1,0:T(8,128)(2,1)}), bf16[8,16,2048]{2,1,0:T(8,128)(2,1)S(1)}, u32[]{:S(2)}, u32[]{:S(2)}) async-start(bf16[8,16,2048]{2,1,0:T(8,128)(2,1)} %bitcast.14), calls=%async_computation.5 | async-start | bytes 1048576 | tf_op jit(solution)/shard_map/all_to_all | solution.py:29
  211.3 17.9 %all-to-all-done.5 = bf16[8,16,2048]{2,1,0:T(8,128)(2,1)S(1)} async-done(((bf16[8,16,2048]{2,1,0:T(8,128)(2,1)}), bf16[8,16,2048]{2,1,0:T(8,128)(2,1)S(1)}, u32[]{:S(2)}, u32[]{:S(2)}) %all-to-all-start.5) | async-done | bytes 524320 | tf_op jit(solution)/shard_map/all_to_all | solution.py:29
  (95 shorter events, 40.6 us)
Async XLA Ops:
  7.2 12.4 %copy-start.2 = (bf16[1024,512]{1,0:T(8,128)(2,1)S(1)}, bf16[1024,512]{1,0:T(8,128)(2,1)}, u32[]{:S(2)}) copy-start(bf16[1024,512]{1,0:T(8,128)(2,1)} %param.6) | copy-start | bytes 3145732
  8.8 11.8 %copy-start.3 = (bf16[1024,512]{1,0:T(8,128)(2,1)S(1)}, bf16[1024,512]{1,0:T(8,128)(2,1)}, u32[]{:S(2)}) copy-start(bf16[1024,512]{1,0:T(8,128)(2,1)} %param.7) | copy-start | bytes 3145732
  8.9 1.3 collective-permute-start
  11.1 26.3 %all-to-all-start = ((bf16[8,16,2048]{2,1,0:T(8,128)(2,1)}), bf16[8,16,2048]{2,1,0:T(8,128)(2,1)S(1)}, u32[]{:S(2)}, u32[]{:S(2)}) async-start(bf16[8,16,2048]{2,1,0:T(8,128)(2,1)} %broadcast_in_dim.6), calls=%async_computation | async-start | bytes 1048576 | tf_op jit(solution)/shard_map/all_to_all | solution.py:29
  19.5 74.5 %all-gather.3.cloned.1.call-start = ((), (), s32[]{:S(2)}) async-start(), calls=%async_computation.6 | async-start | bytes 2359296 | tf_op jit(solution)/shard_map/all_gather | solution.py:114
  21.7 43.4 %collective-permute-start.7 = (bf16[1024,1024]{1,0:T(8,128)(2,1)}, bf16[1024,1024]{1,0:T(8,128)(2,1)}, u32[]{:S(2)}, u32[]{:S(2)}) collective-permute-start(bf16[1024,1024]{1,0:T(8,128)(2,1)} %constant_dynamic-update-slice_fusion.4), channel_id=1, source_target_pairs={{0,32},{32,0},{1,33},{33,1},{2,34},{34,2},{3,35},{35,3},{4,36},{36... | collective-permute-start | bytes 6291464 | tf_op jit(solution)/shard_map/ppermute | solution.py:25
  21.7 6.5 %collective-permute-start.2 = (bf16[16,2048]{1,0:T(8,128)(2,1)S(1)}, bf16[16,2048]{1,0:T(8,128)(2,1)S(1)}, u32[]{:S(2)}, u32[]{:S(2)}) collective-permute-start(bf16[16,2048]{1,0:T(8,128)(2,1)S(1)} %get-tuple-element.66), channel_id=1, source_target_pairs={{0,16},{8,24},{16,0},{24,8},{1,17},{9,25},{17,1},{25,9},{2,18},{10... | collective-permute-start | bytes 196616 | tf_op jit(solution)/shard_map/ppermute | solution.py:25
  25.0 5.5 %collective-permute-start.1 = (bf16[16,2048]{1,0:T(8,128)(2,1)S(1)}, bf16[16,2048]{1,0:T(8,128)(2,1)S(1)}, u32[]{:S(2)}, u32[]{:S(2)}) collective-permute-start(bf16[16,2048]{1,0:T(8,128)(2,1)S(1)} %get-tuple-element.66), channel_id=1, source_target_pairs={{0,8},{8,16},{16,24},{24,0},{1,9},{9,17},{17,25},{25,1},{2,10},{10... | collective-permute-start | bytes 196616 | tf_op jit(solution)/shard_map/ppermute | solution.py:25
  25.6 4.8 %collective-permute-start.3 = (bf16[16,2048]{1,0:T(8,128)(2,1)S(1)}, bf16[16,2048]{1,0:T(8,128)(2,1)S(1)}, u32[]{:S(2)}, u32[]{:S(2)}) collective-permute-start(bf16[16,2048]{1,0:T(8,128)(2,1)S(1)} %get-tuple-element.66), channel_id=1, source_target_pairs={{0,24},{8,0},{16,8},{24,16},{1,25},{9,1},{17,9},{25,17},{2,26},{10... | collective-permute-start | bytes 196616 | tf_op jit(solution)/shard_map/ppermute | solution.py:25
  37.4 15.2 %collective-permute-start.4 = (bf16[128,2048]{1,0:T(8,128)(2,1)S(1)}, bf16[128,2048]{1,0:T(8,128)(2,1)S(1)}, u32[]{:S(2)}, u32[]{:S(2)}) collective-permute-start(bf16[128,2048]{1,0:T(8,128)(2,1)S(1)} %bitcast.39), channel_id=1, source_target_pairs={{0,8},{8,16},{16,24},{24,0},{1,9},{9,17},{17,25},{25,1},{2,10},{10... | collective-permute-start | bytes 1572872 | tf_op jit(solution)/shard_map/ppermute | solution.py:25
  39.0 26.0 %collective-permute-start.5 = (bf16[128,2048]{1,0:T(8,128)(2,1)S(1)}, bf16[128,2048]{1,0:T(8,128)(2,1)S(1)}, u32[]{:S(2)}, u32[]{:S(2)}) collective-permute-start(bf16[128,2048]{1,0:T(8,128)(2,1)S(1)} %bitcast.40), channel_id=1, source_target_pairs={{0,16},{8,24},{16,0},{24,8},{1,17},{9,25},{17,1},{25,9},{2,18},{10... | collective-permute-start | bytes 1572872 | tf_op jit(solution)/shard_map/ppermute | solution.py:25
  41.9 37.0 %collective-permute-start.9 = (bf16[512,1024]{1,0:T(8,128)(2,1)}, bf16[512,1024]{1,0:T(8,128)(2,1)}, u32[]{:S(2)}, u32[]{:S(2)}) collective-permute-start(bf16[512,1024]{1,0:T(8,128)(2,1)} %param.8), channel_id=1, source_target_pairs={{0,32},{32,0},{1,33},{33,1},{2,34},{34,2},{3,35},{35,3},{4,36},{36... | collective-permute-start | bytes 3145736 | tf_op jit(solution)/shard_map/ppermute | solution.py:25
  41.9 23.1 %collective-permute-start.6 = (bf16[128,2048]{1,0:T(8,128)(2,1)S(1)}, bf16[128,2048]{1,0:T(8,128)(2,1)S(1)}, u32[]{:S(2)}, u32[]{:S(2)}) collective-permute-start(bf16[128,2048]{1,0:T(8,128)(2,1)S(1)} %bitcast.41), channel_id=1, source_target_pairs={{0,24},{8,0},{16,8},{24,16},{1,25},{9,1},{17,9},{25,17},{2,26},{10... | collective-permute-start | bytes 1572872 | tf_op jit(solution)/shard_map/ppermute | solution.py:25
  71.8 19.3 %collective-permute-start.8 = (bf16[512,1024]{1,0:T(8,128)(2,1)}, bf16[512,1024]{1,0:T(8,128)(2,1)}, u32[]{:S(2)}, u32[]{:S(2)}) collective-permute-start(bf16[512,1024]{1,0:T(8,128)(2,1)} %get-tuple-element.56), channel_id=1, source_target_pairs={{0,32},{32,0},{1,33},{33,1},{2,34},{34,2},{3,35},{35,3},{4,36},{36... | collective-permute-start | bytes 3145736 | tf_op jit(solution)/shard_map/ppermute | solution.py:25
  71.8 19.1 %all-to-all-start.1 = ((bf16[4,128,1024]{2,1,0:T(8,128)(2,1)}), bf16[4,128,1024]{2,1,0:T(8,128)(2,1)S(1)}, u32[]{:S(2)}, u32[]{:S(2)}) async-start(bf16[4,128,1024]{2,1,0:T(8,128)(2,1)} %bitcast.43), calls=%async_computation.1 | async-start | bytes 2097152 | tf_op jit(solution)/shard_map/all_to_all | solution.py:29
  99.7 19.3 %all-to-all-start.2 = ((bf16[4,256,512]{2,1,0:T(8,128)(2,1)}), bf16[4,256,512]{2,1,0:T(8,128)(2,1)}, u32[]{:S(2)}, u32[]{:S(2)}) async-start(bf16[4,256,512]{2,1,0:T(8,128)(2,1)} %pad_maximum_fusion.7), calls=%async_computation.2 | async-start | bytes 2097152 | tf_op jit(solution)/shard_map/all_to_all | solution.py:29
  106.9 19.6 %collective-permute-start.10 = (bf16[512,1024]{1,0:T(8,128)(2,1)}, bf16[512,1024]{1,0:T(8,128)(2,1)S(1)}, u32[]{:S(2)}, u32[]{:S(2)}) collective-permute-start(bf16[512,1024]{1,0:T(8,128)(2,1)} %get-tuple-element.54), channel_id=1, source_target_pairs={{0,32},{32,0},{1,33},{33,1},{2,34},{34,2},{3,35},{35,3},{4,36},{36... | collective-permute-start | bytes 3145736 | tf_op jit(solution)/shard_map/ppermute | solution.py:25
  120.9 21.6 %collective-permute-start.11 = (bf16[512,512]{1,0:T(8,128)(2,1)}, bf16[512,512]{1,0:T(8,128)(2,1)}, u32[]{:S(2)}, u32[]{:S(2)}) collective-permute-start(bf16[512,512]{1,0:T(8,128)(2,1)} %bitcast.11), channel_id=1, source_target_pairs={{0,32},{32,0},{1,33},{33,1},{2,34},{34,2},{3,35},{35,3},{4,36},{36... | collective-permute-start | bytes 1572872 | tf_op jit(solution)/shard_map/ppermute | solution.py:25
  122.1 5.4 %copy-start = (bf16[512,1024]{1,0:T(8,128)(2,1)S(1)}, bf16[512,1024]{1,0:T(8,128)(2,1)}, u32[]{:S(2)}) copy-start(bf16[512,1024]{1,0:T(8,128)(2,1)} %get-tuple-element.53) | copy-start | bytes 3145732
  130.2 34.2 %all-to-all-start.3 = ((bf16[4,128,1024]{2,1,0:T(8,128)(2,1)}), bf16[4,128,1024]{2,1,0:T(8,128)(2,1)S(1)}, u32[]{:S(2)}, u32[]{:S(2)}) async-start(bf16[4,128,1024]{2,1,0:T(8,128)(2,1)} %broadcast_in_dim.8), calls=%async_computation.3 | async-start | bytes 2097152 | tf_op jit(solution)/shard_map/all_to_all | solution.py:29
  136.7 16.4 %collective-permute-start.14 = (bf16[128,2048]{1,0:T(8,128)(2,1)S(1)}, bf16[128,2048]{1,0:T(8,128)(2,1)S(1)}, u32[]{:S(2)}, u32[]{:S(2)}) collective-permute-start(bf16[128,2048]{1,0:T(8,128)(2,1)S(1)} %get-tuple-element.50), channel_id=1, source_target_pairs={{0,16},{8,24},{16,0},{24,8},{1,17},{9,25},{17,1},{25,9},{2,18},{10... | collective-permute-start | bytes 1572872 | tf_op jit(solution)/shard_map/ppermute | solution.py:25
  139.3 24.3 %collective-permute-start.13 = (bf16[128,2048]{1,0:T(8,128)(2,1)S(1)}, bf16[128,2048]{1,0:T(8,128)(2,1)S(1)}, u32[]{:S(2)}, u32[]{:S(2)}) collective-permute-start(bf16[128,2048]{1,0:T(8,128)(2,1)S(1)} %get-tuple-element.51), channel_id=1, source_target_pairs={{0,8},{8,16},{16,24},{24,0},{1,9},{9,17},{17,25},{25,1},{2,10},{10... | collective-permute-start | bytes 1572872 | tf_op jit(solution)/shard_map/ppermute | solution.py:25
  139.6 24.7 %collective-permute-start.12 = (bf16[128,2048]{1,0:T(8,128)(2,1)S(1)}, bf16[128,2048]{1,0:T(8,128)(2,1)}, u32[]{:S(2)}, u32[]{:S(2)}) collective-permute-start(bf16[128,2048]{1,0:T(8,128)(2,1)S(1)} %get-tuple-element.52), channel_id=1, source_target_pairs={{0,24},{8,0},{16,8},{24,16},{1,25},{9,1},{17,9},{25,17},{2,26},{10... | collective-permute-start | bytes 1572872 | tf_op jit(solution)/shard_map/ppermute | solution.py:25
  153.0 10.5 %copy-start.5 = (bf16[128,2048]{1,0:T(8,128)(2,1)}, bf16[128,2048]{1,0:T(8,128)(2,1)S(1)}, u32[]{:S(2)}) copy-start(bf16[128,2048]{1,0:T(8,128)(2,1)S(1)} %collective-permute-done.14) | copy-start | bytes 1572868
  170.1 5.6 %collective-permute-start.18 = (bf16[512,1024]{1,0:T(8,128)(2,1)S(1)}, bf16[512,1024]{1,0:T(8,128)(2,1)S(1)}, u32[]{:S(2)}, u32[]{:S(2)}) collective-permute-start(bf16[512,1024]{1,0:T(8,128)(2,1)S(1)} %bitcast.36), channel_id=1, source_target_pairs={{0,32},{32,0},{1,33},{33,1},{2,34},{34,2},{3,35},{35,3},{4,36},{36... | collective-permute-start | bytes 3145736 | tf_op jit(solution)/shard_map/ppermute | solution.py:25
  170.2 15.0 %collective-permute-start.15 = (bf16[128,2048]{1,0:T(8,128)(2,1)}, bf16[128,2048]{1,0:T(8,128)(2,1)}, u32[]{:S(2)}, u32[]{:S(2)}) collective-permute-start(bf16[128,2048]{1,0:T(8,128)(2,1)} %get-tuple-element.47), channel_id=1, source_target_pairs={{0,24},{8,0},{16,8},{24,16},{1,25},{9,1},{17,9},{25,17},{2,26},{10... | collective-permute-start | bytes 1572872 | tf_op jit(solution)/shard_map/ppermute | solution.py:25
  171.5 16.6 %collective-permute-start.17 = (bf16[128,2048]{1,0:T(8,128)(2,1)}, bf16[128,2048]{1,0:T(8,128)(2,1)}, u32[]{:S(2)}, u32[]{:S(2)}) collective-permute-start(bf16[128,2048]{1,0:T(8,128)(2,1)} %get-tuple-element.48), channel_id=1, source_target_pairs={{0,16},{8,24},{16,0},{24,8},{1,17},{9,25},{17,1},{25,9},{2,18},{10... | collective-permute-start | bytes 1572872 | tf_op jit(solution)/shard_map/ppermute | solution.py:25
  173.3 25.3 %collective-permute-start.16 = (bf16[128,2048]{1,0:T(8,128)(2,1)}, bf16[128,2048]{1,0:T(8,128)(2,1)}, u32[]{:S(2)}, u32[]{:S(2)}) collective-permute-start(bf16[128,2048]{1,0:T(8,128)(2,1)} %get-tuple-element.49), channel_id=1, source_target_pairs={{0,8},{8,16},{16,24},{24,0},{1,9},{9,17},{17,25},{25,1},{2,10},{10... | collective-permute-start | bytes 1572872 | tf_op jit(solution)/shard_map/ppermute | solution.py:25
  177.2 30.5 %all-to-all-start.4 = ((bf16[8,16,2048]{2,1,0:T(8,128)(2,1)}), bf16[8,16,2048]{2,1,0:T(8,128)(2,1)S(1)}, u32[]{:S(2)}, u32[]{:S(2)}) async-start(bf16[8,16,2048]{2,1,0:T(8,128)(2,1)} %bitcast.12), calls=%async_computation.4 | async-start | bytes 1048576 | tf_op jit(solution)/shard_map/all_to_all | solution.py:29
  180.9 20.2 %copy-start.1 = (bf16[1024,1024]{1,0:T(8,128)(2,1)S(1)}, bf16[1024,1024]{1,0:T(8,128)(2,1)}, u32[]{:S(2)}) copy-start(bf16[1024,1024]{1,0:T(8,128)(2,1)} %pad_maximum_fusion.3) | copy-start | bytes 6291460
  207.8 21.4 %all-to-all-start.5 = ((bf16[8,16,2048]{2,1,0:T(8,128)(2,1)}), bf16[8,16,2048]{2,1,0:T(8,128)(2,1)S(1)}, u32[]{:S(2)}, u32[]{:S(2)}) async-start(bf16[8,16,2048]{2,1,0:T(8,128)(2,1)} %bitcast.14), calls=%async_computation.5 | async-start | bytes 1048576 | tf_op jit(solution)/shard_map/all_to_all | solution.py:29
  229.3 1.3 collective-permute-start.19
  (6 other events, 16.0 us)
Sparse Core Ops, SparseCore 0:
  37.5 37.4 all-gather.2

commit v5 on v4

v5 whole, which is shorter than its diff:
```python
import jax
import jax.numpy as jnp
from jax import lax
from jax.sharding import Mesh, PartitionSpec as P

BF = jnp.bfloat16
F32 = jnp.float32
X, CORE, Y, Z = 4, 2, 4, 8


def product(left_side, right_side):
    return jnp.dot(left_side, right_side, preferred_element_type=F32)


def product_right_t(left_side, right_side):
    return lax.dot_general(left_side, right_side, (((1,), (1,)), ((), ())), preferred_element_type=F32)


def product_left_t(left_side, right_side):
    return lax.dot_general(left_side, right_side, (((0,), (0,)), ((), ())), preferred_element_type=F32)


def shift(block, axis, step):
    size = lax.axis_size(axis)
    return lax.ppermute(block, axis, [(i, (i + step) % size) for i in range(size)])


def exchange(blocks, axis):
    return lax.all_to_all(blocks, axis, split_axis=0, concat_axis=0, tiled=True)


def gather(block, axis):
    count = lax.axis_size(axis)
    rows, width = block.shape
    copies = jnp.broadcast_to(block[None], (count, rows, width)).reshape(count * rows, width)
    return exchange(copies, axis)


def after(block, *earlier):
    return lax.optimization_barrier((block,) + earlier)[0]


def gather_y(own):
    near = [shift(own, "y", 1), shift(own, "y", 3)]
    return [own, near[0], shift(own, "y", 2), near[1]]


def other_core(block):
    return shift(block, "core", 1)


def sum_parts(parts, count):
    rows = parts.shape[0] // count
    return jnp.sum(parts.reshape((count, rows) + parts.shape[1:]).astype(F32), axis=0)


def reduce_x(partial):
    return sum_parts(exchange(partial, "x"), X)


def split_y(partial):
    rows = partial.shape[0] // Y
    return [partial[j * rows : (j + 1) * rows] for j in range(Y)]


def move_y(pieces):
    return [shift(pieces[1], "y", 3), shift(pieces[3], "y", 1), shift(pieces[2], "y", 2)]


def sum_y(own, moved):
    total = own.astype(F32)
    for piece in moved:
        total = total + piece.astype(F32)
    return total.astype(BF)


def reduce_z(total):
    return sum_parts(exchange(total, "z"), Z).astype(BF)


def swap_rows(blocks, first):
    rows = blocks[0].shape[0] // CORE
    kept = [jnp.where(first, block[:rows], block[rows:]) for block in blocks]
    sent = [jnp.where(first, block[rows:], block[:rows]) for block in blocks]
    received = other_core(jnp.concatenate(sent, axis=0))
    return kept, received


def own_columns(blocks, first):
    columns = blocks[0].shape[1] // CORE
    received = other_core(jnp.stack([block[:, columns:] for block in blocks]))
    return [
        jnp.where(
            first,
            jnp.concatenate([block[:, :columns], received[i]], axis=0),
            jnp.concatenate([received[i], block[:, :columns]], axis=0),
        )
        for i, block in enumerate(blocks)
    ]


def swap_rows(blocks, first):
    rows = blocks[0].shape[0] // CORE
    kept = [jnp.where(first, block[:rows], block[rows:]) for block in blocks]
    sent = [jnp.where(first, block[rows:], block[:rows]) for block in blocks]
    received = other_core(jnp.concatenate(sent, axis=0))
    return kept, received


def own_columns(blocks, first):
    columns = blocks[0].shape[1] // CORE
    received = other_core(jnp.stack([block[:, columns:] for block in blocks]))
    return [
        jnp.where(
            first,
            jnp.concatenate([block[:, :columns], received[i]], axis=0),
            jnp.concatenate([received[i], block[:, :columns]], axis=0),
        )
        for i, block in enumerate(blocks)
    ]


def both_halves(half):
    return jnp.concatenate([half, other_core(half)], axis=0)


def body(tokens, gate_weight, up_weight, down_weight, out_grad):
    width = gate_weight.shape[1]
    first = lax.axis_index("core") == 0

    (tokens_own, grads_own), received = swap_rows((tokens, out_grad), first)
    rows = tokens_own.shape[0]
    tokens_z = gather(tokens_own, "z")
    received = jnp.stack(gather_y(received))
    tokens_z, received = lax.optimization_barrier((tokens_z, received))

    def gather_z_last(block):
        whole = lax.all_gather(block, "z", axis=0, tiled=False)
        return jnp.swapaxes(whole, 0, 1).reshape(Y * Z * rows, -1)

    tokens_far = gather_z_last(received[:, :rows])
    grads_far = gather_z_last(received[:, rows:])
    grads_z = gather(after(grads_own, tokens_z), "z")
    tokens_near = jnp.concatenate(gather_y(tokens_z), axis=0)
    grads_near = jnp.concatenate(gather_y(grads_z), axis=0)
    weights = jnp.concatenate([gate_weight, up_weight], axis=1)
    weights_far = other_core(weights)
    down_far = other_core(down_weight)

    gate_up = (product(tokens_near, weights) + product(tokens_far, weights_far)).astype(BF)
    grads_far = after(grads_far, gate_up)
    gate_up = exchange(gate_up, "x")
    hidden_partial = (product_right_t(grads_near, down_weight) + product_right_t(grads_far, down_far)).astype(BF)
    both_weights = jnp.concatenate([weights, weights_far], axis=0)
    down_weights = jnp.concatenate([down_weight, down_far], axis=1)
    gate_up, hidden_partial, both_weights, down_weights = lax.optimization_barrier(
        (gate_up, hidden_partial, both_weights, down_weights)
    )
    gate_up = sum_parts(gate_up, X)
    gate_value = gate_up[:, :width]
    up_value = gate_up[:, width:]
    sigmoid_gate = jax.nn.sigmoid(gate_value)
    silu_gate = gate_value * sigmoid_gate
    hidden_share = (silu_gate * up_value).astype(BF)

    share = hidden_share.shape[0]
    mixed = jnp.concatenate(
        [jnp.broadcast_to(hidden_share[None], (X, share, width)), hidden_partial.reshape(X, share, width)], axis=1
    )
    mixed = exchange(mixed.reshape(2 * X * share, width), "x").reshape(X, 2 * share, width)
    mixed, tokens_moved, grads_moved = lax.optimization_barrier((mixed, other_core(tokens_far), other_core(grads_far)))
    hidden_half = mixed[:, :share].reshape(X * share, width)
    hidden_grad = jnp.sum(mixed[:, share:].astype(F32), axis=0)
    gate_grad = (hidden_grad * up_value * sigmoid_gate * (1.0 + gate_value * (1.0 - sigmoid_gate))).astype(BF)
    up_grad = (hidden_grad * silu_gate).astype(BF)
    grads_share = jnp.concatenate([gate_grad, up_grad], axis=1)
    grads_both = gather(grads_share, "x")

    hidden_half = after(hidden_half, grads_share)
    output_pieces = split_y(product(hidden_half, down_weights).astype(BF))
    output_moved = move_y(output_pieces)
    grads_both, *output_moved = lax.optimization_barrier((grads_both, *output_moved))
    input_pieces = split_y(product_right_t(grads_both, both_weights).astype(BF))
    input_moved = move_y(input_pieces)

    both_moved = other_core(after(grads_both, *input_pieces))
    hidden_moved = other_core(after(hidden_half, *input_pieces))
    output_total = reduce_z(after(sum_y(output_pieces[0], output_moved), both_moved))

    def over_tokens(left_halves, right_halves):
        return product_left_t(left_halves[0], right_halves[0]) + product_left_t(left_halves[1], right_halves[1])

    all_tokens = (tokens_near, tokens_moved)
    weight_grads = [
        over_tokens(all_tokens, (grads_both[:, :width], both_moved[:, :width])),
        over_tokens(all_tokens, (grads_both[:, width:], both_moved[:, width:])),
        over_tokens((hidden_half, hidden_moved), (grads_near, grads_moved)),
    ]
    input_moved, weight_grads, output_total = lax.optimization_barrier((input_moved, weight_grads, output_total))
    input_total = sum_y(input_pieces[0], input_moved)
    return (*own_columns((output_total, reduce_z(input_total)), first), *weight_grads)


def solution(mesh):
    grid = Mesh(mesh.devices.reshape(X, CORE, Y, Z), ("x", "core", "y", "z"))
    row, col = ("x", "core"), ("y", "z")
    in_specs = (P(col, row), P(row, col), P(row, col), P(col, row), P(col, row))
    out_specs = (P(col, row), P(col, row), P(row, col), P(row, col), P(col, row))
    return jax.shard_map(body, mesh=grid, in_specs=in_specs, out_specs=out_specs, check_vma=False)
```

time: 240 us -> 257 us (1.071)
  starting transfers between devices: 52.8 us -> 60 us
  waiting for transfers between devices: 107 us -> 114 us
  other arithmetic: 14.9 us -> 19.6 us
  local copies, waits for them, and re-layouts: 21.1 us -> 17.6 us
    ppermute x20 -> x23, waiting for transfers between devices: 61.3 us -> 32.1 us  [shift(): lax.ppermute(block, axis, [(i, (i + step) % size) for i in range(size)])]
    all_gather x1 -> x2, waiting for transfers between devices: 0.02 us -> 28.6 us  [gather_z_last(): whole = lax.all_gather(block, 'z', axis=0, tiled=False)]
    all_to_all x6 -> x7, waiting for transfers between devices: 45.9 us -> 52.2 us  [exchange(): return lax.all_to_all(blocks, axis, split_axis=0, concat_axis=0, tiled=True)]
    all_to_all x6 -> x7, starting transfers between devices: 31.1 us -> 35.4 us  [exchange(): return lax.all_to_all(blocks, axis, split_axis=0, concat_axis=0, tiled=True)]
    concatenate x6 -> x5, other arithmetic: 5.2 us -> 8.15 us  [the longest x1 4 us: body(): both_weights = jnp.concatenate([weights, weights_far], axis=0)]
    transpose x1 -> x2, local copies, waits for them, and re-layouts: 1.73 us -> 4.61 us  [gather_z_last(): return jnp.swapaxes(whole, 0, 1).reshape(Y * Z * rows, -1)]
    ppermute x20 -> x23, starting transfers between devices: 21.6 us -> 24.5 us  [shift(): lax.ppermute(block, axis, [(i, (i + step) % size) for i in range(size)])]
    unnamed x28 -> x24, local copies, waits for them, and re-layouts: 6.59 us -> 4.12 us
  transfers between devices with their start and end apart: 27 -> 32, of which waited for: 14 -> 14; matrix products, arithmetic and copies ran while one was open for 19% -> 19% of each run, Pallas kernels for 0% -> 0%
where the time goes in v5:
time: 257 us; the launch traced here: 254 us
  waiting for transfers between devices  114 us (44%)
  starting transfers between devices  60 us (23%)
  matrix products  29.3 us (11%)
  other arithmetic  19.6 us (8%)
  local copies, waits for them, and re-layouts  17.6 us (7%)
  between operations  14.4 us (6%)
    all_to_all x7, waiting for transfers between devices, exchange(): return lax.all_to_all(blocks, axis, split_axis=0, concat_axis=0, tiled=True)  52.2 us
    all_to_all x7, starting transfers between devices, exchange(): return lax.all_to_all(blocks, axis, split_axis=0, concat_axis=0, tiled=True)  35.4 us
    ppermute x23, waiting for transfers between devices, shift(): lax.ppermute(block, axis, [(i, (i + step) % size) for i in range(size)])  32.1 us
    all_gather x2, waiting for transfers between devices, gather_z_last(): whole = lax.all_gather(block, 'z', axis=0, tiled=False)  28.6 us
    ppermute x23, starting transfers between devices, shift(): lax.ppermute(block, axis, [(i, (i + step) % size) for i in range(size)])  24.5 us
    dot_general x6, matrix products, product_left_t(): lax.dot_general(left_side, right_side, (((0,), (0,)), ((), ())), preferre...  11.8 us
    dot_general x3, matrix products, product_right_t(): lax.dot_general(left_side, right_side, (((1,), (1,)), ((), ())), preferre...  9.05 us
    dot_general x3, matrix products, product(): return jnp.dot(left_side, right_side, preferred_element_type=F32)  8.42 us
  transfers between devices with their start and end apart: 32, of which 14 were waited for; matrix products, arithmetic and copies ran while one was open for 19% of the time, Pallas kernels for 0%

profile of v5, /device:TPU:2, one launch (start us, length us, event | category | flops | bytes accessed | tf_op | source)
XLA Modules:
  0.0 254.4 jit_solution(16624606389806842200)
XLA Ops:
  8.8 8.5 %all-to-all-start = ((bf16[8,16,1024]{2,1,0:T(8,128)(2,1)}), bf16[8,16,1024]{2,1,0:T(8,128)(2,1)S(1)}, u32[]{:S(2)}, u32[]{:S(2)}) async-start(bf16[8,16,1024]{2,1,0:T(8,128)(2,1)} %broadcast_in_dim.8), calls=%async_computation | async-start | bytes 524288 | tf_op jit(solution)/shard_map/all_to_all | solution.py:29
  21.0 2.9 %collective-permute-start.2 = (bf16[32,1024]{1,0:T(8,128)(2,1)S(1)}, bf16[32,1024]{1,0:T(8,128)(2,1)S(1)}, u32[]{:S(2)}, u32[]{:S(2)}) collective-permute-start(bf16[32,1024]{1,0:T(8,128)(2,1)S(1)} %collective-permute-done), channel_id=1, source_target_pairs={{0,16},{8,24},{16,0},{24,8},{1,17},{9,25},{17,1},{25,9},{2,18},{10... | collective-permute-start | bytes 196616 | tf_op jit(solution)/shard_map/ppermute | solution.py:25
  33.6 2.9 %collective-permute-start.5 = (bf16[128,1024]{1,0:T(8,128)(2,1)S(1)}, bf16[128,1024]{1,0:T(8,128)(2,1)}, u32[]{:S(2)}, u32[]{:S(2)}) collective-permute-start(bf16[128,1024]{1,0:T(8,128)(2,1)S(1)} %bitcast.58), channel_id=1, source_target_pairs={{0,16},{8,24},{16,0},{24,8},{1,17},{9,25},{17,1},{25,9},{2,18},{10... | collective-permute-start | bytes 786440 | tf_op jit(solution)/shard_map/ppermute | solution.py:25
  38.6 4.9 %all-to-all-start.2 = ((bf16[8,16,1024]{2,1,0:T(8,128)(2,1)}), bf16[8,16,1024]{2,1,0:T(8,128)(2,1)}, u32[]{:S(2)}, u32[]{:S(2)}) async-start(bf16[8,16,1024]{2,1,0:T(8,128)(2,1)} %broadcast_in_dim.9), calls=%async_computation.2 | async-start | bytes 524288 | tf_op jit(solution)/shard_map/all_to_all | solution.py:29
  45.2 3.3 %collective-permute-done.5 = bf16[128,1024]{1,0:T(8,128)(2,1)} collective-permute-done((bf16[128,1024]{1,0:T(8,128)(2,1)S(1)}, bf16[128,1024]{1,0:T(8,128)(2,1)}, u32[]{:S(2)}, u32[]{:S(2)}) %collective-permute-start.5) | collective-permute-done | bytes 262176 | tf_op jit(solution)/shard_map/ppermute | solution.py:25
  50.5 7.0 %all-to-all-done.2 = bf16[8,16,1024]{2,1,0:T(8,128)(2,1)} async-done(((bf16[8,16,1024]{2,1,0:T(8,128)(2,1)}), bf16[8,16,1024]{2,1,0:T(8,128)(2,1)}, u32[]{:S(2)}, u32[]{:S(2)}) %all-to-all-start.2) | async-done | bytes 262176 | tf_op jit(solution)/shard_map/all_to_all | solution.py:29
  59.4 2.4 collective-permute-start.9
  61.9 3.1 %pad_maximum_fusion.1 = bf16[512,2048]{1,0:T(8,128)(2,1)} fusion(bf16[512,1024]{1,0:T(8,128)(2,1)} %collective-permute-done.11, bf16[512,1024]{1,0:T(8,128)(2,1)} %param.8), kind=kLoop, calls=%fused_computation.3 | loop fusion | flops 4194304 | bytes 4194304 | tf_op jit(solution)/shard_map/concatenate | solution.py:155
  64.9 5.2 %all-gather.5.cloned.1.call-done = bf16[32,16,1024]{2,1,0:T(8,128)(2,1)} async-done(((bf16[4,16,1024]{2,1,0:T(8,128)(2,1)}), bf16[32,16,1024]{2,1,0:T(8,128)(2,1)}) %all-gather.5.cloned.1.call-update) | async-done | bytes 1048592 | tf_op jit(solution)/shard_map/all_gather | solution.py:138
  70.2 2.3 copy.12
  72.5 3.2 %fusion.15 = f32[512,1024]{1,0:T(8,128)S(1)} fusion(bf16[512,1024]{1,0:T(8,128)(2,1)} %bitcast.7, bf16[1024,1024]{1,0:T(8,128)(2,1)} %collective-permute-done.7), kind=kOutput, calls=%fused_computation.54 | convolution fusion | flops 1073741824 | bytes 5242880 | tf_op jit(solution)/shard_map/dot_general | solution.py:12
  75.6 2.2 add_convert_fusion
  77.9 4.7 %all-to-all-start.1 = ((bf16[4,128,1024]{2,1,0:T(8,128)(2,1)}), bf16[4,128,1024]{2,1,0:T(8,128)(2,1)}, u32[]{:S(2)}, u32[]{:S(2)}) async-start(bf16[4,128,1024]{2,1,0:T(8,128)(2,1)} %bitcast.56), calls=%async_computation.1 | async-start | bytes 2097152 | tf_op jit(solution)/shard_map/all_to_all | solution.py:29
  82.5 4.0 %pad_maximum_fusion = bf16[2048,1024]{1,0:T(8,128)(2,1)} fusion(bf16[1024,1024]{1,0:T(8,128)(2,1)} %collective-permute-done.7, bf16[1024,1024]{1,0:T(8,128)(2,1)S(1)} %constant_dynamic-update-slice_fusion.4), kind=kLoop, calls=%fused_computation | loop fusion | flops 8388608 | bytes 8388608 | tf_op jit(solution)/shard_map/concatenate | solution.py:154
  86.5 23.4 %all-gather.7.cloned.1.call-done = bf16[32,16,1024]{2,1,0:T(8,128)(2,1)} async-done(((bf16[4,16,1024]{2,1,0:T(8,128)(2,1)}), bf16[32,16,1024]{2,1,0:T(8,128)(2,1)}) %all-gather.7.cloned.1.call-update) | async-done | bytes 1048592 | tf_op jit(solution)/shard_map/all_gather | solution.py:138
  109.9 2.3 copy.13
  112.2 2.3 fusion.16
  119.4 4.9 %all-to-all-start.3 = ((bf16[4,256,512]{2,1,0:T(8,128)(2,1)}), bf16[4,256,512]{2,1,0:T(8,128)(2,1)}, u32[]{:S(2)}, u32[]{:S(2)}) async-start(bf16[4,256,512]{2,1,0:T(8,128)(2,1)} %pad_maximum_fusion.3), calls=%async_computation.3 | async-start | bytes 2097152 | tf_op jit(solution)/shard_map/all_to_all | solution.py:29
  124.3 14.7 %all-to-all-done.3 = bf16[4,256,512]{2,1,0:T(8,128)(2,1)} async-done(((bf16[4,256,512]{2,1,0:T(8,128)(2,1)}), bf16[4,256,512]{2,1,0:T(8,128)(2,1)}, u32[]{:S(2)}, u32[]{:S(2)}) %all-to-all-start.3) | async-done | bytes 1048608 | tf_op jit(solution)/shard_map/all_to_all | solution.py:29
  143.3 4.9 %all-to-all-start.4 = ((bf16[4,128,1024]{2,1,0:T(8,128)(2,1)}), bf16[4,128,1024]{2,1,0:T(8,128)(2,1)S(1)}, u32[]{:S(2)}, u32[]{:S(2)}) async-start(bf16[4,128,1024]{2,1,0:T(8,128)(2,1)} %broadcast_in_dim.11), calls=%async_computation.4 | async-start | bytes 2097152 | tf_op jit(solution)/shard_map/all_to_all | solution.py:29
  148.2 3.0 %convolution_convert_fusion.1 = bf16[512,2048]{1,0:T(8,128)(2,1)S(1)} fusion(bf16[512,512]{1,0:T(8,128)(2,1)} %bitcast.61, bf16[512,2048]{1,0:T(8,128)(2,1)} %pad_maximum_fusion.1), kind=kOutput, calls=%fused_computation.2 | convolution fusion | flops 1074790400 | bytes 4718592 | tf_op jit(solution)/shard_map/dot_general | solution.py:12
  151.4 2.9 %collective-permute-start.14 = (bf16[128,2048]{1,0:T(8,128)(2,1)S(1)}, bf16[128,2048]{1,0:T(8,128)(2,1)S(1)}, u32[]{:S(2)}, u32[]{:S(2)}) collective-permute-start(bf16[128,2048]{1,0:T(8,128)(2,1)S(1)} %get-tuple-element.63), channel_id=1, source_target_pairs={{0,24},{8,0},{16,8},{24,16},{1,25},{9,1},{17,9},{25,17},{2,26},{10... | collective-permute-start | bytes 1572872 | tf_op jit(solution)/shard_map/ppermute | solution.py:25
  156.5 19.9 %collective-permute-done.14 = bf16[128,2048]{1,0:T(8,128)(2,1)S(1)} collective-permute-done((bf16[128,2048]{1,0:T(8,128)(2,1)S(1)}, bf16[128,2048]{1,0:T(8,128)(2,1)S(1)}, u32[]{:S(2)}, u32[]{:S(2)}) %collective-permute-start.14) | collective-permute-done | bytes 524320 | tf_op jit(solution)/shard_map/ppermute | solution.py:25
  176.4 3.4 %collective-permute-done.15 = bf16[128,2048]{1,0:T(8,128)(2,1)S(1)} collective-permute-done((bf16[128,2048]{1,0:T(8,128)(2,1)S(1)}, bf16[128,2048]{1,0:T(8,128)(2,1)S(1)}, u32[]{:S(2)}, u32[]{:S(2)}) %collective-permute-start.15) | collective-permute-done | bytes 524320 | tf_op jit(solution)/shard_map/ppermute | solution.py:25
  180.6 4.6 %convolution_convert_fusion = bf16[512,2048]{1,0:T(8,128)(2,1)S(1)} fusion(bf16[512,1024]{1,0:T(8,128)(2,1)S(1)} %bitcast.49, bf16[2048,1024]{1,0:T(8,128)(2,1)} %pad_maximum_fusion), kind=kOutput, calls=%fused_computation.1 | convolution fusion | flops 2148532224 | bytes 7340032 | tf_op jit(solution)/shard_map/dot_general | solution.py:16
  189.2 2.3 add_convert_fusion.2
  193.5 3.2 %convolution_add_fusion = f32[512,1024]{1,0:T(8,128)} fusion(f32[512,1024]{1,0:T(8,128)S(1)} %fusion.17, bf16[512,512]{1,0:T(8,128)(2,1)S(1)} %bitcast.63, bf16[128,1024]{1,0:T(8,128)(2,1)S(1)} %collective-permute-done.10, bf16[128,1024]{1,0:T(8,128)(2,1)} %collective-permute-done.9, bf16[128,1024]{1,0:T(8,128)(2,1)} %collective-permute-done.8, ...), kind=kOutput, calls=%fused_computation.6 | convolution fusion | flops 541589504 | bytes 5767168 | tf_op jit(solution)/shard_map/dot_general | solution.py:20
  197.6 4.1 %all-to-all-start.5 = ((bf16[8,16,2048]{2,1,0:T(8,128)(2,1)}), bf16[8,16,2048]{2,1,0:T(8,128)(2,1)}, u32[]{:S(2)}, u32[]{:S(2)}) async-start(bf16[8,16,2048]{2,1,0:T(8,128)(2,1)} %bitcast.53), calls=%async_computation.5 | async-start | bytes 1048576 | tf_op jit(solution)/shard_map/all_to_all | solution.py:29
  208.5 11.8 %all-to-all-done.5 = bf16[8,16,2048]{2,1,0:T(8,128)(2,1)} async-done(((bf16[8,16,2048]{2,1,0:T(8,128)(2,1)}), bf16[8,16,2048]{2,1,0:T(8,128)(2,1)}, u32[]{:S(2)}, u32[]{:S(2)}) %all-to-all-start.5) | async-done | bytes 524320 | tf_op jit(solution)/shard_map/all_to_all | solution.py:29
  221.4 2.6 %add_convert_fusion.1 = bf16[128,2048]{1,0:T(8,128)(2,1)} fusion(bf16[128,2048]{1,0:T(8,128)(2,1)} %collective-permute-done.19, bf16[128,2048]{1,0:T(8,128)(2,1)} %collective-permute-done.18, bf16[128,2048]{1,0:T(8,128)(2,1)} %collective-permute-done.17, bf16[512,2048]{1,0:T(8,128)(2,1)} %copy-done), kind=kLoop, calls=%fused_computation.13 | loop fusion | flops 2097152 | bytes 2621440 | tf_op jit(solution)/shard_map/convert_element_type | solution.py:74
  224.0 3.5 %all-to-all-start.6 = ((bf16[8,16,2048]{2,1,0:T(8,128)(2,1)}), bf16[8,16,2048]{2,1,0:T(8,128)(2,1)S(1)}, u32[]{:S(2)}, u32[]{:S(2)}) async-start(bf16[8,16,2048]{2,1,0:T(8,128)(2,1)} %bitcast.20), calls=%async_computation.6 | async-start | bytes 1048576 | tf_op jit(solution)/shard_map/all_to_all | solution.py:29
  227.6 17.8 %all-to-all-done.6 = bf16[8,16,2048]{2,1,0:T(8,128)(2,1)S(1)} async-done(((bf16[8,16,2048]{2,1,0:T(8,128)(2,1)}), bf16[8,16,2048]{2,1,0:T(8,128)(2,1)S(1)}, u32[]{:S(2)}, u32[]{:S(2)}) %all-to-all-start.6) | async-done | bytes 524320 | tf_op jit(solution)/shard_map/all_to_all | solution.py:29
  (103 shorter events, 51.9 us)
Async XLA Ops:
  8.8 20.3 %all-to-all-start = ((bf16[8,16,1024]{2,1,0:T(8,128)(2,1)}), bf16[8,16,1024]{2,1,0:T(8,128)(2,1)S(1)}, u32[]{:S(2)}, u32[]{:S(2)}) async-start(bf16[8,16,1024]{2,1,0:T(8,128)(2,1)} %broadcast_in_dim.8), calls=%async_computation | async-start | bytes 524288 | tf_op jit(solution)/shard_map/all_to_all | solution.py:29
  17.2 52.9 %all-gather.5.cloned.1.call-start = ((), (), s32[]{:S(2)}) async-start(), calls=%async_computation.7 | async-start | bytes 1179648 | tf_op jit(solution)/shard_map/all_gather | solution.py:138
  18.1 1.3 collective-permute-start
  19.4 5.8 %collective-permute-start.1 = (bf16[32,1024]{1,0:T(8,128)(2,1)S(1)}, bf16[32,1024]{1,0:T(8,128)(2,1)S(1)}, u32[]{:S(2)}, u32[]{:S(2)}) collective-permute-start(bf16[32,1024]{1,0:T(8,128)(2,1)S(1)} %collective-permute-done), channel_id=1, source_target_pairs={{0,8},{8,16},{16,24},{24,0},{1,9},{9,17},{17,25},{25,1},{2,10},{10... | collective-permute-start | bytes 196616 | tf_op jit(solution)/shard_map/ppermute | solution.py:25
  21.0 6.4 %collective-permute-start.2 = (bf16[32,1024]{1,0:T(8,128)(2,1)S(1)}, bf16[32,1024]{1,0:T(8,128)(2,1)S(1)}, u32[]{:S(2)}, u32[]{:S(2)}) collective-permute-start(bf16[32,1024]{1,0:T(8,128)(2,1)S(1)} %collective-permute-done), channel_id=1, source_target_pairs={{0,16},{8,24},{16,0},{24,8},{1,17},{9,25},{17,1},{25,9},{2,18},{10... | collective-permute-start | bytes 196616 | tf_op jit(solution)/shard_map/ppermute | solution.py:25
  23.9 4.3 %collective-permute-start.3 = (bf16[32,1024]{1,0:T(8,128)(2,1)S(1)}, bf16[32,1024]{1,0:T(8,128)(2,1)S(1)}, u32[]{:S(2)}, u32[]{:S(2)}) collective-permute-start(bf16[32,1024]{1,0:T(8,128)(2,1)S(1)} %collective-permute-done), channel_id=1, source_target_pairs={{0,24},{8,0},{16,8},{24,16},{1,25},{9,1},{17,9},{25,17},{2,26},{10... | collective-permute-start | bytes 196616 | tf_op jit(solution)/shard_map/ppermute | solution.py:25
  31.4 41.0 %collective-permute-start.7 = (bf16[1024,1024]{1,0:T(8,128)(2,1)S(1)}, bf16[1024,1024]{1,0:T(8,128)(2,1)}, u32[]{:S(2)}, u32[]{:S(2)}) collective-permute-start(bf16[1024,1024]{1,0:T(8,128)(2,1)S(1)} %constant_dynamic-update-slice_fusion.4), channel_id=1, source_target_pairs={{0,32},{32,0},{1,33},{33,1},{2,34},{34,2},{3,35},{35,3},{4,36},{36... | collective-permute-start | bytes 6291464 | tf_op jit(solution)/shard_map/ppermute | solution.py:25
  31.5 30.3 %collective-permute-start.11 = (bf16[512,1024]{1,0:T(8,128)(2,1)}, bf16[512,1024]{1,0:T(8,128)(2,1)}, u32[]{:S(2)}, u32[]{:S(2)}) collective-permute-start(bf16[512,1024]{1,0:T(8,128)(2,1)} %param.8), channel_id=1, source_target_pairs={{0,32},{32,0},{1,33},{33,1},{2,34},{34,2},{3,35},{35,3},{4,36},{36... | collective-permute-start | bytes 3145736 | tf_op jit(solution)/shard_map/ppermute | solution.py:25
  32.0 12.2 %collective-permute-start.4 = (bf16[128,1024]{1,0:T(8,128)(2,1)S(1)}, bf16[128,1024]{1,0:T(8,128)(2,1)}, u32[]{:S(2)}, u32[]{:S(2)}) collective-permute-start(bf16[128,1024]{1,0:T(8,128)(2,1)S(1)} %bitcast.57), channel_id=1, source_target_pairs={{0,8},{8,16},{16,24},{24,0},{1,9},{9,17},{17,25},{25,1},{2,10},{10... | collective-permute-start | bytes 786440 | tf_op jit(solution)/shard_map/ppermute | solution.py:25
  33.6 14.9 %collective-permute-start.5 = (bf16[128,1024]{1,0:T(8,128)(2,1)S(1)}, bf16[128,1024]{1,0:T(8,128)(2,1)}, u32[]{:S(2)}, u32[]{:S(2)}) collective-permute-start(bf16[128,1024]{1,0:T(8,128)(2,1)S(1)} %bitcast.58), channel_id=1, source_target_pairs={{0,16},{8,24},{16,0},{24,8},{1,17},{9,25},{17,1},{25,9},{2,18},{10... | collective-permute-start | bytes 786440 | tf_op jit(solution)/shard_map/ppermute | solution.py:25
  36.5 13.0 %collective-permute-start.6 = (bf16[128,1024]{1,0:T(8,128)(2,1)S(1)}, bf16[128,1024]{1,0:T(8,128)(2,1)}, u32[]{:S(2)}, u32[]{:S(2)}) collective-permute-start(bf16[128,1024]{1,0:T(8,128)(2,1)S(1)} %bitcast.59), channel_id=1, source_target_pairs={{0,24},{8,0},{16,8},{24,16},{1,25},{9,1},{17,9},{25,17},{2,26},{10... | collective-permute-start | bytes 786440 | tf_op jit(solution)/shard_map/ppermute | solution.py:25
  38.6 18.8 %all-to-all-start.2 = ((bf16[8,16,1024]{2,1,0:T(8,128)(2,1)}), bf16[8,16,1024]{2,1,0:T(8,128)(2,1)}, u32[]{:S(2)}, u32[]{:S(2)}) async-start(bf16[8,16,1024]{2,1,0:T(8,128)(2,1)} %broadcast_in_dim.9), calls=%async_computation.2 | async-start | bytes 524288 | tf_op jit(solution)/shard_map/all_to_all | solution.py:29
  43.4 66.5 %all-gather.7.cloned.1.call-start = ((), (), s32[]{:S(2)}) async-start(), calls=%async_computation.8 | async-start | bytes 1179648 | tf_op jit(solution)/shard_map/all_gather | solution.py:138
  57.4 57.1 %collective-permute-start.10 = (bf16[128,1024]{1,0:T(8,128)(2,1)}, bf16[128,1024]{1,0:T(8,128)(2,1)S(1)}, u32[]{:S(2)}, u32[]{:S(2)}) collective-permute-start(bf16[128,1024]{1,0:T(8,128)(2,1)} %bitcast.10), channel_id=1, source_target_pairs={{0,24},{8,0},{16,8},{24,16},{1,25},{9,1},{17,9},{25,17},{2,26},{10... | collective-permute-start | bytes 786440 | tf_op jit(solution)/shard_map/ppermute | solution.py:25
  58.0 56.5 %collective-permute-start.8 = (bf16[128,1024]{1,0:T(8,128)(2,1)}, bf16[128,1024]{1,0:T(8,128)(2,1)}, u32[]{:S(2)}, u32[]{:S(2)}) collective-permute-start(bf16[128,1024]{1,0:T(8,128)(2,1)} %bitcast.10), channel_id=1, source_target_pairs={{0,8},{8,16},{16,24},{24,0},{1,9},{9,17},{17,25},{25,1},{2,10},{10... | collective-permute-start | bytes 786440 | tf_op jit(solution)/shard_map/ppermute | solution.py:25
  59.4 55.1 %collective-permute-start.9 = (bf16[128,1024]{1,0:T(8,128)(2,1)}, bf16[128,1024]{1,0:T(8,128)(2,1)}, u32[]{:S(2)}, u32[]{:S(2)}) collective-permute-start(bf16[128,1024]{1,0:T(8,128)(2,1)} %bitcast.10), channel_id=1, source_target_pairs={{0,16},{8,24},{16,0},{24,8},{1,17},{9,25},{17,1},{25,9},{2,18},{10... | collective-permute-start | bytes 786440 | tf_op jit(solution)/shard_map/ppermute | solution.py:25
  77.9 38.9 %all-to-all-start.1 = ((bf16[4,128,1024]{2,1,0:T(8,128)(2,1)}), bf16[4,128,1024]{2,1,0:T(8,128)(2,1)}, u32[]{:S(2)}, u32[]{:S(2)}) async-start(bf16[4,128,1024]{2,1,0:T(8,128)(2,1)} %bitcast.56), calls=%async_computation.1 | async-start | bytes 2097152 | tf_op jit(solution)/shard_map/all_to_all | solution.py:29
  86.5 37.7 %collective-permute-start.12 = (bf16[512,1024]{1,0:T(8,128)(2,1)}, bf16[512,1024]{1,0:T(8,128)(2,1)S(1)}, u32[]{:S(2)}, u32[]{:S(2)}) collective-permute-start(bf16[512,1024]{1,0:T(8,128)(2,1)} %bitcast.7), channel_id=1, source_target_pairs={{0,32},{32,0},{1,33},{33,1},{2,34},{34,2},{3,35},{35,3},{4,36},{36... | collective-permute-start | bytes 3145736 | tf_op jit(solution)/shard_map/ppermute | solution.py:25
  112.2 12.1 %collective-permute-start.13 = (bf16[512,1024]{1,0:T(8,128)(2,1)}, bf16[512,1024]{1,0:T(8,128)(2,1)}, u32[]{:S(2)}, u32[]{:S(2)}) collective-permute-start(bf16[512,1024]{1,0:T(8,128)(2,1)} %bitcast.13), channel_id=1, source_target_pairs={{0,32},{32,0},{1,33},{33,1},{2,34},{34,2},{3,35},{35,3},{4,36},{36... | collective-permute-start | bytes 3145736 | tf_op jit(solution)/shard_map/ppermute | solution.py:25
  119.4 19.6 %all-to-all-start.3 = ((bf16[4,256,512]{2,1,0:T(8,128)(2,1)}), bf16[4,256,512]{2,1,0:T(8,128)(2,1)}, u32[]{:S(2)}, u32[]{:S(2)}) async-start(bf16[4,256,512]{2,1,0:T(8,128)(2,1)} %pad_maximum_fusion.3), calls=%async_computation.3 | async-start | bytes 2097152 | tf_op jit(solution)/shard_map/all_to_all | solution.py:29
  143.3 37.3 %all-to-all-start.4 = ((bf16[4,128,1024]{2,1,0:T(8,128)(2,1)}), bf16[4,128,1024]{2,1,0:T(8,128)(2,1)S(1)}, u32[]{:S(2)}, u32[]{:S(2)}) async-start(bf16[4,128,1024]{2,1,0:T(8,128)(2,1)} %broadcast_in_dim.11), calls=%async_computation.4 | async-start | bytes 2097152 | tf_op jit(solution)/shard_map/all_to_all | solution.py:29
  151.4 24.9 %collective-permute-start.14 = (bf16[128,2048]{1,0:T(8,128)(2,1)S(1)}, bf16[128,2048]{1,0:T(8,128)(2,1)S(1)}, u32[]{:S(2)}, u32[]{:S(2)}) collective-permute-start(bf16[128,2048]{1,0:T(8,128)(2,1)S(1)} %get-tuple-element.63), channel_id=1, source_target_pairs={{0,24},{8,0},{16,8},{24,16},{1,25},{9,1},{17,9},{25,17},{2,26},{10... | collective-permute-start | bytes 1572872 | tf_op jit(solution)/shard_map/ppermute | solution.py:25
  154.3 25.4 %collective-permute-start.15 = (bf16[128,2048]{1,0:T(8,128)(2,1)S(1)}, bf16[128,2048]{1,0:T(8,128)(2,1)S(1)}, u32[]{:S(2)}, u32[]{:S(2)}) collective-permute-start(bf16[128,2048]{1,0:T(8,128)(2,1)S(1)} %get-tuple-element.62), channel_id=1, source_target_pairs={{0,8},{8,16},{16,24},{24,0},{1,9},{9,17},{17,25},{25,1},{2,10},{10... | collective-permute-start | bytes 1572872 | tf_op jit(solution)/shard_map/ppermute | solution.py:25
  154.3 26.2 %collective-permute-start.16 = (bf16[128,2048]{1,0:T(8,128)(2,1)S(1)}, bf16[128,2048]{1,0:T(8,128)(2,1)}, u32[]{:S(2)}, u32[]{:S(2)}) collective-permute-start(bf16[128,2048]{1,0:T(8,128)(2,1)S(1)} %get-tuple-element.61), channel_id=1, source_target_pairs={{0,16},{8,24},{16,0},{24,8},{1,17},{9,25},{17,1},{25,9},{2,18},{10... | collective-permute-start | bytes 1572872 | tf_op jit(solution)/shard_map/ppermute | solution.py:25
  186.6 4.9 %collective-permute-start.21 = (bf16[512,512]{1,0:T(8,128)(2,1)S(1)}, bf16[512,512]{1,0:T(8,128)(2,1)S(1)}, u32[]{:S(2)}, u32[]{:S(2)}) collective-permute-start(bf16[512,512]{1,0:T(8,128)(2,1)S(1)} %bitcast.62), channel_id=1, source_target_pairs={{0,32},{32,0},{1,33},{33,1},{2,34},{34,2},{3,35},{35,3},{4,36},{36... | collective-permute-start | bytes 1572872 | tf_op jit(solution)/shard_map/ppermute | solution.py:25
  186.6 34.8 %collective-permute-start.17 = (bf16[128,2048]{1,0:T(8,128)(2,1)}, bf16[128,2048]{1,0:T(8,128)(2,1)}, u32[]{:S(2)}, u32[]{:S(2)}) collective-permute-start(bf16[128,2048]{1,0:T(8,128)(2,1)} %get-tuple-element.60), channel_id=1, source_target_pairs={{0,24},{8,0},{16,8},{24,16},{1,25},{9,1},{17,9},{25,17},{2,26},{10... | collective-permute-start | bytes 1572872 | tf_op jit(solution)/shard_map/ppermute | solution.py:25
  187.7 33.7 %collective-permute-start.18 = (bf16[128,2048]{1,0:T(8,128)(2,1)}, bf16[128,2048]{1,0:T(8,128)(2,1)}, u32[]{:S(2)}, u32[]{:S(2)}) collective-permute-start(bf16[128,2048]{1,0:T(8,128)(2,1)} %get-tuple-element.59), channel_id=1, source_target_pairs={{0,8},{8,16},{16,24},{24,0},{1,9},{9,17},{17,25},{25,1},{2,10},{10... | collective-permute-start | bytes 1572872 | tf_op jit(solution)/shard_map/ppermute | solution.py:25
  188.6 32.8 %collective-permute-start.19 = (bf16[128,2048]{1,0:T(8,128)(2,1)}, bf16[128,2048]{1,0:T(8,128)(2,1)}, u32[]{:S(2)}, u32[]{:S(2)}) collective-permute-start(bf16[128,2048]{1,0:T(8,128)(2,1)} %get-tuple-element.58), channel_id=1, source_target_pairs={{0,16},{8,24},{16,0},{24,8},{1,17},{9,25},{17,1},{25,9},{2,18},{10... | collective-permute-start | bytes 1572872 | tf_op jit(solution)/shard_map/ppermute | solution.py:25
  189.2 7.5 %collective-permute-start.20 = (bf16[512,1024]{1,0:T(8,128)(2,1)S(1)}, bf16[512,1024]{1,0:T(8,128)(2,1)S(1)}, u32[]{:S(2)}, u32[]{:S(2)}) collective-permute-start(bf16[512,1024]{1,0:T(8,128)(2,1)S(1)} %bitcast.50), channel_id=1, source_target_pairs={{0,32},{32,0},{1,33},{33,1},{2,34},{34,2},{3,35},{35,3},{4,36},{36... | collective-permute-start | bytes 3145736 | tf_op jit(solution)/shard_map/ppermute | solution.py:25
  197.6 22.6 %all-to-all-start.5 = ((bf16[8,16,2048]{2,1,0:T(8,128)(2,1)}), bf16[8,16,2048]{2,1,0:T(8,128)(2,1)}, u32[]{:S(2)}, u32[]{:S(2)}) async-start(bf16[8,16,2048]{2,1,0:T(8,128)(2,1)} %bitcast.53), calls=%async_computation.5 | async-start | bytes 1048576 | tf_op jit(solution)/shard_map/all_to_all | solution.py:29
  224.0 21.4 %all-to-all-start.6 = ((bf16[8,16,2048]{2,1,0:T(8,128)(2,1)}), bf16[8,16,2048]{2,1,0:T(8,128)(2,1)S(1)}, u32[]{:S(2)}, u32[]{:S(2)}) async-start(bf16[8,16,2048]{2,1,0:T(8,128)(2,1)} %bitcast.20), calls=%async_computation.6 | async-start | bytes 1048576 | tf_op jit(solution)/shard_map/all_to_all | solution.py:29
  245.5 1.3 collective-permute-start.22
  (10 other events, 74.3 us)
Sparse Core Ops, SparseCore 0:
  30.0 40.1 all-gather.4
  72.5 37.3 all-gather.6

commit v6 on v2

--- a/solution.py
+++ b/solution.py
@@ -40,19 +40,6 @@
     return lax.optimization_barrier((block,) + earlier)[0]
 
 
-def gather_y(own):
-    near = [shift(own, "y", 1), shift(own, "y", 3)]
-    return jnp.concatenate([own, near[0], shift(own, "y", 2), near[1]], axis=0)
-
-
-def gather_y_later(own):
-    pieces = lax.all_gather(own, "y", axis=0, tiled=False)
-    place = lax.axis_index("y") + Y
-    return jnp.concatenate(
-        [lax.dynamic_index_in_dim(pieces, lax.bitwise_and(place - j, Y - 1), axis=0, keepdims=False) for j in range(Y)], axis=0
-    )
-
-
 def swap_core(low, high):
     first = lax.axis_index("core") == 0
     return jnp.where(first, low, high), shift(jnp.where(first, high, low), "core", 1)
@@ -79,42 +66,114 @@
     return jnp.concatenate([jnp.where(first, half, other), jnp.where(first, other, half)], axis=0)
 
 
-def reduce_col(partial):
-    rows = partial.shape[0] // Y
-    pieces = [partial[j * rows : (j + 1) * rows] for j in range(Y)]
-    moved = [shift(pieces[1], "y", 3), shift(pieces[3], "y", 1), shift(pieces[2], "y", 2)]
-    total = pieces[0].astype(F32) + moved[0].astype(F32) + moved[1].astype(F32) + moved[2].astype(F32)
-    return sum_parts(exchange(total.astype(BF), "z"), Z).astype(BF)
+def sum_y(own, moved):
+    total = own.astype(F32)
+    for piece in moved:
+        total = total + piece.astype(F32)
+    return total.astype(BF)
+
+
+def reduce_z(total):
+    return sum_parts(exchange(total, "z"), Z).astype(BF)
+
+
+def order_tokens(own, left, right, far):
+    rows = own.shape[0] // (CORE * X)
+    width = own.shape[1]
+    near = jnp.stack([left, right]).reshape(CORE, X, 2 * rows, width)
+    parts = [own.reshape(CORE, X, rows, width), near, far.reshape(CORE, X, rows, width)]
+    return jnp.concatenate(parts, axis=2).reshape(-1, width)
+
+
+def split_tokens(block):
+    width = block.shape[1]
+    rows = block.shape[0] // (CORE * X * Y)
+    parts = block.reshape(CORE, X, Y * rows, width)
+    own, far = parts[:, :, :rows], parts[:, :, 3 * rows :]
+    left, right = parts[0, :, rows : 3 * rows], parts[1, :, rows : 3 * rows]
+    return [piece.reshape(-1, width) for piece in (own, left, right, far)]
+
+
+def add(left_side, right_side):
+    return (left_side.astype(F32) + right_side.astype(F32)).astype(BF)
+
+
+def move_y_far(pieces):
+    half = pieces[3].shape[0] // 2
+    return shift(pieces[3][:half], "y", 1), shift(pieces[3][half:], "y", 3)
+
+
+def add_y_far(pieces, from_left, from_right):
+    half = pieces[3].shape[0] // 2
+    to_right = jnp.concatenate([add(pieces[2][:half], from_left), pieces[2][half:]], axis=0)
+    to_left = jnp.concatenate([pieces[1][:half], add(pieces[1][half:], from_right)], axis=0)
+    return to_right, to_left
+
+
+def move_y(pieces):
+    return shift(pieces[1], "y", 3), shift(pieces[2], "y", 1), shift(pieces[3], "y", 2)
 
 
 def body(tokens, gate_weight, up_weight, down_weight, out_grad):
     width = gate_weight.shape[1]
     both_weights = jnp.concatenate([gate_weight, up_weight], axis=1)
+
     tokens_z = gather(tokens, "z")
-    all_tokens = gather_y(tokens_z)
-    grads_z = gather(after(out_grad, tokens_z), "z")
-    all_grads = gather_y_later(grads_z)
-    gate_up = reduce_x(reduce_core(product(all_tokens, both_weights).astype(BF)))
+    grads_y = jnp.stack([out_grad, shift(out_grad, "y", 1), shift(out_grad, "y", 3), shift(out_grad, "y", 2)])
+    tokens_z, grads_y, both_weights = lax.optimization_barrier((tokens_z, grads_y, both_weights))
+    grads_all = lax.all_gather(grads_y, "z", axis=0, tiled=False)
+    left, right = shift(tokens_z, "y", 1), shift(tokens_z, "y", 3)
+    half = left.shape[0] // 2
+    far = [shift(left[:half], "y", 1), shift(right[half:], "y", 3)]
+
+    def pair_of(chunk):
+        return reduce_core(product(chunk, both_weights).astype(BF))
+
+    own_part = exchange(pair_of(tokens_z), "x")
+    left, right, own_part = lax.optimization_barrier((left, right, own_part))
+    near_part = exchange(pair_of(jnp.concatenate([left, right], axis=0)), "x")
+    far, near_part = lax.optimization_barrier((far, near_part))
+    far = jnp.concatenate(far, axis=0)
+    far_part = exchange(pair_of(far), "x")
+    gate_up = jnp.concatenate([sum_parts(part, X) for part in (own_part, near_part, far_part)], axis=0)
     gate_value = gate_up[:, :width]
     up_value = gate_up[:, width:]
     sigmoid_gate = jax.nn.sigmoid(gate_value)
     silu_gate = gate_value * sigmoid_gate
     hidden_half = gather((silu_gate * up_value).astype(BF), "x")
+
+    grads_all = after(grads_all, far_part)
+    grads_all = [grads_all[:, j].reshape(tokens_z.shape) for j in range(Y)]
+    all_grads = order_tokens(*grads_all)
+    hidden_partial = reduce_core(product_right_t(all_grads, down_weight).astype(BF))
+    hidden_half, hidden_partial = lax.optimization_barrier((hidden_half, hidden_partial))
+    hidden_grad = exchange(hidden_partial, "x")
     hidden = gather_core(hidden_half)
-    output_partial = product(hidden, down_weight).astype(BF)
-    layer_output = reduce_col(output_partial)
-
-    hidden_partial = reduce_core(product_right_t(all_grads, down_weight).astype(BF))
-    hidden_grad = reduce_x(after(hidden_partial, hidden_half))
+    output_pieces = split_tokens(product(hidden, down_weight).astype(BF))
+    output_far = move_y_far(output_pieces)
+    hidden_grad, *output_far = lax.optimization_barrier((hidden_grad, *output_far))
+    to_right, to_left = lax.optimization_barrier(add_y_far(output_pieces, *output_far))
+    output_near = shift(to_right, "y", 1), shift(to_left, "y", 3)
+    hidden_grad = sum_parts(hidden_grad, X)
     gate_grad = (hidden_grad * up_value * sigmoid_gate * (1.0 + gate_value * (1.0 - sigmoid_gate))).astype(BF)
     up_grad = (hidden_grad * silu_gate).astype(BF)
-    both_share = after(jnp.concatenate([gate_grad, up_grad], axis=1), output_partial)
-    both_grads = gather_core(gather(both_share, "x"))
-    input_grad = reduce_col(product_right_t(both_grads, both_weights).astype(BF))
+    grads_half = gather(jnp.concatenate([gate_grad, up_grad], axis=1), "x")
+    all_tokens = order_tokens(tokens_z, left, right, far)
+    down_weight_grad = product_left_t(hidden, all_grads)
+    grads_half, all_tokens, down_weight_grad, *output_near = lax.optimization_barrier(
+        (grads_half, all_tokens, down_weight_grad, *output_near)
+    )
+    both_grads = gather_core(grads_half)
+
+    input_pieces = lax.optimization_barrier(split_tokens(product_right_t(both_grads, both_weights).astype(BF)))
+    input_moved = move_y(input_pieces)
+    output_total = reduce_z(sum_y(after(output_pieces[0], *input_pieces), output_near))
     gate_weight_grad = product_left_t(all_tokens, both_grads[:, :width])
     up_weight_grad = product_left_t(all_tokens, both_grads[:, width:])
-    down_weight_grad = product_left_t(hidden, all_grads)
-    return (layer_output, input_grad, gate_weight_grad, up_weight_grad, down_weight_grad)
+    weight_grads = (gate_weight_grad, up_weight_grad, down_weight_grad)
+    input_moved, weight_grads, output_total = lax.optimization_barrier((input_moved, weight_grads, output_total))
+    input_total = reduce_z(sum_y(input_pieces[0], input_moved))
+    return (output_total, input_total) + weight_grads
 
 
 def solution(mesh):

time: 247 us -> 230 us (0.931)
  waiting for transfers between devices: 97.6 us -> 58.1 us
  starting transfers between devices: 41.2 us -> 60.1 us
  other arithmetic: 11.3 us -> 29 us
  blocking collectives: 43.6 us -> 31.9 us
  matrix products: 25.9 us -> 17.6 us
  local copies, waits for them, and re-layouts: 10.1 us -> 17.8 us
    ppermute x13 -> x20, waiting for transfers between devices: 63.2 us -> 35.5 us  [shift(): lax.ppermute(block, axis, [(i, (i + step) % size) for i in range(size)])]
    ppermute x13 -> x20, starting transfers between devices: 9.43 us -> 21.9 us  [shift(): lax.ppermute(block, axis, [(i, (i + step) % size) for i in range(size)])]
    all_to_all x6 -> x7, waiting for transfers between devices: 34.3 us -> 22.6 us  [exchange(): return lax.all_to_all(blocks, axis, split_axis=0, concat_axis=0, tiled=True)]
    all_to_all x2, blocking collectives: 43.6 us -> 31.9 us  [exchange(): return lax.all_to_all(blocks, axis, split_axis=0, concat_axis=0, tiled=True)]
    slice x2 -> x8, local copies, waits for them, and re-layouts: 0.24 us -> 8.7 us  [the longest x2 2.16 us: split_tokens(): own, far = (parts[:, :, :rows], parts[:, :, 3 * rows:])]
    all_to_all x6 -> x7, starting transfers between devices: 31.8 us -> 38.1 us  [exchange(): return lax.all_to_all(blocks, axis, split_axis=0, concat_axis=0, tiled=True)]
    concatenate x1 -> x7, other arithmetic: 0.02 us -> 5.79 us  [the longest x2 2.91 us: order_tokens(): return jnp.concatenate(parts, axis=2).reshape(-1, width)]
    reduce_sum x4 -> x6, other arithmetic: 1.67 us -> 5.8 us  [sum_parts(): jnp.sum(parts.reshape((count, rows) + parts.shape[1:]).astype(F32), axis=0)]
  transfers between devices with their start and end apart: 20 -> 28, of which waited for: 14 -> 17; matrix products, arithmetic and copies ran while one was open for 17% -> 19% of each run, Pallas kernels for 0% -> 0%
where the time goes in v6:
time: 230 us; the launch traced here: 229 us
  starting transfers between devices  60.1 us (26%)
  waiting for transfers between devices  58.1 us (25%)
  blocking collectives  31.9 us (14%)
  other arithmetic  29 us (13%)
  local copies, waits for them, and re-layouts  17.8 us (8%)
  matrix products  17.6 us (8%)
  between operations  14.5 us (6%)
    all_to_all x7, starting transfers between devices, exchange(): return lax.all_to_all(blocks, axis, split_axis=0, concat_axis=0, tiled=True)  38.1 us
    ppermute x20, waiting for transfers between devices, shift(): lax.ppermute(block, axis, [(i, (i + step) % size) for i in range(size)])  35.5 us
    all_to_all x2, blocking collectives, exchange(): return lax.all_to_all(blocks, axis, split_axis=0, concat_axis=0, tiled=True)  31.9 us
    all_to_all x7, waiting for transfers between devices, exchange(): return lax.all_to_all(blocks, axis, split_axis=0, concat_axis=0, tiled=True)  22.6 us
    ppermute x20, starting transfers between devices, shift(): lax.ppermute(block, axis, [(i, (i + step) % size) for i in range(size)])  21.9 us
    dot_general x3, matrix products, product_left_t(): lax.dot_general(left_side, right_side, (((0,), (0,)), ((), ())), preferre...  8.99 us
    reduce_sum x6, other arithmetic, sum_parts(): jnp.sum(parts.reshape((count, rows) + parts.shape[1:]).astype(F32), axis=0)  5.8 us
    convert_element_type x4, other arithmetic, reduce_core(): return (kept.astype(F32) + received.astype(F32)).astype(BF)  5.43 us
  transfers between devices with their start and end apart: 28, of which 17 were waited for; matrix products, arithmetic and copies ran while one was open for 19% of the time, Pallas kernels for 0%

profile of v6, /device:TPU:2, one launch (start us, length us, event | category | flops | bytes accessed | tf_op | source)
XLA Modules:
  0.0 229.0 jit_solution(5176653704103749058)
XLA Ops:
  9.0 8.5 %all-to-all-start = ((bf16[8,32,1024]{2,1,0:T(8,128)(2,1)}), bf16[8,32,1024]{2,1,0:T(8,128)(2,1)}, u32[]{:S(2)}, u32[]{:S(2)}) async-start(bf16[8,32,1024]{2,1,0:T(8,128)(2,1)} %broadcast_in_dim.6), calls=%async_computation | async-start | bytes 1048576 | tf_op jit(solution)/shard_map/all_to_all | solution.py:29
  19.1 2.9 %collective-permute-start.2 = (bf16[32,1024]{1,0:T(8,128)(2,1)}, bf16[32,1024]{1,0:T(8,128)(2,1)S(1)}, u32[]{:S(2)}, u32[]{:S(2)}) collective-permute-start(bf16[32,1024]{1,0:T(8,128)(2,1)} %param.9), channel_id=1, source_target_pairs={{0,16},{8,24},{16,0},{24,8},{1,17},{9,25},{17,1},{25,9},{2,18},{10... | collective-permute-start | bytes 196616 | tf_op jit(solution)/shard_map/ppermute | solution.py:25
  27.2 7.8 %all-to-all-done = bf16[8,32,1024]{2,1,0:T(8,128)(2,1)} async-done(((bf16[8,32,1024]{2,1,0:T(8,128)(2,1)}), bf16[8,32,1024]{2,1,0:T(8,128)(2,1)}, u32[]{:S(2)}, u32[]{:S(2)}) %all-to-all-start) | async-done | bytes 524320 | tf_op jit(solution)/shard_map/all_to_all | solution.py:29
  38.4 3.1 %collective-permute-start.4 = (bf16[256,1024]{1,0:T(8,128)(2,1)}, bf16[256,1024]{1,0:T(8,128)(2,1)S(1)}, u32[]{:S(2)}, u32[]{:S(2)}) collective-permute-start(bf16[256,1024]{1,0:T(8,128)(2,1)} %bitcast), channel_id=1, source_target_pairs={{0,24},{8,0},{16,8},{24,16},{1,25},{9,1},{17,9},{25,17},{2,26},{10... | collective-permute-start | bytes 1572872 | tf_op jit(solution)/shard_map/ppermute | solution.py:25
  42.6 10.2 %all_to_all.90 = bf16[4,32,1024]{2,1,0:T(8,128)(2,1)S(1)} all-to-all(bf16[4,32,1024]{2,1,0:T(8,128)(2,1)S(1)} %bitcast.84), channel_id=1, replica_groups=mesh['x'=4,'core'=2,'y'=4,'z'=8] {'x'}, dimensions={0} | all-to-all | bytes 524288 | tf_op jit(solution)/shard_map/all_to_all | solution.py:29
  53.6 3.3 %collective-permute-done.3 = bf16[256,1024]{1,0:T(8,128)(2,1)S(1)} collective-permute-done((bf16[256,1024]{1,0:T(8,128)(2,1)}, bf16[256,1024]{1,0:T(8,128)(2,1)S(1)}, u32[]{:S(2)}, u32[]{:S(2)}) %collective-permute-start.3) | collective-permute-done | bytes 524320 | tf_op jit(solution)/shard_map/ppermute | solution.py:25
  58.4 1.9 collective-permute-done.8
  61.3 4.8 %all-to-all-start.2 = ((bf16[4,64,1024]{2,1,0:T(8,128)(2,1)}), bf16[4,64,1024]{2,1,0:T(8,128)(2,1)}, u32[]{:S(2)}, u32[]{:S(2)}) async-start(bf16[4,64,1024]{2,1,0:T(8,128)(2,1)} %bitcast.8), calls=%async_computation.2 | async-start | bytes 1048576 | tf_op jit(solution)/shard_map/all_to_all | solution.py:29
  70.3 4.9 %collective-permute-done.7 = bf16[128,1024]{1,0:T(8,128)(2,1)} collective-permute-done((bf16[128,1024]{1,0:T(8,128)(2,1)S(1)}, bf16[128,1024]{1,0:T(8,128)(2,1)}, u32[]{:S(2)}, u32[]{:S(2)}) %collective-permute-start.7) | collective-permute-done | bytes 262176 | tf_op jit(solution)/shard_map/ppermute | solution.py:25
  75.2 2.3 collective-permute-done.6
  82.6 4.8 %all-to-all-start.3 = ((bf16[4,32,1024]{2,1,0:T(8,128)(2,1)}), bf16[4,32,1024]{2,1,0:T(8,128)(2,1)}, u32[]{:S(2)}, u32[]{:S(2)}) async-start(bf16[4,32,1024]{2,1,0:T(8,128)(2,1)} %bitcast.11), calls=%async_computation.3 | async-start | bytes 524288 | tf_op jit(solution)/shard_map/all_to_all | solution.py:29
  95.9 5.6 %all-to-all-start.4 = ((bf16[4,128,512]{2,1,0:T(8,128)(2,1)}), bf16[4,128,512]{2,1,0:T(8,128)(2,1)}, u32[]{:S(2)}, u32[]{:S(2)}) async-start(bf16[4,128,512]{2,1,0:T(8,128)(2,1)} %broadcast_in_dim.7), calls=%async_computation.4 | async-start | bytes 1048576 | tf_op jit(solution)/shard_map/all_to_all | solution.py:29
  101.4 2.4 %add_convert_fusion.2 = bf16[512,512]{1,0:T(8,128)(2,1)} fusion(bf16[512,512]{1,0:T(8,128)(2,1)} %collective-permute-done.10, pred[]{:T(512)S(6)} %eq.2, bf16[1024,512]{1,0:T(8,128)(2,1)} %copy-done.2), kind=kLoop, calls=%fused_computation.27 | loop fusion | flops 1310720 | bytes 2097153 | tf_op jit(solution)/shard_map/convert_element_type | solution.py:56
  103.8 5.1 %all-to-all-done.4 = bf16[4,128,512]{2,1,0:T(8,128)(2,1)} async-done(((bf16[4,128,512]{2,1,0:T(8,128)(2,1)}), bf16[4,128,512]{2,1,0:T(8,128)(2,1)}, u32[]{:S(2)}, u32[]{:S(2)}) %all-to-all-start.4) | async-done | bytes 524320 | tf_op jit(solution)/shard_map/all_to_all | solution.py:29
  108.9 5.6 %all-to-all-start.5 = ((bf16[4,128,512]{2,1,0:T(8,128)(2,1)}), bf16[4,128,512]{2,1,0:T(8,128)(2,1)}, u32[]{:S(2)}, u32[]{:S(2)}) async-start(bf16[4,128,512]{2,1,0:T(8,128)(2,1)} %bitcast.64), calls=%async_computation.5 | async-start | bytes 1048576 | tf_op jit(solution)/shard_map/all_to_all | solution.py:29
  118.4 2.7 %collective-permute-start.13 = (bf16[128,1024]{1,0:T(8,128)(2,1)}, bf16[128,1024]{1,0:T(8,128)(2,1)}, u32[]{:S(2)}, u32[]{:S(2)}) collective-permute-start(bf16[128,1024]{1,0:T(8,128)(2,1)} %bitcast.23), channel_id=1, source_target_pairs={{0,24},{8,0},{16,8},{24,16},{1,25},{9,1},{17,9},{25,17},{2,26},{10... | collective-permute-start | bytes 786440 | tf_op jit(solution)/shard_map/ppermute | solution.py:25
  123.5 4.4 %collective-permute-done.12 = bf16[128,1024]{1,0:T(8,128)(2,1)} collective-permute-done((bf16[128,1024]{1,0:T(8,128)(2,1)}, bf16[128,1024]{1,0:T(8,128)(2,1)}, u32[]{:S(2)}, u32[]{:S(2)}) %collective-permute-start.12) | collective-permute-done | bytes 262176 | tf_op jit(solution)/shard_map/ppermute | solution.py:25
  131.4 4.8 %all-to-all-start.6 = ((bf16[4,128,1024]{2,1,0:T(8,128)(2,1)}), bf16[4,128,1024]{2,1,0:T(8,128)(2,1)}, u32[]{:S(2)}, u32[]{:S(2)}) async-start(bf16[4,128,1024]{2,1,0:T(8,128)(2,1)} %broadcast_in_dim.8), calls=%async_computation.6 | async-start | bytes 2097152 | tf_op jit(solution)/shard_map/all_to_all | solution.py:29
  138.8 3.2 %collective-permute-start.15 = (bf16[256,1024]{1,0:T(8,128)(2,1)S(1)}, bf16[256,1024]{1,0:T(8,128)(2,1)}, u32[]{:S(2)}, u32[]{:S(2)}) collective-permute-start(bf16[256,1024]{1,0:T(8,128)(2,1)S(1)} %pad_maximum_fusion.12), channel_id=1, source_target_pairs={{0,24},{8,0},{16,8},{24,16},{1,25},{9,1},{17,9},{25,17},{2,26},{10... | collective-permute-start | bytes 1572872 | tf_op jit(solution)/shard_map/ppermute | solution.py:25
  142.0 2.7 %pad_maximum_fusion.4 = bf16[2,4,128,1024]{3,2,1,0:T(8,128)(2,1)} fusion(bf16[2,4,32,1024]{3,2,1,0:T(8,128)(2,1)S(1)} %bitcast.83, bf16[1,4,64,1024]{3,2,1,0:T(8,128)(2,1)S(1)} %bitcast.81, bf16[1,4,64,1024]{3,2,1,0:T(8,128)(2,1)S(1)} %bitcast.82, bf16[2,4,32,1024]{3,2,1,0:T(8,128)(2,1)} %bitcast.26), kind=kLoop, calls=%fused_computation.8 | loop fusion | flops 8388608 | bytes 4194304 | tf_op jit(solution)/shard_map/concatenate | solution.py:85
  144.8 2.6 %fusion.11 = f32[512,1024]{1,0:T(8,128)} fusion(bf16[1024,1024]{1,0:T(8,128)(2,1)S(1)} %bitcast.63, bf16[512,512]{1,0:T(8,128)(2,1)S(1)} %copy-done.6, bf16[512,512]{1,0:T(8,128)(2,1)S(1)} %copy-done.4), kind=kOutput, calls=%fused_computation.31 | convolution fusion | flops 1075838976 | bytes 5242880 | tf_op jit(solution)/shard_map/dot_general | solution.py:20
  147.4 5.6 %collective-permute-done.14 = bf16[256,1024]{1,0:T(8,128)(2,1)S(1)} collective-permute-done((bf16[256,1024]{1,0:T(8,128)(2,1)S(1)}, bf16[256,1024]{1,0:T(8,128)(2,1)S(1)}, u32[]{:S(2)}, u32[]{:S(2)}) %collective-permute-start.14) | collective-permute-done | bytes 524320 | tf_op jit(solution)/shard_map/ppermute | solution.py:25
  158.1 2.4 %fusion.1 = bf16[1024,1024]{1,0:T(8,128)(2,1)S(1)} fusion(bf16[1024,1024]{1,0:T(8,128)(2,1)S(1)} %copy-done.8, bf16[512,1024]{1,0:T(8,128)(2,1)S(1)} %get-tuple-element.76, bf16[512,1024]{1,0:T(8,128)(2,1)S(1)} %get-tuple-element.75), kind=kOutput, calls=%fused_computation.9 | convolution fusion | flops 2152726528 | bytes 6291456 | tf_op jit(solution)/shard_map/dot_general | solution.py:16
  162.7 2.3 %add_convert_fusion.1 = bf16[256,1024]{1,0:T(8,128)(2,1)} fusion(bf16[256,1024]{1,0:T(8,128)(2,1)} %collective-permute-done.15, bf16[256,1024]{1,0:T(8,128)(2,1)S(1)} %copy-done.23, bf16[256,1024]{1,0:T(8,128)(2,1)S(1)} %bitcast.75), kind=kLoop, calls=%fused_computation.26 | loop fusion | flops 1572864 | bytes 2097152 | tf_op jit(solution)/shard_map/convert_element_type | solution.py:73
  165.0 4.1 %all-to-all-start.7 = ((bf16[8,32,1024]{2,1,0:T(8,128)(2,1)}), bf16[8,32,1024]{2,1,0:T(8,128)(2,1)}, u32[]{:S(2)}, u32[]{:S(2)}) async-start(bf16[8,32,1024]{2,1,0:T(8,128)(2,1)} %bitcast.76), calls=%async_computation.7 | async-start | bytes 1048576 | tf_op jit(solution)/shard_map/all_to_all | solution.py:29
  169.1 2.3 %collective-permute-start.17 = (bf16[256,1024]{1,0:T(8,128)(2,1)}, bf16[256,1024]{1,0:T(8,128)(2,1)}, u32[]{:S(2)}, u32[]{:S(2)}) collective-permute-start(bf16[256,1024]{1,0:T(8,128)(2,1)} %bitcast.89), channel_id=1, source_target_pairs={{0,24},{8,0},{16,8},{24,16},{1,25},{9,1},{17,9},{25,17},{2,26},{10... | collective-permute-start | bytes 1572872 | tf_op jit(solution)/shard_map/ppermute | solution.py:25
  173.1 3.8 %fusion.3 = f32[1024,512]{1,0:T(8,128)} fusion(bf16[1024,1024]{1,0:T(8,128)(2,1)S(1)} %bitcast.70, bf16[512,1024]{1,0:T(8,128)(2,1)} %copy-done.18, bf16[512,1024]{1,0:T(8,128)(2,1)} %copy-done.20), kind=kOutput, calls=%fused_computation.16 | convolution fusion | flops 1075838976 | bytes 6291456 | tf_op jit(solution)/shard_map/dot_general | solution.py:20
  176.9 2.6 %fusion.6 = f32[1024,512]{1,0:T(8,128)} fusion(bf16[1024,1024]{1,0:T(8,128)(2,1)S(1)} %bitcast.71, bf16[512,1024]{1,0:T(8,128)(2,1)S(1)} %copy-done.19, bf16[512,1024]{1,0:T(8,128)(2,1)S(1)} %copy-done.21), kind=kOutput, calls=%fused_computation.18 | convolution fusion | flops 1075838976 | bytes 6291456 | tf_op jit(solution)/shard_map/dot_general | solution.py:20
  179.5 7.7 %all-to-all-done.7 = bf16[8,32,1024]{2,1,0:T(8,128)(2,1)} async-done(((bf16[8,32,1024]{2,1,0:T(8,128)(2,1)}), bf16[8,32,1024]{2,1,0:T(8,128)(2,1)}, u32[]{:S(2)}, u32[]{:S(2)}) %all-to-all-start.7) | async-done | bytes 524320 | tf_op jit(solution)/shard_map/all_to_all | solution.py:29
  189.0 5.5 %collective-permute-done.17 = bf16[256,1024]{1,0:T(8,128)(2,1)} collective-permute-done((bf16[256,1024]{1,0:T(8,128)(2,1)}, bf16[256,1024]{1,0:T(8,128)(2,1)}, u32[]{:S(2)}, u32[]{:S(2)}) %collective-permute-start.17) | collective-permute-done | bytes 524320 | tf_op jit(solution)/shard_map/ppermute | solution.py:25
  194.5 3.4 %collective-permute-done.18 = bf16[256,1024]{1,0:T(8,128)(2,1)} collective-permute-done((bf16[256,1024]{1,0:T(8,128)(2,1)}, bf16[256,1024]{1,0:T(8,128)(2,1)}, u32[]{:S(2)}, u32[]{:S(2)}) %collective-permute-start.18) | collective-permute-done | bytes 524320 | tf_op jit(solution)/shard_map/ppermute | solution.py:25
  199.8 21.7 %all_to_all.91 = bf16[8,32,1024]{2,1,0:T(8,128)(2,1)S(1)} all-to-all(bf16[8,32,1024]{2,1,0:T(8,128)(2,1)S(1)} %bitcast.65), channel_id=1, replica_groups=mesh['x'=4,'core'=2,'y'=4,'z'=8] {'z'}, dimensions={0} | all-to-all | bytes 1048576 | tf_op jit(solution)/shard_map/all_to_all | solution.py:29
  (128 shorter events, 59.6 us)
Async XLA Ops:
  7.2 82.2 %copy-start = (bf16[512,1024]{1,0:T(8,128)(2,1)S(1)}, bf16[512,1024]{1,0:T(8,128)(2,1)}, u32[]{:S(2)}) copy-start(bf16[512,1024]{1,0:T(8,128)(2,1)} %param.8) | copy-start | bytes 3145732
  9.0 26.1 %all-to-all-start = ((bf16[8,32,1024]{2,1,0:T(8,128)(2,1)}), bf16[8,32,1024]{2,1,0:T(8,128)(2,1)}, u32[]{:S(2)}, u32[]{:S(2)}) async-start(bf16[8,32,1024]{2,1,0:T(8,128)(2,1)} %broadcast_in_dim.6), calls=%async_computation | async-start | bytes 1048576 | tf_op jit(solution)/shard_map/all_to_all | solution.py:29
  17.4 9.1 %copy-start.24 = (bf16[32,1024]{1,0:T(8,128)(2,1)S(1)}, bf16[32,1024]{1,0:T(8,128)(2,1)}, u32[]{:S(2)}) copy-start(bf16[32,1024]{1,0:T(8,128)(2,1)} %param.9) | copy-start | bytes 196612
  17.4 70.0 %all-gather.3.cloned.1.call-start = ((), (), s32[]{:S(2)}) async-start(), calls=%async_computation.9 | async-start | bytes 2359296 | tf_op jit(solution)/shard_map/all_gather | solution.py:124
  17.5 7.7 %collective-permute-start = (bf16[32,1024]{1,0:T(8,128)(2,1)}, bf16[32,1024]{1,0:T(8,128)(2,1)S(1)}, u32[]{:S(2)}, u32[]{:S(2)}) collective-permute-start(bf16[32,1024]{1,0:T(8,128)(2,1)} %param.9), channel_id=1, source_target_pairs={{0,8},{8,16},{16,24},{24,0},{1,9},{9,17},{17,25},{25,1},{2,10},{10... | collective-permute-start | bytes 196616 | tf_op jit(solution)/shard_map/ppermute | solution.py:25
  19.1 6.1 %collective-permute-start.2 = (bf16[32,1024]{1,0:T(8,128)(2,1)}, bf16[32,1024]{1,0:T(8,128)(2,1)S(1)}, u32[]{:S(2)}, u32[]{:S(2)}) collective-permute-start(bf16[32,1024]{1,0:T(8,128)(2,1)} %param.9), channel_id=1, source_target_pairs={{0,16},{8,24},{16,0},{24,8},{1,17},{9,25},{17,1},{25,9},{2,18},{10... | collective-permute-start | bytes 196616 | tf_op jit(solution)/shard_map/ppermute | solution.py:25
  22.0 4.5 %collective-permute-start.1 = (bf16[32,1024]{1,0:T(8,128)(2,1)}, bf16[32,1024]{1,0:T(8,128)(2,1)S(1)}, u32[]{:S(2)}, u32[]{:S(2)}) collective-permute-start(bf16[32,1024]{1,0:T(8,128)(2,1)} %param.9), channel_id=1, source_target_pairs={{0,24},{8,0},{16,8},{24,16},{1,25},{9,1},{17,9},{25,17},{2,26},{10... | collective-permute-start | bytes 196616 | tf_op jit(solution)/shard_map/ppermute | solution.py:25
  25.2 54.2 %copy-start.7 = (bf16[1024,1024]{1,0:T(8,128)(2,1)}, bf16[1024,1024]{1,0:T(8,128)(2,1)S(1)}, u32[]{:S(2)}) copy-start(bf16[1024,1024]{1,0:T(8,128)(2,1)S(1)} %pad_maximum_fusion.2) | copy-start | bytes 6291460
  38.3 3.1 %collective-permute-start.5 = (bf16[128,1024]{1,0:T(8,128)(2,1)}, bf16[128,1024]{1,0:T(8,128)(2,1)S(1)}, u32[]{:S(2)}, u32[]{:S(2)}) collective-permute-start(bf16[128,1024]{1,0:T(8,128)(2,1)} %broadcast_select_fusion.7), channel_id=1, source_target_pairs={{0,32},{32,0},{1,33},{33,1},{2,34},{34,2},{3,35},{35,3},{4,36},{36... | collective-permute-start | bytes 786440 | tf_op jit(solution)/shard_map/ppermute | solution.py:25
  38.4 15.2 %collective-permute-start.4 = (bf16[256,1024]{1,0:T(8,128)(2,1)}, bf16[256,1024]{1,0:T(8,128)(2,1)S(1)}, u32[]{:S(2)}, u32[]{:S(2)}) collective-permute-start(bf16[256,1024]{1,0:T(8,128)(2,1)} %bitcast), channel_id=1, source_target_pairs={{0,24},{8,0},{16,8},{24,16},{1,25},{9,1},{17,9},{25,17},{2,26},{10... | collective-permute-start | bytes 1572872 | tf_op jit(solution)/shard_map/ppermute | solution.py:25
  41.4 15.5 %collective-permute-start.3 = (bf16[256,1024]{1,0:T(8,128)(2,1)}, bf16[256,1024]{1,0:T(8,128)(2,1)S(1)}, u32[]{:S(2)}, u32[]{:S(2)}) collective-permute-start(bf16[256,1024]{1,0:T(8,128)(2,1)} %bitcast), channel_id=1, source_target_pairs={{0,8},{8,16},{16,24},{24,0},{1,9},{9,17},{17,25},{25,1},{2,10},{10... | collective-permute-start | bytes 1572872 | tf_op jit(solution)/shard_map/ppermute | solution.py:25
  58.3 2.0 collective-permute-start.8
  61.3 16.1 %all-to-all-start.2 = ((bf16[4,64,1024]{2,1,0:T(8,128)(2,1)}), bf16[4,64,1024]{2,1,0:T(8,128)(2,1)}, u32[]{:S(2)}, u32[]{:S(2)}) async-start(bf16[4,64,1024]{2,1,0:T(8,128)(2,1)} %bitcast.8), calls=%async_computation.2 | async-start | bytes 1048576 | tf_op jit(solution)/shard_map/all_to_all | solution.py:29
  67.1 8.1 %collective-permute-start.7 = (bf16[128,1024]{1,0:T(8,128)(2,1)S(1)}, bf16[128,1024]{1,0:T(8,128)(2,1)}, u32[]{:S(2)}, u32[]{:S(2)}) collective-permute-start(bf16[128,1024]{1,0:T(8,128)(2,1)S(1)} %slice.146), channel_id=1, source_target_pairs={{0,24},{8,0},{16,8},{24,16},{1,25},{9,1},{17,9},{25,17},{2,26},{10... | collective-permute-start | bytes 786440 | tf_op jit(solution)/shard_map/ppermute | solution.py:25
  68.5 9.0 %collective-permute-start.6 = (bf16[128,1024]{1,0:T(8,128)(2,1)S(1)}, bf16[128,1024]{1,0:T(8,128)(2,1)}, u32[]{:S(2)}, u32[]{:S(2)}) collective-permute-start(bf16[128,1024]{1,0:T(8,128)(2,1)S(1)} %slice.145), channel_id=1, source_target_pairs={{0,8},{8,16},{16,24},{24,0},{1,9},{9,17},{17,25},{25,1},{2,10},{10... | collective-permute-start | bytes 786440 | tf_op jit(solution)/shard_map/ppermute | solution.py:25
  80.2 1.6 collective-permute-start.9
  82.6 10.5 %all-to-all-start.3 = ((bf16[4,32,1024]{2,1,0:T(8,128)(2,1)}), bf16[4,32,1024]{2,1,0:T(8,128)(2,1)}, u32[]{:S(2)}, u32[]{:S(2)}) async-start(bf16[4,32,1024]{2,1,0:T(8,128)(2,1)} %bitcast.11), calls=%async_computation.3 | async-start | bytes 524288 | tf_op jit(solution)/shard_map/all_to_all | solution.py:29
  92.5 8.9 %collective-permute-start.10 = (bf16[512,512]{1,0:T(8,128)(2,1)}, bf16[512,512]{1,0:T(8,128)(2,1)}, u32[]{:S(2)}, u32[]{:S(2)}) collective-permute-start(bf16[512,512]{1,0:T(8,128)(2,1)} %broadcast_select_fusion.4), channel_id=1, source_target_pairs={{0,32},{32,0},{1,33},{33,1},{2,34},{34,2},{3,35},{35,3},{4,36},{36... | collective-permute-start | bytes 1572872 | tf_op jit(solution)/shard_map/ppermute | solution.py:25
  95.9 13.0 %all-to-all-start.4 = ((bf16[4,128,512]{2,1,0:T(8,128)(2,1)}), bf16[4,128,512]{2,1,0:T(8,128)(2,1)}, u32[]{:S(2)}, u32[]{:S(2)}) async-start(bf16[4,128,512]{2,1,0:T(8,128)(2,1)} %broadcast_in_dim.7), calls=%async_computation.4 | async-start | bytes 1048576 | tf_op jit(solution)/shard_map/all_to_all | solution.py:29
  108.9 5.6 %collective-permute-start.11 = (bf16[512,512]{1,0:T(8,128)(2,1)}, bf16[512,512]{1,0:T(8,128)(2,1)}, u32[]{:S(2)}, u32[]{:S(2)}) collective-permute-start(bf16[512,512]{1,0:T(8,128)(2,1)} %bitcast.12), channel_id=1, source_target_pairs={{0,32},{32,0},{1,33},{33,1},{2,34},{34,2},{3,35},{35,3},{4,36},{36... | collective-permute-start | bytes 1572872 | tf_op jit(solution)/shard_map/ppermute | solution.py:25
  108.9 14.6 %all-to-all-start.5 = ((bf16[4,128,512]{2,1,0:T(8,128)(2,1)}), bf16[4,128,512]{2,1,0:T(8,128)(2,1)}, u32[]{:S(2)}, u32[]{:S(2)}) async-start(bf16[4,128,512]{2,1,0:T(8,128)(2,1)} %bitcast.64), calls=%async_computation.5 | async-start | bytes 1048576 | tf_op jit(solution)/shard_map/all_to_all | solution.py:29
  117.9 10.0 %collective-permute-start.12 = (bf16[128,1024]{1,0:T(8,128)(2,1)}, bf16[128,1024]{1,0:T(8,128)(2,1)}, u32[]{:S(2)}, u32[]{:S(2)}) collective-permute-start(bf16[128,1024]{1,0:T(8,128)(2,1)} %bitcast.22), channel_id=1, source_target_pairs={{0,8},{8,16},{16,24},{24,0},{1,9},{9,17},{17,25},{25,1},{2,10},{10... | collective-permute-start | bytes 786440 | tf_op jit(solution)/shard_map/ppermute | solution.py:25
  118.4 9.4 %collective-permute-start.13 = (bf16[128,1024]{1,0:T(8,128)(2,1)}, bf16[128,1024]{1,0:T(8,128)(2,1)}, u32[]{:S(2)}, u32[]{:S(2)}) collective-permute-start(bf16[128,1024]{1,0:T(8,128)(2,1)} %bitcast.23), channel_id=1, source_target_pairs={{0,24},{8,0},{16,8},{24,16},{1,25},{9,1},{17,9},{25,17},{2,26},{10... | collective-permute-start | bytes 786440 | tf_op jit(solution)/shard_map/ppermute | solution.py:25
  131.4 22.5 %all-to-all-start.6 = ((bf16[4,128,1024]{2,1,0:T(8,128)(2,1)}), bf16[4,128,1024]{2,1,0:T(8,128)(2,1)}, u32[]{:S(2)}, u32[]{:S(2)}) async-start(bf16[4,128,1024]{2,1,0:T(8,128)(2,1)} %broadcast_in_dim.8), calls=%async_computation.6 | async-start | bytes 2097152 | tf_op jit(solution)/shard_map/all_to_all | solution.py:29
  138.7 14.3 %collective-permute-start.14 = (bf16[256,1024]{1,0:T(8,128)(2,1)S(1)}, bf16[256,1024]{1,0:T(8,128)(2,1)S(1)}, u32[]{:S(2)}, u32[]{:S(2)}) collective-permute-start(bf16[256,1024]{1,0:T(8,128)(2,1)S(1)} %pad_maximum_fusion.11), channel_id=1, source_target_pairs={{0,8},{8,16},{16,24},{24,0},{1,9},{9,17},{17,25},{25,1},{2,10},{10... | collective-permute-start | bytes 1572872 | tf_op jit(solution)/shard_map/ppermute | solution.py:25
  138.8 15.0 %collective-permute-start.15 = (bf16[256,1024]{1,0:T(8,128)(2,1)S(1)}, bf16[256,1024]{1,0:T(8,128)(2,1)}, u32[]{:S(2)}, u32[]{:S(2)}) collective-permute-start(bf16[256,1024]{1,0:T(8,128)(2,1)S(1)} %pad_maximum_fusion.12), channel_id=1, source_target_pairs={{0,24},{8,0},{16,8},{24,16},{1,25},{9,1},{17,9},{25,17},{2,26},{10... | collective-permute-start | bytes 1572872 | tf_op jit(solution)/shard_map/ppermute | solution.py:25
  153.8 2.9 %collective-permute-start.16 = (bf16[512,1024]{1,0:T(8,128)(2,1)}, bf16[512,1024]{1,0:T(8,128)(2,1)S(1)}, u32[]{:S(2)}, u32[]{:S(2)}) collective-permute-start(bf16[512,1024]{1,0:T(8,128)(2,1)} %bitcast.25), channel_id=1, source_target_pairs={{0,32},{32,0},{1,33},{33,1},{2,34},{34,2},{3,35},{35,3},{4,36},{36... | collective-permute-start | bytes 3145736 | tf_op jit(solution)/shard_map/ppermute | solution.py:25
  162.7 10.5 %copy-start.10 = (bf16[2,4,128,1024]{3,2,1,0:T(8,128)(2,1)S(1)}, bf16[2,4,128,1024]{3,2,1,0:T(8,128)(2,1)}, u32[]{:S(2)}) copy-start(bf16[2,4,128,1024]{3,2,1,0:T(8,128)(2,1)} %pad_maximum_fusion.4) | copy-start | bytes 6291460
  165.0 22.3 %all-to-all-start.7 = ((bf16[8,32,1024]{2,1,0:T(8,128)(2,1)}), bf16[8,32,1024]{2,1,0:T(8,128)(2,1)}, u32[]{:S(2)}, u32[]{:S(2)}) async-start(bf16[8,32,1024]{2,1,0:T(8,128)(2,1)} %bitcast.76), calls=%async_computation.7 | async-start | bytes 1048576 | tf_op jit(solution)/shard_map/all_to_all | solution.py:29
  169.1 25.4 %collective-permute-start.17 = (bf16[256,1024]{1,0:T(8,128)(2,1)}, bf16[256,1024]{1,0:T(8,128)(2,1)}, u32[]{:S(2)}, u32[]{:S(2)}) collective-permute-start(bf16[256,1024]{1,0:T(8,128)(2,1)} %bitcast.89), channel_id=1, source_target_pairs={{0,24},{8,0},{16,8},{24,16},{1,25},{9,1},{17,9},{25,17},{2,26},{10... | collective-permute-start | bytes 1572872 | tf_op jit(solution)/shard_map/ppermute | solution.py:25
  171.5 26.4 %collective-permute-start.18 = (bf16[256,1024]{1,0:T(8,128)(2,1)}, bf16[256,1024]{1,0:T(8,128)(2,1)}, u32[]{:S(2)}, u32[]{:S(2)}) collective-permute-start(bf16[256,1024]{1,0:T(8,128)(2,1)} %bitcast.88), channel_id=1, source_target_pairs={{0,8},{8,16},{16,24},{24,0},{1,9},{9,17},{17,25},{25,1},{2,10},{10... | collective-permute-start | bytes 1572872 | tf_op jit(solution)/shard_map/ppermute | solution.py:25
  171.5 26.4 %collective-permute-start.19 = (bf16[256,1024]{1,0:T(8,128)(2,1)}, bf16[256,1024]{1,0:T(8,128)(2,1)}, u32[]{:S(2)}, u32[]{:S(2)}) collective-permute-start(bf16[256,1024]{1,0:T(8,128)(2,1)} %bitcast.87), channel_id=1, source_target_pairs={{0,16},{8,24},{16,0},{24,8},{1,17},{9,25},{17,1},{25,9},{2,18},{10... | collective-permute-start | bytes 1572872 | tf_op jit(solution)/shard_map/ppermute | solution.py:25
  (21 other events, 65.6 us)
Sparse Core Ops, SparseCore 0:
  38.5 37.7 all-gather.2

commit v7 on v3

--- a/solution.py
+++ b/solution.py
@@ -1,6 +1,7 @@
 import jax
 import jax.numpy as jnp
 from jax import lax
+from jax.experimental.layout import Layout, with_layout_constraint
 from jax.sharding import Mesh, PartitionSpec as P
 
 BF = jnp.bfloat16
@@ -41,18 +42,8 @@
 
 
 def gather_y(own):
-    rows = own.shape[0] // 2
-    from_left, from_right = shift(own, "y", 1), shift(own, "y", 3)
-    far = [shift(from_left[:rows], "y", 1), shift(from_right[rows:], "y", 3)]
-    return jnp.concatenate([own, from_left] + far + [from_right], axis=0)
-
-
-def gather_y_later(own):
-    pieces = lax.all_gather(own, "y", axis=0, tiled=False)
-    place = lax.axis_index("y") + Y
-    return jnp.concatenate(
-        [lax.dynamic_index_in_dim(pieces, lax.bitwise_and(place - j, Y - 1), axis=0, keepdims=False) for j in range(Y)], axis=0
-    )
+    near = [shift(own, "y", 1), shift(own, "y", 3)]
+    return [own, near[0], shift(own, "y", 2), near[1]]
 
 
 def swap_core(low, high):
@@ -75,6 +66,25 @@
     return sum_parts(exchange(partial, "x"), X)
 
 
+def reduce_row(partial):
+    rows = partial.shape[0] // CORE
+    share = rows // X
+    core, place = lax.axis_index("core"), lax.axis_index("x")
+    received = shift(lax.dynamic_slice_in_dim(partial, (1 - core) * rows, rows, axis=0), "core", 1)
+
+    def block(step):
+        start = lax.bitwise_and(place + step, X - 1) * share
+        kept = lax.dynamic_slice_in_dim(partial, core * rows + start, share, axis=0)
+        return kept.astype(F32) + lax.dynamic_slice_in_dim(received, start, share, axis=0).astype(F32)
+
+    sent = lax.optimization_barrier([block(step).astype(BF) for step in range(1, X)])
+    moved = [shift(sent[step - 1], "x", step) for step in range(1, X)]
+    total = block(0)
+    for piece in moved:
+        total = total + piece.astype(F32)
+    return total
+
+
 def gather_core(half):
     other = shift(half, "core", 1)
     first = lax.axis_index("core") == 0
@@ -95,10 +105,14 @@
     return shift(pieces[2][:rows], "y", 1), shift(pieces[2][rows:], "y", 3)
 
 
-def reduce_y_near(pieces, from_left, from_right):
+def add_y_far(pieces, from_left, from_right):
     rows = pieces[2].shape[0] // 2
     to_right = jnp.concatenate([add(pieces[3][:rows], from_left), pieces[3][rows:]], axis=0)
     to_left = jnp.concatenate([pieces[1][:rows], add(pieces[1][rows:], from_right)], axis=0)
+    return lax.optimization_barrier((to_right, to_left))
+
+
+def move_y_near(to_right, to_left):
     return shift(to_right, "y", 1), shift(to_left, "y", 3)
 
 
@@ -113,19 +127,23 @@
 def body(tokens, gate_weight, up_weight, down_weight, out_grad):
     width = gate_weight.shape[1]
     both_weights = jnp.concatenate([gate_weight, up_weight], axis=1)
+
     tokens_z = gather(tokens, "z")
-    all_tokens = gather_y(tokens_z)
-    grads_z = gather(after(out_grad, tokens_z), "z")
-    all_grads = gather_y_later(grads_z)
+    grads_y = jnp.stack(gather_y(out_grad))
+    tokens_z, grads_y, both_weights = lax.optimization_barrier((tokens_z, grads_y, both_weights))
+    all_tokens = jnp.concatenate(gather_y(tokens_z), axis=0)
+    all_grads = lax.all_gather(grads_y, "z", axis=0, tiled=False)
 
-    gate_up = reduce_x(reduce_core(product(all_tokens, both_weights).astype(BF)))
+    gate_up = with_layout_constraint(product(all_tokens, both_weights).astype(BF), Layout((0, 1)))
+    gate_up = reduce_row(gate_up)
+    all_grads = jnp.swapaxes(all_grads, 0, 1).reshape(all_tokens.shape)
+    hidden_partial = reduce_core(product_right_t(all_grads, down_weight).astype(BF))
     gate_value = gate_up[:, :width]
     up_value = gate_up[:, width:]
     sigmoid_gate = jax.nn.sigmoid(gate_value)
     silu_gate = gate_value * sigmoid_gate
     hidden_share = (silu_gate * up_value).astype(BF)
 
-    hidden_partial = reduce_core(product_right_t(all_grads, down_weight).astype(BF))
     rows = hidden_share.shape[0]
     mixed = jnp.concatenate(
         [jnp.broadcast_to(hidden_share[None], (X, rows, width)), hidden_partial.reshape(X, rows, width)], axis=1
@@ -136,22 +154,28 @@
 
     output_pieces = split_y(product(hidden, down_weight).astype(BF))
     output_far = reduce_y_far(output_pieces)
-    output_near = reduce_y_near(output_pieces, *output_far)
+    to_right, to_left = add_y_far(output_pieces, *output_far)
+    output_near = move_y_near(to_right, to_left)
 
     gate_grad = (hidden_grad * up_value * sigmoid_gate * (1.0 + gate_value * (1.0 - sigmoid_gate))).astype(BF)
     up_grad = (hidden_grad * silu_gate).astype(BF)
-    both_half = after(gather(jnp.concatenate([gate_grad, up_grad], axis=1), "x"), *output_far)
+    both_half = gather(jnp.concatenate([gate_grad, up_grad], axis=1), "x")
+    down_weight_grad = product_left_t(hidden, all_grads)
+    both_half, down_weight_grad, to_right, to_left = lax.optimization_barrier(
+        (both_half, down_weight_grad, to_right, to_left)
+    )
     both_grads = after(gather_core(both_half), *output_near)
 
     input_pieces = split_y(product_right_t(both_grads, both_weights).astype(BF))
-    input_near = reduce_y_near(input_pieces, *reduce_y_far(input_pieces))
-    layer_output = reduce_z(sum_y(output_pieces[0], *output_near))
-    gate_weight_grad = product_left_t(all_tokens, both_grads[:, :width])
-    up_weight_grad = product_left_t(all_tokens, both_grads[:, width:])
-    down_weight_grad = product_left_t(hidden, all_grads)
-    weight_grads = (gate_weight_grad, up_weight_grad, down_weight_grad)
-    input_total, weight_grads = lax.optimization_barrier((sum_y(input_pieces[0], *input_near), weight_grads))
-    return (layer_output, reduce_z(input_total)) + weight_grads
+    input_near = move_y_near(*add_y_far(input_pieces, *reduce_y_far(input_pieces)))
+    output_total = reduce_z(sum_y(output_pieces[0], *output_near))
+    weight_grads = (
+        product_left_t(all_tokens, both_grads[:, :width]),
+        product_left_t(all_tokens, both_grads[:, width:]),
+        down_weight_grad,
+    )
+    input_near, weight_grads, output_total = lax.optimization_barrier((input_near, weight_grads, output_total))
+    return (output_total, reduce_z(sum_y(input_pieces[0], *input_near))) + weight_grads
 
 
 def solution(mesh):

time: 218 us -> 211 us (0.968)
  waiting for transfers between devices: 70.2 us -> 58.4 us
  starting transfers between devices: 43.8 us -> 48.1 us
  other arithmetic: 18.8 us -> 22.9 us
  blocking collectives: 42.7 us -> 39.9 us
  local copies, waits for them, and re-layouts: 11.5 us -> 8.89 us
    all_to_all x5 -> x3, waiting for transfers between devices: 38.5 us -> 12.5 us  [exchange(): return lax.all_to_all(blocks, axis, split_axis=0, concat_axis=0, tiled=True)]
    ppermute x16 -> x21, waiting for transfers between devices: 27.4 us -> 45.9 us  [shift(): lax.ppermute(block, axis, [(i, (i + step) % size) for i in range(size)])]
    ppermute x16 -> x21, starting transfers between devices: 20.8 us -> 29.6 us  [shift(): lax.ppermute(block, axis, [(i, (i + step) % size) for i in range(size)])]
    all_to_all x5 -> x3, starting transfers between devices: 23 us -> 18.5 us  [exchange(): return lax.all_to_all(blocks, axis, split_axis=0, concat_axis=0, tiled=True)]
    concatenate x5, other arithmetic: 1.11 us -> 5.58 us  [the longest x1 2.87 us: body(): both_weights = jnp.concatenate([gate_weight, up_weight], axis=1)]
    all_gather x1, waiting for transfers between devices: 4.36 us -> 0.01 us  [body(): all_grads = lax.all_gather(grads_y, 'z', axis=0, tiled=False)]
    convert_element_type x2 -> x1, other arithmetic: 4.09 us -> 1.25 us  [reduce_core(): return (kept.astype(F32) + received.astype(F32)).astype(BF)]
    all_to_all x2, blocking collectives: 42.7 us -> 39.9 us  [exchange(): return lax.all_to_all(blocks, axis, split_axis=0, concat_axis=0, tiled=True)]
  transfers between devices with their start and end apart: 22 -> 25, of which waited for: 12 -> 11; matrix products, arithmetic and copies ran while one was open for 16% -> 18% of each run, Pallas kernels for 0% -> 0%
where the time goes in v7:
time: 211 us; the launch traced here: 209 us
  waiting for transfers between devices  58.4 us (28%)
  starting transfers between devices  48.1 us (23%)
  blocking collectives  39.9 us (19%)
  other arithmetic  22.9 us (11%)
  matrix products  16.7 us (8%)
  between operations  14.4 us (7%)
  local copies, waits for them, and re-layouts  8.89 us (4%)
    ppermute x21, waiting for transfers between devices, shift(): lax.ppermute(block, axis, [(i, (i + step) % size) for i in range(size)])  45.9 us
    all_to_all x2, blocking collectives, exchange(): return lax.all_to_all(blocks, axis, split_axis=0, concat_axis=0, tiled=True)  39.9 us
    ppermute x21, starting transfers between devices, shift(): lax.ppermute(block, axis, [(i, (i + step) % size) for i in range(size)])  29.6 us
    all_to_all x3, starting transfers between devices, exchange(): return lax.all_to_all(blocks, axis, split_axis=0, concat_axis=0, tiled=True)  18.5 us
    all_to_all x3, waiting for transfers between devices, exchange(): return lax.all_to_all(blocks, axis, split_axis=0, concat_axis=0, tiled=True)  12.5 us
    dot_general x3, matrix products, product_left_t(): lax.dot_general(left_side, right_side, (((0,), (0,)), ((), ())), preferre...  9.4 us
  transfers between devices with their start and end apart: 25, of which 11 were waited for; matrix products, arithmetic and copies ran while one was open for 18% of the time, Pallas kernels for 0%

profile of v7, /device:TPU:2, one launch (start us, length us, event | category | flops | bytes accessed | tf_op | source)
XLA Modules:
  0.0 209.3 jit_solution(14227243781740392827)
XLA Ops:
  7.2 1.8 broadcast_in_dim.6
  9.0 8.5 %all-to-all-start = ((bf16[8,32,1024]{2,1,0:T(8,128)(2,1)}), bf16[8,32,1024]{2,1,0:T(8,128)(2,1)S(1)}, u32[]{:S(2)}, u32[]{:S(2)}) async-start(bf16[8,32,1024]{2,1,0:T(8,128)(2,1)} %broadcast_in_dim.6), calls=%async_computation | async-start | bytes 1048576 | tf_op jit(solution)/shard_map/all_to_all | solution.py:30
  19.2 2.9 %collective-permute-start.1 = (bf16[32,1024]{1,0:T(8,128)(2,1)}, bf16[32,1024]{1,0:T(8,128)(2,1)S(1)}, u32[]{:S(2)}, u32[]{:S(2)}) collective-permute-start(bf16[32,1024]{1,0:T(8,128)(2,1)} %param.9), channel_id=1, source_target_pairs={{0,16},{8,24},{16,0},{24,8},{1,17},{9,25},{17,1},{25,9},{2,18},{10... | collective-permute-start | bytes 196616 | tf_op jit(solution)/shard_map/ppermute | solution.py:26
  23.5 2.9 %pad_maximum_fusion = bf16[1024,1024]{1,0:T(8,128)(2,1)} fusion(bf16[1024,512]{1,0:T(8,128)(2,1)S(1)} %copy-done.9, bf16[1024,512]{1,0:T(8,128)(2,1)} %param.6), kind=kLoop, calls=%fused_computation | loop fusion | flops 4194304 | bytes 4194304 | tf_op jit(solution)/shard_map/concatenate | solution.py:129
  27.3 7.7 %all-to-all-done = bf16[8,32,1024]{2,1,0:T(8,128)(2,1)S(1)} async-done(((bf16[8,32,1024]{2,1,0:T(8,128)(2,1)}), bf16[8,32,1024]{2,1,0:T(8,128)(2,1)S(1)}, u32[]{:S(2)}, u32[]{:S(2)}) %all-to-all-start) | async-done | bytes 524320 | tf_op jit(solution)/shard_map/all_to_all | solution.py:30
  36.7 2.9 %collective-permute-start.4 = (bf16[256,1024]{1,0:T(8,128)(2,1)S(1)}, bf16[256,1024]{1,0:T(8,128)(2,1)S(1)}, u32[]{:S(2)}, u32[]{:S(2)}) collective-permute-start(bf16[256,1024]{1,0:T(8,128)(2,1)S(1)} %bitcast.30), channel_id=1, source_target_pairs={{0,16},{8,24},{16,0},{24,8},{1,17},{9,25},{17,1},{25,9},{2,18},{10... | collective-permute-start | bytes 1572872 | tf_op jit(solution)/shard_map/ppermute | solution.py:26
  41.0 9.3 %collective-permute-done.3 = bf16[256,1024]{1,0:T(8,128)(2,1)S(1)} collective-permute-done((bf16[256,1024]{1,0:T(8,128)(2,1)S(1)}, bf16[256,1024]{1,0:T(8,128)(2,1)S(1)}, u32[]{:S(2)}, u32[]{:S(2)}) %collective-permute-start.3) | collective-permute-done | bytes 524320 | tf_op jit(solution)/shard_map/ppermute | solution.py:26
  50.3 12.4 %collective-permute-done.4 = bf16[256,1024]{1,0:T(8,128)(2,1)S(1)} collective-permute-done((bf16[256,1024]{1,0:T(8,128)(2,1)S(1)}, bf16[256,1024]{1,0:T(8,128)(2,1)S(1)}, u32[]{:S(2)}, u32[]{:S(2)}) %collective-permute-start.4) | collective-permute-done | bytes 524320 | tf_op jit(solution)/shard_map/ppermute | solution.py:26
  62.7 2.3 %convolution_convert_fusion.2 = bf16[1024,1024]{1,0:T(8,128)(2,1)S(1)} fusion(bf16[1024,1024]{1,0:T(8,128)(2,1)S(1)} %constant_dynamic-update-slice_fusion, bf16[1024,1024]{1,0:T(8,128)(2,1)S(1)} %copy-done.4), kind=kOutput, calls=%fused_computation.4 | convolution fusion | flops 2148532224 | bytes 6291456 | tf_op jit(solution)/shard_map/dot_general | solution.py:13
  66.2 3.0 %collective-permute-done.6 = bf16[512,1024]{1,0:T(8,128)(2,1)} collective-permute-done((bf16[512,1024]{1,0:T(8,128)(2,1)}, bf16[512,1024]{1,0:T(8,128)(2,1)}, u32[]{:S(2)}, u32[]{:S(2)}) %collective-permute-start.6) | collective-permute-done | bytes 1048608 | tf_op jit(solution)/shard_map/ppermute | solution.py:26
  69.2 2.2 %add_convert_fusion.7 = (bf16[128,1024]{1,0:T(8,128)(2,1)S(1)}, bf16[128,1024]{1,0:T(8,128)(2,1)}, bf16[128,1024]{1,0:T(8,128)(2,1)}) fusion(bf16[512,1024]{1,0:T(8,128)(2,1)} %collective-permute-done.6, s32[]{:T(128)S(6)} %select_n.68, bf16[1024,1024]{1,0:T(8,128)(2,1)S(1)} %convolution_convert_fusion.2, s32[]{:T(128)S(6)} %select_n.67, s32[]{:T(128)S(6)} %select_n.66, ...), kind=kLoop, calls=%fused_computation.28 | loop fusion | flops 1572864 | bytes 2359320 | tf_op jit(solution)/shard_map/convert_element_type | solution.py:80
  74.1 2.1 %collective-permute-start.9 = (bf16[128,1024]{1,0:T(8,128)(2,1)S(1)}, bf16[128,1024]{1,0:T(8,128)(2,1)}, u32[]{:S(2)}, u32[]{:S(2)}) collective-permute-start(bf16[128,1024]{1,0:T(8,128)(2,1)S(1)} %get-tuple-element.28), channel_id=1, source_target_pairs={{0,192},{64,0},{128,64},{192,128},{1,193},{65,1},{129,65},{193,129... | collective-permute-start | bytes 786440 | tf_op jit(solution)/shard_map/ppermute | solution.py:26
  76.2 1.8 copy.11
  81.2 2.8 %collective-permute-done.8 = bf16[128,1024]{1,0:T(8,128)(2,1)} collective-permute-done((bf16[128,1024]{1,0:T(8,128)(2,1)}, bf16[128,1024]{1,0:T(8,128)(2,1)}, u32[]{:S(2)}, u32[]{:S(2)}) %collective-permute-start.8) | collective-permute-done | bytes 262176 | tf_op jit(solution)/shard_map/ppermute | solution.py:26
  84.0 3.6 %collective-permute-done.9 = bf16[128,1024]{1,0:T(8,128)(2,1)} collective-permute-done((bf16[128,1024]{1,0:T(8,128)(2,1)S(1)}, bf16[128,1024]{1,0:T(8,128)(2,1)}, u32[]{:S(2)}, u32[]{:S(2)}) %collective-permute-start.9) | collective-permute-done | bytes 262176 | tf_op jit(solution)/shard_map/ppermute | solution.py:26
  90.5 18.0 %all_to_all.42 = bf16[4,256,512]{2,1,0:T(8,128)(2,1)S(1)} all-to-all(bf16[4,256,512]{2,1,0:T(8,128)(2,1)S(1)} %pad_maximum_fusion.2), channel_id=1, replica_groups=mesh['x'=4,'core'=2,'y'=4,'z'=8] {'x'}, dimensions={0} | all-to-all | bytes 2097152 | tf_op jit(solution)/shard_map/all_to_all | solution.py:30
  110.8 5.7 %all-to-all-start.2 = ((bf16[4,128,1024]{2,1,0:T(8,128)(2,1)}), bf16[4,128,1024]{2,1,0:T(8,128)(2,1)}, u32[]{:S(2)}, u32[]{:S(2)}) async-start(bf16[4,128,1024]{2,1,0:T(8,128)(2,1)} %broadcast_in_dim.8), calls=%async_computation.2 | async-start | bytes 2097152 | tf_op jit(solution)/shard_map/all_to_all | solution.py:30
  120.4 2.1 collective-permute-start.13
  122.4 2.6 %fusion.4 = f32[512,1024]{1,0:T(8,128)} fusion(bf16[1024,1024]{1,0:T(8,128)(2,1)S(1)} %bitcast.27, bf16[512,512]{1,0:T(8,128)(2,1)S(1)} %get-tuple-element.61, bf16[512,512]{1,0:T(8,128)(2,1)S(1)} %get-tuple-element.60), kind=kOutput, calls=%fused_computation.18 | convolution fusion | flops 1075838976 | bytes 5242880 | tf_op jit(solution)/shard_map/dot_general | solution.py:21
  125.0 3.8 %collective-permute-done.12 = bf16[128,1024]{1,0:T(8,128)(2,1)S(1)} collective-permute-done((bf16[128,1024]{1,0:T(8,128)(2,1)S(1)}, bf16[128,1024]{1,0:T(8,128)(2,1)S(1)}, u32[]{:S(2)}, u32[]{:S(2)}) %collective-permute-start.12) | collective-permute-done | bytes 262176 | tf_op jit(solution)/shard_map/ppermute | solution.py:26
  129.1 2.0 all-to-all-done.2
  132.3 2.1 collective-permute-start.16
  136.0 10.7 %collective-permute-done.15 = bf16[256,1024]{1,0:T(8,128)(2,1)S(1)} collective-permute-done((bf16[256,1024]{1,0:T(8,128)(2,1)S(1)}, bf16[256,1024]{1,0:T(8,128)(2,1)S(1)}, u32[]{:S(2)}, u32[]{:S(2)}) %collective-permute-start.15) | collective-permute-done | bytes 524320 | tf_op jit(solution)/shard_map/ppermute | solution.py:26
  146.7 2.4 %convolution_convert_fusion = bf16[1024,1024]{1,0:T(8,128)(2,1)S(1)} fusion(bf16[1024,1024]{1,0:T(8,128)(2,1)S(1)} %pad_maximum_fusion.1, bf16[1024,1024]{1,0:T(8,128)(2,1)S(1)} %copy-done.5), kind=kOutput, calls=%fused_computation.2 | convolution fusion | flops 2148532224 | bytes 6291456 | tf_op jit(solution)/shard_map/dot_general | solution.py:17
  151.0 2.2 %collective-permute-start.18 = (bf16[128,1024]{1,0:T(8,128)(2,1)}, bf16[128,1024]{1,0:T(8,128)(2,1)}, u32[]{:S(2)}, u32[]{:S(2)}) collective-permute-start(bf16[128,1024]{1,0:T(8,128)(2,1)} %get-tuple-element.47), channel_id=1, source_target_pairs={{0,24},{8,0},{16,8},{24,16},{1,25},{9,1},{17,9},{25,17},{2,26},{10... | collective-permute-start | bytes 786440 | tf_op jit(solution)/shard_map/ppermute | solution.py:26
  153.2 2.1 %add_convert_fusion.1 = bf16[256,1024]{1,0:T(8,128)(2,1)} fusion(bf16[256,1024]{1,0:T(8,128)(2,1)S(1)} %collective-permute-done.16, bf16[256,1024]{1,0:T(8,128)(2,1)S(1)} %collective-permute-done.15, bf16[1024,1024]{1,0:T(8,128)(2,1)} %copy-done.6), kind=kLoop, calls=%fused_computation.9 | loop fusion | flops 1572864 | bytes 2097152 | tf_op jit(solution)/shard_map/convert_element_type | solution.py:120
  155.4 4.4 %all-to-all-start.3 = ((bf16[8,32,1024]{2,1,0:T(8,128)(2,1)}), bf16[8,32,1024]{2,1,0:T(8,128)(2,1)}, u32[]{:S(2)}, u32[]{:S(2)}) async-start(bf16[8,32,1024]{2,1,0:T(8,128)(2,1)} %bitcast.34), calls=%async_computation.3 | async-start | bytes 1048576 | tf_op jit(solution)/shard_map/all_to_all | solution.py:30
  164.1 2.9 %collective-permute-start.20 = (bf16[256,1024]{1,0:T(8,128)(2,1)}, bf16[256,1024]{1,0:T(8,128)(2,1)}, u32[]{:S(2)}, u32[]{:S(2)}) collective-permute-start(bf16[256,1024]{1,0:T(8,128)(2,1)} %pad_maximum_fusion.9), channel_id=1, source_target_pairs={{0,24},{8,0},{16,8},{24,16},{1,25},{9,1},{17,9},{25,17},{2,26},{10... | collective-permute-start | bytes 1572872 | tf_op jit(solution)/shard_map/ppermute | solution.py:26
  167.0 4.2 %fusion = f32[1024,512]{1,0:T(8,128)} fusion(bf16[1024,1024]{1,0:T(8,128)(2,1)} %copy-done.10, bf16[1024,1024]{1,0:T(8,128)(2,1)S(1)} %copy-done.8), kind=kOutput, calls=%fused_computation.10 | convolution fusion | flops 1073741824 | bytes 5242880 | tf_op jit(solution)/shard_map/dot_general | solution.py:21
  171.2 2.6 %fusion.2 = f32[1024,512]{1,0:T(8,128)} fusion(bf16[1024,1024]{1,0:T(8,128)(2,1)S(1)} %copy-done.11, bf16[1024,1024]{1,0:T(8,128)(2,1)S(1)} %copy-done.8), kind=kOutput, calls=%fused_computation.12 | convolution fusion | flops 1073741824 | bytes 5242880 | tf_op jit(solution)/shard_map/dot_general | solution.py:21
  173.8 2.8 %all-to-all-done.3 = bf16[8,32,1024]{2,1,0:T(8,128)(2,1)} async-done(((bf16[8,32,1024]{2,1,0:T(8,128)(2,1)}), bf16[8,32,1024]{2,1,0:T(8,128)(2,1)}, u32[]{:S(2)}, u32[]{:S(2)}) %all-to-all-start.3) | async-done | bytes 524320 | tf_op jit(solution)/shard_map/all_to_all | solution.py:30
  179.9 21.9 %all_to_all.43 = bf16[8,32,1024]{2,1,0:T(8,128)(2,1)S(1)} all-to-all(bf16[8,32,1024]{2,1,0:T(8,128)(2,1)S(1)} %bitcast.35), channel_id=1, replica_groups=mesh['x'=4,'core'=2,'y'=4,'z'=8] {'z'}, dimensions={0} | all-to-all | bytes 1048576 | tf_op jit(solution)/shard_map/all_to_all | solution.py:30
  (89 shorter events, 36.3 us)
Async XLA Ops:
  7.2 70.9 %copy-start = (bf16[512,1024]{1,0:T(8,128)(2,1)S(1)}, bf16[512,1024]{1,0:T(8,128)(2,1)}, u32[]{:S(2)}) copy-start(bf16[512,1024]{1,0:T(8,128)(2,1)} %param.8) | copy-start | bytes 3145732
  7.2 16.3 %copy-start.9 = (bf16[1024,512]{1,0:T(8,128)(2,1)S(1)}, bf16[1024,512]{1,0:T(8,128)(2,1)}, u32[]{:S(2)}) copy-start(bf16[1024,512]{1,0:T(8,128)(2,1)} %param.7) | copy-start | bytes 3145732
  9.0 26.0 %all-to-all-start = ((bf16[8,32,1024]{2,1,0:T(8,128)(2,1)}), bf16[8,32,1024]{2,1,0:T(8,128)(2,1)S(1)}, u32[]{:S(2)}, u32[]{:S(2)}) async-start(bf16[8,32,1024]{2,1,0:T(8,128)(2,1)} %broadcast_in_dim.6), calls=%async_computation | async-start | bytes 1048576 | tf_op jit(solution)/shard_map/all_to_all | solution.py:30
  17.5 9.1 %copy-start.12 = (bf16[32,1024]{1,0:T(8,128)(2,1)S(1)}, bf16[32,1024]{1,0:T(8,128)(2,1)}, u32[]{:S(2)}) copy-start(bf16[32,1024]{1,0:T(8,128)(2,1)} %param.9) | copy-start | bytes 196612
  17.5 58.7 %all-gather.3.cloned.1.call-start = ((), (), s32[]{:S(2)}) async-start(), calls=%async_computation.5 | async-start | bytes 2359296 | tf_op jit(solution)/shard_map/all_gather | solution.py:135
  17.5 8.8 %collective-permute-start = (bf16[32,1024]{1,0:T(8,128)(2,1)}, bf16[32,1024]{1,0:T(8,128)(2,1)S(1)}, u32[]{:S(2)}, u32[]{:S(2)}) collective-permute-start(bf16[32,1024]{1,0:T(8,128)(2,1)} %param.9), channel_id=1, source_target_pairs={{0,8},{8,16},{16,24},{24,0},{1,9},{9,17},{17,25},{25,1},{2,10},{10... | collective-permute-start | bytes 196616 | tf_op jit(solution)/shard_map/ppermute | solution.py:26
  19.2 7.1 %collective-permute-start.1 = (bf16[32,1024]{1,0:T(8,128)(2,1)}, bf16[32,1024]{1,0:T(8,128)(2,1)S(1)}, u32[]{:S(2)}, u32[]{:S(2)}) collective-permute-start(bf16[32,1024]{1,0:T(8,128)(2,1)} %param.9), channel_id=1, source_target_pairs={{0,16},{8,24},{16,0},{24,8},{1,17},{9,25},{17,1},{25,9},{2,18},{10... | collective-permute-start | bytes 196616 | tf_op jit(solution)/shard_map/ppermute | solution.py:26
  22.1 4.5 %collective-permute-start.2 = (bf16[32,1024]{1,0:T(8,128)(2,1)}, bf16[32,1024]{1,0:T(8,128)(2,1)S(1)}, u32[]{:S(2)}, u32[]{:S(2)}) collective-permute-start(bf16[32,1024]{1,0:T(8,128)(2,1)} %param.9), channel_id=1, source_target_pairs={{0,24},{8,0},{16,8},{24,16},{1,25},{9,1},{17,9},{25,17},{2,26},{10... | collective-permute-start | bytes 196616 | tf_op jit(solution)/shard_map/ppermute | solution.py:26
  35.0 15.2 %collective-permute-start.3 = (bf16[256,1024]{1,0:T(8,128)(2,1)S(1)}, bf16[256,1024]{1,0:T(8,128)(2,1)S(1)}, u32[]{:S(2)}, u32[]{:S(2)}) collective-permute-start(bf16[256,1024]{1,0:T(8,128)(2,1)S(1)} %bitcast.29), channel_id=1, source_target_pairs={{0,8},{8,16},{16,24},{24,0},{1,9},{9,17},{17,25},{25,1},{2,10},{10... | collective-permute-start | bytes 1572872 | tf_op jit(solution)/shard_map/ppermute | solution.py:26
  36.7 26.0 %collective-permute-start.4 = (bf16[256,1024]{1,0:T(8,128)(2,1)S(1)}, bf16[256,1024]{1,0:T(8,128)(2,1)S(1)}, u32[]{:S(2)}, u32[]{:S(2)}) collective-permute-start(bf16[256,1024]{1,0:T(8,128)(2,1)S(1)} %bitcast.30), channel_id=1, source_target_pairs={{0,16},{8,24},{16,0},{24,8},{1,17},{9,25},{17,1},{25,9},{2,18},{10... | collective-permute-start | bytes 1572872 | tf_op jit(solution)/shard_map/ppermute | solution.py:26
  39.6 23.1 %collective-permute-start.5 = (bf16[256,1024]{1,0:T(8,128)(2,1)S(1)}, bf16[256,1024]{1,0:T(8,128)(2,1)S(1)}, u32[]{:S(2)}, u32[]{:S(2)}) collective-permute-start(bf16[256,1024]{1,0:T(8,128)(2,1)S(1)} %bitcast.31), channel_id=1, source_target_pairs={{0,24},{8,0},{16,8},{24,16},{1,25},{9,1},{17,9},{25,17},{2,26},{10... | collective-permute-start | bytes 1572872 | tf_op jit(solution)/shard_map/ppermute | solution.py:26
  40.9 21.8 %copy-start.4 = (bf16[1024,1024]{1,0:T(8,128)(2,1)S(1)}, bf16[1024,1024]{1,0:T(8,128)(2,1)}, u32[]{:S(2)}) copy-start(bf16[1024,1024]{1,0:T(8,128)(2,1)} %pad_maximum_fusion) | copy-start | bytes 6291460
  66.2 3.0 %collective-permute-start.6 = (bf16[512,1024]{1,0:T(8,128)(2,1)}, bf16[512,1024]{1,0:T(8,128)(2,1)}, u32[]{:S(2)}, u32[]{:S(2)}) collective-permute-start(bf16[512,1024]{1,0:T(8,128)(2,1)} %constant_dynamic-slice_fusion), channel_id=1, source_target_pairs={{0,32},{32,0},{1,33},{33,1},{2,34},{34,2},{3,35},{35,3},{4,36},{36... | collective-permute-start | bytes 3145736 | tf_op jit(solution)/shard_map/ppermute | solution.py:26
  71.5 9.7 %collective-permute-start.7 = (bf16[128,1024]{1,0:T(8,128)(2,1)}, bf16[128,1024]{1,0:T(8,128)(2,1)}, u32[]{:S(2)}, u32[]{:S(2)}) collective-permute-start(bf16[128,1024]{1,0:T(8,128)(2,1)} %get-tuple-element.26), channel_id=1, source_target_pairs={{0,64},{64,128},{128,192},{192,0},{1,65},{65,129},{129,193},{193,1... | collective-permute-start | bytes 786440 | tf_op jit(solution)/shard_map/ppermute | solution.py:26
  72.9 11.0 %collective-permute-start.8 = (bf16[128,1024]{1,0:T(8,128)(2,1)}, bf16[128,1024]{1,0:T(8,128)(2,1)}, u32[]{:S(2)}, u32[]{:S(2)}) collective-permute-start(bf16[128,1024]{1,0:T(8,128)(2,1)} %get-tuple-element.27), channel_id=1, source_target_pairs={{0,128},{64,192},{128,0},{192,64},{1,129},{65,193},{129,1},{193,65... | collective-permute-start | bytes 786440 | tf_op jit(solution)/shard_map/ppermute | solution.py:26
  74.1 13.5 %collective-permute-start.9 = (bf16[128,1024]{1,0:T(8,128)(2,1)S(1)}, bf16[128,1024]{1,0:T(8,128)(2,1)}, u32[]{:S(2)}, u32[]{:S(2)}) collective-permute-start(bf16[128,1024]{1,0:T(8,128)(2,1)S(1)} %get-tuple-element.28), channel_id=1, source_target_pairs={{0,192},{64,0},{128,64},{192,128},{1,193},{65,1},{129,65},{193,129... | collective-permute-start | bytes 786440 | tf_op jit(solution)/shard_map/ppermute | solution.py:26
  81.2 8.0 %collective-permute-start.10 = (bf16[512,512]{1,0:T(8,128)(2,1)}, bf16[512,512]{1,0:T(8,128)(2,1)}, u32[]{:S(2)}, u32[]{:S(2)}) collective-permute-start(bf16[512,512]{1,0:T(8,128)(2,1)} %broadcast_select_fusion.4), channel_id=1, source_target_pairs={{0,32},{32,0},{1,33},{33,1},{2,34},{34,2},{3,35},{35,3},{4,36},{36... | collective-permute-start | bytes 1572872 | tf_op jit(solution)/shard_map/ppermute | solution.py:26
  109.4 7.1 %collective-permute-start.11 = (bf16[512,512]{1,0:T(8,128)(2,1)}, bf16[512,512]{1,0:T(8,128)(2,1)}, u32[]{:S(2)}, u32[]{:S(2)}) collective-permute-start(bf16[512,512]{1,0:T(8,128)(2,1)} %bitcast.10), channel_id=1, source_target_pairs={{0,32},{32,0},{1,33},{33,1},{2,34},{34,2},{3,35},{35,3},{4,36},{36... | collective-permute-start | bytes 1572872 | tf_op jit(solution)/shard_map/ppermute | solution.py:26
  110.8 20.4 %all-to-all-start.2 = ((bf16[4,128,1024]{2,1,0:T(8,128)(2,1)}), bf16[4,128,1024]{2,1,0:T(8,128)(2,1)}, u32[]{:S(2)}, u32[]{:S(2)}) async-start(bf16[4,128,1024]{2,1,0:T(8,128)(2,1)} %broadcast_in_dim.8), calls=%async_computation.2 | async-start | bytes 2097152 | tf_op jit(solution)/shard_map/all_to_all | solution.py:30
  119.0 9.8 %copy-start.6 = (bf16[1024,1024]{1,0:T(8,128)(2,1)}, bf16[1024,1024]{1,0:T(8,128)(2,1)S(1)}, u32[]{:S(2)}) copy-start(bf16[1024,1024]{1,0:T(8,128)(2,1)S(1)} %convolution_convert_fusion.1) | copy-start | bytes 6291460
  119.1 9.7 %collective-permute-start.12 = (bf16[128,1024]{1,0:T(8,128)(2,1)S(1)}, bf16[128,1024]{1,0:T(8,128)(2,1)S(1)}, u32[]{:S(2)}, u32[]{:S(2)}) collective-permute-start(bf16[128,1024]{1,0:T(8,128)(2,1)S(1)} %get-tuple-element.57), channel_id=1, source_target_pairs={{0,8},{8,16},{16,24},{24,0},{1,9},{9,17},{17,25},{25,1},{2,10},{10... | collective-permute-start | bytes 786440 | tf_op jit(solution)/shard_map/ppermute | solution.py:26
  120.4 8.5 %collective-permute-start.13 = (bf16[128,1024]{1,0:T(8,128)(2,1)S(1)}, bf16[128,1024]{1,0:T(8,128)(2,1)S(1)}, u32[]{:S(2)}, u32[]{:S(2)}) collective-permute-start(bf16[128,1024]{1,0:T(8,128)(2,1)S(1)} %get-tuple-element.55), channel_id=1, source_target_pairs={{0,24},{8,0},{16,8},{24,16},{1,25},{9,1},{17,9},{25,17},{2,26},{10... | collective-permute-start | bytes 786440 | tf_op jit(solution)/shard_map/ppermute | solution.py:26
  131.2 3.2 %collective-permute-start.14 = (bf16[512,1024]{1,0:T(8,128)(2,1)}, bf16[512,1024]{1,0:T(8,128)(2,1)S(1)}, u32[]{:S(2)}, u32[]{:S(2)}) collective-permute-start(bf16[512,1024]{1,0:T(8,128)(2,1)} %bitcast.9), channel_id=1, source_target_pairs={{0,32},{32,0},{1,33},{33,1},{2,34},{34,2},{3,35},{35,3},{4,36},{36... | collective-permute-start | bytes 3145736 | tf_op jit(solution)/shard_map/ppermute | solution.py:26
  131.2 15.5 %collective-permute-start.15 = (bf16[256,1024]{1,0:T(8,128)(2,1)S(1)}, bf16[256,1024]{1,0:T(8,128)(2,1)S(1)}, u32[]{:S(2)}, u32[]{:S(2)}) collective-permute-start(bf16[256,1024]{1,0:T(8,128)(2,1)S(1)} %get-tuple-element.30), channel_id=1, source_target_pairs={{0,8},{8,16},{16,24},{24,0},{1,9},{9,17},{17,25},{25,1},{2,10},{10... | collective-permute-start | bytes 1572872 | tf_op jit(solution)/shard_map/ppermute | solution.py:26
  132.3 14.4 %collective-permute-start.16 = (bf16[256,1024]{1,0:T(8,128)(2,1)S(1)}, bf16[256,1024]{1,0:T(8,128)(2,1)S(1)}, u32[]{:S(2)}, u32[]{:S(2)}) collective-permute-start(bf16[256,1024]{1,0:T(8,128)(2,1)S(1)} %get-tuple-element.31), channel_id=1, source_target_pairs={{0,24},{8,0},{16,8},{24,16},{1,25},{9,1},{17,9},{25,17},{2,26},{10... | collective-permute-start | bytes 1572872 | tf_op jit(solution)/shard_map/ppermute | solution.py:26
  135.8 10.9 %copy-start.5 = (bf16[1024,1024]{1,0:T(8,128)(2,1)S(1)}, bf16[1024,1024]{1,0:T(8,128)(2,1)}, u32[]{:S(2)}) copy-start(bf16[1024,1024]{1,0:T(8,128)(2,1)} %pad_maximum_fusion) | copy-start | bytes 6291460
  136.0 13.1 %copy-start.7 = (bf16[1024,1024]{1,0:T(8,128)(2,1)}, bf16[1024,1024]{1,0:T(8,128)(2,1)S(1)}, u32[]{:S(2)}) copy-start(bf16[1024,1024]{1,0:T(8,128)(2,1)S(1)} %pad_maximum_fusion.1) | copy-start | bytes 6291460
  150.0 9.8 %collective-permute-start.17 = (bf16[128,1024]{1,0:T(8,128)(2,1)}, bf16[128,1024]{1,0:T(8,128)(2,1)}, u32[]{:S(2)}, u32[]{:S(2)}) collective-permute-start(bf16[128,1024]{1,0:T(8,128)(2,1)} %get-tuple-element.49), channel_id=1, source_target_pairs={{0,8},{8,16},{16,24},{24,0},{1,9},{9,17},{17,25},{25,1},{2,10},{10... | collective-permute-start | bytes 786440 | tf_op jit(solution)/shard_map/ppermute | solution.py:26
  151.0 8.8 %collective-permute-start.18 = (bf16[128,1024]{1,0:T(8,128)(2,1)}, bf16[128,1024]{1,0:T(8,128)(2,1)}, u32[]{:S(2)}, u32[]{:S(2)}) collective-permute-start(bf16[128,1024]{1,0:T(8,128)(2,1)} %get-tuple-element.47), channel_id=1, source_target_pairs={{0,24},{8,0},{16,8},{24,16},{1,25},{9,1},{17,9},{25,17},{2,26},{10... | collective-permute-start | bytes 786440 | tf_op jit(solution)/shard_map/ppermute | solution.py:26
  155.4 21.2 %all-to-all-start.3 = ((bf16[8,32,1024]{2,1,0:T(8,128)(2,1)}), bf16[8,32,1024]{2,1,0:T(8,128)(2,1)}, u32[]{:S(2)}, u32[]{:S(2)}) async-start(bf16[8,32,1024]{2,1,0:T(8,128)(2,1)} %bitcast.34), calls=%async_computation.3 | async-start | bytes 1048576 | tf_op jit(solution)/shard_map/all_to_all | solution.py:30
  163.7 14.6 %collective-permute-start.19 = (bf16[256,1024]{1,0:T(8,128)(2,1)}, bf16[256,1024]{1,0:T(8,128)(2,1)}, u32[]{:S(2)}, u32[]{:S(2)}) collective-permute-start(bf16[256,1024]{1,0:T(8,128)(2,1)} %pad_maximum_fusion.8), channel_id=1, source_target_pairs={{0,8},{8,16},{16,24},{24,0},{1,9},{9,17},{17,25},{25,1},{2,10},{10... | collective-permute-start | bytes 1572872 | tf_op jit(solution)/shard_map/ppermute | solution.py:26
  164.1 14.3 %collective-permute-start.20 = (bf16[256,1024]{1,0:T(8,128)(2,1)}, bf16[256,1024]{1,0:T(8,128)(2,1)}, u32[]{:S(2)}, u32[]{:S(2)}) collective-permute-start(bf16[256,1024]{1,0:T(8,128)(2,1)} %pad_maximum_fusion.9), channel_id=1, source_target_pairs={{0,24},{8,0},{16,8},{24,16},{1,25},{9,1},{17,9},{25,17},{2,26},{10... | collective-permute-start | bytes 1572872 | tf_op jit(solution)/shard_map/ppermute | solution.py:26
  (6 other events, 32.4 us)
Sparse Core Ops, SparseCore 0:
  35.1 37.4 all-gather.2

commit v8 on v7

--- a/solution.py
+++ b/solution.py
@@ -82,7 +82,15 @@
     total = block(0)
     for piece in moved:
         total = total + piece.astype(F32)
-    return total
+    return total, sent
+
+
+def gather_x(share):
+    pieces = jnp.stack([share] + [shift(share, "x", step) for step in range(1, X)])
+    place = lax.axis_index("x") + X
+    return jnp.concatenate(
+        [lax.dynamic_index_in_dim(pieces, lax.bitwise_and(place - i, X - 1), 0, keepdims=False) for i in range(X)], axis=0
+    )
 
 
 def gather_core(half):
@@ -128,14 +136,19 @@
     width = gate_weight.shape[1]
     both_weights = jnp.concatenate([gate_weight, up_weight], axis=1)
 
-    tokens_z = gather(tokens, "z")
-    grads_y = jnp.stack(gather_y(out_grad))
-    tokens_z, grads_y, both_weights = lax.optimization_barrier((tokens_z, grads_y, both_weights))
-    all_tokens = jnp.concatenate(gather_y(tokens_z), axis=0)
-    all_grads = lax.all_gather(grads_y, "z", axis=0, tiled=False)
+    features = tokens.shape[1]
+    main = features - features // 4
+    tokens_z = gather(tokens[:, :main], "z")
+    crossed = jnp.stack(gather_y(jnp.concatenate([out_grad, tokens[:, main:]], axis=1)))
+    tokens_z, crossed, both_weights = lax.optimization_barrier((tokens_z, crossed, both_weights))
+    all_grads = lax.all_gather(crossed[:, :, :features], "z", axis=0, tiled=False)
+    rest = gather(crossed[:, :, features:].reshape(-1, features - main), "z")
+    rest = jnp.swapaxes(rest.reshape(Z, Y, -1, features - main), 0, 1).reshape(-1, features - main)
+    all_tokens = jnp.concatenate([jnp.concatenate(gather_y(tokens_z), axis=0), rest], axis=1)
 
     gate_up = with_layout_constraint(product(all_tokens, both_weights).astype(BF), Layout((0, 1)))
-    gate_up = reduce_row(gate_up)
+    gate_up, sent = reduce_row(gate_up)
+    all_grads = after(all_grads, *sent)
     all_grads = jnp.swapaxes(all_grads, 0, 1).reshape(all_tokens.shape)
     hidden_partial = reduce_core(product_right_t(all_grads, down_weight).astype(BF))
     gate_value = gate_up[:, :width]
@@ -144,13 +157,10 @@
     silu_gate = gate_value * sigmoid_gate
     hidden_share = (silu_gate * up_value).astype(BF)
 
-    rows = hidden_share.shape[0]
-    mixed = jnp.concatenate(
-        [jnp.broadcast_to(hidden_share[None], (X, rows, width)), hidden_partial.reshape(X, rows, width)], axis=1
-    )
-    mixed = exchange(mixed.reshape(2 * X * rows, width), "x").reshape(X, 2 * rows, width)
-    hidden = gather_core(mixed[:, :rows].reshape(X * rows, width))
-    hidden_grad = jnp.sum(mixed[:, rows:].astype(F32), axis=0)
+    hidden_half = gather_x(hidden_share)
+    hidden_grad, hidden_half = lax.optimization_barrier((exchange(hidden_partial, "x"), hidden_half))
+    hidden_grad = sum_parts(hidden_grad, X)
+    hidden = gather_core(hidden_half)
 
     output_pieces = split_y(product(hidden, down_weight).astype(BF))
     output_far = reduce_y_far(output_pieces)

time: 211 us -> 209 us (level)
  blocking collectives: 39.9 us -> 21.7 us
  starting transfers between devices: 48.1 us -> 65.2 us
  waiting for transfers between devices: 58.4 us -> 53.5 us
  local copies, waits for them, and re-layouts: 8.89 us -> 12.3 us
    ppermute x21 -> x24, waiting for transfers between devices: 45.9 us -> 22.7 us  [shift(): lax.ppermute(block, axis, [(i, (i + step) % size) for i in range(size)])]
    all_to_all x2 -> x1, blocking collectives: 39.9 us -> 21.7 us  [exchange(): return lax.all_to_all(blocks, axis, split_axis=0, concat_axis=0, tiled=True)]
    all_to_all x3 -> x5, waiting for transfers between devices: 12.5 us -> 29.5 us  [exchange(): return lax.all_to_all(blocks, axis, split_axis=0, concat_axis=0, tiled=True)]
    all_to_all x3 -> x5, starting transfers between devices: 18.5 us -> 28.3 us  [exchange(): return lax.all_to_all(blocks, axis, split_axis=0, concat_axis=0, tiled=True)]
    ppermute x21 -> x24, starting transfers between devices: 29.6 us -> 36.9 us  [shift(): lax.ppermute(block, axis, [(i, (i + step) % size) for i in range(size)])]
  transfers between devices with their start and end apart: 25 -> 30, of which waited for: 11 -> 12; matrix products, arithmetic and copies ran while one was open for 18% -> 20% of each run, Pallas kernels for 0% -> 0%
where the time goes in v8:
time: 209 us; the launch traced here: 208 us
  starting transfers between devices  65.2 us (31%)
  waiting for transfers between devices  53.5 us (26%)
  other arithmetic  22.5 us (11%)
  blocking collectives  21.7 us (10%)
  matrix products  18.2 us (9%)
  between operations  14.4 us (7%)
  local copies, waits for them, and re-layouts  12.3 us (6%)
    ppermute x24, starting transfers between devices, shift(): lax.ppermute(block, axis, [(i, (i + step) % size) for i in range(size)])  36.9 us
    all_to_all x5, waiting for transfers between devices, exchange(): return lax.all_to_all(blocks, axis, split_axis=0, concat_axis=0, tiled=True)  29.5 us
    all_to_all x5, starting transfers between devices, exchange(): return lax.all_to_all(blocks, axis, split_axis=0, concat_axis=0, tiled=True)  28.3 us
    ppermute x24, waiting for transfers between devices, shift(): lax.ppermute(block, axis, [(i, (i + step) % size) for i in range(size)])  22.7 us
    all_to_all x1, blocking collectives, exchange(): return lax.all_to_all(blocks, axis, split_axis=0, concat_axis=0, tiled=True)  21.7 us
    dot_general x3, matrix products, product_left_t(): lax.dot_general(left_side, right_side, (((0,), (0,)), ((), ())), preferre...  8.93 us
    dot_general x2, matrix products, product(): return jnp.dot(left_side, right_side, preferred_element_type=F32)  5.57 us
  transfers between devices with their start and end apart: 30, of which 12 were waited for; matrix products, arithmetic and copies ran while one was open for 20% of the time, Pallas kernels for 0%

profile of v8, /device:TPU:2, one launch (start us, length us, event | category | flops | bytes accessed | tf_op | source)
XLA Modules:
  0.0 207.8 jit_solution(4431470691873657241)
XLA Ops:
  8.9 8.5 %all-to-all-start = ((bf16[8,32,768]{2,1,0:T(8,128)(2,1)}), bf16[8,32,768]{2,1,0:T(8,128)(2,1)S(1)}, u32[]{:S(2)}, u32[]{:S(2)}) async-start(bf16[8,32,768]{2,1,0:T(8,128)(2,1)} %broadcast_in_dim.8), calls=%async_computation | async-start | bytes 786432 | tf_op jit(solution)/shard_map/all_to_all | solution.py:30
  20.7 2.9 %collective-permute-start.1 = (bf16[32,1280]{1,0:T(8,128)(2,1)S(1)}, bf16[32,1280]{1,0:T(8,128)(2,1)S(1)}, u32[]{:S(2)}, u32[]{:S(2)}) collective-permute-start(bf16[32,1280]{1,0:T(8,128)(2,1)S(1)} %get-tuple-element.75), channel_id=1, source_target_pairs={{0,16},{8,24},{16,0},{24,8},{1,17},{9,25},{17,1},{25,9},{2,18},{10... | collective-permute-start | bytes 245768 | tf_op jit(solution)/shard_map/ppermute | solution.py:26
  24.9 2.9 %pad_maximum_fusion = bf16[1024,1024]{1,0:T(8,128)(2,1)} fusion(bf16[1024,512]{1,0:T(8,128)(2,1)S(1)} %copy-done.8, bf16[1024,512]{1,0:T(8,128)(2,1)} %param.6), kind=kLoop, calls=%fused_computation | loop fusion | flops 4194304 | bytes 4194304 | tf_op jit(solution)/shard_map/concatenate | solution.py:137
  28.0 4.0 %all-to-all-done = bf16[8,32,768]{2,1,0:T(8,128)(2,1)S(1)} async-done(((bf16[8,32,768]{2,1,0:T(8,128)(2,1)}), bf16[8,32,768]{2,1,0:T(8,128)(2,1)S(1)}, u32[]{:S(2)}, u32[]{:S(2)}) %all-to-all-start) | async-done | bytes 393248 | tf_op jit(solution)/shard_map/all_to_all | solution.py:30
  33.7 3.5 %all-to-all-start.1 = ((bf16[8,128,256]{2,1,0:T(8,128)(2,1)}), bf16[8,128,256]{2,1,0:T(8,128)(2,1)S(1)}, u32[]{:S(2)}, u32[]{:S(2)}) async-start(bf16[8,128,256]{2,1,0:T(8,128)(2,1)} %broadcast_in_dim.10), calls=%async_computation.1 | async-start | bytes 1048576 | tf_op jit(solution)/shard_map/all_to_all | solution.py:30
  38.9 2.9 %collective-permute-start.4 = (bf16[256,768]{1,0:T(8,128)(2,1)S(1)}, bf16[256,768]{1,0:T(8,128)(2,1)S(1)}, u32[]{:S(2)}, u32[]{:S(2)}) collective-permute-start(bf16[256,768]{1,0:T(8,128)(2,1)S(1)} %bitcast.53), channel_id=1, source_target_pairs={{0,16},{8,24},{16,0},{24,8},{1,17},{9,25},{17,1},{25,9},{2,18},{10... | collective-permute-start | bytes 1179656 | tf_op jit(solution)/shard_map/ppermute | solution.py:26
  43.1 15.0 %all-to-all-done.1 = bf16[8,128,256]{2,1,0:T(8,128)(2,1)S(1)} async-done(((bf16[8,128,256]{2,1,0:T(8,128)(2,1)}), bf16[8,128,256]{2,1,0:T(8,128)(2,1)S(1)}, u32[]{:S(2)}, u32[]{:S(2)}) %all-to-all-start.1) | async-done | bytes 524320 | tf_op jit(solution)/shard_map/all_to_all | solution.py:30
  59.8 4.3 %convolution_convert_fusion.2 = bf16[1024,1024]{1,0:T(8,128)(2,1)S(1)} fusion(bf16[1024,1024]{1,0:T(8,128)(2,1)} %pad_maximum_fusion, bf16[1024,256]{1,0:T(8,128)(2,1)S(1)} %bitcast.49, bf16[256,768]{1,0:T(8,128)(2,1)} %copy-done.19, bf16[256,768]{1,0:T(8,128)(2,1)} %copy-done.17, bf16[256,768]{1,0:T(8,128)(2,1)} %copy-done.15, bf16[256,768]{1,0:T(8,128)(2,1)S(1)} %bitcast.55), kind=kOutput, calls=%fused_computation.5 | convolution fusion | flops 2159017984 | bytes 6291456 | tf_op jit(solution)/shard_map/dot_general | solution.py:13
  65.4 3.0 %collective-permute-done.6 = bf16[512,1024]{1,0:T(8,128)(2,1)} collective-permute-done((bf16[512,1024]{1,0:T(8,128)(2,1)}, bf16[512,1024]{1,0:T(8,128)(2,1)}, u32[]{:S(2)}, u32[]{:S(2)}) %collective-permute-start.6) | collective-permute-done | bytes 1048608 | tf_op jit(solution)/shard_map/ppermute | solution.py:26
  68.4 2.2 %add_convert_fusion.7 = (bf16[128,1024]{1,0:T(8,128)(2,1)}, bf16[128,1024]{1,0:T(8,128)(2,1)S(1)}, bf16[128,1024]{1,0:T(8,128)(2,1)}) fusion(bf16[512,1024]{1,0:T(8,128)(2,1)} %collective-permute-done.6, s32[]{:T(128)S(6)} %select_n.80, bf16[1024,1024]{1,0:T(8,128)(2,1)S(1)} %convolution_convert_fusion.2, s32[]{:T(128)S(6)} %select_n.79, s32[]{:T(128)S(6)} %select_n.78, ...), kind=kLoop, calls=%fused_computation.30 | loop fusion | flops 1572864 | bytes 2359320 | tf_op jit(solution)/shard_map/convert_element_type | solution.py:80
  72.6 3.4 %collective-permute-start.9 = (bf16[128,1024]{1,0:T(8,128)(2,1)S(1)}, bf16[128,1024]{1,0:T(8,128)(2,1)}, u32[]{:S(2)}, u32[]{:S(2)}) collective-permute-start(bf16[128,1024]{1,0:T(8,128)(2,1)S(1)} %get-tuple-element.31), channel_id=1, source_target_pairs={{0,128},{64,192},{128,0},{192,64},{1,129},{65,193},{129,1},{193,65... | collective-permute-start | bytes 786440 | tf_op jit(solution)/shard_map/ppermute | solution.py:26
  77.2 1.8 copy.13
  82.6 3.2 %collective-permute-done.9 = bf16[128,1024]{1,0:T(8,128)(2,1)} collective-permute-done((bf16[128,1024]{1,0:T(8,128)(2,1)S(1)}, bf16[128,1024]{1,0:T(8,128)(2,1)}, u32[]{:S(2)}, u32[]{:S(2)}) %collective-permute-start.9) | collective-permute-done | bytes 262176 | tf_op jit(solution)/shard_map/ppermute | solution.py:26
  87.3 2.1 %collective-permute-start.11 = (bf16[128,512]{1,0:T(8,128)(2,1)S(1)}, bf16[128,512]{1,0:T(8,128)(2,1)S(1)}, u32[]{:S(2)}, u32[]{:S(2)}) collective-permute-start(bf16[128,512]{1,0:T(8,128)(2,1)S(1)} %multiply_convert_fusion.2), channel_id=1, source_target_pairs={{0,64},{64,128},{128,192},{192,0},{1,65},{65,129},{129,193},{193,1... | collective-permute-start | bytes 393224 | tf_op jit(solution)/shard_map/ppermute | solution.py:26
  89.4 4.2 %collective-permute-start.12 = (bf16[128,512]{1,0:T(8,128)(2,1)S(1)}, bf16[128,512]{1,0:T(8,128)(2,1)S(1)}, u32[]{:S(2)}, u32[]{:S(2)}) collective-permute-start(bf16[128,512]{1,0:T(8,128)(2,1)S(1)} %multiply_convert_fusion.2), channel_id=1, source_target_pairs={{0,128},{64,192},{128,0},{192,64},{1,129},{65,193},{129,1},{193,65... | collective-permute-start | bytes 393224 | tf_op jit(solution)/shard_map/ppermute | solution.py:26
  95.0 5.0 %all-to-all-start.2 = ((bf16[4,128,512]{2,1,0:T(8,128)(2,1)}), bf16[4,128,512]{2,1,0:T(8,128)(2,1)S(1)}, u32[]{:S(2)}, u32[]{:S(2)}) async-start(bf16[4,128,512]{2,1,0:T(8,128)(2,1)} %bitcast.12), calls=%async_computation.2 | async-start | bytes 1048576 | tf_op jit(solution)/shard_map/all_to_all | solution.py:30
  101.1 5.4 %all-to-all-done.2 = bf16[4,128,512]{2,1,0:T(8,128)(2,1)S(1)} async-done(((bf16[4,128,512]{2,1,0:T(8,128)(2,1)}), bf16[4,128,512]{2,1,0:T(8,128)(2,1)S(1)}, u32[]{:S(2)}, u32[]{:S(2)}) %all-to-all-start.2) | async-done | bytes 524320 | tf_op jit(solution)/shard_map/all_to_all | solution.py:30
  108.0 4.9 %all-to-all-start.3 = ((bf16[4,128,1024]{2,1,0:T(8,128)(2,1)}), bf16[4,128,1024]{2,1,0:T(8,128)(2,1)S(1)}, u32[]{:S(2)}, u32[]{:S(2)}) async-start(bf16[4,128,1024]{2,1,0:T(8,128)(2,1)} %broadcast_in_dim.22), calls=%async_computation.3 | async-start | bytes 2097152 | tf_op jit(solution)/shard_map/all_to_all | solution.py:30
  118.8 2.6 %fusion.4 = f32[512,1024]{1,0:T(8,128)} fusion(bf16[1024,1024]{1,0:T(8,128)(2,1)S(1)} %bitcast.42, bf16[512,512]{1,0:T(8,128)(2,1)S(1)} %get-tuple-element.67, bf16[512,512]{1,0:T(8,128)(2,1)S(1)} %get-tuple-element.66), kind=kOutput, calls=%fused_computation.18 | convolution fusion | flops 1075838976 | bytes 5242880 | tf_op jit(solution)/shard_map/dot_general | solution.py:21
  121.4 4.0 %collective-permute-done.15 = bf16[128,1024]{1,0:T(8,128)(2,1)S(1)} collective-permute-done((bf16[128,1024]{1,0:T(8,128)(2,1)S(1)}, bf16[128,1024]{1,0:T(8,128)(2,1)S(1)}, u32[]{:S(2)}, u32[]{:S(2)}) %collective-permute-start.15) | collective-permute-done | bytes 262176 | tf_op jit(solution)/shard_map/ppermute | solution.py:26
  125.7 1.8 all-to-all-done.3
  131.1 12.2 %collective-permute-done.18 = bf16[256,1024]{1,0:T(8,128)(2,1)S(1)} collective-permute-done((bf16[256,1024]{1,0:T(8,128)(2,1)S(1)}, bf16[256,1024]{1,0:T(8,128)(2,1)S(1)}, u32[]{:S(2)}, u32[]{:S(2)}) %collective-permute-start.18) | collective-permute-done | bytes 524320 | tf_op jit(solution)/shard_map/ppermute | solution.py:26
  143.3 2.4 %convolution_convert_fusion = bf16[1024,1024]{1,0:T(8,128)(2,1)S(1)} fusion(bf16[1024,1024]{1,0:T(8,128)(2,1)S(1)} %pad_maximum_fusion.2, bf16[1024,1024]{1,0:T(8,128)(2,1)S(1)} %copy-done.4), kind=kOutput, calls=%fused_computation.3 | convolution fusion | flops 2148532224 | bytes 6291456 | tf_op jit(solution)/shard_map/dot_general | solution.py:17
  149.9 2.1 %add_convert_fusion.1 = bf16[256,1024]{1,0:T(8,128)(2,1)} fusion(bf16[256,1024]{1,0:T(8,128)(2,1)S(1)} %collective-permute-done.19, bf16[256,1024]{1,0:T(8,128)(2,1)S(1)} %collective-permute-done.18, bf16[1024,1024]{1,0:T(8,128)(2,1)} %copy-done.5), kind=kLoop, calls=%fused_computation.10 | loop fusion | flops 1572864 | bytes 2097152 | tf_op jit(solution)/shard_map/convert_element_type | solution.py:128
  152.0 6.4 %all-to-all-start.4 = ((bf16[8,32,1024]{2,1,0:T(8,128)(2,1)}), bf16[8,32,1024]{2,1,0:T(8,128)(2,1)}, u32[]{:S(2)}, u32[]{:S(2)}) async-start(bf16[8,32,1024]{2,1,0:T(8,128)(2,1)} %bitcast.47), calls=%async_computation.4 | async-start | bytes 1048576 | tf_op jit(solution)/shard_map/all_to_all | solution.py:30
  159.8 1.8 pad_maximum_fusion.11
  162.5 3.2 %collective-permute-start.23 = (bf16[256,1024]{1,0:T(8,128)(2,1)}, bf16[256,1024]{1,0:T(8,128)(2,1)}, u32[]{:S(2)}, u32[]{:S(2)}) collective-permute-start(bf16[256,1024]{1,0:T(8,128)(2,1)} %pad_maximum_fusion.11), channel_id=1, source_target_pairs={{0,24},{8,0},{16,8},{24,16},{1,25},{9,1},{17,9},{25,17},{2,26},{10... | collective-permute-start | bytes 1572872 | tf_op jit(solution)/shard_map/ppermute | solution.py:26
  165.7 3.7 %fusion = f32[1024,512]{1,0:T(8,128)} fusion(bf16[1024,1024]{1,0:T(8,128)(2,1)S(1)} %copy-done.7, bf16[1024,256]{1,0:T(8,128)(2,1)S(1)} %bitcast.50, bf16[256,768]{1,0:T(8,128)(2,1)} %copy-done.19, bf16[256,768]{1,0:T(8,128)(2,1)} %copy-done.17, bf16[256,768]{1,0:T(8,128)(2,1)S(1)} %copy-done.16, bf16[256,768]{1,0:T(8,128)(2,1)S(1)} %bitcast.56), kind=kOutput, calls=%fused_computation.11 | convolution fusion | flops 1084227584 | bytes 5242880 | tf_op jit(solution)/shard_map/dot_general | solution.py:21
  169.4 2.6 %fusion.2 = f32[1024,512]{1,0:T(8,128)} fusion(bf16[1024,1024]{1,0:T(8,128)(2,1)S(1)} %copy-done.7, bf16[1024,256]{1,0:T(8,128)(2,1)S(1)} %bitcast.51, bf16[256,768]{1,0:T(8,128)(2,1)S(1)} %copy-done.20, bf16[256,768]{1,0:T(8,128)(2,1)S(1)} %copy-done.18, bf16[256,768]{1,0:T(8,128)(2,1)S(1)} %copy-done.16, bf16[256,768]{1,0:T(8,128)(2,1)S(1)} %bitcast.57), kind=kOutput, calls=%fused_computation.13 | convolution fusion | flops 1084227584 | bytes 5242880 | tf_op jit(solution)/shard_map/dot_general | solution.py:21
  172.0 3.3 %all-to-all-done.4 = bf16[8,32,1024]{2,1,0:T(8,128)(2,1)} async-done(((bf16[8,32,1024]{2,1,0:T(8,128)(2,1)}), bf16[8,32,1024]{2,1,0:T(8,128)(2,1)}, u32[]{:S(2)}, u32[]{:S(2)}) %all-to-all-start.4) | async-done | bytes 524320 | tf_op jit(solution)/shard_map/all_to_all | solution.py:30
  175.3 1.8 reduce_sum.34
  178.5 21.7 %all_to_all.54 = bf16[8,32,1024]{2,1,0:T(8,128)(2,1)S(1)} all-to-all(bf16[8,32,1024]{2,1,0:T(8,128)(2,1)S(1)} %bitcast.48), channel_id=1, replica_groups=mesh['x'=4,'core'=2,'y'=4,'z'=8] {'z'}, dimensions={0} | all-to-all | bytes 1048576 | tf_op jit(solution)/shard_map/all_to_all | solution.py:30
  (118 shorter events, 44.7 us)
Async XLA Ops:
  7.2 71.8 %copy-start = (bf16[512,1024]{1,0:T(8,128)(2,1)S(1)}, bf16[512,1024]{1,0:T(8,128)(2,1)}, u32[]{:S(2)}) copy-start(bf16[512,1024]{1,0:T(8,128)(2,1)} %param.8) | copy-start | bytes 3145732
  8.9 23.2 %all-to-all-start = ((bf16[8,32,768]{2,1,0:T(8,128)(2,1)}), bf16[8,32,768]{2,1,0:T(8,128)(2,1)S(1)}, u32[]{:S(2)}, u32[]{:S(2)}) async-start(bf16[8,32,768]{2,1,0:T(8,128)(2,1)} %broadcast_in_dim.8), calls=%async_computation | async-start | bytes 786432 | tf_op jit(solution)/shard_map/all_to_all | solution.py:30
  17.4 59.8 %all-gather.3.cloned.1.call-start = ((), (), s32[]{:S(2)}) async-start(), calls=%async_computation.6 | async-start | bytes 2359296 | tf_op jit(solution)/shard_map/all_gather | solution.py:144
  19.0 8.8 %collective-permute-start = (bf16[32,1280]{1,0:T(8,128)(2,1)S(1)}, bf16[32,1280]{1,0:T(8,128)(2,1)S(1)}, u32[]{:S(2)}, u32[]{:S(2)}) collective-permute-start(bf16[32,1280]{1,0:T(8,128)(2,1)S(1)} %get-tuple-element.75), channel_id=1, source_target_pairs={{0,8},{8,16},{16,24},{24,0},{1,9},{9,17},{17,25},{25,1},{2,10},{10... | collective-permute-start | bytes 245768 | tf_op jit(solution)/shard_map/ppermute | solution.py:26
  20.7 7.1 %collective-permute-start.1 = (bf16[32,1280]{1,0:T(8,128)(2,1)S(1)}, bf16[32,1280]{1,0:T(8,128)(2,1)S(1)}, u32[]{:S(2)}, u32[]{:S(2)}) collective-permute-start(bf16[32,1280]{1,0:T(8,128)(2,1)S(1)} %get-tuple-element.75), channel_id=1, source_target_pairs={{0,16},{8,24},{16,0},{24,8},{1,17},{9,25},{17,1},{25,9},{2,18},{10... | collective-permute-start | bytes 245768 | tf_op jit(solution)/shard_map/ppermute | solution.py:26
  23.6 4.4 %collective-permute-start.2 = (bf16[32,1280]{1,0:T(8,128)(2,1)S(1)}, bf16[32,1280]{1,0:T(8,128)(2,1)S(1)}, u32[]{:S(2)}, u32[]{:S(2)}) collective-permute-start(bf16[32,1280]{1,0:T(8,128)(2,1)S(1)} %get-tuple-element.75), channel_id=1, source_target_pairs={{0,24},{8,0},{16,8},{24,16},{1,25},{9,1},{17,9},{25,17},{2,26},{10... | collective-permute-start | bytes 245768 | tf_op jit(solution)/shard_map/ppermute | solution.py:26
  32.1 32.1 %copy-start.11 = (bf16[8,32,768]{2,1,0:T(8,128)(2,1)}, bf16[8,32,768]{2,1,0:T(8,128)(2,1)S(1)}, u32[]{:S(2)}) copy-start(bf16[8,32,768]{2,1,0:T(8,128)(2,1)S(1)} %all-to-all-done) | copy-start | bytes 1179652
  33.7 24.4 %all-to-all-start.1 = ((bf16[8,128,256]{2,1,0:T(8,128)(2,1)}), bf16[8,128,256]{2,1,0:T(8,128)(2,1)S(1)}, u32[]{:S(2)}, u32[]{:S(2)}) async-start(bf16[8,128,256]{2,1,0:T(8,128)(2,1)} %broadcast_in_dim.10), calls=%async_computation.1 | async-start | bytes 1048576 | tf_op jit(solution)/shard_map/all_to_all | solution.py:30
  37.2 21.0 %collective-permute-start.3 = (bf16[256,768]{1,0:T(8,128)(2,1)S(1)}, bf16[256,768]{1,0:T(8,128)(2,1)S(1)}, u32[]{:S(2)}, u32[]{:S(2)}) collective-permute-start(bf16[256,768]{1,0:T(8,128)(2,1)S(1)} %bitcast.52), channel_id=1, source_target_pairs={{0,8},{8,16},{16,24},{24,0},{1,9},{9,17},{17,25},{25,1},{2,10},{10... | collective-permute-start | bytes 1179656 | tf_op jit(solution)/shard_map/ppermute | solution.py:26
  38.9 19.4 %collective-permute-start.4 = (bf16[256,768]{1,0:T(8,128)(2,1)S(1)}, bf16[256,768]{1,0:T(8,128)(2,1)S(1)}, u32[]{:S(2)}, u32[]{:S(2)}) collective-permute-start(bf16[256,768]{1,0:T(8,128)(2,1)S(1)} %bitcast.53), channel_id=1, source_target_pairs={{0,16},{8,24},{16,0},{24,8},{1,17},{9,25},{17,1},{25,9},{2,18},{10... | collective-permute-start | bytes 1179656 | tf_op jit(solution)/shard_map/ppermute | solution.py:26
  41.8 16.5 %collective-permute-start.5 = (bf16[256,768]{1,0:T(8,128)(2,1)S(1)}, bf16[256,768]{1,0:T(8,128)(2,1)S(1)}, u32[]{:S(2)}, u32[]{:S(2)}) collective-permute-start(bf16[256,768]{1,0:T(8,128)(2,1)S(1)} %bitcast.54), channel_id=1, source_target_pairs={{0,24},{8,0},{16,8},{24,16},{1,25},{9,1},{17,9},{25,17},{2,26},{10... | collective-permute-start | bytes 1179656 | tf_op jit(solution)/shard_map/ppermute | solution.py:26
  65.4 3.0 %collective-permute-start.6 = (bf16[512,1024]{1,0:T(8,128)(2,1)}, bf16[512,1024]{1,0:T(8,128)(2,1)}, u32[]{:S(2)}, u32[]{:S(2)}) collective-permute-start(bf16[512,1024]{1,0:T(8,128)(2,1)} %constant_dynamic-slice_fusion), channel_id=1, source_target_pairs={{0,32},{32,0},{1,33},{33,1},{2,34},{34,2},{3,35},{35,3},{4,36},{36... | collective-permute-start | bytes 3145736 | tf_op jit(solution)/shard_map/ppermute | solution.py:26
  70.6 10.6 %collective-permute-start.10 = (bf16[128,1024]{1,0:T(8,128)(2,1)}, bf16[128,1024]{1,0:T(8,128)(2,1)S(1)}, u32[]{:S(2)}, u32[]{:S(2)}) collective-permute-start(bf16[128,1024]{1,0:T(8,128)(2,1)} %get-tuple-element.32), channel_id=1, source_target_pairs={{0,192},{64,0},{128,64},{192,128},{1,193},{65,1},{129,65},{193,129... | collective-permute-start | bytes 786440 | tf_op jit(solution)/shard_map/ppermute | solution.py:26
  71.1 10.1 %collective-permute-start.8 = (bf16[128,1024]{1,0:T(8,128)(2,1)}, bf16[128,1024]{1,0:T(8,128)(2,1)S(1)}, u32[]{:S(2)}, u32[]{:S(2)}) collective-permute-start(bf16[128,1024]{1,0:T(8,128)(2,1)} %get-tuple-element.30), channel_id=1, source_target_pairs={{0,64},{64,128},{128,192},{192,0},{1,65},{65,129},{129,193},{193,1... | collective-permute-start | bytes 786440 | tf_op jit(solution)/shard_map/ppermute | solution.py:26
  72.6 13.2 %collective-permute-start.9 = (bf16[128,1024]{1,0:T(8,128)(2,1)S(1)}, bf16[128,1024]{1,0:T(8,128)(2,1)}, u32[]{:S(2)}, u32[]{:S(2)}) collective-permute-start(bf16[128,1024]{1,0:T(8,128)(2,1)S(1)} %get-tuple-element.31), channel_id=1, source_target_pairs={{0,128},{64,192},{128,0},{192,64},{1,129},{65,193},{129,1},{193,65... | collective-permute-start | bytes 786440 | tf_op jit(solution)/shard_map/ppermute | solution.py:26
  81.2 12.8 %collective-permute-start.7 = (bf16[512,512]{1,0:T(8,128)(2,1)}, bf16[512,512]{1,0:T(8,128)(2,1)S(1)}, u32[]{:S(2)}, u32[]{:S(2)}) collective-permute-start(bf16[512,512]{1,0:T(8,128)(2,1)} %broadcast_select_fusion.4), channel_id=1, source_target_pairs={{0,32},{32,0},{1,33},{33,1},{2,34},{34,2},{3,35},{35,3},{4,36},{36... | collective-permute-start | bytes 1572872 | tf_op jit(solution)/shard_map/ppermute | solution.py:26
  87.3 12.7 %collective-permute-start.11 = (bf16[128,512]{1,0:T(8,128)(2,1)S(1)}, bf16[128,512]{1,0:T(8,128)(2,1)S(1)}, u32[]{:S(2)}, u32[]{:S(2)}) collective-permute-start(bf16[128,512]{1,0:T(8,128)(2,1)S(1)} %multiply_convert_fusion.2), channel_id=1, source_target_pairs={{0,64},{64,128},{128,192},{192,0},{1,65},{65,129},{129,193},{193,1... | collective-permute-start | bytes 393224 | tf_op jit(solution)/shard_map/ppermute | solution.py:26
  89.4 10.6 %collective-permute-start.12 = (bf16[128,512]{1,0:T(8,128)(2,1)S(1)}, bf16[128,512]{1,0:T(8,128)(2,1)S(1)}, u32[]{:S(2)}, u32[]{:S(2)}) collective-permute-start(bf16[128,512]{1,0:T(8,128)(2,1)S(1)} %multiply_convert_fusion.2), channel_id=1, source_target_pairs={{0,128},{64,192},{128,0},{192,64},{1,129},{65,193},{129,1},{193,65... | collective-permute-start | bytes 393224 | tf_op jit(solution)/shard_map/ppermute | solution.py:26
  93.6 6.5 %collective-permute-start.13 = (bf16[128,512]{1,0:T(8,128)(2,1)S(1)}, bf16[128,512]{1,0:T(8,128)(2,1)}, u32[]{:S(2)}, u32[]{:S(2)}) collective-permute-start(bf16[128,512]{1,0:T(8,128)(2,1)S(1)} %multiply_convert_fusion.2), channel_id=1, source_target_pairs={{0,192},{64,0},{128,64},{192,128},{1,193},{65,1},{129,65},{193,129... | collective-permute-start | bytes 393224 | tf_op jit(solution)/shard_map/ppermute | solution.py:26
  95.0 11.6 %all-to-all-start.2 = ((bf16[4,128,512]{2,1,0:T(8,128)(2,1)}), bf16[4,128,512]{2,1,0:T(8,128)(2,1)S(1)}, u32[]{:S(2)}, u32[]{:S(2)}) async-start(bf16[4,128,512]{2,1,0:T(8,128)(2,1)} %bitcast.12), calls=%async_computation.2 | async-start | bytes 1048576 | tf_op jit(solution)/shard_map/all_to_all | solution.py:30
  106.6 6.3 %collective-permute-start.14 = (bf16[512,512]{1,0:T(8,128)(2,1)S(1)}, bf16[512,512]{1,0:T(8,128)(2,1)}, u32[]{:S(2)}, u32[]{:S(2)}) collective-permute-start(bf16[512,512]{1,0:T(8,128)(2,1)S(1)} %pad_maximum_fusion.7), channel_id=1, source_target_pairs={{0,32},{32,0},{1,33},{33,1},{2,34},{34,2},{3,35},{35,3},{4,36},{36... | collective-permute-start | bytes 1572872 | tf_op jit(solution)/shard_map/ppermute | solution.py:26
  108.0 19.5 %all-to-all-start.3 = ((bf16[4,128,1024]{2,1,0:T(8,128)(2,1)}), bf16[4,128,1024]{2,1,0:T(8,128)(2,1)S(1)}, u32[]{:S(2)}, u32[]{:S(2)}) async-start(bf16[4,128,1024]{2,1,0:T(8,128)(2,1)} %broadcast_in_dim.22), calls=%async_computation.3 | async-start | bytes 2097152 | tf_op jit(solution)/shard_map/all_to_all | solution.py:30
  115.4 10.0 %collective-permute-start.15 = (bf16[128,1024]{1,0:T(8,128)(2,1)S(1)}, bf16[128,1024]{1,0:T(8,128)(2,1)S(1)}, u32[]{:S(2)}, u32[]{:S(2)}) collective-permute-start(bf16[128,1024]{1,0:T(8,128)(2,1)S(1)} %get-tuple-element.63), channel_id=1, source_target_pairs={{0,8},{8,16},{16,24},{24,0},{1,9},{9,17},{17,25},{25,1},{2,10},{10... | collective-permute-start | bytes 786440 | tf_op jit(solution)/shard_map/ppermute | solution.py:26
  117.1 8.3 %collective-permute-start.16 = (bf16[128,1024]{1,0:T(8,128)(2,1)S(1)}, bf16[128,1024]{1,0:T(8,128)(2,1)S(1)}, u32[]{:S(2)}, u32[]{:S(2)}) collective-permute-start(bf16[128,1024]{1,0:T(8,128)(2,1)S(1)} %get-tuple-element.61), channel_id=1, source_target_pairs={{0,24},{8,0},{16,8},{24,16},{1,25},{9,1},{17,9},{25,17},{2,26},{10... | collective-permute-start | bytes 786440 | tf_op jit(solution)/shard_map/ppermute | solution.py:26
  127.5 3.2 %collective-permute-start.17 = (bf16[512,1024]{1,0:T(8,128)(2,1)S(1)}, bf16[512,1024]{1,0:T(8,128)(2,1)S(1)}, u32[]{:S(2)}, u32[]{:S(2)}) collective-permute-start(bf16[512,1024]{1,0:T(8,128)(2,1)S(1)} %bitcast.43), channel_id=1, source_target_pairs={{0,32},{32,0},{1,33},{33,1},{2,34},{34,2},{3,35},{35,3},{4,36},{36... | collective-permute-start | bytes 3145736 | tf_op jit(solution)/shard_map/ppermute | solution.py:26
  127.5 15.8 %collective-permute-start.18 = (bf16[256,1024]{1,0:T(8,128)(2,1)S(1)}, bf16[256,1024]{1,0:T(8,128)(2,1)S(1)}, u32[]{:S(2)}, u32[]{:S(2)}) collective-permute-start(bf16[256,1024]{1,0:T(8,128)(2,1)S(1)} %get-tuple-element.36), channel_id=1, source_target_pairs={{0,8},{8,16},{16,24},{24,0},{1,9},{9,17},{17,25},{25,1},{2,10},{10... | collective-permute-start | bytes 1572872 | tf_op jit(solution)/shard_map/ppermute | solution.py:26
  129.1 14.2 %collective-permute-start.19 = (bf16[256,1024]{1,0:T(8,128)(2,1)S(1)}, bf16[256,1024]{1,0:T(8,128)(2,1)S(1)}, u32[]{:S(2)}, u32[]{:S(2)}) collective-permute-start(bf16[256,1024]{1,0:T(8,128)(2,1)S(1)} %get-tuple-element.37), channel_id=1, source_target_pairs={{0,24},{8,0},{16,8},{24,16},{1,25},{9,1},{17,9},{25,17},{2,26},{10... | collective-permute-start | bytes 1572872 | tf_op jit(solution)/shard_map/ppermute | solution.py:26
  146.6 11.8 %collective-permute-start.20 = (bf16[128,1024]{1,0:T(8,128)(2,1)}, bf16[128,1024]{1,0:T(8,128)(2,1)}, u32[]{:S(2)}, u32[]{:S(2)}) collective-permute-start(bf16[128,1024]{1,0:T(8,128)(2,1)} %get-tuple-element.55), channel_id=1, source_target_pairs={{0,8},{8,16},{16,24},{24,0},{1,9},{9,17},{17,25},{25,1},{2,10},{10... | collective-permute-start | bytes 786440 | tf_op jit(solution)/shard_map/ppermute | solution.py:26
  148.2 10.3 %collective-permute-start.21 = (bf16[128,1024]{1,0:T(8,128)(2,1)}, bf16[128,1024]{1,0:T(8,128)(2,1)}, u32[]{:S(2)}, u32[]{:S(2)}) collective-permute-start(bf16[128,1024]{1,0:T(8,128)(2,1)} %get-tuple-element.53), channel_id=1, source_target_pairs={{0,24},{8,0},{16,8},{24,16},{1,25},{9,1},{17,9},{25,17},{2,26},{10... | collective-permute-start | bytes 786440 | tf_op jit(solution)/shard_map/ppermute | solution.py:26
  152.0 23.3 %all-to-all-start.4 = ((bf16[8,32,1024]{2,1,0:T(8,128)(2,1)}), bf16[8,32,1024]{2,1,0:T(8,128)(2,1)}, u32[]{:S(2)}, u32[]{:S(2)}) async-start(bf16[8,32,1024]{2,1,0:T(8,128)(2,1)} %bitcast.47), calls=%async_computation.4 | async-start | bytes 1048576 | tf_op jit(solution)/shard_map/all_to_all | solution.py:30
  162.5 14.6 %collective-permute-start.22 = (bf16[256,1024]{1,0:T(8,128)(2,1)}, bf16[256,1024]{1,0:T(8,128)(2,1)}, u32[]{:S(2)}, u32[]{:S(2)}) collective-permute-start(bf16[256,1024]{1,0:T(8,128)(2,1)} %pad_maximum_fusion.10), channel_id=1, source_target_pairs={{0,8},{8,16},{16,24},{24,0},{1,9},{9,17},{17,25},{25,1},{2,10},{10... | collective-permute-start | bytes 1572872 | tf_op jit(solution)/shard_map/ppermute | solution.py:26
  162.5 14.6 %collective-permute-start.23 = (bf16[256,1024]{1,0:T(8,128)(2,1)}, bf16[256,1024]{1,0:T(8,128)(2,1)}, u32[]{:S(2)}, u32[]{:S(2)}) collective-permute-start(bf16[256,1024]{1,0:T(8,128)(2,1)} %pad_maximum_fusion.11), channel_id=1, source_target_pairs={{0,24},{8,0},{16,8},{24,16},{1,25},{9,1},{17,9},{25,17},{2,26},{10... | collective-permute-start | bytes 1572872 | tf_op jit(solution)/shard_map/ppermute | solution.py:26
  (19 other events, 119.2 us)
Sparse Core Ops, SparseCore 0:
  33.0 44.2 all-gather.2

commit v9 on v8

--- a/solution.py
+++ b/solution.py
@@ -124,8 +124,11 @@
     return shift(to_right, "y", 1), shift(to_left, "y", 3)
 
 
-def sum_y(own, from_left, from_right):
-    return (own.astype(F32) + from_left.astype(F32) + from_right.astype(F32)).astype(BF)
+def sum_y(own, *moved):
+    total = own.astype(F32)
+    for piece in moved:
+        total = total + piece.astype(F32)
+    return total.astype(BF)
 
 
 def reduce_z(total):
@@ -136,15 +139,11 @@
     width = gate_weight.shape[1]
     both_weights = jnp.concatenate([gate_weight, up_weight], axis=1)
 
-    features = tokens.shape[1]
-    main = features - features // 4
-    tokens_z = gather(tokens[:, :main], "z")
-    crossed = jnp.stack(gather_y(jnp.concatenate([out_grad, tokens[:, main:]], axis=1)))
-    tokens_z, crossed, both_weights = lax.optimization_barrier((tokens_z, crossed, both_weights))
-    all_grads = lax.all_gather(crossed[:, :, :features], "z", axis=0, tiled=False)
-    rest = gather(crossed[:, :, features:].reshape(-1, features - main), "z")
-    rest = jnp.swapaxes(rest.reshape(Z, Y, -1, features - main), 0, 1).reshape(-1, features - main)
-    all_tokens = jnp.concatenate([jnp.concatenate(gather_y(tokens_z), axis=0), rest], axis=1)
+    tokens_z = gather(tokens, "z")
+    grads_y = jnp.stack(gather_y(out_grad))
+    tokens_z, grads_y, both_weights = lax.optimization_barrier((tokens_z, grads_y, both_weights))
+    all_tokens = jnp.concatenate(gather_y(tokens_z), axis=0)
+    all_grads = lax.all_gather(grads_y, "z", axis=0, tiled=False)
 
     gate_up = with_layout_constraint(product(all_tokens, both_weights).astype(BF), Layout((0, 1)))
     gate_up, sent = reduce_row(gate_up)
@@ -170,22 +169,20 @@
     gate_grad = (hidden_grad * up_value * sigmoid_gate * (1.0 + gate_value * (1.0 - sigmoid_gate))).astype(BF)
     up_grad = (hidden_grad * silu_gate).astype(BF)
     both_half = gather(jnp.concatenate([gate_grad, up_grad], axis=1), "x")
-    down_weight_grad = product_left_t(hidden, all_grads)
-    both_half, down_weight_grad, to_right, to_left = lax.optimization_barrier(
-        (both_half, down_weight_grad, to_right, to_left)
-    )
+    both_half, to_right, to_left = lax.optimization_barrier((both_half, to_right, to_left))
     both_grads = after(gather_core(both_half), *output_near)
 
-    input_pieces = split_y(product_right_t(both_grads, both_weights).astype(BF))
-    input_near = move_y_near(*add_y_far(input_pieces, *reduce_y_far(input_pieces)))
-    output_total = reduce_z(sum_y(output_pieces[0], *output_near))
-    weight_grads = (
-        product_left_t(all_tokens, both_grads[:, :width]),
-        product_left_t(all_tokens, both_grads[:, width:]),
-        down_weight_grad,
+    input_pieces = lax.optimization_barrier(split_y(product_right_t(both_grads, both_weights).astype(BF)))
+    input_moved = [shift(input_pieces[1], "y", 3), shift(input_pieces[3], "y", 1), shift(input_pieces[2], "y", 2)]
+    down_weight_grad = product_left_t(after(hidden, *input_pieces), all_grads)
+    gate_weight_grad = product_left_t(all_tokens, both_grads[:, :width])
+    up_weight_grad = product_left_t(all_tokens, both_grads[:, width:])
+    output_total = reduce_z(sum_y(after(output_pieces[0], *input_pieces), *output_near))
+    input_moved, gate_weight_grad, up_weight_grad, down_weight_grad, output_total = lax.optimization_barrier(
+        (input_moved, gate_weight_grad, up_weight_grad, down_weight_grad, output_total)
     )
-    input_near, weight_grads, output_total = lax.optimization_barrier((input_near, weight_grads, output_total))
-    return (output_total, reduce_z(sum_y(input_pieces[0], *input_near))) + weight_grads
+    input_total = sum_y(input_pieces[0], *input_moved)
+    return (output_total, reduce_z(input_total), gate_weight_grad, up_weight_grad, down_weight_grad)
 
 
 def solution(mesh):

time: 209 us -> 204 us (0.976)
  waiting for transfers between devices: 53.5 us -> 74.7 us
  starting transfers between devices: 65.2 us -> 53.2 us
  blocking collectives: 21.7 us -> 17.4 us
  local copies, waits for them, and re-layouts: 12.3 us -> 8.22 us
  other arithmetic: 22.5 us -> 18.7 us
    ppermute x24 -> x23, waiting for transfers between devices: 22.7 us -> 54.9 us  [shift(): lax.ppermute(block, axis, [(i, (i + step) % size) for i in range(size)])]
    all_to_all x5 -> x4, waiting for transfers between devices: 29.5 us -> 19.7 us  [exchange(): return lax.all_to_all(blocks, axis, split_axis=0, concat_axis=0, tiled=True)]
    ppermute x24 -> x23, starting transfers between devices: 36.9 us -> 30.1 us  [shift(): lax.ppermute(block, axis, [(i, (i + step) % size) for i in range(size)])]
    all_to_all x5 -> x4, starting transfers between devices: 28.3 us -> 23.1 us  [exchange(): return lax.all_to_all(blocks, axis, split_axis=0, concat_axis=0, tiled=True)]
    all_to_all x1, blocking collectives: 21.7 us -> 17.4 us  [exchange(): return lax.all_to_all(blocks, axis, split_axis=0, concat_axis=0, tiled=True)]
    unnamed x42 -> x37, local copies, waits for them, and re-layouts: 3.09 us -> 0.92 us
  transfers between devices with their start and end apart: 30 -> 28, of which waited for: 12 -> 14; matrix products, arithmetic and copies ran while one was open for 20% -> 17% of each run, Pallas kernels for 0% -> 0%
where the time goes in v9:
time: 204 us
  waiting for transfers between devices  74.7 us (37%)
  starting transfers between devices  53.2 us (26%)
  other arithmetic  18.7 us (9%)
  blocking collectives  17.4 us (9%)
  matrix products  17.1 us (8%)
  between operations  14.4 us (7%)
  local copies, waits for them, and re-layouts  8.22 us (4%)
    ppermute x23, waiting for transfers between devices, shift(): lax.ppermute(block, axis, [(i, (i + step) % size) for i in range(size)])  54.9 us
    ppermute x23, starting transfers between devices, shift(): lax.ppermute(block, axis, [(i, (i + step) % size) for i in range(size)])  30.1 us
    all_to_all x4, starting transfers between devices, exchange(): return lax.all_to_all(blocks, axis, split_axis=0, concat_axis=0, tiled=True)  23.1 us
    all_to_all x4, waiting for transfers between devices, exchange(): return lax.all_to_all(blocks, axis, split_axis=0, concat_axis=0, tiled=True)  19.7 us
    all_to_all x1, blocking collectives, exchange(): return lax.all_to_all(blocks, axis, split_axis=0, concat_axis=0, tiled=True)  17.4 us
    dot_general x3, matrix products, product_left_t(): lax.dot_general(left_side, right_side, (((0,), (0,)), ((), ())), preferre...  9.83 us
  transfers between devices with their start and end apart: 28, of which 14 were waited for; matrix products, arithmetic and copies ran while one was open for 17% of the time, Pallas kernels for 0%

profile of v9, /device:TPU:2, one launch (start us, length us, event | category | flops | bytes accessed | tf_op | source)
XLA Modules:
  0.0 203.8 jit_solution(5180160817617455218)
XLA Ops:
  7.2 1.8 broadcast_in_dim.4
  9.0 8.5 %all-to-all-start = ((bf16[8,32,1024]{2,1,0:T(8,128)(2,1)}), bf16[8,32,1024]{2,1,0:T(8,128)(2,1)S(1)}, u32[]{:S(2)}, u32[]{:S(2)}) async-start(bf16[8,32,1024]{2,1,0:T(8,128)(2,1)} %broadcast_in_dim.4), calls=%async_computation | async-start | bytes 1048576 | tf_op jit(solution)/shard_map/all_to_all | solution.py:30
  20.9 2.0 collective-permute-start.1
  22.8 2.9 %pad_maximum_fusion = bf16[1024,1024]{1,0:T(8,128)(2,1)} fusion(bf16[1024,512]{1,0:T(8,128)(2,1)S(1)} %copy-done.11, bf16[1024,512]{1,0:T(8,128)(2,1)} %param.6), kind=kLoop, calls=%fused_computation | loop fusion | flops 4194304 | bytes 4194304 | tf_op jit(solution)/shard_map/concatenate | solution.py:140
  27.6 7.4 %all-to-all-done = bf16[8,32,1024]{2,1,0:T(8,128)(2,1)S(1)} async-done(((bf16[8,32,1024]{2,1,0:T(8,128)(2,1)}), bf16[8,32,1024]{2,1,0:T(8,128)(2,1)S(1)}, u32[]{:S(2)}, u32[]{:S(2)}) %all-to-all-start) | async-done | bytes 524320 | tf_op jit(solution)/shard_map/all_to_all | solution.py:30
  36.7 2.9 %collective-permute-start.4 = (bf16[256,1024]{1,0:T(8,128)(2,1)S(1)}, bf16[256,1024]{1,0:T(8,128)(2,1)S(1)}, u32[]{:S(2)}, u32[]{:S(2)}) collective-permute-start(bf16[256,1024]{1,0:T(8,128)(2,1)S(1)} %bitcast.46), channel_id=1, source_target_pairs={{0,16},{8,24},{16,0},{24,8},{1,17},{9,25},{17,1},{25,9},{2,18},{10... | collective-permute-start | bytes 1572872 | tf_op jit(solution)/shard_map/ppermute | solution.py:26
  41.0 9.3 %collective-permute-done.3 = bf16[256,1024]{1,0:T(8,128)(2,1)S(1)} collective-permute-done((bf16[256,1024]{1,0:T(8,128)(2,1)S(1)}, bf16[256,1024]{1,0:T(8,128)(2,1)S(1)}, u32[]{:S(2)}, u32[]{:S(2)}) %collective-permute-start.3) | collective-permute-done | bytes 524320 | tf_op jit(solution)/shard_map/ppermute | solution.py:26
  50.3 12.4 %collective-permute-done.4 = bf16[256,1024]{1,0:T(8,128)(2,1)S(1)} collective-permute-done((bf16[256,1024]{1,0:T(8,128)(2,1)S(1)}, bf16[256,1024]{1,0:T(8,128)(2,1)S(1)}, u32[]{:S(2)}, u32[]{:S(2)}) %collective-permute-start.4) | collective-permute-done | bytes 524320 | tf_op jit(solution)/shard_map/ppermute | solution.py:26
  62.7 2.3 %convolution_convert_fusion.2 = bf16[1024,1024]{1,0:T(8,128)(2,1)S(1)} fusion(bf16[1024,1024]{1,0:T(8,128)(2,1)S(1)} %constant_dynamic-update-slice_fusion, bf16[1024,1024]{1,0:T(8,128)(2,1)S(1)} %copy-done.5), kind=kOutput, calls=%fused_computation.4 | convolution fusion | flops 2148532224 | bytes 6291456 | tf_op jit(solution)/shard_map/dot_general | solution.py:13
  66.4 3.0 %collective-permute-done.6 = bf16[512,1024]{1,0:T(8,128)(2,1)} collective-permute-done((bf16[512,1024]{1,0:T(8,128)(2,1)}, bf16[512,1024]{1,0:T(8,128)(2,1)}, u32[]{:S(2)}, u32[]{:S(2)}) %collective-permute-start.6) | collective-permute-done | bytes 1048608 | tf_op jit(solution)/shard_map/ppermute | solution.py:26
  69.4 2.2 %add_convert_fusion.5 = (bf16[128,1024]{1,0:T(8,128)(2,1)S(1)}, bf16[128,1024]{1,0:T(8,128)(2,1)}, bf16[128,1024]{1,0:T(8,128)(2,1)}) fusion(bf16[512,1024]{1,0:T(8,128)(2,1)} %collective-permute-done.6, s32[]{:T(128)S(6)} %select_n.80, bf16[1024,1024]{1,0:T(8,128)(2,1)S(1)} %convolution_convert_fusion.2, s32[]{:T(128)S(6)} %select_n.79, s32[]{:T(128)S(6)} %select_n.78, ...), kind=kLoop, calls=%fused_computation.24 | loop fusion | flops 1572864 | bytes 2359320 | tf_op jit(solution)/shard_map/convert_element_type | solution.py:80
  74.2 2.2 %collective-permute-start.10 = (bf16[128,1024]{1,0:T(8,128)(2,1)S(1)}, bf16[128,1024]{1,0:T(8,128)(2,1)}, u32[]{:S(2)}, u32[]{:S(2)}) collective-permute-start(bf16[128,1024]{1,0:T(8,128)(2,1)S(1)} %get-tuple-element.36), channel_id=1, source_target_pairs={{0,192},{64,0},{128,64},{192,128},{1,193},{65,1},{129,65},{193,129... | collective-permute-start | bytes 786440 | tf_op jit(solution)/shard_map/ppermute | solution.py:26
  80.9 3.0 %collective-permute-done.9 = bf16[128,1024]{1,0:T(8,128)(2,1)S(1)} collective-permute-done((bf16[128,1024]{1,0:T(8,128)(2,1)}, bf16[128,1024]{1,0:T(8,128)(2,1)S(1)}, u32[]{:S(2)}, u32[]{:S(2)}) %collective-permute-start.9) | collective-permute-done | bytes 262176 | tf_op jit(solution)/shard_map/ppermute | solution.py:26
  84.7 3.0 %collective-permute-done.10 = bf16[128,1024]{1,0:T(8,128)(2,1)} collective-permute-done((bf16[128,1024]{1,0:T(8,128)(2,1)S(1)}, bf16[128,1024]{1,0:T(8,128)(2,1)}, u32[]{:S(2)}, u32[]{:S(2)}) %collective-permute-start.10) | collective-permute-done | bytes 262176 | tf_op jit(solution)/shard_map/ppermute | solution.py:26
  89.3 2.3 %collective-permute-start.12 = (bf16[128,512]{1,0:T(8,128)(2,1)S(1)}, bf16[128,512]{1,0:T(8,128)(2,1)S(1)}, u32[]{:S(2)}, u32[]{:S(2)}) collective-permute-start(bf16[128,512]{1,0:T(8,128)(2,1)S(1)} %multiply_convert_fusion.2), channel_id=1, source_target_pairs={{0,128},{64,192},{128,0},{192,64},{1,129},{65,193},{129,1},{193,65... | collective-permute-start | bytes 393224 | tf_op jit(solution)/shard_map/ppermute | solution.py:26
  94.5 6.2 %all-to-all-start.1 = ((bf16[4,128,512]{2,1,0:T(8,128)(2,1)}), bf16[4,128,512]{2,1,0:T(8,128)(2,1)S(1)}, u32[]{:S(2)}, u32[]{:S(2)}) async-start(bf16[4,128,512]{2,1,0:T(8,128)(2,1)} %bitcast.8), calls=%async_computation.1 | async-start | bytes 1048576 | tf_op jit(solution)/shard_map/all_to_all | solution.py:30
  101.9 5.5 %all-to-all-done.1 = bf16[4,128,512]{2,1,0:T(8,128)(2,1)S(1)} async-done(((bf16[4,128,512]{2,1,0:T(8,128)(2,1)}), bf16[4,128,512]{2,1,0:T(8,128)(2,1)S(1)}, u32[]{:S(2)}, u32[]{:S(2)}) %all-to-all-start.1) | async-done | bytes 524320 | tf_op jit(solution)/shard_map/all_to_all | solution.py:30
  108.8 4.9 %all-to-all-start.2 = ((bf16[4,128,1024]{2,1,0:T(8,128)(2,1)}), bf16[4,128,1024]{2,1,0:T(8,128)(2,1)S(1)}, u32[]{:S(2)}, u32[]{:S(2)}) async-start(bf16[4,128,1024]{2,1,0:T(8,128)(2,1)} %broadcast_in_dim.5), calls=%async_computation.2 | async-start | bytes 2097152 | tf_op jit(solution)/shard_map/all_to_all | solution.py:30
  116.2 2.2 %collective-permute-start.16 = (bf16[128,1024]{1,0:T(8,128)(2,1)S(1)}, bf16[128,1024]{1,0:T(8,128)(2,1)S(1)}, u32[]{:S(2)}, u32[]{:S(2)}) collective-permute-start(bf16[128,1024]{1,0:T(8,128)(2,1)S(1)} %get-tuple-element.67), channel_id=1, source_target_pairs={{0,24},{8,0},{16,8},{24,16},{1,25},{9,1},{17,9},{25,17},{2,26},{10... | collective-permute-start | bytes 786440 | tf_op jit(solution)/shard_map/ppermute | solution.py:26
  118.4 6.3 %collective-permute-done.16 = bf16[128,1024]{1,0:T(8,128)(2,1)S(1)} collective-permute-done((bf16[128,1024]{1,0:T(8,128)(2,1)S(1)}, bf16[128,1024]{1,0:T(8,128)(2,1)S(1)}, u32[]{:S(2)}, u32[]{:S(2)}) %collective-permute-start.16) | collective-permute-done | bytes 262176 | tf_op jit(solution)/shard_map/ppermute | solution.py:26
  124.8 3.0 %collective-permute-done.15 = bf16[128,1024]{1,0:T(8,128)(2,1)S(1)} collective-permute-done((bf16[128,1024]{1,0:T(8,128)(2,1)S(1)}, bf16[128,1024]{1,0:T(8,128)(2,1)S(1)}, u32[]{:S(2)}, u32[]{:S(2)}) %collective-permute-start.15) | collective-permute-done | bytes 262176 | tf_op jit(solution)/shard_map/ppermute | solution.py:26
  129.5 2.8 %collective-permute-start.19 = (bf16[256,1024]{1,0:T(8,128)(2,1)}, bf16[256,1024]{1,0:T(8,128)(2,1)S(1)}, u32[]{:S(2)}, u32[]{:S(2)}) collective-permute-start(bf16[256,1024]{1,0:T(8,128)(2,1)} %get-tuple-element.41), channel_id=1, source_target_pairs={{0,24},{8,0},{16,8},{24,16},{1,25},{9,1},{17,9},{25,17},{2,26},{10... | collective-permute-start | bytes 1572872 | tf_op jit(solution)/shard_map/ppermute | solution.py:26
  133.9 10.9 %collective-permute-done.18 = bf16[256,1024]{1,0:T(8,128)(2,1)S(1)} collective-permute-done((bf16[256,1024]{1,0:T(8,128)(2,1)}, bf16[256,1024]{1,0:T(8,128)(2,1)S(1)}, u32[]{:S(2)}, u32[]{:S(2)}) %collective-permute-start.18) | collective-permute-done | bytes 524320 | tf_op jit(solution)/shard_map/ppermute | solution.py:26
  144.8 2.4 %convolution_convert_fusion = bf16[1024,1024]{1,0:T(8,128)(2,1)S(1)} fusion(bf16[1024,1024]{1,0:T(8,128)(2,1)S(1)} %pad_maximum_fusion.1, bf16[1024,1024]{1,0:T(8,128)(2,1)S(1)} %copy-done.6), kind=kOutput, calls=%fused_computation.2 | convolution fusion | flops 2148532224 | bytes 6291456 | tf_op jit(solution)/shard_map/dot_general | solution.py:17
  148.4 3.0 %collective-permute-start.20 = (bf16[256,1024]{1,0:T(8,128)(2,1)}, bf16[256,1024]{1,0:T(8,128)(2,1)}, u32[]{:S(2)}, u32[]{:S(2)}) collective-permute-start(bf16[256,1024]{1,0:T(8,128)(2,1)} %get-tuple-element.44), channel_id=1, source_target_pairs={{0,24},{8,0},{16,8},{24,16},{1,25},{9,1},{17,9},{25,17},{2,26},{10... | collective-permute-start | bytes 1572872 | tf_op jit(solution)/shard_map/ppermute | solution.py:26
  154.0 3.5 %all-to-all-start.3 = ((bf16[8,32,1024]{2,1,0:T(8,128)(2,1)}), bf16[8,32,1024]{2,1,0:T(8,128)(2,1)S(1)}, u32[]{:S(2)}, u32[]{:S(2)}) async-start(bf16[8,32,1024]{2,1,0:T(8,128)(2,1)} %bitcast.20), calls=%async_computation.3 | async-start | bytes 1048576 | tf_op jit(solution)/shard_map/all_to_all | solution.py:30
  157.5 4.6 %fusion = f32[1024,512]{1,0:T(8,128)} fusion(bf16[1024,1024]{1,0:T(8,128)(2,1)} %copy-done.14, bf16[1024,1024]{1,0:T(8,128)(2,1)} %copy-done.7), kind=kOutput, calls=%fused_computation.10 | convolution fusion | flops 1073741824 | bytes 5242880 | tf_op jit(solution)/shard_map/dot_general | solution.py:21
  162.1 2.6 %fusion.2 = f32[1024,512]{1,0:T(8,128)} fusion(bf16[1024,1024]{1,0:T(8,128)(2,1)S(1)} %copy-done.15, bf16[1024,1024]{1,0:T(8,128)(2,1)S(1)} %copy-done.8), kind=kOutput, calls=%fused_computation.12 | convolution fusion | flops 1073741824 | bytes 5242880 | tf_op jit(solution)/shard_map/dot_general | solution.py:21
  164.7 2.6 %fusion.7 = f32[512,1024]{1,0:T(8,128)} fusion(bf16[1024,512]{1,0:T(8,128)(2,1)S(1)} %pad_maximum_fusion.2, bf16[1024,1024]{1,0:T(8,128)(2,1)S(1)} %bitcast.40), kind=kOutput, calls=%fused_computation.48 | convolution fusion | flops 1073741824 | bytes 5242880 | tf_op jit(solution)/shard_map/dot_general | solution.py:21
  167.3 6.8 %all-to-all-done.3 = bf16[8,32,1024]{2,1,0:T(8,128)(2,1)S(1)} async-done(((bf16[8,32,1024]{2,1,0:T(8,128)(2,1)}), bf16[8,32,1024]{2,1,0:T(8,128)(2,1)S(1)}, u32[]{:S(2)}, u32[]{:S(2)}) %all-to-all-start.3) | async-done | bytes 524320 | tf_op jit(solution)/shard_map/all_to_all | solution.py:30
  174.9 2.2 %collective-permute-done.21 = bf16[256,1024]{1,0:T(8,128)(2,1)} collective-permute-done((bf16[256,1024]{1,0:T(8,128)(2,1)}, bf16[256,1024]{1,0:T(8,128)(2,1)}, u32[]{:S(2)}, u32[]{:S(2)}) %collective-permute-start.21) | collective-permute-done | bytes 524320 | tf_op jit(solution)/shard_map/ppermute | solution.py:26
  178.8 17.4 %all_to_all.48 = bf16[8,32,1024]{2,1,0:T(8,128)(2,1)S(1)} all-to-all(bf16[8,32,1024]{2,1,0:T(8,128)(2,1)S(1)} %bitcast.43), channel_id=1, replica_groups=mesh['x'=4,'core'=2,'y'=4,'z'=8] {'z'}, dimensions={0} | all-to-all | bytes 1048576 | tf_op jit(solution)/shard_map/all_to_all | solution.py:30
  (103 shorter events, 37.3 us)
Async XLA Ops:
  7.2 70.9 %copy-start = (bf16[512,1024]{1,0:T(8,128)(2,1)S(1)}, bf16[512,1024]{1,0:T(8,128)(2,1)}, u32[]{:S(2)}) copy-start(bf16[512,1024]{1,0:T(8,128)(2,1)} %param.8) | copy-start | bytes 3145732
  7.2 15.7 %copy-start.11 = (bf16[1024,512]{1,0:T(8,128)(2,1)S(1)}, bf16[1024,512]{1,0:T(8,128)(2,1)}, u32[]{:S(2)}) copy-start(bf16[1024,512]{1,0:T(8,128)(2,1)} %param.7) | copy-start | bytes 3145732
  9.0 26.0 %all-to-all-start = ((bf16[8,32,1024]{2,1,0:T(8,128)(2,1)}), bf16[8,32,1024]{2,1,0:T(8,128)(2,1)S(1)}, u32[]{:S(2)}, u32[]{:S(2)}) async-start(bf16[8,32,1024]{2,1,0:T(8,128)(2,1)} %broadcast_in_dim.4), calls=%async_computation | async-start | bytes 1048576 | tf_op jit(solution)/shard_map/all_to_all | solution.py:30
  17.5 58.8 %all-gather.3.cloned.1.call-start = ((), (), s32[]{:S(2)}) async-start(), calls=%async_computation.5 | async-start | bytes 2359296 | tf_op jit(solution)/shard_map/all_gather | solution.py:146
  17.5 8.2 %collective-permute-start = (bf16[32,1024]{1,0:T(8,128)(2,1)}, bf16[32,1024]{1,0:T(8,128)(2,1)S(1)}, u32[]{:S(2)}, u32[]{:S(2)}) collective-permute-start(bf16[32,1024]{1,0:T(8,128)(2,1)} %param.9), channel_id=1, source_target_pairs={{0,8},{8,16},{16,24},{24,0},{1,9},{9,17},{17,25},{25,1},{2,10},{10... | collective-permute-start | bytes 196616 | tf_op jit(solution)/shard_map/ppermute | solution.py:26
  19.2 6.5 %collective-permute-start.2 = (bf16[32,1024]{1,0:T(8,128)(2,1)}, bf16[32,1024]{1,0:T(8,128)(2,1)S(1)}, u32[]{:S(2)}, u32[]{:S(2)}) collective-permute-start(bf16[32,1024]{1,0:T(8,128)(2,1)} %param.9), channel_id=1, source_target_pairs={{0,24},{8,0},{16,8},{24,16},{1,25},{9,1},{17,9},{25,17},{2,26},{10... | collective-permute-start | bytes 196616 | tf_op jit(solution)/shard_map/ppermute | solution.py:26
  20.9 6.0 %collective-permute-start.1 = (bf16[32,1024]{1,0:T(8,128)(2,1)}, bf16[32,1024]{1,0:T(8,128)(2,1)S(1)}, u32[]{:S(2)}, u32[]{:S(2)}) collective-permute-start(bf16[32,1024]{1,0:T(8,128)(2,1)} %param.9), channel_id=1, source_target_pairs={{0,16},{8,24},{16,0},{24,8},{1,17},{9,25},{17,1},{25,9},{2,18},{10... | collective-permute-start | bytes 196616 | tf_op jit(solution)/shard_map/ppermute | solution.py:26
  35.0 15.2 %collective-permute-start.3 = (bf16[256,1024]{1,0:T(8,128)(2,1)S(1)}, bf16[256,1024]{1,0:T(8,128)(2,1)S(1)}, u32[]{:S(2)}, u32[]{:S(2)}) collective-permute-start(bf16[256,1024]{1,0:T(8,128)(2,1)S(1)} %bitcast.45), channel_id=1, source_target_pairs={{0,8},{8,16},{16,24},{24,0},{1,9},{9,17},{17,25},{25,1},{2,10},{10... | collective-permute-start | bytes 1572872 | tf_op jit(solution)/shard_map/ppermute | solution.py:26
  36.7 26.0 %collective-permute-start.4 = (bf16[256,1024]{1,0:T(8,128)(2,1)S(1)}, bf16[256,1024]{1,0:T(8,128)(2,1)S(1)}, u32[]{:S(2)}, u32[]{:S(2)}) collective-permute-start(bf16[256,1024]{1,0:T(8,128)(2,1)S(1)} %bitcast.46), channel_id=1, source_target_pairs={{0,16},{8,24},{16,0},{24,8},{1,17},{9,25},{17,1},{25,9},{2,18},{10... | collective-permute-start | bytes 1572872 | tf_op jit(solution)/shard_map/ppermute | solution.py:26
  39.6 23.1 %collective-permute-start.5 = (bf16[256,1024]{1,0:T(8,128)(2,1)S(1)}, bf16[256,1024]{1,0:T(8,128)(2,1)S(1)}, u32[]{:S(2)}, u32[]{:S(2)}) collective-permute-start(bf16[256,1024]{1,0:T(8,128)(2,1)S(1)} %bitcast.47), channel_id=1, source_target_pairs={{0,24},{8,0},{16,8},{24,16},{1,25},{9,1},{17,9},{25,17},{2,26},{10... | collective-permute-start | bytes 1572872 | tf_op jit(solution)/shard_map/ppermute | solution.py:26
  40.9 21.8 %copy-start.5 = (bf16[1024,1024]{1,0:T(8,128)(2,1)S(1)}, bf16[1024,1024]{1,0:T(8,128)(2,1)}, u32[]{:S(2)}) copy-start(bf16[1024,1024]{1,0:T(8,128)(2,1)} %pad_maximum_fusion) | copy-start | bytes 6291460
  66.4 3.0 %collective-permute-start.6 = (bf16[512,1024]{1,0:T(8,128)(2,1)}, bf16[512,1024]{1,0:T(8,128)(2,1)}, u32[]{:S(2)}, u32[]{:S(2)}) collective-permute-start(bf16[512,1024]{1,0:T(8,128)(2,1)} %constant_dynamic-slice_fusion), channel_id=1, source_target_pairs={{0,32},{32,0},{1,33},{33,1},{2,34},{34,2},{3,35},{35,3},{4,36},{36... | collective-permute-start | bytes 3145736 | tf_op jit(solution)/shard_map/ppermute | solution.py:26
  71.6 9.4 %collective-permute-start.8 = (bf16[128,1024]{1,0:T(8,128)(2,1)}, bf16[128,1024]{1,0:T(8,128)(2,1)S(1)}, u32[]{:S(2)}, u32[]{:S(2)}) collective-permute-start(bf16[128,1024]{1,0:T(8,128)(2,1)} %get-tuple-element.34), channel_id=1, source_target_pairs={{0,64},{64,128},{128,192},{192,0},{1,65},{65,129},{129,193},{193,1... | collective-permute-start | bytes 786440 | tf_op jit(solution)/shard_map/ppermute | solution.py:26
  73.1 10.9 %collective-permute-start.9 = (bf16[128,1024]{1,0:T(8,128)(2,1)}, bf16[128,1024]{1,0:T(8,128)(2,1)S(1)}, u32[]{:S(2)}, u32[]{:S(2)}) collective-permute-start(bf16[128,1024]{1,0:T(8,128)(2,1)} %get-tuple-element.35), channel_id=1, source_target_pairs={{0,128},{64,192},{128,0},{192,64},{1,129},{65,193},{129,1},{193,65... | collective-permute-start | bytes 786440 | tf_op jit(solution)/shard_map/ppermute | solution.py:26
  74.2 13.5 %collective-permute-start.10 = (bf16[128,1024]{1,0:T(8,128)(2,1)S(1)}, bf16[128,1024]{1,0:T(8,128)(2,1)}, u32[]{:S(2)}, u32[]{:S(2)}) collective-permute-start(bf16[128,1024]{1,0:T(8,128)(2,1)S(1)} %get-tuple-element.36), channel_id=1, source_target_pairs={{0,192},{64,0},{128,64},{192,128},{1,193},{65,1},{129,65},{193,129... | collective-permute-start | bytes 786440 | tf_op jit(solution)/shard_map/ppermute | solution.py:26
  80.3 13.3 %collective-permute-start.7 = (bf16[512,512]{1,0:T(8,128)(2,1)}, bf16[512,512]{1,0:T(8,128)(2,1)S(1)}, u32[]{:S(2)}, u32[]{:S(2)}) collective-permute-start(bf16[512,512]{1,0:T(8,128)(2,1)} %broadcast_select_fusion.4), channel_id=1, source_target_pairs={{0,32},{32,0},{1,33},{33,1},{2,34},{34,2},{3,35},{35,3},{4,36},{36... | collective-permute-start | bytes 1572872 | tf_op jit(solution)/shard_map/ppermute | solution.py:26
  89.3 11.6 %collective-permute-start.12 = (bf16[128,512]{1,0:T(8,128)(2,1)S(1)}, bf16[128,512]{1,0:T(8,128)(2,1)S(1)}, u32[]{:S(2)}, u32[]{:S(2)}) collective-permute-start(bf16[128,512]{1,0:T(8,128)(2,1)S(1)} %multiply_convert_fusion.2), channel_id=1, source_target_pairs={{0,128},{64,192},{128,0},{192,64},{1,129},{65,193},{129,1},{193,65... | collective-permute-start | bytes 393224 | tf_op jit(solution)/shard_map/ppermute | solution.py:26
  91.5 9.3 %collective-permute-start.11 = (bf16[128,512]{1,0:T(8,128)(2,1)S(1)}, bf16[128,512]{1,0:T(8,128)(2,1)S(1)}, u32[]{:S(2)}, u32[]{:S(2)}) collective-permute-start(bf16[128,512]{1,0:T(8,128)(2,1)S(1)} %multiply_convert_fusion.2), channel_id=1, source_target_pairs={{0,64},{64,128},{128,192},{192,0},{1,65},{65,129},{129,193},{193,1... | collective-permute-start | bytes 393224 | tf_op jit(solution)/shard_map/ppermute | solution.py:26
  92.5 8.4 %collective-permute-start.13 = (bf16[128,512]{1,0:T(8,128)(2,1)S(1)}, bf16[128,512]{1,0:T(8,128)(2,1)}, u32[]{:S(2)}, u32[]{:S(2)}) collective-permute-start(bf16[128,512]{1,0:T(8,128)(2,1)S(1)} %multiply_convert_fusion.2), channel_id=1, source_target_pairs={{0,192},{64,0},{128,64},{192,128},{1,193},{65,1},{129,65},{193,129... | collective-permute-start | bytes 393224 | tf_op jit(solution)/shard_map/ppermute | solution.py:26
  94.5 12.9 %all-to-all-start.1 = ((bf16[4,128,512]{2,1,0:T(8,128)(2,1)}), bf16[4,128,512]{2,1,0:T(8,128)(2,1)S(1)}, u32[]{:S(2)}, u32[]{:S(2)}) async-start(bf16[4,128,512]{2,1,0:T(8,128)(2,1)} %bitcast.8), calls=%async_computation.1 | async-start | bytes 1048576 | tf_op jit(solution)/shard_map/all_to_all | solution.py:30
  107.4 6.3 %collective-permute-start.14 = (bf16[512,512]{1,0:T(8,128)(2,1)S(1)}, bf16[512,512]{1,0:T(8,128)(2,1)}, u32[]{:S(2)}, u32[]{:S(2)}) collective-permute-start(bf16[512,512]{1,0:T(8,128)(2,1)S(1)} %pad_maximum_fusion.4), channel_id=1, source_target_pairs={{0,32},{32,0},{1,33},{33,1},{2,34},{34,2},{3,35},{35,3},{4,36},{36... | collective-permute-start | bytes 1572872 | tf_op jit(solution)/shard_map/ppermute | solution.py:26
  108.8 20.3 %all-to-all-start.2 = ((bf16[4,128,1024]{2,1,0:T(8,128)(2,1)}), bf16[4,128,1024]{2,1,0:T(8,128)(2,1)S(1)}, u32[]{:S(2)}, u32[]{:S(2)}) async-start(bf16[4,128,1024]{2,1,0:T(8,128)(2,1)} %broadcast_in_dim.5), calls=%async_computation.2 | async-start | bytes 2097152 | tf_op jit(solution)/shard_map/all_to_all | solution.py:30
  116.2 8.5 %collective-permute-start.16 = (bf16[128,1024]{1,0:T(8,128)(2,1)S(1)}, bf16[128,1024]{1,0:T(8,128)(2,1)S(1)}, u32[]{:S(2)}, u32[]{:S(2)}) collective-permute-start(bf16[128,1024]{1,0:T(8,128)(2,1)S(1)} %get-tuple-element.67), channel_id=1, source_target_pairs={{0,24},{8,0},{16,8},{24,16},{1,25},{9,1},{17,9},{25,17},{2,26},{10... | collective-permute-start | bytes 786440 | tf_op jit(solution)/shard_map/ppermute | solution.py:26
  118.4 9.4 %collective-permute-start.15 = (bf16[128,1024]{1,0:T(8,128)(2,1)S(1)}, bf16[128,1024]{1,0:T(8,128)(2,1)S(1)}, u32[]{:S(2)}, u32[]{:S(2)}) collective-permute-start(bf16[128,1024]{1,0:T(8,128)(2,1)S(1)} %get-tuple-element.69), channel_id=1, source_target_pairs={{0,8},{8,16},{16,24},{24,0},{1,9},{9,17},{17,25},{25,1},{2,10},{10... | collective-permute-start | bytes 786440 | tf_op jit(solution)/shard_map/ppermute | solution.py:26
  129.1 4.5 %collective-permute-start.17 = (bf16[512,1024]{1,0:T(8,128)(2,1)S(1)}, bf16[512,1024]{1,0:T(8,128)(2,1)S(1)}, u32[]{:S(2)}, u32[]{:S(2)}) collective-permute-start(bf16[512,1024]{1,0:T(8,128)(2,1)S(1)} %bitcast.41), channel_id=1, source_target_pairs={{0,32},{32,0},{1,33},{33,1},{2,34},{34,2},{3,35},{35,3},{4,36},{36... | collective-permute-start | bytes 3145736 | tf_op jit(solution)/shard_map/ppermute | solution.py:26
  129.1 15.8 %collective-permute-start.18 = (bf16[256,1024]{1,0:T(8,128)(2,1)}, bf16[256,1024]{1,0:T(8,128)(2,1)S(1)}, u32[]{:S(2)}, u32[]{:S(2)}) collective-permute-start(bf16[256,1024]{1,0:T(8,128)(2,1)} %get-tuple-element.40), channel_id=1, source_target_pairs={{0,8},{8,16},{16,24},{24,0},{1,9},{9,17},{17,25},{25,1},{2,10},{10... | collective-permute-start | bytes 1572872 | tf_op jit(solution)/shard_map/ppermute | solution.py:26
  129.5 15.3 %collective-permute-start.19 = (bf16[256,1024]{1,0:T(8,128)(2,1)}, bf16[256,1024]{1,0:T(8,128)(2,1)S(1)}, u32[]{:S(2)}, u32[]{:S(2)}) collective-permute-start(bf16[256,1024]{1,0:T(8,128)(2,1)} %get-tuple-element.41), channel_id=1, source_target_pairs={{0,24},{8,0},{16,8},{24,16},{1,25},{9,1},{17,9},{25,17},{2,26},{10... | collective-permute-start | bytes 1572872 | tf_op jit(solution)/shard_map/ppermute | solution.py:26
  133.9 13.3 %copy-start.7 = (bf16[1024,1024]{1,0:T(8,128)(2,1)}, bf16[1024,1024]{1,0:T(8,128)(2,1)S(1)}, u32[]{:S(2)}) copy-start(bf16[1024,1024]{1,0:T(8,128)(2,1)S(1)} %pad_maximum_fusion.1) | copy-start | bytes 6291460
  148.4 26.4 %collective-permute-start.20 = (bf16[256,1024]{1,0:T(8,128)(2,1)}, bf16[256,1024]{1,0:T(8,128)(2,1)}, u32[]{:S(2)}, u32[]{:S(2)}) collective-permute-start(bf16[256,1024]{1,0:T(8,128)(2,1)} %get-tuple-element.44), channel_id=1, source_target_pairs={{0,24},{8,0},{16,8},{24,16},{1,25},{9,1},{17,9},{25,17},{2,26},{10... | collective-permute-start | bytes 1572872 | tf_op jit(solution)/shard_map/ppermute | solution.py:26
  151.4 25.7 %collective-permute-start.21 = (bf16[256,1024]{1,0:T(8,128)(2,1)}, bf16[256,1024]{1,0:T(8,128)(2,1)}, u32[]{:S(2)}, u32[]{:S(2)}) collective-permute-start(bf16[256,1024]{1,0:T(8,128)(2,1)} %get-tuple-element.45), channel_id=1, source_target_pairs={{0,8},{8,16},{16,24},{24,0},{1,9},{9,17},{17,25},{25,1},{2,10},{10... | collective-permute-start | bytes 1572872 | tf_op jit(solution)/shard_map/ppermute | solution.py:26
  151.4 25.7 %collective-permute-start.22 = (bf16[256,1024]{1,0:T(8,128)(2,1)}, bf16[256,1024]{1,0:T(8,128)(2,1)}, u32[]{:S(2)}, u32[]{:S(2)}) collective-permute-start(bf16[256,1024]{1,0:T(8,128)(2,1)} %get-tuple-element.46), channel_id=1, source_target_pairs={{0,16},{8,24},{16,0},{24,8},{1,17},{9,25},{17,1},{25,9},{2,18},{10... | collective-permute-start | bytes 1572872 | tf_op jit(solution)/shard_map/ppermute | solution.py:26
  154.0 20.2 %all-to-all-start.3 = ((bf16[8,32,1024]{2,1,0:T(8,128)(2,1)}), bf16[8,32,1024]{2,1,0:T(8,128)(2,1)S(1)}, u32[]{:S(2)}, u32[]{:S(2)}) async-start(bf16[8,32,1024]{2,1,0:T(8,128)(2,1)} %bitcast.20), calls=%async_computation.3 | async-start | bytes 1048576 | tf_op jit(solution)/shard_map/all_to_all | solution.py:30
  (14 other events, 66.3 us)
Sparse Core Ops, SparseCore 0:
  35.1 37.4 all-gather.2

commit v10 on v9

--- a/solution.py
+++ b/solution.py
@@ -44,6 +44,15 @@
 def gather_y(own):
     near = [shift(own, "y", 1), shift(own, "y", 3)]
     return [own, near[0], shift(own, "y", 2), near[1]]
+
+
+def gather_y_halves(own):
+    half = own.shape[0] // 2
+    top, bottom = own[:half], own[half:]
+    left_top, right_bottom = shift(top, "y", 1), shift(bottom, "y", 3)
+    left_bottom, right_top = shift(bottom, "y", 1), shift(top, "y", 3)
+    far_top, far_bottom = shift(left_top, "y", 1), shift(right_bottom, "y", 3)
+    return [own, left_top, left_bottom, far_top, far_bottom, right_top, right_bottom]
 
 
 def swap_core(low, high):
@@ -108,20 +117,28 @@
     return [partial[j * rows : (j + 1) * rows] for j in range(Y)]
 
 
-def reduce_y_far(pieces):
-    rows = pieces[2].shape[0] // 2
-    return shift(pieces[2][:rows], "y", 1), shift(pieces[2][rows:], "y", 3)
-
-
-def add_y_far(pieces, from_left, from_right):
-    rows = pieces[2].shape[0] // 2
-    to_right = jnp.concatenate([add(pieces[3][:rows], from_left), pieces[3][rows:]], axis=0)
-    to_left = jnp.concatenate([pieces[1][:rows], add(pieces[1][rows:], from_right)], axis=0)
-    return lax.optimization_barrier((to_right, to_left))
-
-
-def move_y_near(to_right, to_left):
+def move_y_first(pieces):
+    half = pieces[2].shape[0] // 2
+    to_right = jnp.concatenate([pieces[2][:half], pieces[3][half:]], axis=0)
+    to_left = jnp.concatenate([pieces[2][half:], pieces[1][:half]], axis=0)
     return shift(to_right, "y", 1), shift(to_left, "y", 3)
+
+
+def add_y_first(pieces, from_left, from_right):
+    half = pieces[2].shape[0] // 2
+    return lax.optimization_barrier(
+        (add(pieces[3][:half], from_left[:half]), add(pieces[1][half:], from_right[:half]))
+    )
+
+
+def move_y_second(to_right, to_left):
+    return shift(to_right, "y", 1), shift(to_left, "y", 3)
+
+
+def sum_y_steps(own, first, second):
+    half = own.shape[0] // 2
+    top = sum_y(own[:half], second[0], first[1][half:])
+    return jnp.concatenate([top, sum_y(own[half:], first[0][half:], second[1])], axis=0)
 
 
 def sum_y(own, *moved):
@@ -142,7 +159,7 @@
     tokens_z = gather(tokens, "z")
     grads_y = jnp.stack(gather_y(out_grad))
     tokens_z, grads_y, both_weights = lax.optimization_barrier((tokens_z, grads_y, both_weights))
-    all_tokens = jnp.concatenate(gather_y(tokens_z), axis=0)
+    all_tokens = jnp.concatenate(gather_y_halves(tokens_z), axis=0)
     all_grads = lax.all_gather(grads_y, "z", axis=0, tiled=False)
 
     gate_up = with_layout_constraint(product(all_tokens, both_weights).astype(BF), Layout((0, 1)))
@@ -162,22 +179,22 @@
     hidden = gather_core(hidden_half)
 
     output_pieces = split_y(product(hidden, down_weight).astype(BF))
-    output_far = reduce_y_far(output_pieces)
-    to_right, to_left = add_y_far(output_pieces, *output_far)
-    output_near = move_y_near(to_right, to_left)
+    output_first = move_y_first(output_pieces)
+    to_right, to_left = add_y_first(output_pieces, *output_first)
+    output_second = move_y_second(to_right, to_left)
 
     gate_grad = (hidden_grad * up_value * sigmoid_gate * (1.0 + gate_value * (1.0 - sigmoid_gate))).astype(BF)
     up_grad = (hidden_grad * silu_gate).astype(BF)
     both_half = gather(jnp.concatenate([gate_grad, up_grad], axis=1), "x")
     both_half, to_right, to_left = lax.optimization_barrier((both_half, to_right, to_left))
-    both_grads = after(gather_core(both_half), *output_near)
+    both_grads = after(gather_core(both_half), *output_second)
 
     input_pieces = lax.optimization_barrier(split_y(product_right_t(both_grads, both_weights).astype(BF)))
     input_moved = [shift(input_pieces[1], "y", 3), shift(input_pieces[3], "y", 1), shift(input_pieces[2], "y", 2)]
     down_weight_grad = product_left_t(after(hidden, *input_pieces), all_grads)
     gate_weight_grad = product_left_t(all_tokens, both_grads[:, :width])
     up_weight_grad = product_left_t(all_tokens, both_grads[:, width:])
-    output_total = reduce_z(sum_y(after(output_pieces[0], *input_pieces), *output_near))
+    output_total = reduce_z(sum_y_steps(after(output_pieces[0], *input_pieces), output_first, output_second))
     input_moved, gate_weight_grad, up_weight_grad, down_weight_grad, output_total = lax.optimization_barrier(
         (input_moved, gate_weight_grad, up_weight_grad, down_weight_grad, output_total)
     )

time: 204 us -> 197 us (0.966)
  waiting for transfers between devices: 74.7 us -> 61.8 us
  starting transfers between devices: 53.2 us -> 58.9 us
    ppermute x23 -> x26, waiting for transfers between devices: 54.9 us -> 38.8 us  [shift(): lax.ppermute(block, axis, [(i, (i + step) % size) for i in range(size)])]
    ppermute x23 -> x26, starting transfers between devices: 30.1 us -> 35.7 us  [shift(): lax.ppermute(block, axis, [(i, (i + step) % size) for i in range(size)])]
    all_gather x1, waiting for transfers between devices: 0.01 us -> 3.23 us  [body(): all_grads = lax.all_gather(grads_y, 'z', axis=0, tiled=False)]
  transfers between devices with their start and end apart: 28 -> 31, of which waited for: 14 -> 15; matrix products, arithmetic and copies ran while one was open for 17% -> 18% of each run, Pallas kernels for 0% -> 0%
where the time goes in v10:
time: 197 us
  waiting for transfers between devices  61.8 us (31%)
  starting transfers between devices  58.9 us (30%)
  other arithmetic  18.6 us (9%)
  blocking collectives  17.4 us (9%)
  matrix products  17.1 us (9%)
  between operations  14.5 us (7%)
  local copies, waits for them, and re-layouts  8.57 us (4%)
    ppermute x26, waiting for transfers between devices, shift(): lax.ppermute(block, axis, [(i, (i + step) % size) for i in range(size)])  38.8 us
    ppermute x26, starting transfers between devices, shift(): lax.ppermute(block, axis, [(i, (i + step) % size) for i in range(size)])  35.7 us
    all_to_all x4, starting transfers between devices, exchange(): return lax.all_to_all(blocks, axis, split_axis=0, concat_axis=0, tiled=True)  23.1 us
    all_to_all x4, waiting for transfers between devices, exchange(): return lax.all_to_all(blocks, axis, split_axis=0, concat_axis=0, tiled=True)  19.8 us
    all_to_all x1, blocking collectives, exchange(): return lax.all_to_all(blocks, axis, split_axis=0, concat_axis=0, tiled=True)  17.4 us
    dot_general x3, matrix products, product_left_t(): lax.dot_general(left_side, right_side, (((0,), (0,)), ((), ())), preferre...  9.83 us
  transfers between devices with their start and end apart: 31, of which 15 were waited for; matrix products, arithmetic and copies ran while one was open for 18% of the time, Pallas kernels for 0%

profile of v10, /device:TPU:2, one launch (start us, length us, event | category | flops | bytes accessed | tf_op | source)
XLA Modules:
  0.0 196.8 jit_solution(9632048746560588057)
XLA Ops:
  7.2 1.8 broadcast_in_dim.4
  9.0 8.5 %all-to-all-start = ((bf16[8,32,1024]{2,1,0:T(8,128)(2,1)}), bf16[8,32,1024]{2,1,0:T(8,128)(2,1)S(1)}, u32[]{:S(2)}, u32[]{:S(2)}) async-start(bf16[8,32,1024]{2,1,0:T(8,128)(2,1)} %broadcast_in_dim.4), calls=%async_computation | async-start | bytes 1048576 | tf_op jit(solution)/shard_map/all_to_all | solution.py:30
  20.9 2.0 %collective-permute-start.1 = (bf16[32,1024]{1,0:T(8,128)(2,1)}, bf16[32,1024]{1,0:T(8,128)(2,1)S(1)}, u32[]{:S(2)}, u32[]{:S(2)}) collective-permute-start(bf16[32,1024]{1,0:T(8,128)(2,1)} %param.9), channel_id=1, source_target_pairs={{0,16},{8,24},{16,0},{24,8},{1,17},{9,25},{17,1},{25,9},{2,18},{10... | collective-permute-start | bytes 196616 | tf_op jit(solution)/shard_map/ppermute | solution.py:26
  22.8 2.9 %pad_maximum_fusion = bf16[1024,1024]{1,0:T(8,128)(2,1)} fusion(bf16[1024,512]{1,0:T(8,128)(2,1)S(1)} %copy-done.11, bf16[1024,512]{1,0:T(8,128)(2,1)} %param.6), kind=kLoop, calls=%fused_computation | loop fusion | flops 4194304 | bytes 4194304 | tf_op jit(solution)/shard_map/concatenate | solution.py:157
  27.6 7.4 %all-to-all-done = bf16[8,32,1024]{2,1,0:T(8,128)(2,1)S(1)} async-done(((bf16[8,32,1024]{2,1,0:T(8,128)(2,1)}), bf16[8,32,1024]{2,1,0:T(8,128)(2,1)S(1)}, u32[]{:S(2)}, u32[]{:S(2)}) %all-to-all-start) | async-done | bytes 524320 | tf_op jit(solution)/shard_map/all_to_all | solution.py:30
  38.7 2.9 %collective-permute-start.8 = (bf16[128,1024]{1,0:T(8,128)(2,1)S(1)}, bf16[128,1024]{1,0:T(8,128)(2,1)S(1)}, u32[]{:S(2)}, u32[]{:S(2)}) collective-permute-start(bf16[128,1024]{1,0:T(8,128)(2,1)S(1)} %get-tuple-element.83), channel_id=1, source_target_pairs={{0,24},{8,0},{16,8},{24,16},{1,25},{9,1},{17,9},{25,17},{2,26},{10... | collective-permute-start | bytes 786440 | tf_op jit(solution)/shard_map/ppermute | solution.py:26
  41.6 3.9 %collective-permute-done.3 = bf16[128,1024]{1,0:T(8,128)(2,1)S(1)} collective-permute-done((bf16[128,1024]{1,0:T(8,128)(2,1)S(1)}, bf16[128,1024]{1,0:T(8,128)(2,1)S(1)}, u32[]{:S(2)}, u32[]{:S(2)}) %collective-permute-start.3) | collective-permute-done | bytes 262176 | tf_op jit(solution)/shard_map/ppermute | solution.py:26
  45.9 2.9 %collective-permute-start.7 = (bf16[128,1024]{1,0:T(8,128)(2,1)S(1)}, bf16[128,1024]{1,0:T(8,128)(2,1)S(1)}, u32[]{:S(2)}, u32[]{:S(2)}) collective-permute-start(bf16[128,1024]{1,0:T(8,128)(2,1)S(1)} %collective-permute-done.6), channel_id=1, source_target_pairs={{0,24},{8,0},{16,8},{24,16},{1,25},{9,1},{17,9},{25,17},{2,26},{10... | collective-permute-start | bytes 786440 | tf_op jit(solution)/shard_map/ppermute | solution.py:26
  48.9 2.2 %collective-permute-done.4 = bf16[128,1024]{1,0:T(8,128)(2,1)S(1)} collective-permute-done((bf16[128,1024]{1,0:T(8,128)(2,1)S(1)}, bf16[128,1024]{1,0:T(8,128)(2,1)S(1)}, u32[]{:S(2)}, u32[]{:S(2)}) %collective-permute-start.4) | collective-permute-done | bytes 262176 | tf_op jit(solution)/shard_map/ppermute | solution.py:26
  51.1 4.7 %collective-permute-done.5 = bf16[128,1024]{1,0:T(8,128)(2,1)S(1)} collective-permute-done((bf16[128,1024]{1,0:T(8,128)(2,1)S(1)}, bf16[128,1024]{1,0:T(8,128)(2,1)S(1)}, u32[]{:S(2)}, u32[]{:S(2)}) %collective-permute-start.5) | collective-permute-done | bytes 262176 | tf_op jit(solution)/shard_map/ppermute | solution.py:26
  56.0 2.3 %convolution_convert_fusion.2 = bf16[1024,1024]{1,0:T(8,128)(2,1)S(1)} fusion(bf16[1024,1024]{1,0:T(8,128)(2,1)S(1)} %constant_dynamic-update-slice_fusion, bf16[1024,1024]{1,0:T(8,128)(2,1)S(1)} %copy-done.5), kind=kOutput, calls=%fused_computation.4 | convolution fusion | flops 2148532224 | bytes 6291456 | tf_op jit(solution)/shard_map/dot_general | solution.py:13
  59.6 3.0 %collective-permute-done.9 = bf16[512,1024]{1,0:T(8,128)(2,1)} collective-permute-done((bf16[512,1024]{1,0:T(8,128)(2,1)}, bf16[512,1024]{1,0:T(8,128)(2,1)}, u32[]{:S(2)}, u32[]{:S(2)}) %collective-permute-start.9) | collective-permute-done | bytes 1048608 | tf_op jit(solution)/shard_map/ppermute | solution.py:26
  62.6 2.2 %add_convert_fusion.6 = (bf16[128,1024]{1,0:T(8,128)(2,1)S(1)}, bf16[128,1024]{1,0:T(8,128)(2,1)}, bf16[128,1024]{1,0:T(8,128)(2,1)}) fusion(bf16[512,1024]{1,0:T(8,128)(2,1)} %collective-permute-done.9, s32[]{:T(128)S(6)} %select_n.80, bf16[1024,1024]{1,0:T(8,128)(2,1)S(1)} %convolution_convert_fusion.2, s32[]{:T(128)S(6)} %select_n.79, s32[]{:T(128)S(6)} %select_n.78, ...), kind=kLoop, calls=%fused_computation.26 | loop fusion | flops 1572864 | bytes 2359320 | tf_op jit(solution)/shard_map/convert_element_type | solution.py:89
  67.5 2.2 %collective-permute-start.13 = (bf16[128,1024]{1,0:T(8,128)(2,1)S(1)}, bf16[128,1024]{1,0:T(8,128)(2,1)}, u32[]{:S(2)}, u32[]{:S(2)}) collective-permute-start(bf16[128,1024]{1,0:T(8,128)(2,1)S(1)} %get-tuple-element.36), channel_id=1, source_target_pairs={{0,192},{64,0},{128,64},{192,128},{1,193},{65,1},{129,65},{193,129... | collective-permute-start | bytes 786440 | tf_op jit(solution)/shard_map/ppermute | solution.py:26
  69.6 3.2 %all-gather.3.cloned.1.call-done = bf16[32,32,1024]{2,1,0:T(8,128)(2,1)} async-done(((bf16[4,32,1024]{2,1,0:T(8,128)(2,1)}), bf16[32,32,1024]{2,1,0:T(8,128)(2,1)}) %all-gather.3.cloned.1.call-update) | async-done | bytes 2097168 | tf_op jit(solution)/shard_map/all_gather | solution.py:163
  78.3 2.7 %collective-permute-done.13 = bf16[128,1024]{1,0:T(8,128)(2,1)} collective-permute-done((bf16[128,1024]{1,0:T(8,128)(2,1)S(1)}, bf16[128,1024]{1,0:T(8,128)(2,1)}, u32[]{:S(2)}, u32[]{:S(2)}) %collective-permute-start.13) | collective-permute-done | bytes 262176 | tf_op jit(solution)/shard_map/ppermute | solution.py:26
  82.5 2.1 %collective-permute-start.15 = (bf16[128,512]{1,0:T(8,128)(2,1)S(1)}, bf16[128,512]{1,0:T(8,128)(2,1)S(1)}, u32[]{:S(2)}, u32[]{:S(2)}) collective-permute-start(bf16[128,512]{1,0:T(8,128)(2,1)S(1)} %multiply_convert_fusion.2), channel_id=1, source_target_pairs={{0,128},{64,192},{128,0},{192,64},{1,129},{65,193},{129,1},{193,65... | collective-permute-start | bytes 393224 | tf_op jit(solution)/shard_map/ppermute | solution.py:26
  87.6 6.2 %all-to-all-start.1 = ((bf16[4,128,512]{2,1,0:T(8,128)(2,1)}), bf16[4,128,512]{2,1,0:T(8,128)(2,1)S(1)}, u32[]{:S(2)}, u32[]{:S(2)}) async-start(bf16[4,128,512]{2,1,0:T(8,128)(2,1)} %bitcast.8), calls=%async_computation.1 | async-start | bytes 1048576 | tf_op jit(solution)/shard_map/all_to_all | solution.py:30
  95.0 5.5 %all-to-all-done.1 = bf16[4,128,512]{2,1,0:T(8,128)(2,1)S(1)} async-done(((bf16[4,128,512]{2,1,0:T(8,128)(2,1)}), bf16[4,128,512]{2,1,0:T(8,128)(2,1)S(1)}, u32[]{:S(2)}, u32[]{:S(2)}) %all-to-all-start.1) | async-done | bytes 524320 | tf_op jit(solution)/shard_map/all_to_all | solution.py:30
  101.9 4.9 %all-to-all-start.2 = ((bf16[4,128,1024]{2,1,0:T(8,128)(2,1)}), bf16[4,128,1024]{2,1,0:T(8,128)(2,1)S(1)}, u32[]{:S(2)}, u32[]{:S(2)}) async-start(bf16[4,128,1024]{2,1,0:T(8,128)(2,1)} %broadcast_in_dim.5), calls=%async_computation.2 | async-start | bytes 2097152 | tf_op jit(solution)/shard_map/all_to_all | solution.py:30
  112.8 11.9 %collective-permute-done.18 = bf16[256,1024]{1,0:T(8,128)(2,1)S(1)} collective-permute-done((bf16[256,1024]{1,0:T(8,128)(2,1)S(1)}, bf16[256,1024]{1,0:T(8,128)(2,1)S(1)}, u32[]{:S(2)}, u32[]{:S(2)}) %collective-permute-start.18) | collective-permute-done | bytes 524320 | tf_op jit(solution)/shard_map/ppermute | solution.py:26
  128.6 2.0 %collective-permute-start.22 = (bf16[128,1024]{1,0:T(8,128)(2,1)S(1)}, bf16[128,1024]{1,0:T(8,128)(2,1)S(1)}, u32[]{:S(2)}, u32[]{:S(2)}) collective-permute-start(bf16[128,1024]{1,0:T(8,128)(2,1)S(1)} %get-tuple-element.41), channel_id=1, source_target_pairs={{0,24},{8,0},{16,8},{24,16},{1,25},{9,1},{17,9},{25,17},{2,26},{10... | collective-permute-start | bytes 786440 | tf_op jit(solution)/shard_map/ppermute | solution.py:26
  130.9 6.3 %collective-permute-done.21 = bf16[128,1024]{1,0:T(8,128)(2,1)S(1)} collective-permute-done((bf16[128,1024]{1,0:T(8,128)(2,1)S(1)}, bf16[128,1024]{1,0:T(8,128)(2,1)S(1)}, u32[]{:S(2)}, u32[]{:S(2)}) %collective-permute-start.21) | collective-permute-done | bytes 262176 | tf_op jit(solution)/shard_map/ppermute | solution.py:26
  137.3 2.4 %convolution_convert_fusion = bf16[1024,1024]{1,0:T(8,128)(2,1)S(1)} fusion(bf16[1024,1024]{1,0:T(8,128)(2,1)S(1)} %pad_maximum_fusion.1, bf16[1024,1024]{1,0:T(8,128)(2,1)S(1)} %copy-done.6), kind=kOutput, calls=%fused_computation.2 | convolution fusion | flops 2148532224 | bytes 6291456 | tf_op jit(solution)/shard_map/dot_general | solution.py:17
  140.9 3.2 %collective-permute-start.23 = (bf16[256,1024]{1,0:T(8,128)(2,1)}, bf16[256,1024]{1,0:T(8,128)(2,1)}, u32[]{:S(2)}, u32[]{:S(2)}) collective-permute-start(bf16[256,1024]{1,0:T(8,128)(2,1)} %get-tuple-element.44), channel_id=1, source_target_pairs={{0,24},{8,0},{16,8},{24,16},{1,25},{9,1},{17,9},{25,17},{2,26},{10... | collective-permute-start | bytes 1572872 | tf_op jit(solution)/shard_map/ppermute | solution.py:26
  146.9 3.5 %all-to-all-start.3 = ((bf16[8,32,1024]{2,1,0:T(8,128)(2,1)}), bf16[8,32,1024]{2,1,0:T(8,128)(2,1)S(1)}, u32[]{:S(2)}, u32[]{:S(2)}) async-start(bf16[8,32,1024]{2,1,0:T(8,128)(2,1)} %bitcast.20), calls=%async_computation.3 | async-start | bytes 1048576 | tf_op jit(solution)/shard_map/all_to_all | solution.py:30
  150.5 4.6 %fusion = f32[1024,512]{1,0:T(8,128)} fusion(bf16[1024,1024]{1,0:T(8,128)(2,1)} %copy-done.19, bf16[1024,1024]{1,0:T(8,128)(2,1)} %copy-done.7), kind=kOutput, calls=%fused_computation.9 | convolution fusion | flops 1073741824 | bytes 5242880 | tf_op jit(solution)/shard_map/dot_general | solution.py:21
  155.1 2.6 %fusion.2 = f32[1024,512]{1,0:T(8,128)} fusion(bf16[1024,1024]{1,0:T(8,128)(2,1)S(1)} %copy-done.20, bf16[1024,1024]{1,0:T(8,128)(2,1)S(1)} %copy-done.8), kind=kOutput, calls=%fused_computation.11 | convolution fusion | flops 1073741824 | bytes 5242880 | tf_op jit(solution)/shard_map/dot_general | solution.py:21
  157.7 2.6 %fusion.8 = f32[512,1024]{1,0:T(8,128)} fusion(bf16[1024,512]{1,0:T(8,128)(2,1)S(1)} %pad_maximum_fusion.2, bf16[1024,1024]{1,0:T(8,128)(2,1)S(1)} %bitcast.40), kind=kOutput, calls=%fused_computation.54 | convolution fusion | flops 1073741824 | bytes 5242880 | tf_op jit(solution)/shard_map/dot_general | solution.py:21
  160.3 6.9 %all-to-all-done.3 = bf16[8,32,1024]{2,1,0:T(8,128)(2,1)S(1)} async-done(((bf16[8,32,1024]{2,1,0:T(8,128)(2,1)}), bf16[8,32,1024]{2,1,0:T(8,128)(2,1)S(1)}, u32[]{:S(2)}, u32[]{:S(2)}) %all-to-all-start.3) | async-done | bytes 524320 | tf_op jit(solution)/shard_map/all_to_all | solution.py:30
  167.9 2.2 %collective-permute-done.24 = bf16[256,1024]{1,0:T(8,128)(2,1)} collective-permute-done((bf16[256,1024]{1,0:T(8,128)(2,1)}, bf16[256,1024]{1,0:T(8,128)(2,1)}, u32[]{:S(2)}, u32[]{:S(2)}) %collective-permute-start.24) | collective-permute-done | bytes 524320 | tf_op jit(solution)/shard_map/ppermute | solution.py:26
  171.8 17.4 %all_to_all.48 = bf16[8,32,1024]{2,1,0:T(8,128)(2,1)S(1)} all-to-all(bf16[8,32,1024]{2,1,0:T(8,128)(2,1)S(1)} %bitcast.45), channel_id=1, replica_groups=mesh['x'=4,'core'=2,'y'=4,'z'=8] {'z'}, dimensions={0} | all-to-all | bytes 1048576 | tf_op jit(solution)/shard_map/all_to_all | solution.py:30
  (125 shorter events, 43.0 us)
Async XLA Ops:
  7.2 67.5 %copy-start = (bf16[512,1024]{1,0:T(8,128)(2,1)S(1)}, bf16[512,1024]{1,0:T(8,128)(2,1)}, u32[]{:S(2)}) copy-start(bf16[512,1024]{1,0:T(8,128)(2,1)} %param.8) | copy-start | bytes 3145732
  9.0 26.0 %all-to-all-start = ((bf16[8,32,1024]{2,1,0:T(8,128)(2,1)}), bf16[8,32,1024]{2,1,0:T(8,128)(2,1)S(1)}, u32[]{:S(2)}, u32[]{:S(2)}) async-start(bf16[8,32,1024]{2,1,0:T(8,128)(2,1)} %broadcast_in_dim.4), calls=%async_computation | async-start | bytes 1048576 | tf_op jit(solution)/shard_map/all_to_all | solution.py:30
  17.5 55.3 %all-gather.3.cloned.1.call-start = ((), (), s32[]{:S(2)}) async-start(), calls=%async_computation.5 | async-start | bytes 2359296 | tf_op jit(solution)/shard_map/all_gather | solution.py:163
  17.5 8.2 %collective-permute-start = (bf16[32,1024]{1,0:T(8,128)(2,1)}, bf16[32,1024]{1,0:T(8,128)(2,1)S(1)}, u32[]{:S(2)}, u32[]{:S(2)}) collective-permute-start(bf16[32,1024]{1,0:T(8,128)(2,1)} %param.9), channel_id=1, source_target_pairs={{0,8},{8,16},{16,24},{24,0},{1,9},{9,17},{17,25},{25,1},{2,10},{10... | collective-permute-start | bytes 196616 | tf_op jit(solution)/shard_map/ppermute | solution.py:26
  19.2 6.5 %collective-permute-start.2 = (bf16[32,1024]{1,0:T(8,128)(2,1)}, bf16[32,1024]{1,0:T(8,128)(2,1)S(1)}, u32[]{:S(2)}, u32[]{:S(2)}) collective-permute-start(bf16[32,1024]{1,0:T(8,128)(2,1)} %param.9), channel_id=1, source_target_pairs={{0,24},{8,0},{16,8},{24,16},{1,25},{9,1},{17,9},{25,17},{2,26},{10... | collective-permute-start | bytes 196616 | tf_op jit(solution)/shard_map/ppermute | solution.py:26
  20.9 6.0 %collective-permute-start.1 = (bf16[32,1024]{1,0:T(8,128)(2,1)}, bf16[32,1024]{1,0:T(8,128)(2,1)S(1)}, u32[]{:S(2)}, u32[]{:S(2)}) collective-permute-start(bf16[32,1024]{1,0:T(8,128)(2,1)} %param.9), channel_id=1, source_target_pairs={{0,16},{8,24},{16,0},{24,8},{1,17},{9,25},{17,1},{25,9},{2,18},{10... | collective-permute-start | bytes 196616 | tf_op jit(solution)/shard_map/ppermute | solution.py:26
  35.1 10.5 %collective-permute-start.3 = (bf16[128,1024]{1,0:T(8,128)(2,1)S(1)}, bf16[128,1024]{1,0:T(8,128)(2,1)S(1)}, u32[]{:S(2)}, u32[]{:S(2)}) collective-permute-start(bf16[128,1024]{1,0:T(8,128)(2,1)S(1)} %get-tuple-element.83), channel_id=1, source_target_pairs={{0,8},{8,16},{16,24},{24,0},{1,9},{9,17},{17,25},{25,1},{2,10},{10... | collective-permute-start | bytes 786440 | tf_op jit(solution)/shard_map/ppermute | solution.py:26
  36.7 9.2 %collective-permute-start.6 = (bf16[128,1024]{1,0:T(8,128)(2,1)S(1)}, bf16[128,1024]{1,0:T(8,128)(2,1)S(1)}, u32[]{:S(2)}, u32[]{:S(2)}) collective-permute-start(bf16[128,1024]{1,0:T(8,128)(2,1)S(1)} %get-tuple-element.82), channel_id=1, source_target_pairs={{0,24},{8,0},{16,8},{24,16},{1,25},{9,1},{17,9},{25,17},{2,26},{10... | collective-permute-start | bytes 786440 | tf_op jit(solution)/shard_map/ppermute | solution.py:26
  38.4 12.8 %collective-permute-start.4 = (bf16[128,1024]{1,0:T(8,128)(2,1)S(1)}, bf16[128,1024]{1,0:T(8,128)(2,1)S(1)}, u32[]{:S(2)}, u32[]{:S(2)}) collective-permute-start(bf16[128,1024]{1,0:T(8,128)(2,1)S(1)} %get-tuple-element.82), channel_id=1, source_target_pairs={{0,8},{8,16},{16,24},{24,0},{1,9},{9,17},{17,25},{25,1},{2,10},{10... | collective-permute-start | bytes 786440 | tf_op jit(solution)/shard_map/ppermute | solution.py:26
  38.7 17.2 %collective-permute-start.8 = (bf16[128,1024]{1,0:T(8,128)(2,1)S(1)}, bf16[128,1024]{1,0:T(8,128)(2,1)S(1)}, u32[]{:S(2)}, u32[]{:S(2)}) collective-permute-start(bf16[128,1024]{1,0:T(8,128)(2,1)S(1)} %get-tuple-element.83), channel_id=1, source_target_pairs={{0,24},{8,0},{16,8},{24,16},{1,25},{9,1},{17,9},{25,17},{2,26},{10... | collective-permute-start | bytes 786440 | tf_op jit(solution)/shard_map/ppermute | solution.py:26
  45.5 10.4 %collective-permute-start.5 = (bf16[128,1024]{1,0:T(8,128)(2,1)S(1)}, bf16[128,1024]{1,0:T(8,128)(2,1)S(1)}, u32[]{:S(2)}, u32[]{:S(2)}) collective-permute-start(bf16[128,1024]{1,0:T(8,128)(2,1)S(1)} %collective-permute-done.3), channel_id=1, source_target_pairs={{0,8},{8,16},{16,24},{24,0},{1,9},{9,17},{17,25},{25,1},{2,10},{10... | collective-permute-start | bytes 786440 | tf_op jit(solution)/shard_map/ppermute | solution.py:26
  45.9 10.0 %collective-permute-start.7 = (bf16[128,1024]{1,0:T(8,128)(2,1)S(1)}, bf16[128,1024]{1,0:T(8,128)(2,1)S(1)}, u32[]{:S(2)}, u32[]{:S(2)}) collective-permute-start(bf16[128,1024]{1,0:T(8,128)(2,1)S(1)} %collective-permute-done.6), channel_id=1, source_target_pairs={{0,24},{8,0},{16,8},{24,16},{1,25},{9,1},{17,9},{25,17},{2,26},{10... | collective-permute-start | bytes 786440 | tf_op jit(solution)/shard_map/ppermute | solution.py:26
  59.6 3.0 %collective-permute-start.9 = (bf16[512,1024]{1,0:T(8,128)(2,1)}, bf16[512,1024]{1,0:T(8,128)(2,1)}, u32[]{:S(2)}, u32[]{:S(2)}) collective-permute-start(bf16[512,1024]{1,0:T(8,128)(2,1)} %constant_dynamic-slice_fusion), channel_id=1, source_target_pairs={{0,32},{32,0},{1,33},{33,1},{2,34},{34,2},{3,35},{35,3},{4,36},{36... | collective-permute-start | bytes 3145736 | tf_op jit(solution)/shard_map/ppermute | solution.py:26
  64.8 12.0 %collective-permute-start.11 = (bf16[128,1024]{1,0:T(8,128)(2,1)}, bf16[128,1024]{1,0:T(8,128)(2,1)S(1)}, u32[]{:S(2)}, u32[]{:S(2)}) collective-permute-start(bf16[128,1024]{1,0:T(8,128)(2,1)} %get-tuple-element.34), channel_id=1, source_target_pairs={{0,64},{64,128},{128,192},{192,0},{1,65},{65,129},{129,193},{193,1... | collective-permute-start | bytes 786440 | tf_op jit(solution)/shard_map/ppermute | solution.py:26
  66.3 10.9 %collective-permute-start.12 = (bf16[128,1024]{1,0:T(8,128)(2,1)}, bf16[128,1024]{1,0:T(8,128)(2,1)S(1)}, u32[]{:S(2)}, u32[]{:S(2)}) collective-permute-start(bf16[128,1024]{1,0:T(8,128)(2,1)} %get-tuple-element.35), channel_id=1, source_target_pairs={{0,128},{64,192},{128,0},{192,64},{1,129},{65,193},{129,1},{193,65... | collective-permute-start | bytes 786440 | tf_op jit(solution)/shard_map/ppermute | solution.py:26
  67.5 13.5 %collective-permute-start.13 = (bf16[128,1024]{1,0:T(8,128)(2,1)S(1)}, bf16[128,1024]{1,0:T(8,128)(2,1)}, u32[]{:S(2)}, u32[]{:S(2)}) collective-permute-start(bf16[128,1024]{1,0:T(8,128)(2,1)S(1)} %get-tuple-element.36), channel_id=1, source_target_pairs={{0,192},{64,0},{128,64},{192,128},{1,193},{65,1},{129,65},{193,129... | collective-permute-start | bytes 786440 | tf_op jit(solution)/shard_map/ppermute | solution.py:26
  76.8 9.8 %collective-permute-start.10 = (bf16[512,512]{1,0:T(8,128)(2,1)}, bf16[512,512]{1,0:T(8,128)(2,1)S(1)}, u32[]{:S(2)}, u32[]{:S(2)}) collective-permute-start(bf16[512,512]{1,0:T(8,128)(2,1)} %broadcast_select_fusion.4), channel_id=1, source_target_pairs={{0,32},{32,0},{1,33},{33,1},{2,34},{34,2},{3,35},{35,3},{4,36},{36... | collective-permute-start | bytes 1572872 | tf_op jit(solution)/shard_map/ppermute | solution.py:26
  82.5 11.4 %collective-permute-start.15 = (bf16[128,512]{1,0:T(8,128)(2,1)S(1)}, bf16[128,512]{1,0:T(8,128)(2,1)S(1)}, u32[]{:S(2)}, u32[]{:S(2)}) collective-permute-start(bf16[128,512]{1,0:T(8,128)(2,1)S(1)} %multiply_convert_fusion.2), channel_id=1, source_target_pairs={{0,128},{64,192},{128,0},{192,64},{1,129},{65,193},{129,1},{193,65... | collective-permute-start | bytes 393224 | tf_op jit(solution)/shard_map/ppermute | solution.py:26
  84.6 9.3 %collective-permute-start.14 = (bf16[128,512]{1,0:T(8,128)(2,1)S(1)}, bf16[128,512]{1,0:T(8,128)(2,1)S(1)}, u32[]{:S(2)}, u32[]{:S(2)}) collective-permute-start(bf16[128,512]{1,0:T(8,128)(2,1)S(1)} %multiply_convert_fusion.2), channel_id=1, source_target_pairs={{0,64},{64,128},{128,192},{192,0},{1,65},{65,129},{129,193},{193,1... | collective-permute-start | bytes 393224 | tf_op jit(solution)/shard_map/ppermute | solution.py:26
  85.6 8.4 %collective-permute-start.16 = (bf16[128,512]{1,0:T(8,128)(2,1)S(1)}, bf16[128,512]{1,0:T(8,128)(2,1)}, u32[]{:S(2)}, u32[]{:S(2)}) collective-permute-start(bf16[128,512]{1,0:T(8,128)(2,1)S(1)} %multiply_convert_fusion.2), channel_id=1, source_target_pairs={{0,192},{64,0},{128,64},{192,128},{1,193},{65,1},{129,65},{193,129... | collective-permute-start | bytes 393224 | tf_op jit(solution)/shard_map/ppermute | solution.py:26
  87.6 12.9 %all-to-all-start.1 = ((bf16[4,128,512]{2,1,0:T(8,128)(2,1)}), bf16[4,128,512]{2,1,0:T(8,128)(2,1)S(1)}, u32[]{:S(2)}, u32[]{:S(2)}) async-start(bf16[4,128,512]{2,1,0:T(8,128)(2,1)} %bitcast.8), calls=%async_computation.1 | async-start | bytes 1048576 | tf_op jit(solution)/shard_map/all_to_all | solution.py:30
  100.5 6.3 %collective-permute-start.17 = (bf16[512,512]{1,0:T(8,128)(2,1)S(1)}, bf16[512,512]{1,0:T(8,128)(2,1)}, u32[]{:S(2)}, u32[]{:S(2)}) collective-permute-start(bf16[512,512]{1,0:T(8,128)(2,1)S(1)} %pad_maximum_fusion.4), channel_id=1, source_target_pairs={{0,32},{32,0},{1,33},{33,1},{2,34},{34,2},{3,35},{35,3},{4,36},{36... | collective-permute-start | bytes 1572872 | tf_op jit(solution)/shard_map/ppermute | solution.py:26
  101.9 24.0 %all-to-all-start.2 = ((bf16[4,128,1024]{2,1,0:T(8,128)(2,1)}), bf16[4,128,1024]{2,1,0:T(8,128)(2,1)S(1)}, u32[]{:S(2)}, u32[]{:S(2)}) async-start(bf16[4,128,1024]{2,1,0:T(8,128)(2,1)} %broadcast_in_dim.5), calls=%async_computation.2 | async-start | bytes 2097152 | tf_op jit(solution)/shard_map/all_to_all | solution.py:30
  109.4 15.4 %collective-permute-start.18 = (bf16[256,1024]{1,0:T(8,128)(2,1)S(1)}, bf16[256,1024]{1,0:T(8,128)(2,1)S(1)}, u32[]{:S(2)}, u32[]{:S(2)}) collective-permute-start(bf16[256,1024]{1,0:T(8,128)(2,1)S(1)} %pad_maximum_fusion.5), channel_id=1, source_target_pairs={{0,8},{8,16},{16,24},{24,0},{1,9},{9,17},{17,25},{25,1},{2,10},{10... | collective-permute-start | bytes 1572872 | tf_op jit(solution)/shard_map/ppermute | solution.py:26
  111.1 13.9 %collective-permute-start.19 = (bf16[256,1024]{1,0:T(8,128)(2,1)S(1)}, bf16[256,1024]{1,0:T(8,128)(2,1)S(1)}, u32[]{:S(2)}, u32[]{:S(2)}) collective-permute-start(bf16[256,1024]{1,0:T(8,128)(2,1)S(1)} %pad_maximum_fusion.6), channel_id=1, source_target_pairs={{0,24},{8,0},{16,8},{24,16},{1,25},{9,1},{17,9},{25,17},{2,26},{10... | collective-permute-start | bytes 1572872 | tf_op jit(solution)/shard_map/ppermute | solution.py:26
  125.9 4.7 %collective-permute-start.20 = (bf16[512,1024]{1,0:T(8,128)(2,1)S(1)}, bf16[512,1024]{1,0:T(8,128)(2,1)S(1)}, u32[]{:S(2)}, u32[]{:S(2)}) collective-permute-start(bf16[512,1024]{1,0:T(8,128)(2,1)S(1)} %bitcast.43), channel_id=1, source_target_pairs={{0,32},{32,0},{1,33},{33,1},{2,34},{34,2},{3,35},{35,3},{4,36},{36... | collective-permute-start | bytes 3145736 | tf_op jit(solution)/shard_map/ppermute | solution.py:26
  127.3 10.0 %collective-permute-start.21 = (bf16[128,1024]{1,0:T(8,128)(2,1)S(1)}, bf16[128,1024]{1,0:T(8,128)(2,1)S(1)}, u32[]{:S(2)}, u32[]{:S(2)}) collective-permute-start(bf16[128,1024]{1,0:T(8,128)(2,1)S(1)} %copy-done.18), channel_id=1, source_target_pairs={{0,8},{8,16},{16,24},{24,0},{1,9},{9,17},{17,25},{25,1},{2,10},{10... | collective-permute-start | bytes 786440 | tf_op jit(solution)/shard_map/ppermute | solution.py:26
  128.6 8.7 %collective-permute-start.22 = (bf16[128,1024]{1,0:T(8,128)(2,1)S(1)}, bf16[128,1024]{1,0:T(8,128)(2,1)S(1)}, u32[]{:S(2)}, u32[]{:S(2)}) collective-permute-start(bf16[128,1024]{1,0:T(8,128)(2,1)S(1)} %get-tuple-element.41), channel_id=1, source_target_pairs={{0,24},{8,0},{16,8},{24,16},{1,25},{9,1},{17,9},{25,17},{2,26},{10... | collective-permute-start | bytes 786440 | tf_op jit(solution)/shard_map/ppermute | solution.py:26
  140.9 27.0 %collective-permute-start.23 = (bf16[256,1024]{1,0:T(8,128)(2,1)}, bf16[256,1024]{1,0:T(8,128)(2,1)}, u32[]{:S(2)}, u32[]{:S(2)}) collective-permute-start(bf16[256,1024]{1,0:T(8,128)(2,1)} %get-tuple-element.44), channel_id=1, source_target_pairs={{0,24},{8,0},{16,8},{24,16},{1,25},{9,1},{17,9},{25,17},{2,26},{10... | collective-permute-start | bytes 1572872 | tf_op jit(solution)/shard_map/ppermute | solution.py:26
  144.1 26.0 %collective-permute-start.24 = (bf16[256,1024]{1,0:T(8,128)(2,1)}, bf16[256,1024]{1,0:T(8,128)(2,1)}, u32[]{:S(2)}, u32[]{:S(2)}) collective-permute-start(bf16[256,1024]{1,0:T(8,128)(2,1)} %get-tuple-element.45), channel_id=1, source_target_pairs={{0,8},{8,16},{16,24},{24,0},{1,9},{9,17},{17,25},{25,1},{2,10},{10... | collective-permute-start | bytes 1572872 | tf_op jit(solution)/shard_map/ppermute | solution.py:26
  144.1 26.0 %collective-permute-start.25 = (bf16[256,1024]{1,0:T(8,128)(2,1)}, bf16[256,1024]{1,0:T(8,128)(2,1)}, u32[]{:S(2)}, u32[]{:S(2)}) collective-permute-start(bf16[256,1024]{1,0:T(8,128)(2,1)} %get-tuple-element.46), channel_id=1, source_target_pairs={{0,16},{8,24},{16,0},{24,8},{1,17},{9,25},{17,1},{25,9},{2,18},{10... | collective-permute-start | bytes 1572872 | tf_op jit(solution)/shard_map/ppermute | solution.py:26
  146.9 20.3 %all-to-all-start.3 = ((bf16[8,32,1024]{2,1,0:T(8,128)(2,1)}), bf16[8,32,1024]{2,1,0:T(8,128)(2,1)S(1)}, u32[]{:S(2)}, u32[]{:S(2)}) async-start(bf16[8,32,1024]{2,1,0:T(8,128)(2,1)} %bitcast.20), calls=%async_computation.3 | async-start | bytes 1048576 | tf_op jit(solution)/shard_map/all_to_all | solution.py:30
  (22 other events, 121.1 us)
Sparse Core Ops, SparseCore 0:
  35.1 37.6 all-gather.2

commit v11 on v10

--- a/solution.py
+++ b/solution.py
@@ -158,7 +158,7 @@
 
     tokens_z = gather(tokens, "z")
     grads_y = jnp.stack(gather_y(out_grad))
-    tokens_z, grads_y, both_weights = lax.optimization_barrier((tokens_z, grads_y, both_weights))
+    tokens_z = after(tokens_z, grads_y)
     all_tokens = jnp.concatenate(gather_y_halves(tokens_z), axis=0)
     all_grads = lax.all_gather(grads_y, "z", axis=0, tiled=False)
 

time: 197 us -> 198 us (level)
  other arithmetic: 18.6 us -> 16.5 us
    ppermute x26, waiting for transfers between devices: 38.8 us -> 43.3 us  [shift(): lax.ppermute(block, axis, [(i, (i + step) % size) for i in range(size)])]
    concatenate x1 -> x0, other arithmetic: 2.87 us -> none  [body(): both_weights = jnp.concatenate([gate_weight, up_weight], axis=1)]
    all_gather x1, waiting for transfers between devices: 3.23 us -> 0.52 us  [body(): all_grads = lax.all_gather(grads_y, 'z', axis=0, tiled=False)]
  transfers between devices with their start and end apart: 31 -> 31, of which waited for: 15 -> 20; matrix products, arithmetic and copies ran while one was open for 18% -> 17% of each run, Pallas kernels for 0% -> 0%
where the time goes in v11:
time: 198 us; the launch traced here: 197 us
  waiting for transfers between devices  62.7 us (32%)
  starting transfers between devices  58.8 us (30%)
  blocking collectives  17.4 us (9%)
  matrix products  17.1 us (9%)
  other arithmetic  16.5 us (8%)
  between operations  14.5 us (7%)
  local copies, waits for them, and re-layouts  9.88 us (5%)
    ppermute x26, waiting for transfers between devices, shift(): lax.ppermute(block, axis, [(i, (i + step) % size) for i in range(size)])  43.3 us
    ppermute x26, starting transfers between devices, shift(): lax.ppermute(block, axis, [(i, (i + step) % size) for i in range(size)])  35.7 us
    all_to_all x4, starting transfers between devices, exchange(): return lax.all_to_all(blocks, axis, split_axis=0, concat_axis=0, tiled=True)  23.1 us
    all_to_all x4, waiting for transfers between devices, exchange(): return lax.all_to_all(blocks, axis, split_axis=0, concat_axis=0, tiled=True)  18.9 us
    all_to_all x1, blocking collectives, exchange(): return lax.all_to_all(blocks, axis, split_axis=0, concat_axis=0, tiled=True)  17.4 us
    dot_general x3, matrix products, product_left_t(): lax.dot_general(left_side, right_side, (((0,), (0,)), ((), ())), preferre...  9.83 us
  transfers between devices with their start and end apart: 31, of which 20 were waited for; matrix products, arithmetic and copies ran while one was open for 17% of the time, Pallas kernels for 0%

profile of v11, /device:TPU:2, one launch (start us, length us, event | category | flops | bytes accessed | tf_op | source)
XLA Modules:
  0.0 196.9 jit_solution(18053754005393867250)
XLA Ops:
  7.2 1.8 broadcast_in_dim.4
  9.0 8.5 %all-to-all-start = ((bf16[8,32,1024]{2,1,0:T(8,128)(2,1)}), bf16[8,32,1024]{2,1,0:T(8,128)(2,1)S(1)}, u32[]{:S(2)}, u32[]{:S(2)}) async-start(bf16[8,32,1024]{2,1,0:T(8,128)(2,1)} %broadcast_in_dim.4), calls=%async_computation | async-start | bytes 1048576 | tf_op jit(solution)/shard_map/all_to_all | solution.py:30
  20.9 2.0 %collective-permute-start.1 = (bf16[32,1024]{1,0:T(8,128)(2,1)}, bf16[32,1024]{1,0:T(8,128)(2,1)S(1)}, u32[]{:S(2)}, u32[]{:S(2)}) collective-permute-start(bf16[32,1024]{1,0:T(8,128)(2,1)} %param.9), channel_id=1, source_target_pairs={{0,16},{8,24},{16,0},{24,8},{1,17},{9,25},{17,1},{25,9},{2,18},{10... | collective-permute-start | bytes 196616 | tf_op jit(solution)/shard_map/ppermute | solution.py:26
  24.0 2.8 %collective-permute-done.1 = bf16[32,1024]{1,0:T(8,128)(2,1)S(1)} collective-permute-done((bf16[32,1024]{1,0:T(8,128)(2,1)}, bf16[32,1024]{1,0:T(8,128)(2,1)S(1)}, u32[]{:S(2)}, u32[]{:S(2)}) %collective-permute-start.1) | collective-permute-done | bytes 65568 | tf_op jit(solution)/shard_map/ppermute | solution.py:26
  28.4 6.5 %all-to-all-done = bf16[8,32,1024]{2,1,0:T(8,128)(2,1)S(1)} async-done(((bf16[8,32,1024]{2,1,0:T(8,128)(2,1)}), bf16[8,32,1024]{2,1,0:T(8,128)(2,1)S(1)}, u32[]{:S(2)}, u32[]{:S(2)}) %all-to-all-start) | async-done | bytes 524320 | tf_op jit(solution)/shard_map/all_to_all | solution.py:30
  40.4 2.9 %collective-permute-start.8 = (bf16[128,1024]{1,0:T(8,128)(2,1)S(1)}, bf16[128,1024]{1,0:T(8,128)(2,1)S(1)}, u32[]{:S(2)}, u32[]{:S(2)}) collective-permute-start(bf16[128,1024]{1,0:T(8,128)(2,1)S(1)} %get-tuple-element.79), channel_id=1, source_target_pairs={{0,24},{8,0},{16,8},{24,16},{1,25},{9,1},{17,9},{25,17},{2,26},{10... | collective-permute-start | bytes 786440 | tf_op jit(solution)/shard_map/ppermute | solution.py:26
  43.3 2.2 %collective-permute-done.3 = bf16[128,1024]{1,0:T(8,128)(2,1)S(1)} collective-permute-done((bf16[128,1024]{1,0:T(8,128)(2,1)S(1)}, bf16[128,1024]{1,0:T(8,128)(2,1)S(1)}, u32[]{:S(2)}, u32[]{:S(2)}) %collective-permute-start.3) | collective-permute-done | bytes 262176 | tf_op jit(solution)/shard_map/ppermute | solution.py:26
  46.1 2.9 %collective-permute-start.7 = (bf16[128,1024]{1,0:T(8,128)(2,1)S(1)}, bf16[128,1024]{1,0:T(8,128)(2,1)S(1)}, u32[]{:S(2)}, u32[]{:S(2)}) collective-permute-start(bf16[128,1024]{1,0:T(8,128)(2,1)S(1)} %collective-permute-done.6), channel_id=1, source_target_pairs={{0,24},{8,0},{16,8},{24,16},{1,25},{9,1},{17,9},{25,17},{2,26},{10... | collective-permute-start | bytes 786440 | tf_op jit(solution)/shard_map/ppermute | solution.py:26
  49.0 2.1 %collective-permute-done.4 = bf16[128,1024]{1,0:T(8,128)(2,1)S(1)} collective-permute-done((bf16[128,1024]{1,0:T(8,128)(2,1)S(1)}, bf16[128,1024]{1,0:T(8,128)(2,1)S(1)}, u32[]{:S(2)}, u32[]{:S(2)}) %collective-permute-start.4) | collective-permute-done | bytes 262176 | tf_op jit(solution)/shard_map/ppermute | solution.py:26
  51.1 4.7 %collective-permute-done.5 = bf16[128,1024]{1,0:T(8,128)(2,1)S(1)} collective-permute-done((bf16[128,1024]{1,0:T(8,128)(2,1)S(1)}, bf16[128,1024]{1,0:T(8,128)(2,1)S(1)}, u32[]{:S(2)}, u32[]{:S(2)}) %collective-permute-start.5) | collective-permute-done | bytes 262176 | tf_op jit(solution)/shard_map/ppermute | solution.py:26
  56.2 2.3 %convolution_convert_fusion.2 = bf16[1024,1024]{1,0:T(8,128)(2,1)S(1)} fusion(bf16[1024,1024]{1,0:T(8,128)(2,1)S(1)} %constant_dynamic-update-slice_fusion, bf16[1024,1024]{1,0:T(8,128)(2,1)S(1)} %copy-done.12), kind=kOutput, calls=%fused_computation.3 | convolution fusion | flops 2148532224 | bytes 6291456 | tf_op jit(solution)/shard_map/dot_general | solution.py:13
  59.8 3.0 %collective-permute-done.9 = bf16[512,1024]{1,0:T(8,128)(2,1)} collective-permute-done((bf16[512,1024]{1,0:T(8,128)(2,1)}, bf16[512,1024]{1,0:T(8,128)(2,1)}, u32[]{:S(2)}, u32[]{:S(2)}) %collective-permute-start.9) | collective-permute-done | bytes 1048608 | tf_op jit(solution)/shard_map/ppermute | solution.py:26
  62.8 2.2 %add_convert_fusion.6 = (bf16[128,1024]{1,0:T(8,128)(2,1)S(1)}, bf16[128,1024]{1,0:T(8,128)(2,1)}, bf16[128,1024]{1,0:T(8,128)(2,1)}) fusion(bf16[512,1024]{1,0:T(8,128)(2,1)} %collective-permute-done.9, s32[]{:T(128)S(6)} %select_n.80, bf16[1024,1024]{1,0:T(8,128)(2,1)S(1)} %convolution_convert_fusion.2, s32[]{:T(128)S(6)} %select_n.79, s32[]{:T(128)S(6)} %select_n.78, ...), kind=kLoop, calls=%fused_computation.25 | loop fusion | flops 1572864 | bytes 2359320 | tf_op jit(solution)/shard_map/convert_element_type | solution.py:89
  67.6 2.1 %collective-permute-start.13 = (bf16[128,1024]{1,0:T(8,128)(2,1)S(1)}, bf16[128,1024]{1,0:T(8,128)(2,1)}, u32[]{:S(2)}, u32[]{:S(2)}) collective-permute-start(bf16[128,1024]{1,0:T(8,128)(2,1)S(1)} %get-tuple-element.32), channel_id=1, source_target_pairs={{0,192},{64,0},{128,64},{192,128},{1,193},{65,1},{129,65},{193,129... | collective-permute-start | bytes 786440 | tf_op jit(solution)/shard_map/ppermute | solution.py:26
  74.4 3.0 %collective-permute-done.12 = bf16[128,1024]{1,0:T(8,128)(2,1)S(1)} collective-permute-done((bf16[128,1024]{1,0:T(8,128)(2,1)}, bf16[128,1024]{1,0:T(8,128)(2,1)S(1)}, u32[]{:S(2)}, u32[]{:S(2)}) %collective-permute-start.12) | collective-permute-done | bytes 262176 | tf_op jit(solution)/shard_map/ppermute | solution.py:26
  78.1 3.0 %collective-permute-done.13 = bf16[128,1024]{1,0:T(8,128)(2,1)} collective-permute-done((bf16[128,1024]{1,0:T(8,128)(2,1)S(1)}, bf16[128,1024]{1,0:T(8,128)(2,1)}, u32[]{:S(2)}, u32[]{:S(2)}) %collective-permute-start.13) | collective-permute-done | bytes 262176 | tf_op jit(solution)/shard_map/ppermute | solution.py:26
  82.7 2.1 %collective-permute-start.15 = (bf16[128,512]{1,0:T(8,128)(2,1)S(1)}, bf16[128,512]{1,0:T(8,128)(2,1)S(1)}, u32[]{:S(2)}, u32[]{:S(2)}) collective-permute-start(bf16[128,512]{1,0:T(8,128)(2,1)S(1)} %multiply_convert_fusion.2), channel_id=1, source_target_pairs={{0,128},{64,192},{128,0},{192,64},{1,129},{65,193},{129,1},{193,65... | collective-permute-start | bytes 393224 | tf_op jit(solution)/shard_map/ppermute | solution.py:26
  87.8 6.2 %all-to-all-start.1 = ((bf16[4,128,512]{2,1,0:T(8,128)(2,1)}), bf16[4,128,512]{2,1,0:T(8,128)(2,1)S(1)}, u32[]{:S(2)}, u32[]{:S(2)}) async-start(bf16[4,128,512]{2,1,0:T(8,128)(2,1)} %bitcast.8), calls=%async_computation.1 | async-start | bytes 1048576 | tf_op jit(solution)/shard_map/all_to_all | solution.py:30
  95.2 5.5 %all-to-all-done.1 = bf16[4,128,512]{2,1,0:T(8,128)(2,1)S(1)} async-done(((bf16[4,128,512]{2,1,0:T(8,128)(2,1)}), bf16[4,128,512]{2,1,0:T(8,128)(2,1)S(1)}, u32[]{:S(2)}, u32[]{:S(2)}) %all-to-all-start.1) | async-done | bytes 524320 | tf_op jit(solution)/shard_map/all_to_all | solution.py:30
  102.1 4.9 %all-to-all-start.2 = ((bf16[4,128,1024]{2,1,0:T(8,128)(2,1)}), bf16[4,128,1024]{2,1,0:T(8,128)(2,1)S(1)}, u32[]{:S(2)}, u32[]{:S(2)}) async-start(bf16[4,128,1024]{2,1,0:T(8,128)(2,1)} %broadcast_in_dim.5), calls=%async_computation.2 | async-start | bytes 2097152 | tf_op jit(solution)/shard_map/all_to_all | solution.py:30
  113.0 11.9 %collective-permute-done.18 = bf16[256,1024]{1,0:T(8,128)(2,1)S(1)} collective-permute-done((bf16[256,1024]{1,0:T(8,128)(2,1)S(1)}, bf16[256,1024]{1,0:T(8,128)(2,1)S(1)}, u32[]{:S(2)}, u32[]{:S(2)}) %collective-permute-start.18) | collective-permute-done | bytes 524320 | tf_op jit(solution)/shard_map/ppermute | solution.py:26
  128.8 1.9 collective-permute-start.22
  131.1 6.3 %collective-permute-done.21 = bf16[128,1024]{1,0:T(8,128)(2,1)S(1)} collective-permute-done((bf16[128,1024]{1,0:T(8,128)(2,1)S(1)}, bf16[128,1024]{1,0:T(8,128)(2,1)S(1)}, u32[]{:S(2)}, u32[]{:S(2)}) %collective-permute-start.21) | collective-permute-done | bytes 262176 | tf_op jit(solution)/shard_map/ppermute | solution.py:26
  137.4 2.4 %convolution_convert_fusion = bf16[1024,1024]{1,0:T(8,128)(2,1)S(1)} fusion(bf16[1024,1024]{1,0:T(8,128)(2,1)S(1)} %pad_maximum_fusion, bf16[1024,1024]{1,0:T(8,128)(2,1)S(1)} %copy-done.13), kind=kOutput, calls=%fused_computation.1 | convolution fusion | flops 2148532224 | bytes 6291456 | tf_op jit(solution)/shard_map/dot_general | solution.py:17
  141.1 3.2 %collective-permute-start.23 = (bf16[256,1024]{1,0:T(8,128)(2,1)}, bf16[256,1024]{1,0:T(8,128)(2,1)}, u32[]{:S(2)}, u32[]{:S(2)}) collective-permute-start(bf16[256,1024]{1,0:T(8,128)(2,1)} %get-tuple-element.40), channel_id=1, source_target_pairs={{0,24},{8,0},{16,8},{24,16},{1,25},{9,1},{17,9},{25,17},{2,26},{10... | collective-permute-start | bytes 1572872 | tf_op jit(solution)/shard_map/ppermute | solution.py:26
  147.1 3.5 %all-to-all-start.3 = ((bf16[8,32,1024]{2,1,0:T(8,128)(2,1)}), bf16[8,32,1024]{2,1,0:T(8,128)(2,1)S(1)}, u32[]{:S(2)}, u32[]{:S(2)}) async-start(bf16[8,32,1024]{2,1,0:T(8,128)(2,1)} %bitcast.20), calls=%async_computation.3 | async-start | bytes 1048576 | tf_op jit(solution)/shard_map/all_to_all | solution.py:30
  150.6 4.6 %fusion = f32[1024,512]{1,0:T(8,128)} fusion(bf16[1024,1024]{1,0:T(8,128)(2,1)} %copy-done.21, bf16[1024,1024]{1,0:T(8,128)(2,1)} %copy-done.5), kind=kOutput, calls=%fused_computation.8 | convolution fusion | flops 1073741824 | bytes 5242880 | tf_op jit(solution)/shard_map/dot_general | solution.py:21
  155.2 2.6 %fusion.2 = f32[1024,512]{1,0:T(8,128)} fusion(bf16[1024,1024]{1,0:T(8,128)(2,1)S(1)} %copy-done.22, bf16[1024,1024]{1,0:T(8,128)(2,1)S(1)} %copy-done.6), kind=kOutput, calls=%fused_computation.10 | convolution fusion | flops 1073741824 | bytes 5242880 | tf_op jit(solution)/shard_map/dot_general | solution.py:21
  157.8 2.6 %fusion.8 = f32[512,1024]{1,0:T(8,128)} fusion(bf16[1024,512]{1,0:T(8,128)(2,1)S(1)} %pad_maximum_fusion.1, bf16[1024,1024]{1,0:T(8,128)(2,1)S(1)} %bitcast.40), kind=kOutput, calls=%fused_computation.55 | convolution fusion | flops 1073741824 | bytes 5242880 | tf_op jit(solution)/shard_map/dot_general | solution.py:21
  160.4 6.9 %all-to-all-done.3 = bf16[8,32,1024]{2,1,0:T(8,128)(2,1)S(1)} async-done(((bf16[8,32,1024]{2,1,0:T(8,128)(2,1)}), bf16[8,32,1024]{2,1,0:T(8,128)(2,1)S(1)}, u32[]{:S(2)}, u32[]{:S(2)}) %all-to-all-start.3) | async-done | bytes 524320 | tf_op jit(solution)/shard_map/all_to_all | solution.py:30
  168.0 2.2 %collective-permute-done.24 = bf16[256,1024]{1,0:T(8,128)(2,1)} collective-permute-done((bf16[256,1024]{1,0:T(8,128)(2,1)}, bf16[256,1024]{1,0:T(8,128)(2,1)}, u32[]{:S(2)}, u32[]{:S(2)}) %collective-permute-start.24) | collective-permute-done | bytes 524320 | tf_op jit(solution)/shard_map/ppermute | solution.py:26
  171.9 17.4 %all_to_all.48 = bf16[8,32,1024]{2,1,0:T(8,128)(2,1)S(1)} all-to-all(bf16[8,32,1024]{2,1,0:T(8,128)(2,1)S(1)} %bitcast.45), channel_id=1, replica_groups=mesh['x'=4,'core'=2,'y'=4,'z'=8] {'z'}, dimensions={0} | all-to-all | bytes 1048576 | tf_op jit(solution)/shard_map/all_to_all | solution.py:30
  (128 shorter events, 46.1 us)
Async XLA Ops:
  7.2 64.9 %copy-start = (bf16[512,1024]{1,0:T(8,128)(2,1)S(1)}, bf16[512,1024]{1,0:T(8,128)(2,1)}, u32[]{:S(2)}) copy-start(bf16[512,1024]{1,0:T(8,128)(2,1)} %param.8) | copy-start | bytes 3145732
  9.0 26.0 %all-to-all-start = ((bf16[8,32,1024]{2,1,0:T(8,128)(2,1)}), bf16[8,32,1024]{2,1,0:T(8,128)(2,1)S(1)}, u32[]{:S(2)}, u32[]{:S(2)}) async-start(bf16[8,32,1024]{2,1,0:T(8,128)(2,1)} %broadcast_in_dim.4), calls=%async_computation | async-start | bytes 1048576 | tf_op jit(solution)/shard_map/all_to_all | solution.py:30
  17.5 52.8 %all-gather.3.cloned.1.call-start = ((), (), s32[]{:S(2)}) async-start(), calls=%async_computation.5 | async-start | bytes 2359296 | tf_op jit(solution)/shard_map/all_gather | solution.py:163
  17.5 5.8 %collective-permute-start = (bf16[32,1024]{1,0:T(8,128)(2,1)}, bf16[32,1024]{1,0:T(8,128)(2,1)S(1)}, u32[]{:S(2)}, u32[]{:S(2)}) collective-permute-start(bf16[32,1024]{1,0:T(8,128)(2,1)} %param.9), channel_id=1, source_target_pairs={{0,8},{8,16},{16,24},{24,0},{1,9},{9,17},{17,25},{25,1},{2,10},{10... | collective-permute-start | bytes 196616 | tf_op jit(solution)/shard_map/ppermute | solution.py:26
  19.2 4.9 %collective-permute-start.2 = (bf16[32,1024]{1,0:T(8,128)(2,1)}, bf16[32,1024]{1,0:T(8,128)(2,1)S(1)}, u32[]{:S(2)}, u32[]{:S(2)}) collective-permute-start(bf16[32,1024]{1,0:T(8,128)(2,1)} %param.9), channel_id=1, source_target_pairs={{0,24},{8,0},{16,8},{24,16},{1,25},{9,1},{17,9},{25,17},{2,26},{10... | collective-permute-start | bytes 196616 | tf_op jit(solution)/shard_map/ppermute | solution.py:26
  20.9 6.0 %collective-permute-start.1 = (bf16[32,1024]{1,0:T(8,128)(2,1)}, bf16[32,1024]{1,0:T(8,128)(2,1)S(1)}, u32[]{:S(2)}, u32[]{:S(2)}) collective-permute-start(bf16[32,1024]{1,0:T(8,128)(2,1)} %param.9), channel_id=1, source_target_pairs={{0,16},{8,24},{16,0},{24,8},{1,17},{9,25},{17,1},{25,9},{2,18},{10... | collective-permute-start | bytes 196616 | tf_op jit(solution)/shard_map/ppermute | solution.py:26
  35.0 10.5 %collective-permute-start.3 = (bf16[128,1024]{1,0:T(8,128)(2,1)S(1)}, bf16[128,1024]{1,0:T(8,128)(2,1)S(1)}, u32[]{:S(2)}, u32[]{:S(2)}) collective-permute-start(bf16[128,1024]{1,0:T(8,128)(2,1)S(1)} %get-tuple-element.79), channel_id=1, source_target_pairs={{0,8},{8,16},{16,24},{24,0},{1,9},{9,17},{17,25},{25,1},{2,10},{10... | collective-permute-start | bytes 786440 | tf_op jit(solution)/shard_map/ppermute | solution.py:26
  36.8 9.3 %collective-permute-start.6 = (bf16[128,1024]{1,0:T(8,128)(2,1)S(1)}, bf16[128,1024]{1,0:T(8,128)(2,1)S(1)}, u32[]{:S(2)}, u32[]{:S(2)}) collective-permute-start(bf16[128,1024]{1,0:T(8,128)(2,1)S(1)} %get-tuple-element.78), channel_id=1, source_target_pairs={{0,24},{8,0},{16,8},{24,16},{1,25},{9,1},{17,9},{25,17},{2,26},{10... | collective-permute-start | bytes 786440 | tf_op jit(solution)/shard_map/ppermute | solution.py:26
  38.6 12.5 %collective-permute-start.4 = (bf16[128,1024]{1,0:T(8,128)(2,1)S(1)}, bf16[128,1024]{1,0:T(8,128)(2,1)S(1)}, u32[]{:S(2)}, u32[]{:S(2)}) collective-permute-start(bf16[128,1024]{1,0:T(8,128)(2,1)S(1)} %get-tuple-element.78), channel_id=1, source_target_pairs={{0,8},{8,16},{16,24},{24,0},{1,9},{9,17},{17,25},{25,1},{2,10},{10... | collective-permute-start | bytes 786440 | tf_op jit(solution)/shard_map/ppermute | solution.py:26
  40.4 15.7 %collective-permute-start.8 = (bf16[128,1024]{1,0:T(8,128)(2,1)S(1)}, bf16[128,1024]{1,0:T(8,128)(2,1)S(1)}, u32[]{:S(2)}, u32[]{:S(2)}) collective-permute-start(bf16[128,1024]{1,0:T(8,128)(2,1)S(1)} %get-tuple-element.79), channel_id=1, source_target_pairs={{0,24},{8,0},{16,8},{24,16},{1,25},{9,1},{17,9},{25,17},{2,26},{10... | collective-permute-start | bytes 786440 | tf_op jit(solution)/shard_map/ppermute | solution.py:26
  45.5 10.4 %collective-permute-start.5 = (bf16[128,1024]{1,0:T(8,128)(2,1)S(1)}, bf16[128,1024]{1,0:T(8,128)(2,1)S(1)}, u32[]{:S(2)}, u32[]{:S(2)}) collective-permute-start(bf16[128,1024]{1,0:T(8,128)(2,1)S(1)} %collective-permute-done.3), channel_id=1, source_target_pairs={{0,8},{8,16},{16,24},{24,0},{1,9},{9,17},{17,25},{25,1},{2,10},{10... | collective-permute-start | bytes 786440 | tf_op jit(solution)/shard_map/ppermute | solution.py:26
  46.1 10.0 %collective-permute-start.7 = (bf16[128,1024]{1,0:T(8,128)(2,1)S(1)}, bf16[128,1024]{1,0:T(8,128)(2,1)S(1)}, u32[]{:S(2)}, u32[]{:S(2)}) collective-permute-start(bf16[128,1024]{1,0:T(8,128)(2,1)S(1)} %collective-permute-done.6), channel_id=1, source_target_pairs={{0,24},{8,0},{16,8},{24,16},{1,25},{9,1},{17,9},{25,17},{2,26},{10... | collective-permute-start | bytes 786440 | tf_op jit(solution)/shard_map/ppermute | solution.py:26
  59.8 3.0 %collective-permute-start.9 = (bf16[512,1024]{1,0:T(8,128)(2,1)}, bf16[512,1024]{1,0:T(8,128)(2,1)}, u32[]{:S(2)}, u32[]{:S(2)}) collective-permute-start(bf16[512,1024]{1,0:T(8,128)(2,1)} %constant_dynamic-slice_fusion), channel_id=1, source_target_pairs={{0,32},{32,0},{1,33},{33,1},{2,34},{34,2},{3,35},{35,3},{4,36},{36... | collective-permute-start | bytes 3145736 | tf_op jit(solution)/shard_map/ppermute | solution.py:26
  65.0 9.4 %collective-permute-start.11 = (bf16[128,1024]{1,0:T(8,128)(2,1)}, bf16[128,1024]{1,0:T(8,128)(2,1)S(1)}, u32[]{:S(2)}, u32[]{:S(2)}) collective-permute-start(bf16[128,1024]{1,0:T(8,128)(2,1)} %get-tuple-element.30), channel_id=1, source_target_pairs={{0,64},{64,128},{128,192},{192,0},{1,65},{65,129},{129,193},{193,1... | collective-permute-start | bytes 786440 | tf_op jit(solution)/shard_map/ppermute | solution.py:26
  66.5 10.9 %collective-permute-start.12 = (bf16[128,1024]{1,0:T(8,128)(2,1)}, bf16[128,1024]{1,0:T(8,128)(2,1)S(1)}, u32[]{:S(2)}, u32[]{:S(2)}) collective-permute-start(bf16[128,1024]{1,0:T(8,128)(2,1)} %get-tuple-element.31), channel_id=1, source_target_pairs={{0,128},{64,192},{128,0},{192,64},{1,129},{65,193},{129,1},{193,65... | collective-permute-start | bytes 786440 | tf_op jit(solution)/shard_map/ppermute | solution.py:26
  67.6 13.5 %collective-permute-start.13 = (bf16[128,1024]{1,0:T(8,128)(2,1)S(1)}, bf16[128,1024]{1,0:T(8,128)(2,1)}, u32[]{:S(2)}, u32[]{:S(2)}) collective-permute-start(bf16[128,1024]{1,0:T(8,128)(2,1)S(1)} %get-tuple-element.32), channel_id=1, source_target_pairs={{0,192},{64,0},{128,64},{192,128},{1,193},{65,1},{129,65},{193,129... | collective-permute-start | bytes 786440 | tf_op jit(solution)/shard_map/ppermute | solution.py:26
  74.3 12.5 %collective-permute-start.10 = (bf16[512,512]{1,0:T(8,128)(2,1)}, bf16[512,512]{1,0:T(8,128)(2,1)S(1)}, u32[]{:S(2)}, u32[]{:S(2)}) collective-permute-start(bf16[512,512]{1,0:T(8,128)(2,1)} %broadcast_select_fusion.4), channel_id=1, source_target_pairs={{0,32},{32,0},{1,33},{33,1},{2,34},{34,2},{3,35},{35,3},{4,36},{36... | collective-permute-start | bytes 1572872 | tf_op jit(solution)/shard_map/ppermute | solution.py:26
  82.7 11.4 %collective-permute-start.15 = (bf16[128,512]{1,0:T(8,128)(2,1)S(1)}, bf16[128,512]{1,0:T(8,128)(2,1)S(1)}, u32[]{:S(2)}, u32[]{:S(2)}) collective-permute-start(bf16[128,512]{1,0:T(8,128)(2,1)S(1)} %multiply_convert_fusion.2), channel_id=1, source_target_pairs={{0,128},{64,192},{128,0},{192,64},{1,129},{65,193},{129,1},{193,65... | collective-permute-start | bytes 393224 | tf_op jit(solution)/shard_map/ppermute | solution.py:26
  84.8 9.3 %collective-permute-start.14 = (bf16[128,512]{1,0:T(8,128)(2,1)S(1)}, bf16[128,512]{1,0:T(8,128)(2,1)S(1)}, u32[]{:S(2)}, u32[]{:S(2)}) collective-permute-start(bf16[128,512]{1,0:T(8,128)(2,1)S(1)} %multiply_convert_fusion.2), channel_id=1, source_target_pairs={{0,64},{64,128},{128,192},{192,0},{1,65},{65,129},{129,193},{193,1... | collective-permute-start | bytes 393224 | tf_op jit(solution)/shard_map/ppermute | solution.py:26
  85.8 8.4 %collective-permute-start.16 = (bf16[128,512]{1,0:T(8,128)(2,1)S(1)}, bf16[128,512]{1,0:T(8,128)(2,1)}, u32[]{:S(2)}, u32[]{:S(2)}) collective-permute-start(bf16[128,512]{1,0:T(8,128)(2,1)S(1)} %multiply_convert_fusion.2), channel_id=1, source_target_pairs={{0,192},{64,0},{128,64},{192,128},{1,193},{65,1},{129,65},{193,129... | collective-permute-start | bytes 393224 | tf_op jit(solution)/shard_map/ppermute | solution.py:26
  87.8 12.9 %all-to-all-start.1 = ((bf16[4,128,512]{2,1,0:T(8,128)(2,1)}), bf16[4,128,512]{2,1,0:T(8,128)(2,1)S(1)}, u32[]{:S(2)}, u32[]{:S(2)}) async-start(bf16[4,128,512]{2,1,0:T(8,128)(2,1)} %bitcast.8), calls=%async_computation.1 | async-start | bytes 1048576 | tf_op jit(solution)/shard_map/all_to_all | solution.py:30
  100.7 6.3 %collective-permute-start.17 = (bf16[512,512]{1,0:T(8,128)(2,1)S(1)}, bf16[512,512]{1,0:T(8,128)(2,1)}, u32[]{:S(2)}, u32[]{:S(2)}) collective-permute-start(bf16[512,512]{1,0:T(8,128)(2,1)S(1)} %pad_maximum_fusion.3), channel_id=1, source_target_pairs={{0,32},{32,0},{1,33},{33,1},{2,34},{34,2},{3,35},{35,3},{4,36},{36... | collective-permute-start | bytes 1572872 | tf_op jit(solution)/shard_map/ppermute | solution.py:26
  102.1 24.0 %all-to-all-start.2 = ((bf16[4,128,1024]{2,1,0:T(8,128)(2,1)}), bf16[4,128,1024]{2,1,0:T(8,128)(2,1)S(1)}, u32[]{:S(2)}, u32[]{:S(2)}) async-start(bf16[4,128,1024]{2,1,0:T(8,128)(2,1)} %broadcast_in_dim.5), calls=%async_computation.2 | async-start | bytes 2097152 | tf_op jit(solution)/shard_map/all_to_all | solution.py:30
  109.6 15.3 %collective-permute-start.18 = (bf16[256,1024]{1,0:T(8,128)(2,1)S(1)}, bf16[256,1024]{1,0:T(8,128)(2,1)S(1)}, u32[]{:S(2)}, u32[]{:S(2)}) collective-permute-start(bf16[256,1024]{1,0:T(8,128)(2,1)S(1)} %pad_maximum_fusion.4), channel_id=1, source_target_pairs={{0,8},{8,16},{16,24},{24,0},{1,9},{9,17},{17,25},{25,1},{2,10},{10... | collective-permute-start | bytes 1572872 | tf_op jit(solution)/shard_map/ppermute | solution.py:26
  111.3 13.9 %collective-permute-start.19 = (bf16[256,1024]{1,0:T(8,128)(2,1)S(1)}, bf16[256,1024]{1,0:T(8,128)(2,1)S(1)}, u32[]{:S(2)}, u32[]{:S(2)}) collective-permute-start(bf16[256,1024]{1,0:T(8,128)(2,1)S(1)} %pad_maximum_fusion.5), channel_id=1, source_target_pairs={{0,24},{8,0},{16,8},{24,16},{1,25},{9,1},{17,9},{25,17},{2,26},{10... | collective-permute-start | bytes 1572872 | tf_op jit(solution)/shard_map/ppermute | solution.py:26
  126.0 4.7 %collective-permute-start.20 = (bf16[512,1024]{1,0:T(8,128)(2,1)S(1)}, bf16[512,1024]{1,0:T(8,128)(2,1)S(1)}, u32[]{:S(2)}, u32[]{:S(2)}) collective-permute-start(bf16[512,1024]{1,0:T(8,128)(2,1)S(1)} %bitcast.43), channel_id=1, source_target_pairs={{0,32},{32,0},{1,33},{33,1},{2,34},{34,2},{3,35},{35,3},{4,36},{36... | collective-permute-start | bytes 3145736 | tf_op jit(solution)/shard_map/ppermute | solution.py:26
  127.4 10.0 %collective-permute-start.21 = (bf16[128,1024]{1,0:T(8,128)(2,1)S(1)}, bf16[128,1024]{1,0:T(8,128)(2,1)S(1)}, u32[]{:S(2)}, u32[]{:S(2)}) collective-permute-start(bf16[128,1024]{1,0:T(8,128)(2,1)S(1)} %copy-done.20), channel_id=1, source_target_pairs={{0,8},{8,16},{16,24},{24,0},{1,9},{9,17},{17,25},{25,1},{2,10},{10... | collective-permute-start | bytes 786440 | tf_op jit(solution)/shard_map/ppermute | solution.py:26
  128.8 8.6 %collective-permute-start.22 = (bf16[128,1024]{1,0:T(8,128)(2,1)S(1)}, bf16[128,1024]{1,0:T(8,128)(2,1)S(1)}, u32[]{:S(2)}, u32[]{:S(2)}) collective-permute-start(bf16[128,1024]{1,0:T(8,128)(2,1)S(1)} %get-tuple-element.37), channel_id=1, source_target_pairs={{0,24},{8,0},{16,8},{24,16},{1,25},{9,1},{17,9},{25,17},{2,26},{10... | collective-permute-start | bytes 786440 | tf_op jit(solution)/shard_map/ppermute | solution.py:26
  141.1 27.0 %collective-permute-start.23 = (bf16[256,1024]{1,0:T(8,128)(2,1)}, bf16[256,1024]{1,0:T(8,128)(2,1)}, u32[]{:S(2)}, u32[]{:S(2)}) collective-permute-start(bf16[256,1024]{1,0:T(8,128)(2,1)} %get-tuple-element.40), channel_id=1, source_target_pairs={{0,24},{8,0},{16,8},{24,16},{1,25},{9,1},{17,9},{25,17},{2,26},{10... | collective-permute-start | bytes 1572872 | tf_op jit(solution)/shard_map/ppermute | solution.py:26
  144.2 26.0 %collective-permute-start.24 = (bf16[256,1024]{1,0:T(8,128)(2,1)}, bf16[256,1024]{1,0:T(8,128)(2,1)}, u32[]{:S(2)}, u32[]{:S(2)}) collective-permute-start(bf16[256,1024]{1,0:T(8,128)(2,1)} %get-tuple-element.41), channel_id=1, source_target_pairs={{0,8},{8,16},{16,24},{24,0},{1,9},{9,17},{17,25},{25,1},{2,10},{10... | collective-permute-start | bytes 1572872 | tf_op jit(solution)/shard_map/ppermute | solution.py:26
  144.2 26.0 %collective-permute-start.25 = (bf16[256,1024]{1,0:T(8,128)(2,1)}, bf16[256,1024]{1,0:T(8,128)(2,1)}, u32[]{:S(2)}, u32[]{:S(2)}) collective-permute-start(bf16[256,1024]{1,0:T(8,128)(2,1)} %get-tuple-element.42), channel_id=1, source_target_pairs={{0,16},{8,24},{16,0},{24,8},{1,17},{9,25},{17,1},{25,9},{2,18},{10... | collective-permute-start | bytes 1572872 | tf_op jit(solution)/shard_map/ppermute | solution.py:26
  147.1 20.2 %all-to-all-start.3 = ((bf16[8,32,1024]{2,1,0:T(8,128)(2,1)}), bf16[8,32,1024]{2,1,0:T(8,128)(2,1)S(1)}, u32[]{:S(2)}, u32[]{:S(2)}) async-start(bf16[8,32,1024]{2,1,0:T(8,128)(2,1)} %bitcast.20), calls=%async_computation.3 | async-start | bytes 1048576 | tf_op jit(solution)/shard_map/all_to_all | solution.py:30
  (23 other events, 131.6 us)
Sparse Core Ops, SparseCore 0:
  28.6 41.6 all-gather.2

commit v12 on v11

--- a/solution.py
+++ b/solution.py
@@ -75,16 +75,21 @@
     return sum_parts(exchange(partial, "x"), X)
 
 
-def reduce_row(partial):
-    rows = partial.shape[0] // CORE
+def reduce_row(operand, weights):
+    rows = operand.shape[0] // CORE
     share = rows // X
     core, place = lax.axis_index("core"), lax.axis_index("x")
-    received = shift(lax.dynamic_slice_in_dim(partial, (1 - core) * rows, rows, axis=0), "core", 1)
+
+    def half_of(index):
+        part = product(lax.dynamic_slice_in_dim(operand, index * rows, rows, axis=0), weights).astype(BF)
+        return with_layout_constraint(part, Layout((0, 1)))
+
+    received = shift(half_of(1 - core), "core", 1)
+    kept = half_of(core)
 
     def block(step):
         start = lax.bitwise_and(place + step, X - 1) * share
-        kept = lax.dynamic_slice_in_dim(partial, core * rows + start, share, axis=0)
-        return kept.astype(F32) + lax.dynamic_slice_in_dim(received, start, share, axis=0).astype(F32)
+        return sum(lax.dynamic_slice_in_dim(part, start, share, axis=0).astype(F32) for part in (kept, received))
 
     sent = lax.optimization_barrier([block(step).astype(BF) for step in range(1, X)])
     moved = [shift(sent[step - 1], "x", step) for step in range(1, X)]
@@ -117,21 +122,19 @@
     return [partial[j * rows : (j + 1) * rows] for j in range(Y)]
 
 
-def move_y_first(pieces):
+def first_rows(pieces):
     half = pieces[2].shape[0] // 2
     to_right = jnp.concatenate([pieces[2][:half], pieces[3][half:]], axis=0)
     to_left = jnp.concatenate([pieces[2][half:], pieces[1][:half]], axis=0)
-    return shift(to_right, "y", 1), shift(to_left, "y", 3)
-
-
-def add_y_first(pieces, from_left, from_right):
-    half = pieces[2].shape[0] // 2
-    return lax.optimization_barrier(
-        (add(pieces[3][:half], from_left[:half]), add(pieces[1][half:], from_right[:half]))
-    )
-
-
-def move_y_second(to_right, to_left):
+    return to_right, to_left, pieces[3][:half], pieces[1][half:], pieces[0]
+
+
+def add_y_first(to_right, to_left, from_left, from_right):
+    half = to_right.shape[0]
+    return lax.optimization_barrier((add(to_right, from_left[:half]), add(to_left, from_right[:half])))
+
+
+def move_y_both(to_right, to_left):
     return shift(to_right, "y", 1), shift(to_left, "y", 3)
 
 
@@ -162,8 +165,7 @@
     all_tokens = jnp.concatenate(gather_y_halves(tokens_z), axis=0)
     all_grads = lax.all_gather(grads_y, "z", axis=0, tiled=False)
 
-    gate_up = with_layout_constraint(product(all_tokens, both_weights).astype(BF), Layout((0, 1)))
-    gate_up, sent = reduce_row(gate_up)
+    gate_up, sent = reduce_row(all_tokens, both_weights)
     all_grads = after(all_grads, *sent)
     all_grads = jnp.swapaxes(all_grads, 0, 1).reshape(all_tokens.shape)
     hidden_partial = reduce_core(product_right_t(all_grads, down_weight).astype(BF))
@@ -178,10 +180,11 @@
     hidden_grad = sum_parts(hidden_grad, X)
     hidden = gather_core(hidden_half)
 
-    output_pieces = split_y(product(hidden, down_weight).astype(BF))
-    output_first = move_y_first(output_pieces)
-    to_right, to_left = add_y_first(output_pieces, *output_first)
-    output_second = move_y_second(to_right, to_left)
+    output_rows = first_rows(split_y(hidden))
+    output_parts = [product(part, down_weight).astype(BF) for part in output_rows[:4]]
+    output_first = move_y_both(*output_parts[:2])
+    to_right, to_left = add_y_first(*output_parts[2:4], *output_first)
+    output_second = move_y_both(to_right, to_left)
 
     gate_grad = (hidden_grad * up_value * sigmoid_gate * (1.0 + gate_value * (1.0 - sigmoid_gate))).astype(BF)
     up_grad = (hidden_grad * silu_gate).astype(BF)
@@ -189,12 +192,13 @@
     both_half, to_right, to_left = lax.optimization_barrier((both_half, to_right, to_left))
     both_grads = after(gather_core(both_half), *output_second)
 
-    input_pieces = lax.optimization_barrier(split_y(product_right_t(both_grads, both_weights).astype(BF)))
+    input_pieces = lax.optimization_barrier([product_right_t(part, both_weights).astype(BF) for part in split_y(both_grads)])
     input_moved = [shift(input_pieces[1], "y", 3), shift(input_pieces[3], "y", 1), shift(input_pieces[2], "y", 2)]
     down_weight_grad = product_left_t(after(hidden, *input_pieces), all_grads)
-    gate_weight_grad = product_left_t(all_tokens, both_grads[:, :width])
-    up_weight_grad = product_left_t(all_tokens, both_grads[:, width:])
-    output_total = reduce_z(sum_y_steps(after(output_pieces[0], *input_pieces), output_first, output_second))
+    later_grads = after(both_grads, *input_pieces)
+    gate_weight_grad = product_left_t(all_tokens, later_grads[:, :width])
+    up_weight_grad = product_left_t(all_tokens, later_grads[:, width:])
+    output_total = reduce_z(sum_y_steps(product(after(output_rows[4], *input_pieces), down_weight).astype(BF), output_first, output_second))
     input_moved, gate_weight_grad, up_weight_grad, down_weight_grad, output_total = lax.optimization_barrier(
         (input_moved, gate_weight_grad, up_weight_grad, down_weight_grad, output_total)
     )

time: 198 us -> 215 us (1.086)
  matrix products: 17.1 us -> 28.1 us
  other arithmetic: 16.5 us -> 22.9 us
  waiting for transfers between devices: 62.7 us -> 59.7 us
    ppermute x26, waiting for transfers between devices: 43.3 us -> 30.5 us  [shift(): lax.ppermute(block, axis, [(i, (i + step) % size) for i in range(size)])]
    all_to_all x4, waiting for transfers between devices: 18.9 us -> 29.2 us  [exchange(): return lax.all_to_all(blocks, axis, split_axis=0, concat_axis=0, tiled=True)]
    dot_general x2 -> x7, matrix products: 3.6 us -> 10.8 us  [product(): return jnp.dot(left_side, right_side, preferred_element_type=F32)]
    dot_general x2 -> x5, matrix products: 3.66 us -> 7.52 us  [product_right_t(): lax.dot_general(left_side, right_side, (((1,), (1,)), ((), ())), preferre...]
    reduce_sum x3, other arithmetic: 1.48 us -> 3.67 us  [sum_parts(): jnp.sum(parts.reshape((count, rows) + parts.shape[1:]).astype(F32), axis=0)]
    unnamed x53 -> x47, local copies, waits for them, and re-layouts: 2.46 us -> 4.46 us
  transfers between devices with their start and end apart: 31 -> 31, of which waited for: 20 -> 13; matrix products, arithmetic and copies ran while one was open for 17% -> 22% of each run, Pallas kernels for 0% -> 0%
where the time goes in v12:
time: 215 us; the launch traced here: 213 us
  waiting for transfers between devices  59.7 us (28%)
  starting transfers between devices  58.8 us (27%)
  matrix products  28.1 us (13%)
  other arithmetic  22.9 us (11%)
  blocking collectives  18.2 us (8%)
  between operations  14.5 us (7%)
  local copies, waits for them, and re-layouts  10.4 us (5%)
    ppermute x26, starting transfers between devices, shift(): lax.ppermute(block, axis, [(i, (i + step) % size) for i in range(size)])  34.8 us
    ppermute x26, waiting for transfers between devices, shift(): lax.ppermute(block, axis, [(i, (i + step) % size) for i in range(size)])  30.5 us
    all_to_all x4, waiting for transfers between devices, exchange(): return lax.all_to_all(blocks, axis, split_axis=0, concat_axis=0, tiled=True)  29.2 us
    all_to_all x4, starting transfers between devices, exchange(): return lax.all_to_all(blocks, axis, split_axis=0, concat_axis=0, tiled=True)  24 us
    all_to_all x1, blocking collectives, exchange(): return lax.all_to_all(blocks, axis, split_axis=0, concat_axis=0, tiled=True)  18.2 us
    dot_general x7, matrix products, product(): return jnp.dot(left_side, right_side, preferred_element_type=F32)  10.8 us
    dot_general x3, matrix products, product_left_t(): lax.dot_general(left_side, right_side, (((0,), (0,)), ((), ())), preferre...  9.84 us
    dot_general x5, matrix products, product_right_t(): lax.dot_general(left_side, right_side, (((1,), (1,)), ((), ())), preferre...  7.52 us
  transfers between devices with their start and end apart: 31, of which 13 were waited for; matrix products, arithmetic and copies ran while one was open for 22% of the time, Pallas kernels for 0%

profile of v12, /device:TPU:2, one launch (start us, length us, event | category | flops | bytes accessed | tf_op | source)
XLA Modules:
  0.0 212.6 jit_solution(147556603376702501)
XLA Ops:
  8.8 2.9 %collective-permute-start.1 = (bf16[32,1024]{1,0:T(8,128)(2,1)}, bf16[32,1024]{1,0:T(8,128)(2,1)S(1)}, u32[]{:S(2)}, u32[]{:S(2)}) collective-permute-start(bf16[32,1024]{1,0:T(8,128)(2,1)} %param.9), channel_id=1, source_target_pairs={{0,16},{8,24},{16,0},{24,8},{1,17},{9,25},{17,1},{25,9},{2,18},{10... | collective-permute-start | bytes 196616 | tf_op jit(solution)/shard_map/ppermute | solution.py:26
  14.8 8.5 %all-to-all-start = ((bf16[8,32,1024]{2,1,0:T(8,128)(2,1)}), bf16[8,32,1024]{2,1,0:T(8,128)(2,1)S(1)}, u32[]{:S(2)}, u32[]{:S(2)}) async-start(bf16[8,32,1024]{2,1,0:T(8,128)(2,1)} %broadcast_in_dim.4), calls=%async_computation | async-start | bytes 1048576 | tf_op jit(solution)/shard_map/all_to_all | solution.py:30
  25.0 15.0 %all-to-all-done = bf16[8,32,1024]{2,1,0:T(8,128)(2,1)S(1)} async-done(((bf16[8,32,1024]{2,1,0:T(8,128)(2,1)}), bf16[8,32,1024]{2,1,0:T(8,128)(2,1)S(1)}, u32[]{:S(2)}, u32[]{:S(2)}) %all-to-all-start) | async-done | bytes 524320 | tf_op jit(solution)/shard_map/all_to_all | solution.py:30
  41.0 3.2 %collective-permute-start.6 = (bf16[128,1024]{1,0:T(8,128)(2,1)S(1)}, bf16[128,1024]{1,0:T(8,128)(2,1)S(1)}, u32[]{:S(2)}, u32[]{:S(2)}) collective-permute-start(bf16[128,1024]{1,0:T(8,128)(2,1)S(1)} %get-tuple-element.73), channel_id=1, source_target_pairs={{0,24},{8,0},{16,8},{24,16},{1,25},{9,1},{17,9},{25,17},{2,26},{10... | collective-permute-start | bytes 786440 | tf_op jit(solution)/shard_map/ppermute | solution.py:26
  45.7 4.8 %collective-permute-done.3 = bf16[128,1024]{1,0:T(8,128)(2,1)S(1)} collective-permute-done((bf16[128,1024]{1,0:T(8,128)(2,1)S(1)}, bf16[128,1024]{1,0:T(8,128)(2,1)S(1)}, u32[]{:S(2)}, u32[]{:S(2)}) %collective-permute-start.3) | collective-permute-done | bytes 262176 | tf_op jit(solution)/shard_map/ppermute | solution.py:26
  50.5 3.3 %collective-permute-start.8 = (bf16[128,1024]{1,0:T(8,128)(2,1)S(1)}, bf16[128,1024]{1,0:T(8,128)(2,1)S(1)}, u32[]{:S(2)}, u32[]{:S(2)}) collective-permute-start(bf16[128,1024]{1,0:T(8,128)(2,1)S(1)} %get-tuple-element.74), channel_id=1, source_target_pairs={{0,24},{8,0},{16,8},{24,16},{1,25},{9,1},{17,9},{25,17},{2,26},{10... | collective-permute-start | bytes 786440 | tf_op jit(solution)/shard_map/ppermute | solution.py:26
  54.0 1.9 collective-permute-done.4
  55.9 2.8 %collective-permute-done.5 = bf16[128,1024]{1,0:T(8,128)(2,1)S(1)} collective-permute-done((bf16[128,1024]{1,0:T(8,128)(2,1)S(1)}, bf16[128,1024]{1,0:T(8,128)(2,1)S(1)}, u32[]{:S(2)}, u32[]{:S(2)}) %collective-permute-start.5) | collective-permute-done | bytes 262176 | tf_op jit(solution)/shard_map/ppermute | solution.py:26
  62.0 3.2 %convolution_convert_fusion.2 = bf16[512,1024]{1,0:T(8,128)(2,1)S(1)} fusion(bf16[1024,1024]{1,0:T(8,128)(2,1)} %copy-done.14, bf16[1024,1024]{1,0:T(8,128)(2,1)} %copy-done.18, s32[]{:T(128)S(6)} %select_n.69), kind=kOutput, calls=%fused_computation.3 | convolution fusion | flops 1074266112 | bytes 4194308 | tf_op jit(solution)/shard_map/dot_general | solution.py:13
  70.0 2.2 %collective-permute-start.13 = (bf16[128,1024]{1,0:T(8,128)(2,1)S(1)}, bf16[128,1024]{1,0:T(8,128)(2,1)}, u32[]{:S(2)}, u32[]{:S(2)}) collective-permute-start(bf16[128,1024]{1,0:T(8,128)(2,1)S(1)} %get-tuple-element.33), channel_id=1, source_target_pairs={{0,192},{64,0},{128,64},{192,128},{1,193},{65,1},{129,65},{193,129... | collective-permute-start | bytes 786440 | tf_op jit(solution)/shard_map/ppermute | solution.py:26
  77.1 2.8 %collective-permute-done.12 = bf16[128,1024]{1,0:T(8,128)(2,1)} collective-permute-done((bf16[128,1024]{1,0:T(8,128)(2,1)}, bf16[128,1024]{1,0:T(8,128)(2,1)}, u32[]{:S(2)}, u32[]{:S(2)}) %collective-permute-start.12) | collective-permute-done | bytes 262176 | tf_op jit(solution)/shard_map/ppermute | solution.py:26
  79.9 3.9 %collective-permute-done.13 = bf16[128,1024]{1,0:T(8,128)(2,1)} collective-permute-done((bf16[128,1024]{1,0:T(8,128)(2,1)S(1)}, bf16[128,1024]{1,0:T(8,128)(2,1)}, u32[]{:S(2)}, u32[]{:S(2)}) %collective-permute-start.13) | collective-permute-done | bytes 262176 | tf_op jit(solution)/shard_map/ppermute | solution.py:26
  90.9 2.1 add_convert_fusion.1
  92.9 5.7 %all-to-all-start.1 = ((bf16[4,128,512]{2,1,0:T(8,128)(2,1)}), bf16[4,128,512]{2,1,0:T(8,128)(2,1)}, u32[]{:S(2)}, u32[]{:S(2)}) async-start(bf16[4,128,512]{2,1,0:T(8,128)(2,1)} %bitcast.50), calls=%async_computation.1 | async-start | bytes 1048576 | tf_op jit(solution)/shard_map/all_to_all | solution.py:30
  101.6 4.1 %all-to-all-done.1 = bf16[4,128,512]{2,1,0:T(8,128)(2,1)} async-done(((bf16[4,128,512]{2,1,0:T(8,128)(2,1)}), bf16[4,128,512]{2,1,0:T(8,128)(2,1)}, u32[]{:S(2)}, u32[]{:S(2)}) %all-to-all-start.1) | async-done | bytes 524320 | tf_op jit(solution)/shard_map/all_to_all | solution.py:30
  109.5 3.7 %collective-permute-start.19 = (bf16[256,1024]{1,0:T(8,128)(2,1)}, bf16[256,1024]{1,0:T(8,128)(2,1)}, u32[]{:S(2)}, u32[]{:S(2)}) collective-permute-start(bf16[256,1024]{1,0:T(8,128)(2,1)} %convolution_convert_fusion.4), channel_id=1, source_target_pairs={{0,24},{8,0},{16,8},{24,16},{1,25},{9,1},{17,9},{25,17},{2,26},{10... | collective-permute-start | bytes 1572872 | tf_op jit(solution)/shard_map/ppermute | solution.py:26
  115.6 5.7 %all-to-all-start.2 = ((bf16[4,128,1024]{2,1,0:T(8,128)(2,1)}), bf16[4,128,1024]{2,1,0:T(8,128)(2,1)}, u32[]{:S(2)}, u32[]{:S(2)}) async-start(bf16[4,128,1024]{2,1,0:T(8,128)(2,1)} %broadcast_in_dim.5), calls=%async_computation.2 | async-start | bytes 2097152 | tf_op jit(solution)/shard_map/all_to_all | solution.py:30
  121.2 4.1 %collective-permute-done.19 = bf16[256,1024]{1,0:T(8,128)(2,1)} collective-permute-done((bf16[256,1024]{1,0:T(8,128)(2,1)}, bf16[256,1024]{1,0:T(8,128)(2,1)}, u32[]{:S(2)}, u32[]{:S(2)}) %collective-permute-start.19) | collective-permute-done | bytes 524320 | tf_op jit(solution)/shard_map/ppermute | solution.py:26
  126.6 3.3 %collective-permute-done.18 = bf16[256,1024]{1,0:T(8,128)(2,1)} collective-permute-done((bf16[256,1024]{1,0:T(8,128)(2,1)}, bf16[256,1024]{1,0:T(8,128)(2,1)}, u32[]{:S(2)}, u32[]{:S(2)}) %collective-permute-start.18) | collective-permute-done | bytes 524320 | tf_op jit(solution)/shard_map/ppermute | solution.py:26
  130.0 2.0 fusion.2
  132.0 3.6 %all-to-all-done.2 = bf16[4,128,1024]{2,1,0:T(8,128)(2,1)} async-done(((bf16[4,128,1024]{2,1,0:T(8,128)(2,1)}), bf16[4,128,1024]{2,1,0:T(8,128)(2,1)}, u32[]{:S(2)}, u32[]{:S(2)}) %all-to-all-start.2) | async-done | bytes 1048608 | tf_op jit(solution)/shard_map/all_to_all | solution.py:30
  136.6 2.3 %pad_maximum_fusion.1 = bf16[1024,512]{1,0:T(8,128)(2,1)} fusion(bf16[512,512]{1,0:T(8,128)(2,1)} %copy-done.3, bf16[512,512]{1,0:T(8,128)(2,1)} %copy-done.2), kind=kLoop, calls=%fused_computation.19 | loop fusion | flops 2097152 | bytes 2097152 | tf_op jit(solution)/shard_map/concatenate | solution.py:113
  138.9 3.2 %collective-permute-start.22 = (bf16[128,1024]{1,0:T(8,128)(2,1)S(1)}, bf16[128,1024]{1,0:T(8,128)(2,1)S(1)}, u32[]{:S(2)}, u32[]{:S(2)}) collective-permute-start(bf16[128,1024]{1,0:T(8,128)(2,1)S(1)} %fusion.5), channel_id=1, source_target_pairs={{0,24},{8,0},{16,8},{24,16},{1,25},{9,1},{17,9},{25,17},{2,26},{10... | collective-permute-start | bytes 786440 | tf_op jit(solution)/shard_map/ppermute | solution.py:26
  143.7 5.1 %collective-permute-done.21 = bf16[128,1024]{1,0:T(8,128)(2,1)S(1)} collective-permute-done((bf16[128,1024]{1,0:T(8,128)(2,1)S(1)}, bf16[128,1024]{1,0:T(8,128)(2,1)S(1)}, u32[]{:S(2)}, u32[]{:S(2)}) %collective-permute-start.21) | collective-permute-done | bytes 262176 | tf_op jit(solution)/shard_map/ppermute | solution.py:26
  155.0 2.9 %collective-permute-start.23 = (bf16[256,1024]{1,0:T(8,128)(2,1)}, bf16[256,1024]{1,0:T(8,128)(2,1)}, u32[]{:S(2)}, u32[]{:S(2)}) collective-permute-start(bf16[256,1024]{1,0:T(8,128)(2,1)} %convolution_convert_fusion.8), channel_id=1, source_target_pairs={{0,24},{8,0},{16,8},{24,16},{1,25},{9,1},{17,9},{25,17},{2,26},{10... | collective-permute-start | bytes 1572872 | tf_op jit(solution)/shard_map/ppermute | solution.py:26
  158.0 2.0 collective-permute-start.25
  162.6 4.2 %all-to-all-start.3 = ((bf16[8,32,1024]{2,1,0:T(8,128)(2,1)}), bf16[8,32,1024]{2,1,0:T(8,128)(2,1)}, u32[]{:S(2)}, u32[]{:S(2)}) async-start(bf16[8,32,1024]{2,1,0:T(8,128)(2,1)} %bitcast.53), calls=%async_computation.3 | async-start | bytes 1048576 | tf_op jit(solution)/shard_map/all_to_all | solution.py:30
  166.8 4.6 %fusion.6 = f32[1024,512]{1,0:T(8,128)} fusion(bf16[1024,1024]{1,0:T(8,128)(2,1)} %copy-done.18, bf16[1024,1024]{1,0:T(8,128)(2,1)} %copy-done.8), kind=kOutput, calls=%fused_computation.22 | convolution fusion | flops 1073741824 | bytes 5242880 | tf_op jit(solution)/shard_map/dot_general | solution.py:21
  171.4 2.6 %fusion.8 = f32[1024,512]{1,0:T(8,128)} fusion(bf16[1024,1024]{1,0:T(8,128)(2,1)S(1)} %copy-done.19, bf16[1024,1024]{1,0:T(8,128)(2,1)S(1)} %copy-done.9), kind=kOutput, calls=%fused_computation.24 | convolution fusion | flops 1073741824 | bytes 5242880 | tf_op jit(solution)/shard_map/dot_general | solution.py:21
  174.0 2.6 %fusion.31 = f32[512,1024]{1,0:T(8,128)} fusion(bf16[1024,512]{1,0:T(8,128)(2,1)S(1)} %copy-done.4, bf16[1024,1024]{1,0:T(8,128)(2,1)S(1)} %bitcast.47), kind=kOutput, calls=%fused_computation.81 | convolution fusion | flops 1073741824 | bytes 5242880 | tf_op jit(solution)/shard_map/dot_general | solution.py:21
  176.6 6.6 %all-to-all-done.3 = bf16[8,32,1024]{2,1,0:T(8,128)(2,1)} async-done(((bf16[8,32,1024]{2,1,0:T(8,128)(2,1)}), bf16[8,32,1024]{2,1,0:T(8,128)(2,1)}, u32[]{:S(2)}, u32[]{:S(2)}) %all-to-all-start.3) | async-done | bytes 524320 | tf_op jit(solution)/shard_map/all_to_all | solution.py:30
  186.8 18.2 %all_to_all.48 = bf16[8,32,1024]{2,1,0:T(8,128)(2,1)S(1)} all-to-all(bf16[8,32,1024]{2,1,0:T(8,128)(2,1)S(1)} %bitcast.51), channel_id=1, replica_groups=mesh['x'=4,'core'=2,'y'=4,'z'=8] {'z'}, dimensions={0} | all-to-all | bytes 1048576 | tf_op jit(solution)/shard_map/all_to_all | solution.py:30
  (125 shorter events, 55.2 us)
Async XLA Ops:
  7.2 66.8 %copy-start = (bf16[512,1024]{1,0:T(8,128)(2,1)S(1)}, bf16[512,1024]{1,0:T(8,128)(2,1)}, u32[]{:S(2)}) copy-start(bf16[512,1024]{1,0:T(8,128)(2,1)} %param.8) | copy-start | bytes 3145732
  7.2 16.1 %collective-permute-start = (bf16[32,1024]{1,0:T(8,128)(2,1)}, bf16[32,1024]{1,0:T(8,128)(2,1)S(1)}, u32[]{:S(2)}, u32[]{:S(2)}) collective-permute-start(bf16[32,1024]{1,0:T(8,128)(2,1)} %param.9), channel_id=1, source_target_pairs={{0,8},{8,16},{16,24},{24,0},{1,9},{9,17},{17,25},{25,1},{2,10},{10... | collective-permute-start | bytes 196616 | tf_op jit(solution)/shard_map/ppermute | solution.py:26
  8.8 14.5 %collective-permute-start.1 = (bf16[32,1024]{1,0:T(8,128)(2,1)}, bf16[32,1024]{1,0:T(8,128)(2,1)S(1)}, u32[]{:S(2)}, u32[]{:S(2)}) collective-permute-start(bf16[32,1024]{1,0:T(8,128)(2,1)} %param.9), channel_id=1, source_target_pairs={{0,16},{8,24},{16,0},{24,8},{1,17},{9,25},{17,1},{25,9},{2,18},{10... | collective-permute-start | bytes 196616 | tf_op jit(solution)/shard_map/ppermute | solution.py:26
  11.7 11.6 %collective-permute-start.2 = (bf16[32,1024]{1,0:T(8,128)(2,1)}, bf16[32,1024]{1,0:T(8,128)(2,1)S(1)}, u32[]{:S(2)}, u32[]{:S(2)}) collective-permute-start(bf16[32,1024]{1,0:T(8,128)(2,1)} %param.9), channel_id=1, source_target_pairs={{0,24},{8,0},{16,8},{24,16},{1,25},{9,1},{17,9},{25,17},{2,26},{10... | collective-permute-start | bytes 196616 | tf_op jit(solution)/shard_map/ppermute | solution.py:26
  14.8 25.1 %all-to-all-start = ((bf16[8,32,1024]{2,1,0:T(8,128)(2,1)}), bf16[8,32,1024]{2,1,0:T(8,128)(2,1)S(1)}, u32[]{:S(2)}, u32[]{:S(2)}) async-start(bf16[8,32,1024]{2,1,0:T(8,128)(2,1)} %broadcast_in_dim.4), calls=%async_computation | async-start | bytes 1048576 | tf_op jit(solution)/shard_map/all_to_all | solution.py:30
  23.3 48.9 %all-gather.3.cloned.1.call-start = ((), (), s32[]{:S(2)}) async-start(), calls=%async_computation.5 | async-start | bytes 2359296 | tf_op jit(solution)/shard_map/all_gather | solution.py:166
  39.9 10.5 %collective-permute-start.3 = (bf16[128,1024]{1,0:T(8,128)(2,1)S(1)}, bf16[128,1024]{1,0:T(8,128)(2,1)S(1)}, u32[]{:S(2)}, u32[]{:S(2)}) collective-permute-start(bf16[128,1024]{1,0:T(8,128)(2,1)S(1)} %get-tuple-element.74), channel_id=1, source_target_pairs={{0,8},{8,16},{16,24},{24,0},{1,9},{9,17},{17,25},{25,1},{2,10},{10... | collective-permute-start | bytes 786440 | tf_op jit(solution)/shard_map/ppermute | solution.py:26
  40.9 15.0 %collective-permute-start.4 = (bf16[128,1024]{1,0:T(8,128)(2,1)S(1)}, bf16[128,1024]{1,0:T(8,128)(2,1)S(1)}, u32[]{:S(2)}, u32[]{:S(2)}) collective-permute-start(bf16[128,1024]{1,0:T(8,128)(2,1)S(1)} %get-tuple-element.73), channel_id=1, source_target_pairs={{0,8},{8,16},{16,24},{24,0},{1,9},{9,17},{17,25},{25,1},{2,10},{10... | collective-permute-start | bytes 786440 | tf_op jit(solution)/shard_map/ppermute | solution.py:26
  41.0 12.9 %collective-permute-start.6 = (bf16[128,1024]{1,0:T(8,128)(2,1)S(1)}, bf16[128,1024]{1,0:T(8,128)(2,1)S(1)}, u32[]{:S(2)}, u32[]{:S(2)}) collective-permute-start(bf16[128,1024]{1,0:T(8,128)(2,1)S(1)} %get-tuple-element.73), channel_id=1, source_target_pairs={{0,24},{8,0},{16,8},{24,16},{1,25},{9,1},{17,9},{25,17},{2,26},{10... | collective-permute-start | bytes 786440 | tf_op jit(solution)/shard_map/ppermute | solution.py:26
  50.5 8.2 %collective-permute-start.5 = (bf16[128,1024]{1,0:T(8,128)(2,1)S(1)}, bf16[128,1024]{1,0:T(8,128)(2,1)S(1)}, u32[]{:S(2)}, u32[]{:S(2)}) collective-permute-start(bf16[128,1024]{1,0:T(8,128)(2,1)S(1)} %collective-permute-done.3), channel_id=1, source_target_pairs={{0,8},{8,16},{16,24},{24,0},{1,9},{9,17},{17,25},{25,1},{2,10},{10... | collective-permute-start | bytes 786440 | tf_op jit(solution)/shard_map/ppermute | solution.py:26
  50.5 10.0 %collective-permute-start.8 = (bf16[128,1024]{1,0:T(8,128)(2,1)S(1)}, bf16[128,1024]{1,0:T(8,128)(2,1)S(1)}, u32[]{:S(2)}, u32[]{:S(2)}) collective-permute-start(bf16[128,1024]{1,0:T(8,128)(2,1)S(1)} %get-tuple-element.74), channel_id=1, source_target_pairs={{0,24},{8,0},{16,8},{24,16},{1,25},{9,1},{17,9},{25,17},{2,26},{10... | collective-permute-start | bytes 786440 | tf_op jit(solution)/shard_map/ppermute | solution.py:26
  53.8 6.7 %collective-permute-start.7 = (bf16[128,1024]{1,0:T(8,128)(2,1)S(1)}, bf16[128,1024]{1,0:T(8,128)(2,1)S(1)}, u32[]{:S(2)}, u32[]{:S(2)}) collective-permute-start(bf16[128,1024]{1,0:T(8,128)(2,1)S(1)} %collective-permute-done.6), channel_id=1, source_target_pairs={{0,24},{8,0},{16,8},{24,16},{1,25},{9,1},{17,9},{25,17},{2,26},{10... | collective-permute-start | bytes 786440 | tf_op jit(solution)/shard_map/ppermute | solution.py:26
  62.0 3.3 %collective-permute-start.9 = (bf16[512,1024]{1,0:T(8,128)(2,1)S(1)}, bf16[512,1024]{1,0:T(8,128)(2,1)S(1)}, u32[]{:S(2)}, u32[]{:S(2)}) collective-permute-start(bf16[512,1024]{1,0:T(8,128)(2,1)S(1)} %convolution_convert_fusion.1), channel_id=1, source_target_pairs={{0,32},{32,0},{1,33},{33,1},{2,34},{34,2},{3,35},{35,3},{4,36},{36... | collective-permute-start | bytes 3145736 | tf_op jit(solution)/shard_map/ppermute | solution.py:26
  67.4 9.7 %collective-permute-start.11 = (bf16[128,1024]{1,0:T(8,128)(2,1)}, bf16[128,1024]{1,0:T(8,128)(2,1)}, u32[]{:S(2)}, u32[]{:S(2)}) collective-permute-start(bf16[128,1024]{1,0:T(8,128)(2,1)} %get-tuple-element.31), channel_id=1, source_target_pairs={{0,64},{64,128},{128,192},{192,0},{1,65},{65,129},{129,193},{193,1... | collective-permute-start | bytes 786440 | tf_op jit(solution)/shard_map/ppermute | solution.py:26
  68.9 11.0 %collective-permute-start.12 = (bf16[128,1024]{1,0:T(8,128)(2,1)}, bf16[128,1024]{1,0:T(8,128)(2,1)}, u32[]{:S(2)}, u32[]{:S(2)}) collective-permute-start(bf16[128,1024]{1,0:T(8,128)(2,1)} %get-tuple-element.32), channel_id=1, source_target_pairs={{0,128},{64,192},{128,0},{192,64},{1,129},{65,193},{129,1},{193,65... | collective-permute-start | bytes 786440 | tf_op jit(solution)/shard_map/ppermute | solution.py:26
  70.0 13.8 %collective-permute-start.13 = (bf16[128,1024]{1,0:T(8,128)(2,1)S(1)}, bf16[128,1024]{1,0:T(8,128)(2,1)}, u32[]{:S(2)}, u32[]{:S(2)}) collective-permute-start(bf16[128,1024]{1,0:T(8,128)(2,1)S(1)} %get-tuple-element.33), channel_id=1, source_target_pairs={{0,192},{64,0},{128,64},{192,128},{1,193},{65,1},{129,65},{193,129... | collective-permute-start | bytes 786440 | tf_op jit(solution)/shard_map/ppermute | solution.py:26
  77.1 13.7 %collective-permute-start.10 = (bf16[512,512]{1,0:T(8,128)(2,1)}, bf16[512,512]{1,0:T(8,128)(2,1)}, u32[]{:S(2)}, u32[]{:S(2)}) collective-permute-start(bf16[512,512]{1,0:T(8,128)(2,1)} %broadcast_select_fusion.4), channel_id=1, source_target_pairs={{0,32},{32,0},{1,33},{33,1},{2,34},{34,2},{3,35},{35,3},{4,36},{36... | collective-permute-start | bytes 1572872 | tf_op jit(solution)/shard_map/ppermute | solution.py:26
  86.1 13.6 %collective-permute-start.14 = (bf16[128,512]{1,0:T(8,128)(2,1)S(1)}, bf16[128,512]{1,0:T(8,128)(2,1)S(1)}, u32[]{:S(2)}, u32[]{:S(2)}) collective-permute-start(bf16[128,512]{1,0:T(8,128)(2,1)S(1)} %multiply_convert_fusion.2), channel_id=1, source_target_pairs={{0,64},{64,128},{128,192},{192,0},{1,65},{65,129},{129,193},{193,1... | collective-permute-start | bytes 393224 | tf_op jit(solution)/shard_map/ppermute | solution.py:26
  87.7 12.0 %collective-permute-start.15 = (bf16[128,512]{1,0:T(8,128)(2,1)S(1)}, bf16[128,512]{1,0:T(8,128)(2,1)S(1)}, u32[]{:S(2)}, u32[]{:S(2)}) collective-permute-start(bf16[128,512]{1,0:T(8,128)(2,1)S(1)} %multiply_convert_fusion.2), channel_id=1, source_target_pairs={{0,128},{64,192},{128,0},{192,64},{1,129},{65,193},{129,1},{193,65... | collective-permute-start | bytes 393224 | tf_op jit(solution)/shard_map/ppermute | solution.py:26
  89.2 10.5 %collective-permute-start.16 = (bf16[128,512]{1,0:T(8,128)(2,1)S(1)}, bf16[128,512]{1,0:T(8,128)(2,1)}, u32[]{:S(2)}, u32[]{:S(2)}) collective-permute-start(bf16[128,512]{1,0:T(8,128)(2,1)S(1)} %multiply_convert_fusion.2), channel_id=1, source_target_pairs={{0,192},{64,0},{128,64},{192,128},{1,193},{65,1},{129,65},{193,129... | collective-permute-start | bytes 393224 | tf_op jit(solution)/shard_map/ppermute | solution.py:26
  92.9 12.7 %all-to-all-start.1 = ((bf16[4,128,512]{2,1,0:T(8,128)(2,1)}), bf16[4,128,512]{2,1,0:T(8,128)(2,1)}, u32[]{:S(2)}, u32[]{:S(2)}) async-start(bf16[4,128,512]{2,1,0:T(8,128)(2,1)} %bitcast.50), calls=%async_computation.1 | async-start | bytes 1048576 | tf_op jit(solution)/shard_map/all_to_all | solution.py:30
  105.7 2.4 %collective-permute-start.17 = (bf16[512,512]{1,0:T(8,128)(2,1)}, bf16[512,512]{1,0:T(8,128)(2,1)S(1)}, u32[]{:S(2)}, u32[]{:S(2)}) collective-permute-start(bf16[512,512]{1,0:T(8,128)(2,1)} %pad_maximum_fusion.3), channel_id=1, source_target_pairs={{0,32},{32,0},{1,33},{33,1},{2,34},{34,2},{3,35},{35,3},{4,36},{36... | collective-permute-start | bytes 1572872 | tf_op jit(solution)/shard_map/ppermute | solution.py:26
  109.5 15.8 %collective-permute-start.19 = (bf16[256,1024]{1,0:T(8,128)(2,1)}, bf16[256,1024]{1,0:T(8,128)(2,1)}, u32[]{:S(2)}, u32[]{:S(2)}) collective-permute-start(bf16[256,1024]{1,0:T(8,128)(2,1)} %convolution_convert_fusion.4), channel_id=1, source_target_pairs={{0,24},{8,0},{16,8},{24,16},{1,25},{9,1},{17,9},{25,17},{2,26},{10... | collective-permute-start | bytes 1572872 | tf_op jit(solution)/shard_map/ppermute | solution.py:26
  114.4 15.5 %collective-permute-start.18 = (bf16[256,1024]{1,0:T(8,128)(2,1)}, bf16[256,1024]{1,0:T(8,128)(2,1)}, u32[]{:S(2)}, u32[]{:S(2)}) collective-permute-start(bf16[256,1024]{1,0:T(8,128)(2,1)} %convolution_convert_fusion.5), channel_id=1, source_target_pairs={{0,8},{8,16},{16,24},{24,0},{1,9},{9,17},{17,25},{25,1},{2,10},{10... | collective-permute-start | bytes 1572872 | tf_op jit(solution)/shard_map/ppermute | solution.py:26
  115.6 20.0 %all-to-all-start.2 = ((bf16[4,128,1024]{2,1,0:T(8,128)(2,1)}), bf16[4,128,1024]{2,1,0:T(8,128)(2,1)}, u32[]{:S(2)}, u32[]{:S(2)}) async-start(bf16[4,128,1024]{2,1,0:T(8,128)(2,1)} %broadcast_in_dim.5), calls=%async_computation.2 | async-start | bytes 2097152 | tf_op jit(solution)/shard_map/all_to_all | solution.py:30
  135.6 6.5 %collective-permute-start.20 = (bf16[512,1024]{1,0:T(8,128)(2,1)}, bf16[512,1024]{1,0:T(8,128)(2,1)S(1)}, u32[]{:S(2)}, u32[]{:S(2)}) collective-permute-start(bf16[512,1024]{1,0:T(8,128)(2,1)} %bitcast.19), channel_id=1, source_target_pairs={{0,32},{32,0},{1,33},{33,1},{2,34},{34,2},{3,35},{35,3},{4,36},{36... | collective-permute-start | bytes 3145736 | tf_op jit(solution)/shard_map/ppermute | solution.py:26
  138.9 9.9 %collective-permute-start.21 = (bf16[128,1024]{1,0:T(8,128)(2,1)S(1)}, bf16[128,1024]{1,0:T(8,128)(2,1)S(1)}, u32[]{:S(2)}, u32[]{:S(2)}) collective-permute-start(bf16[128,1024]{1,0:T(8,128)(2,1)S(1)} %copy-done.17), channel_id=1, source_target_pairs={{0,8},{8,16},{16,24},{24,0},{1,9},{9,17},{17,25},{25,1},{2,10},{10... | collective-permute-start | bytes 786440 | tf_op jit(solution)/shard_map/ppermute | solution.py:26
  138.9 9.9 %collective-permute-start.22 = (bf16[128,1024]{1,0:T(8,128)(2,1)S(1)}, bf16[128,1024]{1,0:T(8,128)(2,1)S(1)}, u32[]{:S(2)}, u32[]{:S(2)}) collective-permute-start(bf16[128,1024]{1,0:T(8,128)(2,1)S(1)} %fusion.5), channel_id=1, source_target_pairs={{0,24},{8,0},{16,8},{24,16},{1,25},{9,1},{17,9},{25,17},{2,26},{10... | collective-permute-start | bytes 786440 | tf_op jit(solution)/shard_map/ppermute | solution.py:26
  155.0 29.9 %collective-permute-start.23 = (bf16[256,1024]{1,0:T(8,128)(2,1)}, bf16[256,1024]{1,0:T(8,128)(2,1)}, u32[]{:S(2)}, u32[]{:S(2)}) collective-permute-start(bf16[256,1024]{1,0:T(8,128)(2,1)} %convolution_convert_fusion.8), channel_id=1, source_target_pairs={{0,24},{8,0},{16,8},{24,16},{1,25},{9,1},{17,9},{25,17},{2,26},{10... | collective-permute-start | bytes 1572872 | tf_op jit(solution)/shard_map/ppermute | solution.py:26
  158.0 27.0 %collective-permute-start.24 = (bf16[256,1024]{1,0:T(8,128)(2,1)}, bf16[256,1024]{1,0:T(8,128)(2,1)}, u32[]{:S(2)}, u32[]{:S(2)}) collective-permute-start(bf16[256,1024]{1,0:T(8,128)(2,1)} %convolution_convert_fusion.6), channel_id=1, source_target_pairs={{0,8},{8,16},{16,24},{24,0},{1,9},{9,17},{17,25},{25,1},{2,10},{10... | collective-permute-start | bytes 1572872 | tf_op jit(solution)/shard_map/ppermute | solution.py:26
  158.0 27.0 %collective-permute-start.25 = (bf16[256,1024]{1,0:T(8,128)(2,1)}, bf16[256,1024]{1,0:T(8,128)(2,1)}, u32[]{:S(2)}, u32[]{:S(2)}) collective-permute-start(bf16[256,1024]{1,0:T(8,128)(2,1)} %convolution_convert_fusion.7), channel_id=1, source_target_pairs={{0,16},{8,24},{16,0},{24,8},{1,17},{9,25},{17,1},{25,9},{2,18},{10... | collective-permute-start | bytes 1572872 | tf_op jit(solution)/shard_map/ppermute | solution.py:26
  162.6 20.6 %all-to-all-start.3 = ((bf16[8,32,1024]{2,1,0:T(8,128)(2,1)}), bf16[8,32,1024]{2,1,0:T(8,128)(2,1)}, u32[]{:S(2)}, u32[]{:S(2)}) async-start(bf16[8,32,1024]{2,1,0:T(8,128)(2,1)} %bitcast.53), calls=%async_computation.3 | async-start | bytes 1048576 | tf_op jit(solution)/shard_map/all_to_all | solution.py:30
  (19 other events, 123.0 us)
Sparse Core Ops, SparseCore 0:
  25.9 40.4 all-gather.2

commit v13 on v11

--- a/solution.py
+++ b/solution.py
@@ -165,8 +165,10 @@
     gate_up = with_layout_constraint(product(all_tokens, both_weights).astype(BF), Layout((0, 1)))
     gate_up, sent = reduce_row(gate_up)
     all_grads = after(all_grads, *sent)
+    hidden_partial = product_right_t(all_grads.reshape(all_tokens.shape), down_weight).astype(BF)
+    hidden_partial = jnp.swapaxes(hidden_partial.reshape(all_grads.shape[:3] + (width,)), 0, 1).reshape(-1, width)
+    hidden_partial = reduce_core(hidden_partial)
     all_grads = jnp.swapaxes(all_grads, 0, 1).reshape(all_tokens.shape)
-    hidden_partial = reduce_core(product_right_t(all_grads, down_weight).astype(BF))
     gate_value = gate_up[:, :width]
     up_value = gate_up[:, width:]
     sigmoid_gate = jax.nn.sigmoid(gate_value)
@@ -174,7 +176,9 @@
     hidden_share = (silu_gate * up_value).astype(BF)
 
     hidden_half = gather_x(hidden_share)
-    hidden_grad, hidden_half = lax.optimization_barrier((exchange(hidden_partial, "x"), hidden_half))
+    hidden_grad, hidden_half, all_grads = lax.optimization_barrier(
+        (exchange(hidden_partial, "x"), hidden_half, all_grads)
+    )
     hidden_grad = sum_parts(hidden_grad, X)
     hidden = gather_core(hidden_half)
 

time: 198 us -> 198 us (level)
    all_to_all x4, waiting for transfers between devices: 18.9 us -> 16.9 us  [exchange(): return lax.all_to_all(blocks, axis, split_axis=0, concat_axis=0, tiled=True)]
where the time goes in v13:
time: 198 us; the launch traced here: 197 us
  waiting for transfers between devices  61.5 us (31%)
  starting transfers between devices  58.9 us (30%)
  matrix products  18.7 us (9%)
  blocking collectives  17.4 us (9%)
  other arithmetic  15.8 us (8%)
  between operations  14.5 us (7%)
  local copies, waits for them, and re-layouts  9.98 us (5%)
    ppermute x26, waiting for transfers between devices, shift(): lax.ppermute(block, axis, [(i, (i + step) % size) for i in range(size)])  44.1 us
    ppermute x26, starting transfers between devices, shift(): lax.ppermute(block, axis, [(i, (i + step) % size) for i in range(size)])  35.8 us
    all_to_all x4, starting transfers between devices, exchange(): return lax.all_to_all(blocks, axis, split_axis=0, concat_axis=0, tiled=True)  23.1 us
    all_to_all x1, blocking collectives, exchange(): return lax.all_to_all(blocks, axis, split_axis=0, concat_axis=0, tiled=True)  17.4 us
    all_to_all x4, waiting for transfers between devices, exchange(): return lax.all_to_all(blocks, axis, split_axis=0, concat_axis=0, tiled=True)  16.9 us
    dot_general x3, matrix products, product_left_t(): lax.dot_general(left_side, right_side, (((0,), (0,)), ((), ())), preferre...  9.83 us
    dot_general x2, matrix products, product_right_t(): lax.dot_general(left_side, right_side, (((1,), (1,)), ((), ())), preferre...  5.26 us
  transfers between devices with their start and end apart: 31, of which 20 were waited for; matrix products, arithmetic and copies ran while one was open for 17% of the time, Pallas kernels for 0%

profile of v13, /device:TPU:2, one launch (start us, length us, event | category | flops | bytes accessed | tf_op | source)
XLA Modules:
  0.0 196.9 jit_solution(5419957911107258139)
XLA Ops:
  9.0 8.5 %all-to-all-start = ((bf16[8,32,1024]{2,1,0:T(8,128)(2,1)}), bf16[8,32,1024]{2,1,0:T(8,128)(2,1)S(1)}, u32[]{:S(2)}, u32[]{:S(2)}) async-start(bf16[8,32,1024]{2,1,0:T(8,128)(2,1)} %broadcast_in_dim.4), calls=%async_computation | async-start | bytes 1048576 | tf_op jit(solution)/shard_map/all_to_all | solution.py:30
  20.9 2.0 %collective-permute-start.1 = (bf16[32,1024]{1,0:T(8,128)(2,1)}, bf16[32,1024]{1,0:T(8,128)(2,1)S(1)}, u32[]{:S(2)}, u32[]{:S(2)}) collective-permute-start(bf16[32,1024]{1,0:T(8,128)(2,1)} %param.9), channel_id=1, source_target_pairs={{0,16},{8,24},{16,0},{24,8},{1,17},{9,25},{17,1},{25,9},{2,18},{10... | collective-permute-start | bytes 196616 | tf_op jit(solution)/shard_map/ppermute | solution.py:26
  24.0 2.8 %collective-permute-done.1 = bf16[32,1024]{1,0:T(8,128)(2,1)S(1)} collective-permute-done((bf16[32,1024]{1,0:T(8,128)(2,1)}, bf16[32,1024]{1,0:T(8,128)(2,1)S(1)}, u32[]{:S(2)}, u32[]{:S(2)}) %collective-permute-start.1) | collective-permute-done | bytes 65568 | tf_op jit(solution)/shard_map/ppermute | solution.py:26
  28.5 6.5 %all-to-all-done = bf16[8,32,1024]{2,1,0:T(8,128)(2,1)S(1)} async-done(((bf16[8,32,1024]{2,1,0:T(8,128)(2,1)}), bf16[8,32,1024]{2,1,0:T(8,128)(2,1)S(1)}, u32[]{:S(2)}, u32[]{:S(2)}) %all-to-all-start) | async-done | bytes 524320 | tf_op jit(solution)/shard_map/all_to_all | solution.py:30
  40.4 2.9 %collective-permute-start.8 = (bf16[128,1024]{1,0:T(8,128)(2,1)S(1)}, bf16[128,1024]{1,0:T(8,128)(2,1)S(1)}, u32[]{:S(2)}, u32[]{:S(2)}) collective-permute-start(bf16[128,1024]{1,0:T(8,128)(2,1)S(1)} %get-tuple-element.83), channel_id=1, source_target_pairs={{0,24},{8,0},{16,8},{24,16},{1,25},{9,1},{17,9},{25,17},{2,26},{10... | collective-permute-start | bytes 786440 | tf_op jit(solution)/shard_map/ppermute | solution.py:26
  43.3 2.2 %collective-permute-done.3 = bf16[128,1024]{1,0:T(8,128)(2,1)S(1)} collective-permute-done((bf16[128,1024]{1,0:T(8,128)(2,1)S(1)}, bf16[128,1024]{1,0:T(8,128)(2,1)S(1)}, u32[]{:S(2)}, u32[]{:S(2)}) %collective-permute-start.3) | collective-permute-done | bytes 262176 | tf_op jit(solution)/shard_map/ppermute | solution.py:26
  46.1 2.9 %collective-permute-start.7 = (bf16[128,1024]{1,0:T(8,128)(2,1)S(1)}, bf16[128,1024]{1,0:T(8,128)(2,1)S(1)}, u32[]{:S(2)}, u32[]{:S(2)}) collective-permute-start(bf16[128,1024]{1,0:T(8,128)(2,1)S(1)} %collective-permute-done.6), channel_id=1, source_target_pairs={{0,24},{8,0},{16,8},{24,16},{1,25},{9,1},{17,9},{25,17},{2,26},{10... | collective-permute-start | bytes 786440 | tf_op jit(solution)/shard_map/ppermute | solution.py:26
  49.0 2.1 %collective-permute-done.4 = bf16[128,1024]{1,0:T(8,128)(2,1)S(1)} collective-permute-done((bf16[128,1024]{1,0:T(8,128)(2,1)S(1)}, bf16[128,1024]{1,0:T(8,128)(2,1)S(1)}, u32[]{:S(2)}, u32[]{:S(2)}) %collective-permute-start.4) | collective-permute-done | bytes 262176 | tf_op jit(solution)/shard_map/ppermute | solution.py:26
  51.1 4.7 %collective-permute-done.5 = bf16[128,1024]{1,0:T(8,128)(2,1)S(1)} collective-permute-done((bf16[128,1024]{1,0:T(8,128)(2,1)S(1)}, bf16[128,1024]{1,0:T(8,128)(2,1)S(1)}, u32[]{:S(2)}, u32[]{:S(2)}) %collective-permute-start.5) | collective-permute-done | bytes 262176 | tf_op jit(solution)/shard_map/ppermute | solution.py:26
  56.2 2.3 %convolution_convert_fusion.2 = bf16[1024,1024]{1,0:T(8,128)(2,1)S(1)} fusion(bf16[1024,1024]{1,0:T(8,128)(2,1)S(1)} %constant_dynamic-update-slice_fusion, bf16[1024,1024]{1,0:T(8,128)(2,1)S(1)} %copy-done.12), kind=kOutput, calls=%fused_computation.3 | convolution fusion | flops 2148532224 | bytes 6291456 | tf_op jit(solution)/shard_map/dot_general | solution.py:13
  59.8 3.0 %collective-permute-done.9 = bf16[512,1024]{1,0:T(8,128)(2,1)} collective-permute-done((bf16[512,1024]{1,0:T(8,128)(2,1)}, bf16[512,1024]{1,0:T(8,128)(2,1)}, u32[]{:S(2)}, u32[]{:S(2)}) %collective-permute-start.9) | collective-permute-done | bytes 1048608 | tf_op jit(solution)/shard_map/ppermute | solution.py:26
  62.8 2.2 %add_convert_fusion.5 = (bf16[128,1024]{1,0:T(8,128)(2,1)S(1)}, bf16[128,1024]{1,0:T(8,128)(2,1)}, bf16[128,1024]{1,0:T(8,128)(2,1)}) fusion(bf16[512,1024]{1,0:T(8,128)(2,1)} %collective-permute-done.9, s32[]{:T(128)S(6)} %select_n.86, bf16[1024,1024]{1,0:T(8,128)(2,1)S(1)} %convolution_convert_fusion.2, s32[]{:T(128)S(6)} %select_n.85, s32[]{:T(128)S(6)} %select_n.84, ...), kind=kLoop, calls=%fused_computation.27 | loop fusion | flops 1572864 | bytes 2359320 | tf_op jit(solution)/shard_map/convert_element_type | solution.py:89
  67.6 2.1 %collective-permute-start.13 = (bf16[128,1024]{1,0:T(8,128)(2,1)S(1)}, bf16[128,1024]{1,0:T(8,128)(2,1)}, u32[]{:S(2)}, u32[]{:S(2)}) collective-permute-start(bf16[128,1024]{1,0:T(8,128)(2,1)S(1)} %get-tuple-element.33), channel_id=1, source_target_pairs={{0,192},{64,0},{128,64},{192,128},{1,193},{65,1},{129,65},{193,129... | collective-permute-start | bytes 786440 | tf_op jit(solution)/shard_map/ppermute | solution.py:26
  70.3 2.9 %convolution_convert_fusion.3 = bf16[1024,512]{1,0:T(8,128)(2,1)S(1)} fusion(bf16[1024,1024]{1,0:T(8,128)(2,1)} %bitcast.55, bf16[512,1024]{1,0:T(8,128)(2,1)S(1)} %copy-done), kind=kOutput, calls=%fused_computation.4 | convolution fusion | flops 1074266112 | bytes 4194304 | tf_op jit(solution)/shard_map/dot_general | solution.py:17
  74.4 3.0 %collective-permute-done.12 = bf16[128,1024]{1,0:T(8,128)(2,1)S(1)} collective-permute-done((bf16[128,1024]{1,0:T(8,128)(2,1)}, bf16[128,1024]{1,0:T(8,128)(2,1)S(1)}, u32[]{:S(2)}, u32[]{:S(2)}) %collective-permute-start.12) | collective-permute-done | bytes 262176 | tf_op jit(solution)/shard_map/ppermute | solution.py:26
  78.1 3.0 %collective-permute-done.13 = bf16[128,1024]{1,0:T(8,128)(2,1)} collective-permute-done((bf16[128,1024]{1,0:T(8,128)(2,1)S(1)}, bf16[128,1024]{1,0:T(8,128)(2,1)}, u32[]{:S(2)}, u32[]{:S(2)}) %collective-permute-start.13) | collective-permute-done | bytes 262176 | tf_op jit(solution)/shard_map/ppermute | solution.py:26
  82.7 2.1 %collective-permute-start.15 = (bf16[128,512]{1,0:T(8,128)(2,1)S(1)}, bf16[128,512]{1,0:T(8,128)(2,1)S(1)}, u32[]{:S(2)}, u32[]{:S(2)}) collective-permute-start(bf16[128,512]{1,0:T(8,128)(2,1)S(1)} %multiply_convert_fusion.2), channel_id=1, source_target_pairs={{0,128},{64,192},{128,0},{192,64},{1,129},{65,193},{129,1},{193,65... | collective-permute-start | bytes 393224 | tf_op jit(solution)/shard_map/ppermute | solution.py:26
  87.8 6.2 %all-to-all-start.1 = ((bf16[4,128,512]{2,1,0:T(8,128)(2,1)}), bf16[4,128,512]{2,1,0:T(8,128)(2,1)S(1)}, u32[]{:S(2)}, u32[]{:S(2)}) async-start(bf16[4,128,512]{2,1,0:T(8,128)(2,1)} %bitcast.11), calls=%async_computation.1 | async-start | bytes 1048576 | tf_op jit(solution)/shard_map/all_to_all | solution.py:30
  97.1 3.5 %all-to-all-done.1 = bf16[4,128,512]{2,1,0:T(8,128)(2,1)S(1)} async-done(((bf16[4,128,512]{2,1,0:T(8,128)(2,1)}), bf16[4,128,512]{2,1,0:T(8,128)(2,1)S(1)}, u32[]{:S(2)}, u32[]{:S(2)}) %all-to-all-start.1) | async-done | bytes 524320 | tf_op jit(solution)/shard_map/all_to_all | solution.py:30
  102.0 4.9 %all-to-all-start.2 = ((bf16[4,128,1024]{2,1,0:T(8,128)(2,1)}), bf16[4,128,1024]{2,1,0:T(8,128)(2,1)S(1)}, u32[]{:S(2)}, u32[]{:S(2)}) async-start(bf16[4,128,1024]{2,1,0:T(8,128)(2,1)} %broadcast_in_dim.5), calls=%async_computation.2 | async-start | bytes 2097152 | tf_op jit(solution)/shard_map/all_to_all | solution.py:30
  112.9 11.9 %collective-permute-done.18 = bf16[256,1024]{1,0:T(8,128)(2,1)S(1)} collective-permute-done((bf16[256,1024]{1,0:T(8,128)(2,1)S(1)}, bf16[256,1024]{1,0:T(8,128)(2,1)S(1)}, u32[]{:S(2)}, u32[]{:S(2)}) %collective-permute-start.18) | collective-permute-done | bytes 524320 | tf_op jit(solution)/shard_map/ppermute | solution.py:26
  128.8 1.9 collective-permute-start.22
  131.1 6.3 %collective-permute-done.21 = bf16[128,1024]{1,0:T(8,128)(2,1)S(1)} collective-permute-done((bf16[128,1024]{1,0:T(8,128)(2,1)S(1)}, bf16[128,1024]{1,0:T(8,128)(2,1)S(1)}, u32[]{:S(2)}, u32[]{:S(2)}) %collective-permute-start.21) | collective-permute-done | bytes 262176 | tf_op jit(solution)/shard_map/ppermute | solution.py:26
  137.4 2.4 %convolution_convert_fusion = bf16[1024,1024]{1,0:T(8,128)(2,1)S(1)} fusion(bf16[1024,1024]{1,0:T(8,128)(2,1)S(1)} %pad_maximum_fusion, bf16[1024,1024]{1,0:T(8,128)(2,1)S(1)} %copy-done.13), kind=kOutput, calls=%fused_computation.1 | convolution fusion | flops 2148532224 | bytes 6291456 | tf_op jit(solution)/shard_map/dot_general | solution.py:17
  141.0 3.2 %collective-permute-start.23 = (bf16[256,1024]{1,0:T(8,128)(2,1)}, bf16[256,1024]{1,0:T(8,128)(2,1)}, u32[]{:S(2)}, u32[]{:S(2)}) collective-permute-start(bf16[256,1024]{1,0:T(8,128)(2,1)} %get-tuple-element.41), channel_id=1, source_target_pairs={{0,24},{8,0},{16,8},{24,16},{1,25},{9,1},{17,9},{25,17},{2,26},{10... | collective-permute-start | bytes 1572872 | tf_op jit(solution)/shard_map/ppermute | solution.py:26
  147.0 3.5 %all-to-all-start.3 = ((bf16[8,32,1024]{2,1,0:T(8,128)(2,1)}), bf16[8,32,1024]{2,1,0:T(8,128)(2,1)S(1)}, u32[]{:S(2)}, u32[]{:S(2)}) async-start(bf16[8,32,1024]{2,1,0:T(8,128)(2,1)} %bitcast.25), calls=%async_computation.3 | async-start | bytes 1048576 | tf_op jit(solution)/shard_map/all_to_all | solution.py:30
  150.5 4.6 %fusion.1 = f32[1024,512]{1,0:T(8,128)} fusion(bf16[1024,1024]{1,0:T(8,128)(2,1)} %copy-done.21, bf16[1024,1024]{1,0:T(8,128)(2,1)} %copy-done.5), kind=kOutput, calls=%fused_computation.11 | convolution fusion | flops 1073741824 | bytes 5242880 | tf_op jit(solution)/shard_map/dot_general | solution.py:21
  155.2 2.6 %fusion.3 = f32[1024,512]{1,0:T(8,128)} fusion(bf16[1024,1024]{1,0:T(8,128)(2,1)S(1)} %copy-done.22, bf16[1024,1024]{1,0:T(8,128)(2,1)S(1)} %copy-done.6), kind=kOutput, calls=%fused_computation.13 | convolution fusion | flops 1073741824 | bytes 5242880 | tf_op jit(solution)/shard_map/dot_general | solution.py:21
  157.8 2.6 %fusion.9 = f32[512,1024]{1,0:T(8,128)} fusion(bf16[1024,512]{1,0:T(8,128)(2,1)S(1)} %pad_maximum_fusion.1, bf16[1024,1024]{1,0:T(8,128)(2,1)S(1)} %bitcast.48), kind=kOutput, calls=%fused_computation.58 | convolution fusion | flops 1073741824 | bytes 5242880 | tf_op jit(solution)/shard_map/dot_general | solution.py:21
  160.4 6.9 %all-to-all-done.3 = bf16[8,32,1024]{2,1,0:T(8,128)(2,1)S(1)} async-done(((bf16[8,32,1024]{2,1,0:T(8,128)(2,1)}), bf16[8,32,1024]{2,1,0:T(8,128)(2,1)S(1)}, u32[]{:S(2)}, u32[]{:S(2)}) %all-to-all-start.3) | async-done | bytes 524320 | tf_op jit(solution)/shard_map/all_to_all | solution.py:30
  168.0 2.2 %collective-permute-done.24 = bf16[256,1024]{1,0:T(8,128)(2,1)} collective-permute-done((bf16[256,1024]{1,0:T(8,128)(2,1)}, bf16[256,1024]{1,0:T(8,128)(2,1)}, u32[]{:S(2)}, u32[]{:S(2)}) %collective-permute-start.24) | collective-permute-done | bytes 524320 | tf_op jit(solution)/shard_map/ppermute | solution.py:26
  171.9 17.4 %all_to_all.48 = bf16[8,32,1024]{2,1,0:T(8,128)(2,1)S(1)} all-to-all(bf16[8,32,1024]{2,1,0:T(8,128)(2,1)S(1)} %bitcast.54), channel_id=1, replica_groups=mesh['x'=4,'core'=2,'y'=4,'z'=8] {'z'}, dimensions={0} | all-to-all | bytes 1048576 | tf_op jit(solution)/shard_map/all_to_all | solution.py:30
  (129 shorter events, 47.0 us)
Async XLA Ops:
  7.2 63.2 %copy-start = (bf16[512,1024]{1,0:T(8,128)(2,1)S(1)}, bf16[512,1024]{1,0:T(8,128)(2,1)}, u32[]{:S(2)}) copy-start(bf16[512,1024]{1,0:T(8,128)(2,1)} %param.8) | copy-start | bytes 3145732
  9.0 26.0 %all-to-all-start = ((bf16[8,32,1024]{2,1,0:T(8,128)(2,1)}), bf16[8,32,1024]{2,1,0:T(8,128)(2,1)S(1)}, u32[]{:S(2)}, u32[]{:S(2)}) async-start(bf16[8,32,1024]{2,1,0:T(8,128)(2,1)} %broadcast_in_dim.4), calls=%async_computation | async-start | bytes 1048576 | tf_op jit(solution)/shard_map/all_to_all | solution.py:30
  17.5 52.8 %all-gather.3.cloned.1.call-start = ((), (), s32[]{:S(2)}) async-start(), calls=%async_computation.5 | async-start | bytes 2359296 | tf_op jit(solution)/shard_map/all_gather | solution.py:163
  17.5 5.8 %collective-permute-start = (bf16[32,1024]{1,0:T(8,128)(2,1)}, bf16[32,1024]{1,0:T(8,128)(2,1)S(1)}, u32[]{:S(2)}, u32[]{:S(2)}) collective-permute-start(bf16[32,1024]{1,0:T(8,128)(2,1)} %param.9), channel_id=1, source_target_pairs={{0,8},{8,16},{16,24},{24,0},{1,9},{9,17},{17,25},{25,1},{2,10},{10... | collective-permute-start | bytes 196616 | tf_op jit(solution)/shard_map/ppermute | solution.py:26
  19.2 4.9 %collective-permute-start.2 = (bf16[32,1024]{1,0:T(8,128)(2,1)}, bf16[32,1024]{1,0:T(8,128)(2,1)S(1)}, u32[]{:S(2)}, u32[]{:S(2)}) collective-permute-start(bf16[32,1024]{1,0:T(8,128)(2,1)} %param.9), channel_id=1, source_target_pairs={{0,24},{8,0},{16,8},{24,16},{1,25},{9,1},{17,9},{25,17},{2,26},{10... | collective-permute-start | bytes 196616 | tf_op jit(solution)/shard_map/ppermute | solution.py:26
  20.9 6.0 %collective-permute-start.1 = (bf16[32,1024]{1,0:T(8,128)(2,1)}, bf16[32,1024]{1,0:T(8,128)(2,1)S(1)}, u32[]{:S(2)}, u32[]{:S(2)}) collective-permute-start(bf16[32,1024]{1,0:T(8,128)(2,1)} %param.9), channel_id=1, source_target_pairs={{0,16},{8,24},{16,0},{24,8},{1,17},{9,25},{17,1},{25,9},{2,18},{10... | collective-permute-start | bytes 196616 | tf_op jit(solution)/shard_map/ppermute | solution.py:26
  35.0 10.5 %collective-permute-start.3 = (bf16[128,1024]{1,0:T(8,128)(2,1)S(1)}, bf16[128,1024]{1,0:T(8,128)(2,1)S(1)}, u32[]{:S(2)}, u32[]{:S(2)}) collective-permute-start(bf16[128,1024]{1,0:T(8,128)(2,1)S(1)} %get-tuple-element.83), channel_id=1, source_target_pairs={{0,8},{8,16},{16,24},{24,0},{1,9},{9,17},{17,25},{25,1},{2,10},{10... | collective-permute-start | bytes 786440 | tf_op jit(solution)/shard_map/ppermute | solution.py:26
  36.8 9.3 %collective-permute-start.6 = (bf16[128,1024]{1,0:T(8,128)(2,1)S(1)}, bf16[128,1024]{1,0:T(8,128)(2,1)S(1)}, u32[]{:S(2)}, u32[]{:S(2)}) collective-permute-start(bf16[128,1024]{1,0:T(8,128)(2,1)S(1)} %get-tuple-element.82), channel_id=1, source_target_pairs={{0,24},{8,0},{16,8},{24,16},{1,25},{9,1},{17,9},{25,17},{2,26},{10... | collective-permute-start | bytes 786440 | tf_op jit(solution)/shard_map/ppermute | solution.py:26
  38.6 12.5 %collective-permute-start.4 = (bf16[128,1024]{1,0:T(8,128)(2,1)S(1)}, bf16[128,1024]{1,0:T(8,128)(2,1)S(1)}, u32[]{:S(2)}, u32[]{:S(2)}) collective-permute-start(bf16[128,1024]{1,0:T(8,128)(2,1)S(1)} %get-tuple-element.82), channel_id=1, source_target_pairs={{0,8},{8,16},{16,24},{24,0},{1,9},{9,17},{17,25},{25,1},{2,10},{10... | collective-permute-start | bytes 786440 | tf_op jit(solution)/shard_map/ppermute | solution.py:26
  40.4 15.7 %collective-permute-start.8 = (bf16[128,1024]{1,0:T(8,128)(2,1)S(1)}, bf16[128,1024]{1,0:T(8,128)(2,1)S(1)}, u32[]{:S(2)}, u32[]{:S(2)}) collective-permute-start(bf16[128,1024]{1,0:T(8,128)(2,1)S(1)} %get-tuple-element.83), channel_id=1, source_target_pairs={{0,24},{8,0},{16,8},{24,16},{1,25},{9,1},{17,9},{25,17},{2,26},{10... | collective-permute-start | bytes 786440 | tf_op jit(solution)/shard_map/ppermute | solution.py:26
  45.5 10.4 %collective-permute-start.5 = (bf16[128,1024]{1,0:T(8,128)(2,1)S(1)}, bf16[128,1024]{1,0:T(8,128)(2,1)S(1)}, u32[]{:S(2)}, u32[]{:S(2)}) collective-permute-start(bf16[128,1024]{1,0:T(8,128)(2,1)S(1)} %collective-permute-done.3), channel_id=1, source_target_pairs={{0,8},{8,16},{16,24},{24,0},{1,9},{9,17},{17,25},{25,1},{2,10},{10... | collective-permute-start | bytes 786440 | tf_op jit(solution)/shard_map/ppermute | solution.py:26
  46.1 10.0 %collective-permute-start.7 = (bf16[128,1024]{1,0:T(8,128)(2,1)S(1)}, bf16[128,1024]{1,0:T(8,128)(2,1)S(1)}, u32[]{:S(2)}, u32[]{:S(2)}) collective-permute-start(bf16[128,1024]{1,0:T(8,128)(2,1)S(1)} %collective-permute-done.6), channel_id=1, source_target_pairs={{0,24},{8,0},{16,8},{24,16},{1,25},{9,1},{17,9},{25,17},{2,26},{10... | collective-permute-start | bytes 786440 | tf_op jit(solution)/shard_map/ppermute | solution.py:26
  59.8 3.0 %collective-permute-start.9 = (bf16[512,1024]{1,0:T(8,128)(2,1)}, bf16[512,1024]{1,0:T(8,128)(2,1)}, u32[]{:S(2)}, u32[]{:S(2)}) collective-permute-start(bf16[512,1024]{1,0:T(8,128)(2,1)} %constant_dynamic-slice_fusion), channel_id=1, source_target_pairs={{0,32},{32,0},{1,33},{33,1},{2,34},{34,2},{3,35},{35,3},{4,36},{36... | collective-permute-start | bytes 3145736 | tf_op jit(solution)/shard_map/ppermute | solution.py:26
  65.0 9.4 %collective-permute-start.11 = (bf16[128,1024]{1,0:T(8,128)(2,1)}, bf16[128,1024]{1,0:T(8,128)(2,1)S(1)}, u32[]{:S(2)}, u32[]{:S(2)}) collective-permute-start(bf16[128,1024]{1,0:T(8,128)(2,1)} %get-tuple-element.31), channel_id=1, source_target_pairs={{0,64},{64,128},{128,192},{192,0},{1,65},{65,129},{129,193},{193,1... | collective-permute-start | bytes 786440 | tf_op jit(solution)/shard_map/ppermute | solution.py:26
  66.5 10.9 %collective-permute-start.12 = (bf16[128,1024]{1,0:T(8,128)(2,1)}, bf16[128,1024]{1,0:T(8,128)(2,1)S(1)}, u32[]{:S(2)}, u32[]{:S(2)}) collective-permute-start(bf16[128,1024]{1,0:T(8,128)(2,1)} %get-tuple-element.32), channel_id=1, source_target_pairs={{0,128},{64,192},{128,0},{192,64},{1,129},{65,193},{129,1},{193,65... | collective-permute-start | bytes 786440 | tf_op jit(solution)/shard_map/ppermute | solution.py:26
  67.6 13.5 %collective-permute-start.13 = (bf16[128,1024]{1,0:T(8,128)(2,1)S(1)}, bf16[128,1024]{1,0:T(8,128)(2,1)}, u32[]{:S(2)}, u32[]{:S(2)}) collective-permute-start(bf16[128,1024]{1,0:T(8,128)(2,1)S(1)} %get-tuple-element.33), channel_id=1, source_target_pairs={{0,192},{64,0},{128,64},{192,128},{1,193},{65,1},{129,65},{193,129... | collective-permute-start | bytes 786440 | tf_op jit(solution)/shard_map/ppermute | solution.py:26
  73.4 13.4 %collective-permute-start.10 = (bf16[512,512]{1,0:T(8,128)(2,1)S(1)}, bf16[512,512]{1,0:T(8,128)(2,1)S(1)}, u32[]{:S(2)}, u32[]{:S(2)}) collective-permute-start(bf16[512,512]{1,0:T(8,128)(2,1)S(1)} %bitcast.58), channel_id=1, source_target_pairs={{0,32},{32,0},{1,33},{33,1},{2,34},{34,2},{3,35},{35,3},{4,36},{36... | collective-permute-start | bytes 1572872 | tf_op jit(solution)/shard_map/ppermute | solution.py:26
  82.7 11.4 %collective-permute-start.15 = (bf16[128,512]{1,0:T(8,128)(2,1)S(1)}, bf16[128,512]{1,0:T(8,128)(2,1)S(1)}, u32[]{:S(2)}, u32[]{:S(2)}) collective-permute-start(bf16[128,512]{1,0:T(8,128)(2,1)S(1)} %multiply_convert_fusion.2), channel_id=1, source_target_pairs={{0,128},{64,192},{128,0},{192,64},{1,129},{65,193},{129,1},{193,65... | collective-permute-start | bytes 393224 | tf_op jit(solution)/shard_map/ppermute | solution.py:26
  84.8 9.3 %collective-permute-start.14 = (bf16[128,512]{1,0:T(8,128)(2,1)S(1)}, bf16[128,512]{1,0:T(8,128)(2,1)S(1)}, u32[]{:S(2)}, u32[]{:S(2)}) collective-permute-start(bf16[128,512]{1,0:T(8,128)(2,1)S(1)} %multiply_convert_fusion.2), channel_id=1, source_target_pairs={{0,64},{64,128},{128,192},{192,0},{1,65},{65,129},{129,193},{193,1... | collective-permute-start | bytes 393224 | tf_op jit(solution)/shard_map/ppermute | solution.py:26
  85.7 8.3 %collective-permute-start.16 = (bf16[128,512]{1,0:T(8,128)(2,1)S(1)}, bf16[128,512]{1,0:T(8,128)(2,1)}, u32[]{:S(2)}, u32[]{:S(2)}) collective-permute-start(bf16[128,512]{1,0:T(8,128)(2,1)S(1)} %multiply_convert_fusion.2), channel_id=1, source_target_pairs={{0,192},{64,0},{128,64},{192,128},{1,193},{65,1},{129,65},{193,129... | collective-permute-start | bytes 393224 | tf_op jit(solution)/shard_map/ppermute | solution.py:26
  87.8 12.9 %all-to-all-start.1 = ((bf16[4,128,512]{2,1,0:T(8,128)(2,1)}), bf16[4,128,512]{2,1,0:T(8,128)(2,1)S(1)}, u32[]{:S(2)}, u32[]{:S(2)}) async-start(bf16[4,128,512]{2,1,0:T(8,128)(2,1)} %bitcast.11), calls=%async_computation.1 | async-start | bytes 1048576 | tf_op jit(solution)/shard_map/all_to_all | solution.py:30
  100.6 6.3 %collective-permute-start.17 = (bf16[512,512]{1,0:T(8,128)(2,1)S(1)}, bf16[512,512]{1,0:T(8,128)(2,1)}, u32[]{:S(2)}, u32[]{:S(2)}) collective-permute-start(bf16[512,512]{1,0:T(8,128)(2,1)S(1)} %pad_maximum_fusion.3), channel_id=1, source_target_pairs={{0,32},{32,0},{1,33},{33,1},{2,34},{34,2},{3,35},{35,3},{4,36},{36... | collective-permute-start | bytes 1572872 | tf_op jit(solution)/shard_map/ppermute | solution.py:26
  102.0 24.0 %all-to-all-start.2 = ((bf16[4,128,1024]{2,1,0:T(8,128)(2,1)}), bf16[4,128,1024]{2,1,0:T(8,128)(2,1)S(1)}, u32[]{:S(2)}, u32[]{:S(2)}) async-start(bf16[4,128,1024]{2,1,0:T(8,128)(2,1)} %broadcast_in_dim.5), calls=%async_computation.2 | async-start | bytes 2097152 | tf_op jit(solution)/shard_map/all_to_all | solution.py:30
  109.5 15.3 %collective-permute-start.18 = (bf16[256,1024]{1,0:T(8,128)(2,1)S(1)}, bf16[256,1024]{1,0:T(8,128)(2,1)S(1)}, u32[]{:S(2)}, u32[]{:S(2)}) collective-permute-start(bf16[256,1024]{1,0:T(8,128)(2,1)S(1)} %pad_maximum_fusion.4), channel_id=1, source_target_pairs={{0,8},{8,16},{16,24},{24,0},{1,9},{9,17},{17,25},{25,1},{2,10},{10... | collective-permute-start | bytes 1572872 | tf_op jit(solution)/shard_map/ppermute | solution.py:26
  111.2 13.9 %collective-permute-start.19 = (bf16[256,1024]{1,0:T(8,128)(2,1)S(1)}, bf16[256,1024]{1,0:T(8,128)(2,1)S(1)}, u32[]{:S(2)}, u32[]{:S(2)}) collective-permute-start(bf16[256,1024]{1,0:T(8,128)(2,1)S(1)} %pad_maximum_fusion.5), channel_id=1, source_target_pairs={{0,24},{8,0},{16,8},{24,16},{1,25},{9,1},{17,9},{25,17},{2,26},{10... | collective-permute-start | bytes 1572872 | tf_op jit(solution)/shard_map/ppermute | solution.py:26
  126.0 4.7 %collective-permute-start.20 = (bf16[512,1024]{1,0:T(8,128)(2,1)S(1)}, bf16[512,1024]{1,0:T(8,128)(2,1)S(1)}, u32[]{:S(2)}, u32[]{:S(2)}) collective-permute-start(bf16[512,1024]{1,0:T(8,128)(2,1)S(1)} %bitcast.51), channel_id=1, source_target_pairs={{0,32},{32,0},{1,33},{33,1},{2,34},{34,2},{3,35},{35,3},{4,36},{36... | collective-permute-start | bytes 3145736 | tf_op jit(solution)/shard_map/ppermute | solution.py:26
  127.4 10.0 %collective-permute-start.21 = (bf16[128,1024]{1,0:T(8,128)(2,1)S(1)}, bf16[128,1024]{1,0:T(8,128)(2,1)S(1)}, u32[]{:S(2)}, u32[]{:S(2)}) collective-permute-start(bf16[128,1024]{1,0:T(8,128)(2,1)S(1)} %copy-done.20), channel_id=1, source_target_pairs={{0,8},{8,16},{16,24},{24,0},{1,9},{9,17},{17,25},{25,1},{2,10},{10... | collective-permute-start | bytes 786440 | tf_op jit(solution)/shard_map/ppermute | solution.py:26
  128.8 8.6 %collective-permute-start.22 = (bf16[128,1024]{1,0:T(8,128)(2,1)S(1)}, bf16[128,1024]{1,0:T(8,128)(2,1)S(1)}, u32[]{:S(2)}, u32[]{:S(2)}) collective-permute-start(bf16[128,1024]{1,0:T(8,128)(2,1)S(1)} %get-tuple-element.38), channel_id=1, source_target_pairs={{0,24},{8,0},{16,8},{24,16},{1,25},{9,1},{17,9},{25,17},{2,26},{10... | collective-permute-start | bytes 786440 | tf_op jit(solution)/shard_map/ppermute | solution.py:26
  141.0 26.9 %collective-permute-start.23 = (bf16[256,1024]{1,0:T(8,128)(2,1)}, bf16[256,1024]{1,0:T(8,128)(2,1)}, u32[]{:S(2)}, u32[]{:S(2)}) collective-permute-start(bf16[256,1024]{1,0:T(8,128)(2,1)} %get-tuple-element.41), channel_id=1, source_target_pairs={{0,24},{8,0},{16,8},{24,16},{1,25},{9,1},{17,9},{25,17},{2,26},{10... | collective-permute-start | bytes 1572872 | tf_op jit(solution)/shard_map/ppermute | solution.py:26
  144.2 26.0 %collective-permute-start.24 = (bf16[256,1024]{1,0:T(8,128)(2,1)}, bf16[256,1024]{1,0:T(8,128)(2,1)}, u32[]{:S(2)}, u32[]{:S(2)}) collective-permute-start(bf16[256,1024]{1,0:T(8,128)(2,1)} %get-tuple-element.42), channel_id=1, source_target_pairs={{0,8},{8,16},{16,24},{24,0},{1,9},{9,17},{17,25},{25,1},{2,10},{10... | collective-permute-start | bytes 1572872 | tf_op jit(solution)/shard_map/ppermute | solution.py:26
  144.2 26.0 %collective-permute-start.25 = (bf16[256,1024]{1,0:T(8,128)(2,1)}, bf16[256,1024]{1,0:T(8,128)(2,1)}, u32[]{:S(2)}, u32[]{:S(2)}) collective-permute-start(bf16[256,1024]{1,0:T(8,128)(2,1)} %get-tuple-element.43), channel_id=1, source_target_pairs={{0,16},{8,24},{16,0},{24,8},{1,17},{9,25},{17,1},{25,9},{2,18},{10... | collective-permute-start | bytes 1572872 | tf_op jit(solution)/shard_map/ppermute | solution.py:26
  147.0 20.2 %all-to-all-start.3 = ((bf16[8,32,1024]{2,1,0:T(8,128)(2,1)}), bf16[8,32,1024]{2,1,0:T(8,128)(2,1)S(1)}, u32[]{:S(2)}, u32[]{:S(2)}) async-start(bf16[8,32,1024]{2,1,0:T(8,128)(2,1)} %bitcast.25), calls=%async_computation.3 | async-start | bytes 1048576 | tf_op jit(solution)/shard_map/all_to_all | solution.py:30
  (23 other events, 131.9 us)
Sparse Core Ops, SparseCore 0:
  28.6 41.6 all-gather.2
